TPU v7x, 32 devices: a whole 2x2x4 slice. The times are simulated.
32 devices in a mesh: seq: 8 (over y, x, core), mem: 4 (over z).
Axes of the slice: x: 2, y: 2, z: 4, core: 2. Of those that a mesh axis runs over, the one named last changes fastest.
Arguments:
- tokens: bfloat16 [32, 1024, 768], P(('seq', 'mem')), may hold values from -6 to 6
- memory: bfloat16 [32, 1024, 768], P('seq', 'mem')
- cotangent: bfloat16 [32, 1024, 768], P(('seq', 'mem'))
- table_len: int32 [32], P(('seq', 'mem')), may hold values from 512 to 1024, as said below
- patch_count: int32 [32], P(('seq', 'mem')), may hold values from 512 to 1024, as said below
- attn_master: float32 [8, 768, 768], P(None, ('seq', 'mem'))
- attn_first: float32 [8, 768, 768], P(None, ('seq', 'mem')), may hold values from -0.00048828125 to 0.00048828125
- attn_second: float32 [8, 768, 768], P(None, ('seq', 'mem')), may hold values from 5.2968973e-11 to 8.4750357e-10
- mlp_master: float32 [3, 768, 2048], P(None, ('seq', 'mem'))
- mlp_first: float32 [3, 768, 2048], P(None, ('seq', 'mem')), may hold values from -0.00048828125 to 0.00048828125
- mlp_second: float32 [3, 768, 2048], P(None, ('seq', 'mem')), may hold values from 5.2968973e-11 to 8.4750357e-10
- gain_master: float32 [3, 768], P(None, ('seq', 'mem'))
- gain_first: float32 [3, 768], P(None, ('seq', 'mem')), may hold values from -0.0017089844 to 0.0017089844
- gain_second: float32 [3, 768], P(None, ('seq', 'mem')), may hold values from 4.767208e-10 to 7.627532e-09
Outputs:
- mixed_out: bfloat16 [32, 1024, 768], P(('seq', 'mem'))
- grad_tokens: float32 [32, 1024, 768], P(('seq', 'mem'))
- grad_memory: float32 [32, 1024, 768], P('seq', 'mem')
- grad_norm: float32 [], replicated
- attn_new: float32 [8, 768, 768], P(None, ('seq', 'mem'))
- attn_first_new: float32 [8, 768, 768], P(None, ('seq', 'mem'))
- attn_second_new: float32 [8, 768, 768], P(None, ('seq', 'mem'))
- mlp_new: float32 [3, 768, 2048], P(None, ('seq', 'mem'))
- mlp_first_new: float32 [3, 768, 2048], P(None, ('seq', 'mem'))
- mlp_second_new: float32 [3, 768, 2048], P(None, ('seq', 'mem'))
- gain_new: float32 [3, 768], P(None, ('seq', 'mem'))
- gain_first_new: float32 [3, 768], P(None, ('seq', 'mem'))
- gain_second_new: float32 [3, 768], P(None, ('seq', 'mem'))
Inputs may be any that keep to these rules, and one draw needn't show every extreme that they name: The tokens of table i fill its first table_len[i] slots; some table fills all 1024. The live patches of plot i are its first patch_count[i] slots; in each run of 4 plots starting at a multiple of 4, one plot has all 1024 live.
All inputs are finite; a program needn't handle non-finite values.
Results may differ from a plain program's by a relative error of at most 0.02.
The roundings to bfloat16 on the way count: a program that leaves them out, or rounds other values in their place, can miss the bound.
Values may be sent and summed in bfloat16 or wider, within the bound.
No kernel may reach another device: no remote copies, remote signals or barrier semaphores. Data moves between devices by JAX's collectives and lax.ppermute only.
A program may use at most 384 MiB of HBM per device.

v0:
```python
import jax
import jax.numpy as jnp
from jax import lax
from jax.sharding import PartitionSpec as P

HEADS = 12
HD = 64
STEP = 10


NORM_EPSILON = 1e-06
NEG_LARGE = -1e30
CLIP_NORM = 1.0
BETA_FIRST = 0.9
BETA_SECOND = 0.999
ADAM_EPSILON = 1e-08
RATE_MATRIX = 0.06
RATE_GAIN = 0.6
DECAY_MATRIX = 0.01


def norm_apply(residual, gain_row):
    return (
        residual
        * lax.rsqrt(jnp.mean(residual * residual, axis=-1, keepdims=True) + NORM_EPSILON)
        * gain_row
    )


def norm_back(residual, gain_row, grad_normed):
    normed_value, pull_norm = jax.vjp(norm_apply, residual, gain_row)
    return pull_norm(grad_normed)


def gated_unit(gate_pre, up_pre):
    return jax.nn.gelu(gate_pre, approximate=True) * up_pre


def project(input_tokens, weight_matrix):
    return jnp.einsum(
        "xpu,uy->xpy", input_tokens, weight_matrix, preferred_element_type=jnp.float32
    )


def project_back(gradient_row_list, weight_matrix):
    return jnp.einsum(
        "vhf,yf->vhy", gradient_row_list, weight_matrix, preferred_element_type=jnp.float32
    )


def weight_grad(input_tokens, gradient_row_list):
    return jnp.einsum(
        "fyu,fyw->uw", input_tokens, gradient_row_list, preferred_element_type=jnp.float32
    )


def to_heads(array_in):
    return array_in.reshape(array_in.shape[0], array_in.shape[1], HEADS, HD)


def from_heads(array_in):
    return array_in.reshape(array_in.shape[0], array_in.shape[1], HEADS * HD)


def score_block(query_block, key_rows, allowed):
    scores = jnp.einsum(
        "sqhd,skhd->shqk", query_block, key_rows, preferred_element_type=jnp.float32
    ) * HD ** (-0.5)
    return jnp.where(allowed, scores, NEG_LARGE)


def key_limit(offset, block_rows, key_total, causal):
    if causal:
        return min(key_total, offset + block_rows)
    return key_total


def attend_forward(queries, key_rows, value_rows, allowed_fn, causal):
    row_count = queries.shape[1]
    block_rows = min(512, row_count)
    outputs = []
    totals = []
    for offset in range(0, row_count, block_rows):
        key_end = key_limit(offset, block_rows, key_rows.shape[1], causal)
        query_block = queries[:, offset : offset + block_rows]
        scores = score_block(
            query_block, key_rows[:, :key_end], allowed_fn(offset, block_rows, key_end)
        )
        row_peak = jnp.max(scores, axis=-1, keepdims=True)
        exponent = jnp.exp(scores - row_peak)
        row_total = jnp.sum(exponent, axis=-1, keepdims=True)
        weights_soft = (exponent / row_total).astype(jnp.bfloat16)
        outputs.append(
            jnp.einsum(
                "shqk,skhd->sqhd",
                weights_soft,
                value_rows[:, :key_end],
                preferred_element_type=jnp.float32,
            )
        )
        totals.append(row_peak + jnp.log(row_total))
    return (jnp.concatenate(outputs, axis=1), jnp.concatenate(totals, axis=2))


def attend_backward(queries, key_rows, value_rows, allowed_fn, causal, log_totals, grad_mixed):
    row_count = queries.shape[1]
    block_rows = min(512, row_count)
    grad_queries = []
    grad_keys = jnp.zeros(key_rows.shape, jnp.float32)
    grad_values = jnp.zeros(value_rows.shape, jnp.float32)
    for offset in range(0, row_count, block_rows):
        key_end = key_limit(offset, block_rows, key_rows.shape[1], causal)
        keys_used = key_rows[:, :key_end]
        values_used = value_rows[:, :key_end]
        query_block = queries[:, offset : offset + block_rows]
        grad_block = grad_mixed[:, offset : offset + block_rows]
        scores = score_block(query_block, keys_used, allowed_fn(offset, block_rows, key_end))
        weights_full = jnp.exp(scores - log_totals[:, :, offset : offset + block_rows])
        grad_weights = jnp.einsum(
            "sqhd,skhd->shqk", grad_block, values_used, preferred_element_type=jnp.float32
        )
        inner_sum = jnp.sum(weights_full * grad_weights, axis=-1, keepdims=True)
        grad_scores = (weights_full * (grad_weights - inner_sum)).astype(jnp.bfloat16)
        grad_queries.append(
            jnp.einsum(
                "shqk,skhd->sqhd", grad_scores, keys_used, preferred_element_type=jnp.float32
            )
            * HD ** (-0.5)
        )
        grad_keys = grad_keys.at[:, :key_end].add(
            jnp.einsum(
                "shqk,sqhd->skhd", grad_scores, query_block, preferred_element_type=jnp.float32
            )
            * HD ** (-0.5)
        )
        grad_values = grad_values.at[:, :key_end].add(
            jnp.einsum(
                "shqk,sqhd->skhd",
                weights_full.astype(jnp.bfloat16),
                grad_block,
                preferred_element_type=jnp.float32,
            )
        )
    return (jnp.concatenate(grad_queries, axis=1), grad_keys, grad_values)


def adam_step(master, grad, first, second, rate, decay):
    first_new = BETA_FIRST * first + (1.0 - BETA_FIRST) * grad
    second_new = BETA_SECOND * second + (1.0 - BETA_SECOND) * grad * grad
    first_hat = first_new / (1.0 - BETA_FIRST**STEP)
    second_hat = second_new / (1.0 - BETA_SECOND**STEP)
    master_new = master - rate * (
        first_hat / (jnp.sqrt(second_hat) + ADAM_EPSILON) + decay * master
    )
    return (master_new, first_new, second_new)


def on_device(
    tokens,
    memory,
    cotangent,
    table_len,
    patch_count,
    attn_master,
    attn_first,
    attn_second,
    mlp_master,
    mlp_first,
    mlp_second,
    gain_master,
    gain_first,
    gain_second,
):
    attention_complete, feedforward_complete, gain_full = (
        lax.all_gather(attn_master.astype(jnp.bfloat16), ("seq", "mem"), axis=1, tiled=True),
        lax.all_gather(mlp_master.astype(jnp.bfloat16), ("seq", "mem"), axis=1, tiled=True),
        lax.all_gather(gain_master.astype(jnp.bfloat16), ("seq", "mem"), axis=1, tiled=True),
    )
    gains = gain_full.astype(jnp.float32)
    seq_len = tokens.shape[1]
    positions = jnp.arange(seq_len, dtype=jnp.int32)
    token_live = positions[None, :] < table_len[:, None]

    def self_mask(offset, block_rows, key_end):
        query_index = offset + jnp.arange(block_rows, dtype=jnp.int32)
        causal = positions[None, :key_end] <= query_index[:, None]
        return (token_live[:, None, :key_end] & causal[None])[:, None]

    residual_in = tokens.astype(jnp.float32)
    first_normalized = norm_apply(residual_in, gains[0]).astype(jnp.bfloat16)
    self_proj = jnp.einsum(
        "bhf,gft->gbht",
        first_normalized,
        attention_complete[0:3],
        preferred_element_type=jnp.float32,
    ).astype(jnp.bfloat16)
    queries = to_heads(self_proj[0])
    key_rows = to_heads(self_proj[1])
    value_rows = to_heads(self_proj[2])
    mixed_float, self_totals = attend_forward(queries, key_rows, value_rows, self_mask, True)
    mixed_one = from_heads(mixed_float).astype(jnp.bfloat16)
    hidden_one = residual_in + project_back(mixed_one, attention_complete[3])
    local_kv = jnp.einsum(
        "gpd,jde->jgpe", memory, attention_complete[5:7], preferred_element_type=jnp.float32
    ).astype(jnp.bfloat16)
    memory_keys, memory_values = (
        lax.all_to_all(local_kv[0], "mem", split_axis=0, concat_axis=1, tiled=True),
        lax.all_to_all(local_kv[1], "mem", split_axis=0, concat_axis=1, tiled=True),
    )
    patch_index = jnp.arange(memory_keys.shape[1], dtype=jnp.int32)
    patch_live = (patch_index[None, :] < patch_count[:, None])[:, None, None, :]

    def cross_mask(offset, block_rows, key_end):
        return patch_live

    normed_two = norm_apply(hidden_one, gains[1]).astype(jnp.bfloat16)
    cross_queries = project(normed_two, attention_complete[4]).astype(jnp.bfloat16)
    cross_float, cross_totals = attend_forward(
        to_heads(cross_queries), to_heads(memory_keys), to_heads(memory_values), cross_mask, False
    )
    mixed_two = from_heads(cross_float).astype(jnp.bfloat16)
    hidden_two = hidden_one + project_back(mixed_two, attention_complete[7])
    third_normalized = norm_apply(hidden_two, gains[2]).astype(jnp.bfloat16)
    gate_up = jnp.einsum(
        "itz,czg->citg",
        third_normalized,
        feedforward_complete[0:2],
        preferred_element_type=jnp.float32,
    )
    inner_act = gated_unit(gate_up[0], gate_up[1]).astype(jnp.bfloat16)
    output = hidden_two + project_back(inner_act, feedforward_complete[2])
    mixed_out = output.astype(jnp.bfloat16)
    grad_out = cotangent.astype(jnp.float32) * token_live.astype(jnp.float32)[:, :, None]
    grad_branch_three = grad_out.astype(jnp.bfloat16)
    grad_down = weight_grad(grad_branch_three, inner_act)
    grad_inner = project(grad_branch_three, feedforward_complete[2])
    glu_value, glu_pull = jax.vjp(gated_unit, gate_up[0], gate_up[1])
    grad_gate, grad_up = glu_pull(grad_inner)
    grad_gate = grad_gate.astype(jnp.bfloat16)
    grad_up = grad_up.astype(jnp.bfloat16)
    grad_mlp = jnp.stack(
        [
            weight_grad(third_normalized, grad_gate),
            weight_grad(third_normalized, grad_up),
            grad_down,
        ]
    )
    grad_normed_three = project_back(grad_gate, feedforward_complete[0]) + project_back(
        grad_up, feedforward_complete[1]
    )
    grad_res_three, grad_gain_three = norm_back(hidden_two, gains[2], grad_normed_three)
    grad_hidden_two = grad_out + grad_res_three
    grad_branch_two = grad_hidden_two.astype(jnp.bfloat16)
    grad_out_cross = weight_grad(grad_branch_two, mixed_two)
    grad_mixed_two = project(grad_branch_two, attention_complete[7]).astype(jnp.bfloat16)
    grad_cq, grad_mk, grad_mv = attend_backward(
        to_heads(cross_queries),
        to_heads(memory_keys),
        to_heads(memory_values),
        cross_mask,
        False,
        cross_totals,
        to_heads(grad_mixed_two),
    )
    grad_cq = from_heads(grad_cq).astype(jnp.bfloat16)
    grad_mk = from_heads(grad_mk).astype(jnp.bfloat16)
    grad_mv = from_heads(grad_mv).astype(jnp.bfloat16)
    grad_cross_query = weight_grad(normed_two, grad_cq)
    back_keys, back_values = (
        lax.all_to_all(grad_mk, "mem", split_axis=1, concat_axis=0, tiled=True),
        lax.all_to_all(grad_mv, "mem", split_axis=1, concat_axis=0, tiled=True),
    )
    grad_key_weight = weight_grad(memory, back_keys)
    grad_value_weight = weight_grad(memory, back_values)
    grad_memory = project_back(back_keys, attention_complete[5]) + project_back(
        back_values, attention_complete[6]
    )
    grad_normed_two = project_back(grad_cq, attention_complete[4])
    grad_res_two, grad_gain_two = norm_back(hidden_one, gains[1], grad_normed_two)
    grad_hidden_one = grad_hidden_two + grad_res_two
    grad_branch_one = grad_hidden_one.astype(jnp.bfloat16)
    grad_out_self = weight_grad(grad_branch_one, mixed_one)
    grad_mixed_one = project(grad_branch_one, attention_complete[3]).astype(jnp.bfloat16)
    grad_sq, grad_sk, grad_sv = attend_backward(
        queries, key_rows, value_rows, self_mask, True, self_totals, to_heads(grad_mixed_one)
    )
    self_attention_gradient = jnp.stack(
        [from_heads(grad_sq), from_heads(grad_sk), from_heads(grad_sv)]
    ).astype(jnp.bfloat16)
    grad_self_weights = jnp.einsum(
        "nyw,xnyu->xwu",
        first_normalized,
        self_attention_gradient,
        preferred_element_type=jnp.float32,
    )
    grad_normed_one = jnp.einsum(
        "xtph,xvh->tpv",
        self_attention_gradient,
        attention_complete[0:3],
        preferred_element_type=jnp.float32,
    )
    grad_res_one, grad_gain_one = norm_back(residual_in, gains[0], grad_normed_one)
    grad_tokens = grad_hidden_one + grad_res_one
    grad_attn = jnp.concatenate(
        [
            grad_self_weights,
            jnp.stack(
                [
                    grad_out_self,
                    grad_cross_query,
                    grad_key_weight,
                    grad_value_weight,
                    grad_out_cross,
                ]
            ),
        ],
        axis=0,
    )
    grad_gain = jnp.stack([grad_gain_one, grad_gain_two, grad_gain_three])
    attn_reduced, mlp_reduced, gain_reduced = (
        lax.psum_scatter(grad_attn, ("seq", "mem"), scatter_dimension=1, tiled=True),
        lax.psum_scatter(grad_mlp, ("seq", "mem"), scatter_dimension=1, tiled=True),
        lax.psum_scatter(grad_gain, ("seq", "mem"), scatter_dimension=1, tiled=True),
    )
    squares = (
        jnp.sum(attn_reduced * attn_reduced)
        + jnp.sum(mlp_reduced * mlp_reduced)
        + jnp.sum(gain_reduced * gain_reduced)
    )
    grad_norm = jnp.sqrt(lax.psum(squares, ("seq", "mem")))
    factor = CLIP_NORM / jnp.maximum(grad_norm, CLIP_NORM)
    attn_new, attn_first_new, attn_second_new = adam_step(
        attn_master, attn_reduced * factor, attn_first, attn_second, RATE_MATRIX, DECAY_MATRIX
    )
    mlp_new, mlp_first_new, mlp_second_new = adam_step(
        mlp_master, mlp_reduced * factor, mlp_first, mlp_second, RATE_MATRIX, DECAY_MATRIX
    )
    gain_new, gain_first_new, gain_second_new = adam_step(
        gain_master, gain_reduced * factor, gain_first, gain_second, RATE_GAIN, 0.0
    )
    return (
        mixed_out,
        grad_tokens,
        grad_memory,
        grad_norm,
        attn_new,
        attn_first_new,
        attn_second_new,
        mlp_new,
        mlp_first_new,
        mlp_second_new,
        gain_new,
        gain_first_new,
        gain_second_new,
    )


def solution(mesh):
    return jax.shard_map(
        on_device,
        mesh=mesh,
        in_specs=(
            P(("seq", "mem"), None, None),
            P("seq", "mem", None),
            P(("seq", "mem"), None, None),
            P(("seq", "mem")),
            P(("seq", "mem")),
            P(None, ("seq", "mem"), None),
            P(None, ("seq", "mem"), None),
            P(None, ("seq", "mem"), None),
            P(None, ("seq", "mem"), None),
            P(None, ("seq", "mem"), None),
            P(None, ("seq", "mem"), None),
            P(None, ("seq", "mem")),
            P(None, ("seq", "mem")),
            P(None, ("seq", "mem")),
        ),
        out_specs=(
            P(("seq", "mem"), None, None),
            P(("seq", "mem"), None, None),
            P("seq", "mem", None),
            P(),
            P(None, ("seq", "mem"), None),
            P(None, ("seq", "mem"), None),
            P(None, ("seq", "mem"), None),
            P(None, ("seq", "mem"), None),
            P(None, ("seq", "mem"), None),
            P(None, ("seq", "mem"), None),
            P(None, ("seq", "mem")),
            P(None, ("seq", "mem")),
            P(None, ("seq", "mem")),
        ),
        check_vma=False,
    )
```

profile of v0, /device:TPU:0, one launch (start us, length us, event | category | flops | bytes accessed | tf_op | source)
XLA Modules:
  0.0 1080.0 jit_solution(15471196621385688391)
XLA Ops:
  13.8 70.4 %all-gather = bf16[32,24,3]{1,2,0:T(4,128)(2,1)S(1)} all-gather(bf16[1,24,3]{1,2,0:T(4,128)(2,1)S(1)} %convert_bitcast_fusion.2), channel_id=1, replica_groups=mesh['seq'=8,'mem'=4] {'seq','mem'}, dimensions={0}, use_global_device_ids=true | all-gather | bytes 4752 | tf_op jit(solution)/shard_map/all_gather | solution.py:177
  96.0 7.5 slice.360
  103.5 6.7 copy.297
  121.2 7.0 slice.351
  128.3 8.0 copy.295
  136.3 6.2 convert_bitcast_fusion
  144.2 10.7 fusion.22
  154.9 14.0 %fusion = f32[12,512]{1,0:T(8,128)S(1)} fusion(f32[12,512]{1,0:T(8,128)S(1)} %get-tuple-element.260, f32[12,512,1024]{2,1,0:T(8,128)} %get-tuple-element.261, pred[512,1024]{1,0:T(8,128)(4,1)S(1)} %copy-done.15), kind=kLoop, calls=%fused_computation.18 | loop fusion | flops 25159680 | bytes 25739264 | tf_op jit(solution)/shard_map/reduce_sum | solution.py:91
  168.9 29.1 %fusion.168 = (bf16[1,768,768]{2,0,1:T(2,128)(2,1)}, bf16[1,768,768]{2,0,1:T(2,128)(2,1)}, bf16[1,768,768]{2,0,1:T(2,128)(2,1)}, bf16[1,768,768]{2,0,1:T(2,128)(2,1)}, bf16[1,768,768]{2,0,1:T(2,128)(2,1)}) fusion(bf16[8,768,768]{2,0,1:T(8,128)(2,1)} %all-gather.4.cloned.1.call-done), kind=kLoop, calls=%fused_computation.276 | loop fusion | bytes 11796480 | tf_op jit(solution)/shard_map/slice | solution.py:276
  198.0 10.0 fusion.107
  222.9 7.1 fusion.104
  242.5 17.5 %all-to-all-done = bf16[4,256,768]{1,2,0:T(8,128)(2,1)} async-done(((bf16[4,256,768]{1,2,0:T(8,128)(2,1)}), bf16[4,256,768]{1,2,0:T(8,128)(2,1)}, u32[]{:S(2)}, u32[]{:S(2)}) %all-to-all-start) | async-done | bytes 1572896 | tf_op jit(solution)/shard_map/all_to_all | solution.py:208
  267.6 11.4 %fusion.124 = f32[12,512,1024]{2,1,0:T(8,128)} fusion(bf16[1024,12,64]{0,2,1:T(8,128)(2,1)S(1)} %reshape.1187, bf16[1,1024,12,64]{1,3,2,0:T(8,128)(2,1)} %bitcast.422), kind=kOutput, calls=%fused_computation.209 | convolution fusion | flops 805306368 | bytes 27525120 | tf_op jit(solution)/shard_map/sqhd,skhd->shqk/dot_general | solution.py:66
  279.0 16.6 %fusion.19 = (f32[12,512]{1,0:T(8,128)S(1)}, f32[12,512]{1,0:T(8,128)S(1)}, f32[12,512,1024]{2,1,0:T(8,128)}) fusion(pred[1024]{0:T(1024)(128)(4,1)S(1)} %iota_compare_fusion.2, f32[12,512,1024]{2,1,0:T(8,128)} %fusion.124, bf16[1024,12,64]{0,2,1:T(8,128)(2,1)S(1)} %reshape.1187, bf16[1,1024,12,64]{1,3,2,0:T(8,128)(2,1)} %bitcast.423), kind=kOutput, calls=%fused_computation.44 | convolution fusion | flops 843042816 | bytes 52741120 | tf_op jit(solution)/shard_map/sqhd,skhd->shqk/dot_general | solution.py:66
  295.6 18.7 %fusion.1 = (f32[12,512]{1,0:T(8,128)S(1)}, f32[12,512]{1,0:T(8,128)S(1)}) fusion(f32[12,512]{1,0:T(8,128)S(1)} %get-tuple-element.235, f32[12,512,1024]{2,1,0:T(8,128)} %get-tuple-element.266, pred[1024]{0:T(1024)(128)(4,1)S(1)} %iota_compare_fusion.2, f32[12,512]{1,0:T(8,128)S(1)} %get-tuple-element.236, f32[12,512,1024]{2,1,0:T(8,128)} %fusion.124), kind=kLoop, calls=%fused_computation.19 | loop fusion | flops 50319360 | bytes 50430976 | tf_op jit(solution)/shard_map/reduce_sum | solution.py:91
  314.3 11.1 %fusion.106 = bf16[12,64,512]{2,1,0:T(8,128)(2,1)S(1)} fusion(bf16[1024,12,64]{0,2,1:T(8,128)(2,1)S(1)} %copy-done.7, f32[12,512]{1,0:T(8,128)S(1)} %get-tuple-element.233, f32[12,512]{1,0:T(8,128)S(1)} %get-tuple-element.235, f32[12,512,1024]{2,1,0:T(8,128)} %get-tuple-element.266, pred[1024]{0:T(1024)(128)(4,1)S(1)} %iota_compare_fusion.2), kind=kOutput, calls=%fused_computation.175 | convolution fusion | flops 837156864 | bytes 27575296 | tf_op jit(solution)/shard_map/shqk,skhd->sqhd/dot_general | solution.py:94
  325.5 12.3 %fusion.105 = bf16[12,64,512]{2,1,0:T(8,128)(2,1)S(1)} fusion(bf16[1024,12,64]{0,2,1:T(8,128)(2,1)S(1)} %copy-done.7, f32[12,512]{1,0:T(8,128)S(1)} %get-tuple-element.234, f32[12,512]{1,0:T(8,128)S(1)} %get-tuple-element.236, f32[12,512,1024]{2,1,0:T(8,128)} %fusion.124, pred[1024]{0:T(1024)(128)(4,1)S(1)} %iota_compare_fusion.2), kind=kOutput, calls=%fused_computation.174 | convolution fusion | flops 837156864 | bytes 27575296 | tf_op jit(solution)/shard_map/shqk,skhd->sqhd/dot_general | solution.py:94
  342.4 9.7 fusion.45
  364.8 14.4 %fusion.29 = (bf16[1024,2048]{1,0:T(8,128)(2,1)S(1)}, bf16[1024,2048]{1,0:T(8,128)(2,1)}) fusion(f32[2,1,1024,2048]{3,2,0,1:T(8,128)} %bitcast.416, f32[2,1,1024,2048]{3,2,1,0:T(8,128)} %bitcast.417, bf16[3,768,2048]{2,1,0:T(8,128)(2,1)} %all-gather.6.cloned.1.call-done, bf16[1,1024,768]{1,2,0:T(8,128)(2,1)S(1)} %copy-done.30, f32[1024]{0:T(1024)S(1)} %copy-done.66), kind=kOutput, calls=%fused_computation.54 | convolution fusion | flops 3273916416 | bytes 29888512 | tf_op jit(solution)/shard_map/xpu,uy->xpy/dot_general | solution.py:40
  392.4 9.4 fusion.70
  410.2 6.8 pad_maximum_fusion
  417.0 13.1 %fusion.126 = f32[12,512,1024]{2,1,0:T(8,128)} fusion(bf16[1024,12,64]{0,2,1:T(8,128)(2,1)S(1)} %copy-done.7, bf16[1,1024,12,64]{1,3,2,0:T(8,128)(2,1)} %bitcast.439), kind=kOutput, calls=%fused_computation.211 | convolution fusion | flops 805306368 | bytes 27525120 | tf_op jit(solution)/shard_map/sqhd,skhd->shqk/dot_general | solution.py:119
  430.1 12.2 %fusion.8 = f32[12,64,1024]{2,1,0:T(8,128)S(1)} fusion(f32[12,512]{1,0:T(8,128)S(1)} %get-tuple-element.277, f32[12,512,1024]{2,1,0:T(8,128)} %fusion.124, pred[1024]{0:T(1024)(128)(4,1)S(1)} %iota_compare_fusion.2, bf16[1,1024,12,64]{1,3,2,0:T(8,128)(2,1)S(1)} %bitcast.441), kind=kOutput, calls=%fused_computation.26 | convolution fusion | flops 830472192 | bytes 29131776 | tf_op jit(solution)/shard_map/shqk,sqhd->skhd/dot_general | solution.py:137
  442.3 14.3 %add_convert_fusion = bf16[12,64,1024]{2,1,0:T(8,128)(2,1)} fusion(f32[12,64,1024]{2,1,0:T(8,128)S(1)} %fusion.8, f32[12,512]{1,0:T(8,128)S(1)} %get-tuple-element.278, f32[12,512,1024]{2,1,0:T(8,128)} %get-tuple-element.266, pred[1024]{0:T(1024)(128)(4,1)S(1)} %iota_compare_fusion.2, bf16[1,1024,12,64]{1,3,2,0:T(8,128)(2,1)S(1)} %bitcast.442), kind=kOutput, calls=%fused_computation.125 | convolution fusion | flops 832045056 | bytes 30704640 | tf_op jit(solution)/shard_map/shqk,sqhd->skhd/dot_general | solution.py:137
  456.6 8.7 copy.244
  465.8 12.5 %reduce.58 = bf16[1024,768]{1,0:T(8,128)(2,1)} reduce(bf16[1024,1,768]{2,1,0:T(2,128)(2,1)} %bitcast.426, bf16[]{:T(256)} %broadcast.784), dimensions={1}, to_apply=%bitcast.338.reduce_sub_computation | reduce | bytes 3145730
  486.6 36.4 %multiply_reduce_fusion.2 = (f32[12,512]{1,0:T(8,128)S(1)}, f32[12,512]{1,0:T(8,128)S(1)}, f32[12,512,1024]{2,1,0:T(8,128)}) fusion(f32[12,512]{1,0:T(8,128)S(1)} %get-tuple-element.278, f32[12,512,1024]{2,1,0:T(8,128)} %get-tuple-element.266, pred[1024]{0:T(1024)(128)(4,1)S(1)} %iota_compare_fusion.2, f32[12,512,1024]{2,1,0:T(8,128)} %fusion.126, ...), kind=kOutput, calls=%fused_computation.7 | convolution fusion | flops 868208640 | bytes 103121920 | tf_op jit(solution)/shard_map/sqhd,skhd->shqk/dot_general | solution.py:119
  523.0 42.7 %multiply_convert_fusion.2 = (bf16[12,512,1024]{2,1,0:T(8,128)(2,1)}, bf16[12,512,1024]{2,1,0:T(8,128)(2,1)}) fusion(f32[12,512,1024]{2,1,0:T(8,128)} %get-tuple-element.270, f32[12,512]{1,0:T(8,128)S(1)} %get-tuple-element.231, f32[12,512]{1,0:T(8,128)S(1)} %get-tuple-element.278, f32[12,512,1024]{2,1,0:T(8,128)} %get-tuple-element.266, ...), kind=kLoop, calls=%fused_computation.6 | loop fusion | flops 75497472 | bytes 125928448 | tf_op jit(solution)/shard_map/convert_element_type | solution.py:123
  565.7 8.5 multiply_convert_fusion.10
  574.3 9.4 multiply_convert_fusion.9
  596.0 12.9 %fusion.68 = bf16[1,1024,12,64]{1,3,2,0:T(8,128)(2,1)} fusion(f32[1,512,12,64]{1,3,2,0:T(8,128)S(1)} %fusion.101, f32[12,512]{1,0:T(8,128)S(1)} %copy-done.55, f32[12,512,1024]{2,1,0:T(8,128)} %get-tuple-element.261, pred[512,1024]{1,0:T(8,128)(4,1)S(1)} %copy-done.16, bf16[1,1024,12,64]{1,3,2,0:T(8,128)(2,1)S(1)} %bitcast.444), kind=kOutput, calls=%fused_computation.110 | convolution fusion | flops 832045056 | bytes 29655040 | tf_op jit(solution)/shard_map/shqk,sqhd->skhd/dot_general | solution.py:137
  611.6 9.1 fusion.122
  620.7 9.7 multiply_reduce_fusion.3
  630.5 10.0 multiply_convert_fusion.3
  640.4 18.1 %multiply_reduce_fusion = (f32[12,512]{1,0:T(8,128)S(1)}, f32[12,512,1024]{2,1,0:T(8,128)}) fusion(f32[12,512]{1,0:T(8,128)S(1)} %copy-done.55, f32[12,512,1024]{2,1,0:T(8,128)} %get-tuple-element.261, pred[512,1024]{1,0:T(8,128)(4,1)S(1)} %copy-done.16, bf16[1024,12,64]{0,2,1:T(8,128)(2,1)} %bitcast.431, bf16[1,1024,12,64]{1,3,2,0:T(8,128)(2,1)} %bitcast.445), kind=kOutput, calls=%fused_computation.1 | convolution fusion | flops 836757504 | bytes 53264384 | tf_op jit(solution)/shard_map/sqhd,skhd->shqk/dot_general | solution.py:119
  658.5 22.6 %multiply_convert_fusion = bf16[12,512,1024]{2,1,0:T(8,128)(2,1)} fusion(f32[12,512,1024]{2,1,0:T(8,128)} %get-tuple-element.275, f32[12,512]{1,0:T(8,128)S(1)} %get-tuple-element.274, f32[12,512]{1,0:T(8,128)S(1)} %copy-done.55, f32[12,512,1024]{2,1,0:T(8,128)} %get-tuple-element.261, pred[512,1024]{1,0:T(8,128)(4,1)S(1)} %copy-done.16), kind=kLoop, calls=%fused_computation | loop fusion | flops 37748736 | bytes 63488000 | tf_op jit(solution)/shard_map/convert_element_type | solution.py:123
  681.2 7.0 multiply_convert_fusion.4
  693.9 12.5 %reduce.57 = bf16[1024,768]{1,0:T(8,128)(2,1)} reduce(bf16[1024,1,768]{2,1,0:T(2,128)(2,1)} %bitcast.427, bf16[]{:T(256)} %broadcast.784), dimensions={1}, to_apply=%bitcast.336.reduce_sub_computation | reduce | bytes 3145730
  714.5 8.5 fusion.110
  726.9 5.9 multiply_bitcast_fusion
  738.1 8.5 fusion.69
  749.4 9.6 bitcast_dynamic-update-slice_fusion
  790.2 19.2 %copy.253 = f32[8,768,768]{2,0,1:T(8,128)} copy(f32[8,768,768]{1,2,0:T(8,128)} %bitcast_dynamic-update-slice_fusion.3) | data formatting | bytes 37748736 | tf_op jit(solution)/shard_map/concatenate | solution.py:304
  809.5 8.6 fusion.74
  820.8 8.5 fusion.60
  835.7 38.5 %all-reduce.2 = f32[3,768]{1,0:T(4,128)S(1)} all-reduce(f32[3,768]{1,0:T(4,128)S(1)} %pad_maximum_fusion.14), channel_id=4, replica_groups=mesh['seq'=8,'mem'=4] {'seq','mem'}, use_global_device_ids=true, to_apply=%region_25.26.clone | all-reduce | flops 2304 | bytes 18432
  882.0 132.8 %reduce-scatter.4.cloned.1.call-done = f32[8,24,768]{2,0,1:T(8,128)} async-done(((f32[8,768,768]{2,0,1:T(8,128)}), f32[8,24,768]{2,0,1:T(8,128)}) %reduce-scatter.4.cloned.1.call-update) | async-done | bytes 589840 | tf_op jit(solution)/shard_map/reduce_scatter | solution.py:321
  1024.3 39.1 %psum.7 = f32[]{:T(128)} all-reduce(f32[]{:T(128)S(6)} %add.286), channel_id=1, replica_groups=mesh['seq'=8,'mem'=4] {'seq','mem'}, use_global_device_ids=true, to_apply=%region_27.28 | all-reduce | flops 1 | bytes 8 | tf_op jit(solution)/shard_map/psum | solution.py:330
  (305 shorter events, 216.0 us)
Async XLA Ops:
  7.2 103.1 %copy-start = (bf16[4,256,768]{2,1,0:T(8,128)(2,1)S(1)}, bf16[4,256,768]{2,1,0:T(8,128)(2,1)}, u32[]{:S(2)}) copy-start(bf16[4,256,768]{2,1,0:T(8,128)(2,1)} %param.43) | copy-start | bytes 4718596
  7.2 88.8 %all-gather.4.cloned.1.call-start = ((), (), s32[]{:S(2)}) async-start(), calls=%async_computation.6 | async-start | bytes 9732096 | tf_op jit(solution)/shard_map/all_gather | solution.py:175
  9.3 333.1 %all-gather.6.cloned.1.call-start = ((), (), s32[]{:S(2)}) async-start(), calls=%async_computation.7 | async-start | bytes 9732096 | tf_op jit(solution)/shard_map/all_gather | solution.py:176
  85.1 51.2 %copy-start.67 = (f32[768]{0:T(1024)}, f32[768]{0:T(1024)S(1)}, u32[]{:S(2)}) copy-start(f32[768]{0:T(1024)S(1)} %get-tuple-element.230) | copy-start | bytes 9220
  85.1 148.0 %copy-start.62 = (f32[768]{0:T(1024)}, f32[768]{0:T(1024)S(1)}, u32[]{:S(2)}) copy-start(f32[768]{0:T(1024)S(1)} %get-tuple-element.229) | copy-start | bytes 9220
  86.9 49.5 %copy-start.12 = (bf16[1,1024,768]{1,2,0:T(8,128)(2,1)}, bf16[1,1024,768]{1,2,0:T(8,128)(2,1)S(1)}, u32[]{:S(2)}) copy-start(bf16[1,1024,768]{1,2,0:T(8,128)(2,1)S(1)} %copy.213) | copy-start | bytes 4718596
  88.0 48.3 %copy-start.64 = (f32[1024]{0:T(1024)}, f32[1024]{0:T(1024)S(1)}, u32[]{:S(2)}) copy-start(f32[1024]{0:T(1024)S(1)} %fusion.133) | copy-start | bytes 12292
  90.8 132.0 %copy-start.28 = (pred[512,512]{0,1:T(8,128)(4,1)}, pred[512,512]{0,1:T(8,128)(4,1)S(1)}, u32[]{:S(2)}) copy-start(pred[512,512]{0,1:T(8,128)(4,1)S(1)} %fusion.113) | copy-start | bytes 786436
  116.7 100.7 %all-to-all-start.1 = ((bf16[4,256,768]{1,2,0:T(8,128)(2,1)}), bf16[4,256,768]{1,2,0:T(8,128)(2,1)}, u32[]{:S(2)}, u32[]{:S(2)}) async-start(bf16[4,256,768]{1,2,0:T(8,128)(2,1)} %get-tuple-element.256), calls=%async_computation.1 | async-start | bytes 3145728 | tf_op jit(solution)/shard_map/all_to_all | solution.py:207
  144.2 10.7 copy-start.9
  144.2 63.9 %copy-start.4 = (bf16[1,1,1024,768]{2,3,0,1:T(8,128)(2,1)}, bf16[1,1,1024,768]{2,3,0,1:T(8,128)(2,1)S(1)}, u32[]{:S(2)}) copy-start(bf16[1,1,1024,768]{2,3,0,1:T(8,128)(2,1)S(1)} %get-tuple-element.254) | copy-start | bytes 4718596
  154.9 43.1 %slice-start = ((s8[25165824]{0:T(1024)(128)(4,1)}), s8[4194304]{0:T(1024)(128)(4,1)S(1)}, s32[]{:S(2)}) async-start(s8[25165824]{0:T(1024)(128)(4,1)} %bitcast.404), calls=%async_computation.10 | async-start | bytes 8388608
  154.9 43.1 %slice-start.1 = ((s8[25165824]{0:T(1024)(128)(4,1)}), s8[4194304]{0:T(1024)(128)(4,1)S(1)}, s32[]{:S(2)}) async-start(s8[25165824]{0:T(1024)(128)(4,1)} %bitcast.404), calls=%async_computation.11 | async-start | bytes 8388608
  154.9 43.1 %slice-start.2 = ((s8[25165824]{0:T(1024)(128)(4,1)}), s8[4194304]{0:T(1024)(128)(4,1)S(1)}, s32[]{:S(2)}) async-start(s8[25165824]{0:T(1024)(128)(4,1)} %bitcast.404), calls=%async_computation.12 | async-start | bytes 8388608
  154.9 43.1 %slice-start.3 = ((s8[25165824]{0:T(1024)(128)(4,1)}), s8[4194304]{0:T(1024)(128)(4,1)S(1)}, s32[]{:S(2)}) async-start(s8[25165824]{0:T(1024)(128)(4,1)} %bitcast.404), calls=%async_computation.13 | async-start | bytes 8388608
  168.9 29.1 %slice-start.4 = ((s8[25165824]{0:T(1024)(128)(4,1)}), s8[4194304]{0:T(1024)(128)(4,1)S(1)}, s32[]{:S(2)}) async-start(s8[25165824]{0:T(1024)(128)(4,1)} %bitcast.404), calls=%async_computation.14 | async-start | bytes 8388608
  168.9 29.1 %slice-start.5 = ((s8[25165824]{0:T(1024)(128)(4,1)}), s8[4194304]{0:T(1024)(128)(4,1)S(1)}, s32[]{:S(2)}) async-start(s8[25165824]{0:T(1024)(128)(4,1)} %bitcast.404), calls=%async_computation.15 | async-start | bytes 8388608
  198.0 10.0 copy-start.10
  217.4 42.7 %all-to-all-start = ((bf16[4,256,768]{1,2,0:T(8,128)(2,1)}), bf16[4,256,768]{1,2,0:T(8,128)(2,1)}, u32[]{:S(2)}, u32[]{:S(2)}) async-start(bf16[4,256,768]{1,2,0:T(8,128)(2,1)} %get-tuple-element.257), calls=%async_computation | async-start | bytes 3145728 | tf_op jit(solution)/shard_map/all_to_all | solution.py:208
  222.8 657.4 %reduce-scatter.6.cloned.1.call-start = ((), (), s32[]{:S(2)}) async-start(), calls=%async_computation.9 | async-start | bytes 19464192 | tf_op jit(solution)/shard_map/reduce_scatter | solution.py:322
  242.5 36.5 %copy-start.2 = (bf16[1024,12,64]{0,2,1:T(8,128)(2,1)}, bf16[1024,12,64]{0,2,1:T(8,128)(2,1)S(1)}, u32[]{:S(2)}) copy-start(bf16[1024,12,64]{0,2,1:T(8,128)(2,1)S(1)} %reshape.1187) | copy-start | bytes 4718596
  295.6 18.7 %copy-start.7 = (bf16[1024,12,64]{0,2,1:T(8,128)(2,1)S(1)}, bf16[1024,12,64]{0,2,1:T(8,128)(2,1)}, u32[]{:S(2)}) copy-start(bf16[1024,12,64]{0,2,1:T(8,128)(2,1)} %reshape.1183) | copy-start | bytes 4718596
  325.5 12.3 %copy-start.80 = (bf16[12,64,512]{2,1,0:T(8,128)(2,1)}, bf16[12,64,512]{2,1,0:T(8,128)(2,1)S(1)}, u32[]{:S(2)}) copy-start(bf16[12,64,512]{2,1,0:T(8,128)(2,1)S(1)} %fusion.106) | copy-start | bytes 2359300
  325.5 12.3 %copy-start.35 = (f32[1,1024,768]{1,2,0:T(8,128)S(1)}, f32[1,1024,768]{1,2,0:T(8,128)}, u32[]{:S(2)}) copy-start(f32[1,1024,768]{1,2,0:T(8,128)} %copy-done.34) | copy-start | bytes 9437188
  325.5 12.3 %copy-start.41 = (bf16[1,768,768]{2,0,1:T(2,128)(2,1)S(1)}, bf16[1,768,768]{2,0,1:T(2,128)(2,1)}, u32[]{:S(2)}) copy-start(bf16[1,768,768]{2,0,1:T(2,128)(2,1)} %get-tuple-element.249) | copy-start | bytes 3538948
  364.8 14.5 %copy-start.47 = (bf16[1,1024,768]{1,2,0:T(8,128)(2,1)S(1)}, bf16[1,1024,768]{1,2,0:T(8,128)(2,1)}, u32[]{:S(2)}) copy-start(bf16[1,1024,768]{1,2,0:T(8,128)(2,1)} %multiply_convert_fusion.5) | copy-start | bytes 4718596
  417.0 13.1 %copy-start.33 = (bf16[1024,768]{0,1:T(8,128)(2,1)S(1)}, bf16[1024,768]{0,1:T(8,128)(2,1)}, u32[]{:S(2)}) copy-start(bf16[1024,768]{0,1:T(8,128)(2,1)} %convolution_convert_fusion.1) | copy-start | bytes 4718596
  482.0 250.8 %all-to-all-start.3 = ((bf16[4,2,98304]{2,1,0:T(2,128)(2,1)}), bf16[4,2,98304]{2,1,0:T(2,128)(2,1)}, u32[]{:S(2)}, u32[]{:S(2)}) async-start(bf16[4,2,98304]{2,1,0:T(2,128)(2,1)} %reshape.1221), calls=%async_computation.3 | async-start | bytes 3145728 | tf_op jit(solution)/shard_map/all_to_all | solution.py:271
  523.0 42.7 %copy-start.3 = (bf16[1024,12,64]{0,2,1:T(8,128)(2,1)S(1)}, bf16[1024,12,64]{0,2,1:T(8,128)(2,1)}, u32[]{:S(2)}) copy-start(bf16[1024,12,64]{0,2,1:T(8,128)(2,1)} %copy-done.2) | copy-start | bytes 4718596
  574.2 9.4 copy-start.49
  574.2 9.4 copy-start.36
  574.3 9.4 copy-start.40
  574.3 9.4 copy-start.61
  574.3 9.4 copy-start.63
  611.6 9.1 copy-start.27
  611.6 9.1 copy-start.45
  611.6 18.9 %slice-start.9 = ((s8[12582912]{0:T(1024)(128)(4,1)}), s8[4194304]{0:T(1024)(128)(4,1)S(1)}, s32[]{:S(2)}) async-start(s8[12582912]{0:T(1024)(128)(4,1)} %bitcast.408), calls=%async_computation.19 | async-start | bytes 8388608
  611.6 18.9 %slice-start.10 = ((s8[12582912]{0:T(1024)(128)(4,1)}), s8[4194304]{0:T(1024)(128)(4,1)S(1)}, s32[]{:S(2)}) async-start(s8[12582912]{0:T(1024)(128)(4,1)} %bitcast.408), calls=%async_computation.20 | async-start | bytes 8388608
  620.7 9.7 slice-start.11
  658.5 22.6 %copy-start.6 = (f32[12,64,1024]{2,1,0:T(8,128)S(1)}, f32[12,64,1024]{2,1,0:T(8,128)}, u32[]{:S(2)}) copy-start(f32[12,64,1024]{2,1,0:T(8,128)} %fusion.122) | copy-start | bytes 9437188
  658.5 22.6 %copy-start.17 = (bf16[1024,768]{0,1:T(8,128)(2,1)S(1)}, bf16[1024,768]{0,1:T(8,128)(2,1)}, u32[]{:S(2)}) copy-start(bf16[1024,768]{0,1:T(8,128)(2,1)} %convolution_convert_fusion.2) | copy-start | bytes 4718596
  693.9 16.6 %copy-start.5 = (bf16[1,1,1024,768]{2,3,0,1:T(8,128)(2,1)S(1)}, bf16[1,1,1024,768]{2,3,0,1:T(8,128)(2,1)}, u32[]{:S(2)}) copy-start(bf16[1,1,1024,768]{2,3,0,1:T(8,128)(2,1)} %copy-done.4) | copy-start | bytes 4718596
  732.8 42.0 %all-to-all-start.2 = ((bf16[4,2,98304]{2,1,0:T(2,128)(2,1)}), bf16[4,2,98304]{2,1,0:T(2,128)(2,1)}, u32[]{:S(2)}, u32[]{:S(2)}) async-start(bf16[4,2,98304]{2,1,0:T(2,128)(2,1)} %reshape.1219), calls=%async_computation.2 | async-start | bytes 3145728 | tf_op jit(solution)/shard_map/all_to_all | solution.py:270
  738.1 276.8 %reduce-scatter.4.cloned.1.call-start = ((), (), s32[]{:S(2)}) async-start(), calls=%async_computation.8 | async-start | bytes 19464192 | tf_op jit(solution)/shard_map/reduce_scatter | solution.py:321
  749.4 9.6 copy-start.24
  749.4 9.6 copy-start.77
  749.4 9.6 copy-start.79
  874.8 143.8 %copy-start.32 = (bf16[1,1024,768]{2,1,0:T(8,128)(2,1)S(1)}, bf16[1,1024,768]{2,1,0:T(8,128)(2,1)}, u32[]{:S(2)}) copy-start(bf16[1,1024,768]{2,1,0:T(8,128)(2,1)} %copy.293) | copy-start | bytes 4718596
  (58 other events, 251.1 us)
Sparse Core Ops, SparseCore 0:
  11.4 84.5 all-gather.3
  99.5 102.1 all-gather.5
  417.1 239.8 reduce-scatter.5
  809.6 205.2 reduce-scatter.3
where the time goes:
time: 1090 us; the launch traced here: 1080 us
  matrix products  394 us (36%)
  other arithmetic  171 us (16%)
  local copies, waits for them, and re-layouts  169 us (16%)
  waiting for transfers between devices  157 us (14%)
  blocking collectives  148 us (14%)
  between operations  20.4 us (2%)
  starting transfers between devices  19.9 us (2%)
    reduce_scatter x1, waiting for transfers between devices, on_device(): lax.psum_scatter(grad_attn, ('seq', 'mem'), scatter_dimension=1, tiled=True)  133 us
    dot_general x4, matrix products, attend_backward(): jnp.einsum('sqhd,skhd->shqk', grad_block, values_used, preferred_element_...  77.3 us
    convert_element_type x3, other arithmetic, attend_backward(): (weights_full * (grad_weights - inner_sum)).astype(jnp.bfloat16)  75.3 us
    all_gather x1, blocking collectives, on_device(): lax.all_gather(gain_master.astype(jnp.bfloat16), ('seq', 'mem'), axis=1,...  70.4 us
    unnamed x213, local copies, waits for them, and re-layouts  65.3 us
    dot_general x4, matrix products, attend_backward(): jnp.einsum('shqk,sqhd->skhd', weights_full.astype(jnp.bfloat16), grad_blo...  42.7 us
    dot_general x4, matrix products, score_block(): jnp.einsum('sqhd,skhd->shqk', query_block, key_rows, preferred_element_ty...  40.8 us
    dot_general x4, matrix products, attend_forward(): jnp.einsum('shqk,skhd->sqhd', weights_soft, value_rows[:, :key_end], pref...  40.6 us
  transfers between devices with their start and end apart: 8, of which 4 were waited for; matrix products, arithmetic and copies ran while one was open for 59% of the time, Pallas kernels for 0%

commit v1 on v0

v1 whole, which is shorter than its diff:
```python
import functools, math
import jax, jax.numpy as jnp
from jax import lax
from jax.sharding import PartitionSpec as P
from jax.experimental import pallas as pl
from jax.experimental.pallas import tpu as pltpu
bf=jnp.bfloat16; f32=jnp.float32
HD=64; HEADS=12
NEG=-1e30
LOG2E=math.log2(math.e)
TN=(((0,),(0,)),((),())); NN=(((1,),(0,)),((),())); NT=(((1,),(1,)),((),()))
def dg(a,b,dims): return lax.dot_general(a,b,dims,preferred_element_type=f32)
def rows16(cols, width, pad=16):
    idx=lax.broadcasted_iota(jnp.int32,(pad,width),0)
    out=jnp.zeros((pad,width),f32)
    for i,c in enumerate(cols): out=jnp.where(idx==i,c,out)
    return out.astype(bf)
def split3(x):
    hi=x.astype(bf).astype(f32); r=x-hi; mid=r.astype(bf).astype(f32); lo=r-mid
    return hi,mid,lo
def scaled_query(qT):
    s=qT.astype(f32)*(0.125*LOG2E)
    hi=s.astype(bf); lo=(s-hi.astype(f32)).astype(bf)
    return hi,lo


def causal_mask(x,q0,bq,fill):
    ki=lax.broadcasted_iota(jnp.int32,(bq,bq),0); qi=lax.broadcasted_iota(jnp.int32,(bq,bq),1)
    d=jnp.where(ki<=qi,x[q0:],fill)
    return jnp.concatenate([x[:q0],d],axis=0) if q0 else d

def fwd_kernel(len_ref,qT_ref,kT_ref,vT_ref,oT_ref,lse_ref,*,causal,bq,hs):
    L=qT_ref.shape[1]; K=kT_ref.shape[1]
    n=len_ref[0]
    kpos=lax.broadcasted_iota(jnp.int32,(1,K),1)
    kx=rows16([jnp.where(kpos<n,0.0,NEG)],K); qx=rows16([jnp.ones((1,L),f32)],L); vx=rows16([jnp.ones((1,K),f32)],K)
    ops=[]
    for h in range(hs):
        r=slice(h*HD,(h+1)*HD)
        kT=kT_ref[r,:]
        hi,lo=scaled_query(qT_ref[r,:])
        ops.append((jnp.concatenate([kT,kT,kx],axis=0),jnp.concatenate([hi,lo,qx],axis=0),jnp.concatenate([vT_ref[r,:],vx],axis=0)))
    jobs=[(h,q0) for h in range(hs) for q0 in range(0,L,bq)]
    def score(j):
        h,q0=j; ke=min(K,q0+bq) if causal else K
        return dg(ops[h][0][:,:ke],ops[h][1][:,q0:q0+bq],TN)
    nxt=score(jobs[0])
    for i,(h,q0) in enumerate(jobs):
        s=nxt
        if i+1<len(jobs): nxt=score(jobs[i+1])
        ke=s.shape[0]
        if causal: s=causal_mask(s,q0,bq,NEG)
        m=jnp.max(s,axis=0,keepdims=True)
        p=jnp.exp2(s-m).astype(bf)
        o=dg(ops[h][2][:,:ke],p,NN)
        l=o[HD:HD+1]
        oT_ref[h*HD:(h+1)*HD,q0:q0+bq]=(o[:HD]*(1.0/l)).astype(bf)
        lse_ref[h,:,q0:q0+bq]=m+jnp.log2(l)

def attn_fwd(n,qT,kT,vT,causal,bq=256,hs=2):
    D,L=qT.shape; K=kT.shape[1]
    hb=lambda w: pl.BlockSpec((hs*HD,w),lambda h:(h,0))
    return pl.pallas_call(functools.partial(fwd_kernel,causal=causal,bq=bq,hs=hs),grid=(D//HD//hs,),
      in_specs=[pl.BlockSpec(memory_space=pltpu.SMEM),hb(L),hb(K),hb(K)],
      out_specs=[hb(L),pl.BlockSpec((hs,1,L),lambda h:(h,0,0))],
      out_shape=[jax.ShapeDtypeStruct((D,L),bf),jax.ShapeDtypeStruct((D//HD,1,L),f32)],
      compiler_params=pltpu.CompilerParams(vmem_limit_bytes=48*2**20),
    )(n,qT,kT,vT)

def bwd_kernel(len_ref,qT_ref,kT_ref,vT_ref,oT_ref,gT_ref,lse_ref,dq_ref,dk_ref,dv_ref,dka,dva,*,causal,bq,hs):
    L=qT_ref.shape[1]; K=kT_ref.shape[1]
    n=len_ref[0]
    kpos=lax.broadcasted_iota(jnp.int32,(1,K),1)
    bias=jnp.where(kpos<n,0.0,NEG)
    one_k=jnp.ones((1,K),f32)
    kx=rows16([bias,one_k,one_k,one_k],K); vx=rows16([one_k,one_k,one_k],K)
    ops=[]
    for h in range(hs):
        r=slice(h*HD,(h+1)*HD)
        kT=kT_ref[r,:]; qT=qT_ref[r,:]; gT=gT_ref[r,:]
        hi,lo=scaled_query(qT)
        delta=jnp.sum(oT_ref[r,:].astype(f32)*gT.astype(f32),axis=0,keepdims=True)
        ops.append(dict(k=kT,q=qT,g=gT,kaug=jnp.concatenate([kT,kT,kx],axis=0),
          qaug=jnp.concatenate([hi,lo,rows16([jnp.ones((1,L),f32),*split3(-lse_ref[h])],L)],axis=0),
          vaug=jnp.concatenate([vT_ref[r,:],vx],axis=0),
          gaug=jnp.concatenate([gT,rows16(list(split3(-delta)),L)],axis=0)))
    jobs=[(h,q0) for h in range(hs) for q0 in reversed(range(0,L,bq))]
    def score(j):
        h,q0=j; ke=min(K,q0+bq) if causal else K; sl=slice(q0,q0+bq); o=ops[h]
        return dg(o["kaug"][:,:ke],o["qaug"][:,sl],TN),dg(o["vaug"][:,:ke],o["gaug"][:,sl],TN)
    nxt=score(jobs[0])
    for i,(h,q0) in enumerate(jobs):
        s,dp=nxt
        if i+1<len(jobs): nxt=score(jobs[i+1])
        ke=s.shape[0]; sl=slice(q0,q0+bq); o=ops[h]; r=slice(h*HD,(h+1)*HD)
        p=jnp.exp2(s)
        if causal: p=causal_mask(p,q0,bq,0.0)
        ds=(p*dp).astype(bf)
        pb=p.astype(bf)
        dq_ref[r,sl]=(dg(o["k"][:,:ke],ds,NN)*0.125).astype(bf)
        dv=dg(o["g"][:,sl],pb,NT)
        dk=dg(o["q"][:,sl],ds,NT)
        if q0==L-bq:
            dka[r]=dk; dva[r]=dv
        else:
            dka[r,:ke]+=dk; dva[r,:ke]+=dv
    dk_ref[...]=(dka[...]*0.125).astype(bf)
    dv_ref[...]=dva[...].astype(bf)

def attn_bwd(n,qT,kT,vT,oT,gT,lse,causal,bq=256,hs=2):
    D,L=qT.shape; K=kT.shape[1]
    hb=lambda w: pl.BlockSpec((hs*HD,w),lambda h:(h,0))
    return pl.pallas_call(functools.partial(bwd_kernel,causal=causal,bq=bq,hs=hs),grid=(D//HD//hs,),
      in_specs=[pl.BlockSpec(memory_space=pltpu.SMEM),hb(L),hb(K),hb(K),hb(L),hb(L),pl.BlockSpec((hs,1,L),lambda h:(h,0,0))],
      out_specs=[hb(L),hb(K),hb(K)],
      out_shape=[jax.ShapeDtypeStruct((D,L),bf),jax.ShapeDtypeStruct((D,K),bf),jax.ShapeDtypeStruct((D,K),bf)],
      scratch_shapes=[pltpu.VMEM((hs*HD,K),f32),pltpu.VMEM((hs*HD,K),f32)],
      compiler_params=pltpu.CompilerParams(vmem_limit_bytes=48*2**20),
    )(n,qT,kT,vT,oT,gT,lse)

TT=(((0,),(1,)),((),()))
EPS=1e-6
VL=60*2**20
def cp(): return pltpu.CompilerParams(vmem_limit_bytes=VL)
def full(shape): return pl.BlockSpec(shape,lambda i:(0,)*len(shape))
GC=0.7978845608028654

def rms_r(v): return lax.rsqrt(jnp.mean(v*v,axis=-1,keepdims=True)+EPS)

def proj_kernel(x_ref,g_ref,w_ref,n_ref,yT_ref):
    @pl.when(pl.program_id(0)==0)
    def _():
        x=x_ref[...].astype(f32)
        n_ref[...]=(x*rms_r(x)*g_ref[0:1,:]).astype(bf)
    yT_ref[...]=dg(w_ref[...],n_ref[...],TT).astype(bf)
def norm_proj(x,g,w,fb=384):
    L,D=x.shape; F=w.shape[1]
    return pl.pallas_call(proj_kernel,grid=(F//fb,),
      in_specs=[full((L,D)),full((1,D)),pl.BlockSpec((D,fb),lambda i:(0,i))],
      out_specs=[full((L,D)),pl.BlockSpec((fb,L),lambda i:(i,0))],
      out_shape=[jax.ShapeDtypeStruct((L,D),bf),jax.ShapeDtypeStruct((F,L),bf)],compiler_params=cp())(x,g,w)
def memproj_kernel(x_ref,w_ref,yT_ref):
    yT_ref[...]=dg(w_ref[...],x_ref[...],TT).astype(bf)
def mem_proj(x,w,fb=384):
    L,D=x.shape; F=w.shape[1]
    return pl.pallas_call(memproj_kernel,grid=(F//fb,),
      in_specs=[full((L,D)),pl.BlockSpec((D,fb),lambda i:(0,i))],
      out_specs=pl.BlockSpec((fb,L),lambda i:(i,0)),
      out_shape=jax.ShapeDtypeStruct((F,L),bf),compiler_params=cp())(x,w)

def post_self_kernel(x_ref,oT_ref,w3_ref,w4_ref,g_ref,h_ref,n_ref,cT_ref):
    h=x_ref[...].astype(f32)+dg(oT_ref[...],w3_ref[...],TT)
    h_ref[...]=h
    n=(h*rms_r(h)*g_ref[0:1,:]).astype(bf)
    n_ref[...]=n
    cT_ref[...]=dg(n,w4_ref[...],NN).astype(bf).T
def post_self(x,oT,w3,w4,g,tb=256):
    L,D=x.shape
    tok=pl.BlockSpec((tb,D),lambda i:(i,0)); tokT=pl.BlockSpec((D,tb),lambda i:(0,i))
    return pl.pallas_call(post_self_kernel,grid=(L//tb,),
      in_specs=[tok,tokT,full((D,D)),full((D,D)),full((1,D))],
      out_specs=[tok,tok,tokT],
      out_shape=[jax.ShapeDtypeStruct((L,D),f32),jax.ShapeDtypeStruct((L,D),bf),jax.ShapeDtypeStruct((D,L),bf)],compiler_params=cp())(x,oT,w3,w4,g)

def mlp_kernel(len_ref,h1_ref,oT_ref,w7_ref,cot_ref,g_ref,wg_ref,wu_ref,wd_ref,
               out_ref,gh_ref,gmT_ref,dw7_ref,dg_ref,dwg_ref,dwu_ref,dwd_ref,
               h2,n3,gb,oacc,nacc,*,tb):
    L,D=h1_ref.shape
    i=pl.program_id(0); last=pl.num_programs(0)-1
    nt=L//tb
    @pl.when(i==0)
    def _():
        n=len_ref[0]
        def body(t,c):
            sl=pl.ds(pl.multiple_of(t*tb,tb),tb)
            h=h1_ref[sl,:]+dg(oT_ref[:,sl],w7_ref[...],TT)
            h2[sl,:]=h
            n3[sl,:]=(h*rms_r(h)*g_ref[0:1,:]).astype(bf)
            row=t*tb+lax.broadcasted_iota(jnp.int32,(tb,1),0)
            gb[sl,:]=jnp.where(row<n,cot_ref[sl,:].astype(f32),0.0).astype(bf)
            return c
        for t in range(nt): body(t,0)
    n3v=n3[...]; gbv=gb[...]
    wg=wg_ref[...]; wu=wu_ref[...]; wd=wd_ref[...]
    g=dg(n3v,wg,NN); u=dg(n3v,wu,NN); di=dg(gbv,wd,NN)
    g2=g*g
    t=jnp.tanh(g*(GC+(GC*0.044715)*g2))
    hp=0.5+0.5*t
    ge=g*hp
    dge=hp+(0.5*g)*(1.0-t*t)*(GC+(3*GC*0.044715)*g2)
    inner=(ge*u).astype(bf)
    dgate=(di*u*dge).astype(bf)
    dup=(di*ge).astype(bf)
    o=dg(inner,wd,NT)
    dn=dg(dgate,wg,NT)+dg(dup,wu,NT)
    dwg_ref[...]=dg(n3v,dgate,TN).astype(bf)
    dwu_ref[...]=dg(n3v,dup,TN).astype(bf)
    dwd_ref[...]=dg(gbv,inner,TN).astype(bf)
    @pl.when(i==0)
    def _():
        oacc[...]=o; nacc[...]=dn
    @pl.when(i>0)
    def _():
        oacc[...]+=o; nacc[...]+=dn
    @pl.when(i==last)
    def _():
        n=len_ref[0]
        acc=jnp.zeros((1,D),f32)
        for t in range(nt):
            sl=slice(t*tb,(t+1)*tb)
            h=h2[sl,:]; uu=nacc[sl,:]
            out_ref[sl,:]=(h+oacc[sl,:]).astype(bf)
            r=rms_r(h); ug=uu*g_ref[0:1,:]
            gh=gb[sl,:].astype(f32)+r*ug-h*((r*r*r)*jnp.mean(ug*h,axis=-1,keepdims=True))
            acc=acc+jnp.sum(uu*h*r,axis=0,keepdims=True)
            gh_ref[sl,:]=gh
            b=gh.astype(bf)
            n3[sl,:]=b
            gmT_ref[:,sl]=dg(b,w7_ref[...],NN).astype(bf).T
        dg_ref[...]=acc
        dw7_ref[...]=dg(n3[...],oT_ref[...],TT).astype(bf)
def mlp(n,h1,oT,w7,cot,g,wm,fc=512,tb=256):
    L,D=h1.shape; F=wm.shape[1]//3; nc=F//fc
    wb=lambda j: pl.BlockSpec((D,fc),lambda i,j=j:(0,j*nc+i))
    gb_=pl.BlockSpec((D,fc),lambda i:(0,i))
    S=jax.ShapeDtypeStruct
    return pl.pallas_call(functools.partial(mlp_kernel,tb=tb),grid=(nc,),
      in_specs=[pl.BlockSpec(memory_space=pltpu.SMEM),full((L,D)),full((D,L)),full((D,D)),full((L,D)),full((1,D)),wb(0),wb(1),wb(2)],
      out_specs=[full((L,D)),full((L,D)),full((D,L)),full((D,D)),full((1,D)),gb_,gb_,gb_],
      out_shape=[S((L,D),bf),S((L,D),f32),S((D,L),bf),S((D,D),bf),S((1,D),f32)]+[S((D,F),bf)]*3,
      scratch_shapes=[pltpu.VMEM((L,D),f32),pltpu.VMEM((L,D),bf),pltpu.VMEM((L,D),bf),pltpu.VMEM((L,D),f32),pltpu.VMEM((L,D),f32)],
      compiler_params=cp())(n,h1,oT,w7,cot,g,wm,wm,wm)

def mid_kernel(h1_ref,gh2_ref,dcT_ref,w4_ref,w3_ref,g_ref,gh1_ref,gmT_ref,gb_ref,dg_ref):
    i=pl.program_id(0)
    u=dg(dcT_ref[...],w4_ref[...],TT)
    h=h1_ref[...]
    r=rms_r(h); ug=u*g_ref[0:1,:]
    gh=gh2_ref[...]+r*ug-h*((r*r*r)*jnp.mean(ug*h,axis=-1,keepdims=True))
    gh1_ref[...]=gh
    b=gh.astype(bf)
    gb_ref[...]=b
    gmT_ref[...]=dg(b,w3_ref[...],NN).astype(bf).T
    s=jnp.sum(u*h*r,axis=0,keepdims=True)
    @pl.when(i==0)
    def _(): dg_ref[...]=s
    @pl.when(i>0)
    def _(): dg_ref[...]+=s
def mid(h1,gh2,dcT,w4,w3,g,tb=256):
    L,D=h1.shape
    tok=pl.BlockSpec((tb,D),lambda i:(i,0)); tokT=pl.BlockSpec((D,tb),lambda i:(0,i))
    S=jax.ShapeDtypeStruct
    return pl.pallas_call(mid_kernel,grid=(L//tb,),
      in_specs=[tok,tok,tokT,full((D,D)),full((D,D)),full((1,D))],
      out_specs=[tok,tokT,tok,full((1,D))],
      out_shape=[S((L,D),f32),S((D,L),bf),S((L,D),bf),S((1,D),f32)],compiler_params=cp())(h1,gh2,dcT,w4,w3,g)

def wgrad_kernel(a_ref,gT_ref,o_ref):
    o_ref[...]=dg(a_ref[...],gT_ref[...],TT).astype(bf)
def wgrad(a,gT,fb=384):
    L,D=a.shape; F=gT.shape[0]
    return pl.pallas_call(wgrad_kernel,grid=(F//fb,),
      in_specs=[full((L,D)),pl.BlockSpec((fb,L),lambda i:(i,0))],
      out_specs=pl.BlockSpec((D,fb),lambda i:(0,i)),
      out_shape=jax.ShapeDtypeStruct((D,F),bf),compiler_params=cp())(a,gT)

def gmem_kernel(kT_ref,vT_ref,w5_ref,w6_ref,o_ref):
    o_ref[...]=(dg(kT_ref[...],w5_ref[...],TT)+dg(vT_ref[...],w6_ref[...],TT)).astype(bf)
def gmem(kT,vT,w56,tb=256):
    D,L=kT.shape
    tokT=pl.BlockSpec((D,tb),lambda i:(0,i))
    return pl.pallas_call(gmem_kernel,grid=(L//tb,),
      in_specs=[tokT,tokT,pl.BlockSpec((D,D),lambda i:(0,0)),pl.BlockSpec((D,D),lambda i:(0,1))],
      out_specs=pl.BlockSpec((tb,D),lambda i:(i,0)),
      out_shape=jax.ShapeDtypeStruct((L,D),bf),compiler_params=cp())(kT,vT,w56,w56)

def first_kernel(x_ref,gh1_ref,qT_ref,kT_ref,vT_ref,w0_ref,w1_ref,w2_ref,g_ref,gt_ref,dg_ref):
    i=pl.program_id(0)
    u=dg(qT_ref[...],w0_ref[...],TT)+dg(kT_ref[...],w1_ref[...],TT)+dg(vT_ref[...],w2_ref[...],TT)
    h=x_ref[...].astype(f32)
    r=rms_r(h); ug=u*g_ref[0:1,:]
    gt_ref[...]=gh1_ref[...]+r*ug-h*((r*r*r)*jnp.mean(ug*h,axis=-1,keepdims=True))
    s=jnp.sum(u*h*r,axis=0,keepdims=True)
    @pl.when(i==0)
    def _(): dg_ref[...]=s
    @pl.when(i>0)
    def _(): dg_ref[...]+=s
def first(x,gh1,qT,kT,vT,w,g,tb=256):
    L,D=x.shape
    tok=pl.BlockSpec((tb,D),lambda i:(i,0)); tokT=pl.BlockSpec((D,tb),lambda i:(0,i))
    S=jax.ShapeDtypeStruct
    wb=lambda j: pl.BlockSpec((D,D),lambda i,j=j:(0,j))
    return pl.pallas_call(first_kernel,grid=(L//tb,),
      in_specs=[tok,tok,tokT,tokT,tokT,wb(0),wb(1),wb(2),full((1,D))],
      out_specs=[tok,full((1,D))],
      out_shape=[S((L,D),f32),S((1,D),f32)],compiler_params=cp())(x,gh1,qT,kT,vT,w,w,w,g)

STEP=10
CLIP_NORM=1.0
BETA_FIRST=0.9
BETA_SECOND=0.999
ADAM_EPSILON=1e-08
RATE_MATRIX=0.06
RATE_GAIN=0.6
DECAY_MATRIX=0.01
AXES=("seq","mem")


def adam_step(master,grad,first_moment,second_moment,rate,decay):
    first_new=BETA_FIRST*first_moment+(1.0-BETA_FIRST)*grad
    second_new=BETA_SECOND*second_moment+(1.0-BETA_SECOND)*grad*grad
    first_hat=first_new/(1.0-BETA_FIRST**STEP)
    second_hat=second_new/(1.0-BETA_SECOND**STEP)
    master_new=master-rate*(first_hat/(jnp.sqrt(second_hat)+ADAM_EPSILON)+decay*master)
    return (master_new,first_new,second_new)


def columns(stack):
    return jnp.concatenate([stack[i] for i in range(stack.shape[0])],axis=1)


def gather(shard):
    return lax.all_gather(shard,AXES,axis=0,tiled=True)


def scatter(parts):
    return lax.psum_scatter(jnp.concatenate(parts,axis=1),AXES,scatter_dimension=0,tiled=True).astype(f32)


def on_device(tokens,memory,cotangent,table_len,patch_count,attn_master,attn_first,attn_second,mlp_master,mlp_first,mlp_second,gain_master,gain_first,gain_second):
    rows=attn_master.shape[1]
    D=attn_master.shape[2]
    aw=attn_master.astype(bf)
    gain_cols=jnp.pad(gain_master.T,((0,0),(0,125))).astype(bf)
    w_first=gather(jnp.concatenate([columns(aw[:3]),gain_cols],axis=1))
    w_second=gather(columns(aw[3:]))
    w_mlp=gather(columns(mlp_master.astype(bf)))
    mem=lax.all_to_all(memory,"mem",split_axis=0,concat_axis=0,tiled=True).reshape(-1,D)
    gains=w_first[:,3*D:3*D+8].astype(f32).T
    g=[gains[i:i+1] for i in range(3)]
    w_qkv=w_first[:,:3*D]
    w3,w4,w56,w7=w_second[:,:D],w_second[:,D:2*D],w_second[:,2*D:4*D],w_second[:,4*D:]
    x=tokens[0]
    n1,qkv=norm_proj(x,g[0],w_qkv)
    q,k,v=qkv[:D],qkv[D:2*D],qkv[2*D:]
    o1,lse1=attn_fwd(table_len,q,k,v,True,512,4)
    h1,n2,cq=post_self(x,o1,w3,w4,g[1])
    mkv=mem_proj(mem,w56)
    mk,mv=mkv[:D],mkv[D:]
    o2,lse2=attn_fwd(patch_count,cq,mk,mv,False,512,2)
    mixed_out,gh2,gm2,dw7,dg3,dwg,dwu,dwd=mlp(table_len,h1,o2,w7,cotangent[0],g[2],w_mlp)
    r_mlp=scatter([dwg,dwu,dwd])
    dcq,dmk,dmv=attn_bwd(patch_count,cq,mk,mv,o2,gm2,lse2,False,256,2)
    gh1,gm1,gb1,dg2=mid(h1,gh2,dcq,w4,w3,g[1])
    gmem_local=gmem(dmk,dmv,w56)
    grad_memory=lax.all_to_all(gmem_local.reshape(memory.shape),"mem",split_axis=0,concat_axis=0,tiled=True).astype(f32)
    dw4=wgrad(n2,dcq)
    dw5=wgrad(mem,dmk)
    dw6=wgrad(mem,dmv)
    dw3=wgrad(gb1,o1)
    r_second=scatter([dw3,dw4,dw5,dw6,dw7])
    dq,dk,dv=attn_bwd(table_len,q,k,v,o1,gm1,lse1,True,256,2)
    dw0=wgrad(n1,dq); dw1=wgrad(n1,dk); dw2=wgrad(n1,dv)
    grad_tokens,dg1=first(x,gh1,dq,dk,dv,w_qkv,g[0])
    dgain=jnp.pad(jnp.concatenate([dg1,dg2,dg3],axis=0).T,((0,0),(0,125))).astype(bf)
    r_first=scatter([dw0,dw1,dw2,dgain])
    split=lambda r,n,w: jnp.stack([r[:,i*w:(i+1)*w] for i in range(n)])
    attn_red=jnp.concatenate([split(r_first,3,D),split(r_second,5,D)],axis=0)
    mlp_red=split(r_mlp,3,mlp_master.shape[2])
    gain_red=r_first[:,3*D:3*D+3].T
    squares=jnp.sum(attn_red*attn_red)+jnp.sum(mlp_red*mlp_red)+jnp.sum(gain_red*gain_red)
    grad_norm=jnp.sqrt(lax.psum(squares,AXES))
    factor=CLIP_NORM/jnp.maximum(grad_norm,CLIP_NORM)
    a=adam_step(attn_master,attn_red*factor,attn_first,attn_second,RATE_MATRIX,DECAY_MATRIX)
    m=adam_step(mlp_master,mlp_red*factor,mlp_first,mlp_second,RATE_MATRIX,DECAY_MATRIX)
    gn=adam_step(gain_master,gain_red*factor,gain_first,gain_second,RATE_GAIN,0.0)
    return (mixed_out[None],grad_tokens[None],grad_memory,grad_norm)+a+m+gn


def solution(mesh):
    both=P(("seq","mem"),None,None)
    mid_split=P(None,("seq","mem"),None)
    gain_split=P(None,("seq","mem"))
    return jax.shard_map(on_device,mesh=mesh,
        in_specs=(both,P("seq","mem",None),both,P(("seq","mem")),P(("seq","mem")))+(mid_split,)*6+(gain_split,)*3,
        out_specs=(both,both,P("seq","mem",None),P())+(mid_split,)*6+(gain_split,)*3,
        check_vma=False)
```

time: 1090 us -> 835 us (0.77)
  matrix products: 394 us -> 0 us
  waiting for transfers between devices: 157 us -> 467 us
  Pallas kernels: 0 us -> 215 us
  other arithmetic: 171 us -> 30 us
  local copies, waits for them, and re-layouts: 169 us -> 43 us
  blocking collectives: 148 us -> 39.4 us
    dot_general x49 -> x0, matrix products: 394 us -> none  [the longest x4 77.3 us: attend_backward(): jnp.einsum('sqhd,skhd->shqk', grad_block, values_used, preferred_element_...]
    pallas_call x0 -> x18, Pallas kernels: none -> 215 us  [the longest x2 53.7 us: attn_bwd(): pl.pallas_call(functools.partial(bwd_kernel, causal=causal, bq=bq, hs=hs)...]
    all_gather x2 -> x3, waiting for transfers between devices: 3.97 us -> 146 us  [gather(): return lax.all_gather(shard, AXES, axis=0, tiled=True)]
    reduce_scatter x2, waiting for transfers between devices: 133 us -> 254 us  [scatter(): lax.psum_scatter(jnp.concatenate(parts, axis=1), AXES, scatter_dimension=...]
    convert_element_type x7 -> x6, other arithmetic: 83.4 us -> 6.99 us  [the longest x3 2.86 us: scatter(): lax.psum_scatter(jnp.concatenate(parts, axis=1), AXES, scatter_dimension=...]
    all_gather x1 -> x0, blocking collectives: 70.4 us -> none  [on_device(): lax.all_gather(gain_master.astype(jnp.bfloat16), ('seq', 'mem'), axis=1,...]
    unnamed x4 -> x7, waiting for transfers between devices: 0.07 us -> 66.8 us
    unnamed x213 -> x81, local copies, waits for them, and re-layouts: 65.3 us -> 19.3 us
  transfers between devices with their start and end apart: 8 -> 8, of which waited for: 4 -> 6; matrix products, arithmetic and copies ran while one was open for 59% -> 5% of each run, Pallas kernels for 0% -> 10%
where the time goes in v1:
time: 835 us; the launch traced here: 825 us
  waiting for transfers between devices  467 us (56%)
  Pallas kernels  215 us (26%)
  local copies, waits for them, and re-layouts  43 us (5%)
  blocking collectives  39.4 us (5%)
  other arithmetic  30 us (4%)
  between operations  19.8 us (2%)
  starting transfers between devices  10.1 us (1%)
    reduce_scatter x2, waiting for transfers between devices, scatter(): lax.psum_scatter(jnp.concatenate(parts, axis=1), AXES, scatter_dimension=...  254 us
    all_gather x3, waiting for transfers between devices, gather(): return lax.all_gather(shard, AXES, axis=0, tiled=True)  146 us
    unnamed x7, waiting for transfers between devices  66.8 us
    pallas_call x2, Pallas kernels, attn_bwd(): pl.pallas_call(functools.partial(bwd_kernel, causal=causal, bq=bq, hs=hs)...  53.7 us
    pallas_call x1, Pallas kernels, mlp(): pl.pallas_call(functools.partial(mlp_kernel, tb=tb), grid=(nc,), in_specs...  48.6 us
    psum x1, blocking collectives, on_device(): grad_norm = jnp.sqrt(lax.psum(squares, AXES))  39.4 us
    pallas_call x7, Pallas kernels, wgrad(): pl.pallas_call(wgrad_kernel, grid=(F // fb,), in_specs=[full((L, D)), pl....  32 us
    pallas_call x2, Pallas kernels, attn_fwd(): pl.pallas_call(functools.partial(fwd_kernel, causal=causal, bq=bq, hs=hs)...  30.6 us
  transfers between devices with their start and end apart: 8, of which 6 were waited for; matrix products, arithmetic and copies ran while one was open for 5% of the time, Pallas kernels for 10%

profile of v1, /device:TPU:0, one launch (start us, length us, event | category | flops | bytes accessed | tf_op | source)
XLA Modules:
  0.0 824.5 jit_solution(16057992504837169772)
XLA Ops:
  12.6 6.3 all-to-all-start
  20.3 70.3 %all-gather.4.cloned.1.call-done = bf16[768,2432]{1,0:T(8,128)(2,1)} async-done(((bf16[24,2432]{1,0:T(8,128)(2,1)}), bf16[768,2432]{1,0:T(8,128)(2,1)}) %all-gather.4.cloned.1.call-update) | async-done | bytes 3735568 | tf_op jit(solution)/shard_map/all_gather | solution.py:323
  93.9 4.0 slice.163.w_ref.w0_ref.w1_ref.w2_ref
  98.0 9.2 %shard_map.237 = (bf16[1024,768]{1,0:T(8,128)(2,1)}, bf16[2304,1024]{1,0:T(8,128)(2,1)}) custom-call(bf16[1024,768]{1,0:T(8,128)(2,1)} %bitcast.87, f32[1,768]{1,0:T(1,128)} %copy.64.g_ref, bf16[768,2304]{1,0:T(8,128)(2,1)} %slice.163.w_ref.w0_ref.w1_ref.w2_ref), custom_call_target="tpu_custom_call" | custom-call | tf_op jit(solution)/shard_map/pallas_call | solution.py:138
  107.2 4.0 fusion.21
  111.2 11.9 %shard_map.238 = (bf16[768,1024]{1,0:T(8,128)(2,1)S(1)}, f32[12,1,1024]{2,1,0:T(1,128)S(1)}) custom-call(s32[1]{0:T(128)S(6)} %copy.93.len_ref, bf16[768,1024]{1,0:T(8,128)(2,1)S(1)} %get-tuple-element.124.qT_ref, bf16[768,1024]{1,0:T(8,128)(2,1)S(1)} %get-tuple-element.123.kT_ref, bf16[768,1024]{1,0:T(8,128)(2,1)} %get-tuple-element.122.vT_ref), custom_call_target="tpu_custom_call" | custom-call | tf_op jit(solution)/shard_map/pallas_call | solution.py:63
  123.1 1.1 copy-done.3
  124.3 36.1 %all-gather.6.cloned.1.call-done = bf16[768,3840]{1,0:T(8,128)(2,1)} async-done(((bf16[24,3840]{1,0:T(8,128)(2,1)}), bf16[768,3840]{1,0:T(8,128)(2,1)}) %all-gather.6.cloned.1.call-update) | async-done | bytes 5898256 | tf_op jit(solution)/shard_map/all_gather | solution.py:323
  160.4 3.2 slice.172.w_ref.w5_ref.w6_ref
  163.6 6.4 shard_map.240
  170.0 4.0 fusion.20
  174.0 7.8 shard_map.239
  181.9 3.5 fusion.22
  185.3 18.7 %shard_map.241 = (bf16[768,1024]{1,0:T(8,128)(2,1)S(1)}, f32[12,1,1024]{2,1,0:T(1,128)S(1)}) custom-call(s32[1]{0:T(128)S(6)} %copy.94.len_ref, bf16[768,1024]{1,0:T(8,128)(2,1)S(1)} %copy-done.7, bf16[768,1024]{1,0:T(8,128)(2,1)S(1)} %get-tuple-element.126.kT_ref, bf16[768,1024]{1,0:T(8,128)(2,1)} %get-tuple-element.125.vT_ref), custom_call_target="tpu_custom_call" | custom-call | tf_op jit(solution)/shard_map/pallas_call | solution.py:63
  204.1 1.1 copy-done.4
  205.2 39.7 %all-gather.8.cloned.1.call-done.wg_ref.wu_ref.wd_ref = bf16[768,6144]{1,0:T(8,128)(2,1)} async-done(((bf16[24,6144]{1,0:T(8,128)(2,1)}), bf16[768,6144]{1,0:T(8,128)(2,1)}) %all-gather.8.cloned.1.call-update) | async-done | bytes 9437200 | tf_op jit(solution)/shard_map/all_gather | solution.py:323
  244.9 48.6 %shard_map.242 = (bf16[1024,768]{1,0:T(8,128)(2,1)}, f32[1024,768]{1,0:T(8,128)}, bf16[768,1024]{1,0:T(8,128)(2,1)}, bf16[768,768]{1,0:T(8,128)(2,1)}, f32[1,768...) custom-call(s32[1]{0:T(128)S(6)} %copy.93.len_ref, ...), custom_call_target="tpu_custom_call" | custom-call | tf_op jit(solution)/shard_map/pallas_call | solution.py:227
  293.5 32.7 %shard_map.243 = (bf16[768,1024]{1,0:T(8,128)(2,1)S(1)}, bf16[768,1024]{1,0:T(8,128)(2,1)S(1)}, bf16[768,1024]{1,0:T(8,128)(2,1)S(1)}) custom-call(s32[1]{0:T(128)S(6)} %copy.94.len_ref, bf16[768,1024]{1,0:T(8,128)(2,1)} %get-tuple-element.45.qT_ref, bf16[768,1024]{1,0:T(8,128)(2,1)} %copy-done.2, bf16[768,1024]{1,0:T(8,128)(2,1)} %get-tuple-element.125.vT_ref, ...), custom_call_target="tpu_custom_call" | custom-call | tf_op jit(solution)/shard_map/pallas_call | solution.py:113
  327.4 1.2 copy-done.6
  328.5 1.2 copy-done.8
  329.7 9.9 %shard_map.244 = (f32[1024,768]{1,0:T(8,128)}, bf16[768,1024]{1,0:T(8,128)(2,1)}, bf16[1024,768]{1,0:T(8,128)(2,1)}, f32[1,768]{1,0:T(1,128)}) custom-call(f32[1024,768]{1,0:T(8,128)} %get-tuple-element.44.h1_ref, f32[1024,768]{1,0:T(8,128)} %get-tuple-element.48.gh2_ref, bf16[768,1024]{1,0:T(8,128)(2,1)} %copy-done.8, ...), custom_call_target="tpu_custom_call" | custom-call | tf_op jit(solution)/shard_map/pallas_call | solution.py:253
  339.6 21.0 %shard_map.245 = (bf16[768,1024]{1,0:T(8,128)(2,1)S(1)}, bf16[768,1024]{1,0:T(8,128)(2,1)S(1)}, bf16[768,1024]{1,0:T(8,128)(2,1)S(1)}) custom-call(s32[1]{0:T(128)S(6)} %copy.93.len_ref, bf16[768,1024]{1,0:T(8,128)(2,1)} %copy-done.1, bf16[768,1024]{1,0:T(8,128)(2,1)} %copy-done, bf16[768,1024]{1,0:T(8,128)(2,1)} %get-tuple-element.122.vT_ref, ...), custom_call_target="tpu_custom_call" | custom-call | tf_op jit(solution)/shard_map/pallas_call | solution.py:113
  361.7 1.1 copy-done.10
  362.9 1.2 copy-done.11
  364.1 4.5 shard_map.248
  368.6 4.6 shard_map.249
  373.2 4.5 shard_map.250
  377.7 10.4 %shard_map.246 = (f32[1024,768]{1,0:T(8,128)}, f32[1,768]{1,0:T(1,128)}) custom-call(bf16[1024,768]{1,0:T(8,128)(2,1)} %bitcast.89, f32[1024,768]{1,0:T(8,128)} %get-tuple-element.52.gh1_ref, bf16[768,1024]{1,0:T(8,128)(2,1)} %copy-done.9, bf16[768,1024]{1,0:T(8,128)(2,1)} %copy-done.10, bf16[768,1024]{1,0:T(8,128)(2,1)} %copy-done.11, ...), custom_call_target="tpu_custom_call" | custom-call | tf_op jit(solution)/shard_map/pallas_call | solution.py:293
  389.7 2.9 fusion.1
  392.7 4.5 shard_map.251
  397.2 4.6 shard_map.252
  401.8 4.6 shard_map.253
  406.4 4.7 shard_map.254
  411.1 1.2 constant_dynamic-update-slice_fusion.9
  412.3 1.2 constant_dynamic-update-slice_fusion.8
  413.4 1.2 constant_dynamic-update-slice_fusion.7
  415.8 1.2 constant_dynamic-update-slice_fusion.5
  417.1 1.9 copy-done.19
  418.9 8.2 pad_maximum_fusion
  428.2 6.4 shard_map.247
  434.6 3.6 all-to-all-start.1
  438.2 66.7 %reduce-scatter.10.cloned.1.call-done = bf16[24,2432]{1,0:T(8,128)(2,1)} async-done(((bf16[768,2432]{1,0:T(8,128)(2,1)}), bf16[24,2432]{1,0:T(8,128)(2,1)}) %reduce-scatter.10.cloned.1.call-update) | async-done | bytes 116752
  506.5 115.6 %reduce-scatter.6.cloned.1.call-done = bf16[24,3840]{1,0:T(8,128)(2,1)} async-done(((bf16[768,3840]{1,0:T(8,128)(2,1)}), bf16[24,3840]{1,0:T(8,128)(2,1)}) %reduce-scatter.6.cloned.1.call-update) | async-done | bytes 184336 | tf_op jit(solution)/shard_map/reduce_scatter | solution.py:327
  623.9 138.7 %reduce-scatter.8.cloned.1.call-done = bf16[24,6144]{1,0:T(8,128)(2,1)} async-done(((bf16[768,6144]{1,0:T(8,128)(2,1)}), bf16[24,6144]{1,0:T(8,128)(2,1)}) %reduce-scatter.8.cloned.1.call-update) | async-done | bytes 294928 | tf_op jit(solution)/shard_map/reduce_scatter | solution.py:327
  766.3 1.9 convert_element_type.27
  768.3 39.4 %psum.7 = f32[]{:T(128)} all-reduce(f32[]{:T(128)S(6)} %add.64), channel_id=1, replica_groups=mesh['seq'=8,'mem'=4] {'seq','mem'}, use_global_device_ids=true, to_apply=%region_6.7 | all-reduce | flops 1 | bytes 8 | tf_op jit(solution)/shard_map/psum | solution.py:372
  811.0 2.7 multiply_subtract_fusion
  813.8 2.6 multiply_subtract_fusion.1
  (118 shorter events, 22.8 us)
Async XLA Ops:
  7.2 83.4 %all-gather.4.cloned.1.call-start = ((), (), s32[]{:S(2)}) async-start(), calls=%async_computation.5 | async-start | bytes 3852288 | tf_op jit(solution)/shard_map/all_gather | solution.py:323
  9.9 150.5 %all-gather.6.cloned.1.call-start = ((), (), s32[]{:S(2)}) async-start(), calls=%async_computation.6 | async-start | bytes 6082560 | tf_op jit(solution)/shard_map/all_gather | solution.py:323
  10.0 0.7 copy-start.25
  10.7 234.2 %all-gather.8.cloned.1.call-start = ((), (), s32[]{:S(2)}) async-start(), calls=%async_computation.7 | async-start | bytes 9732096 | tf_op jit(solution)/shard_map/all_gather | solution.py:323
  12.6 151.0 %all-to-all-start = ((bf16[4,256,768]{2,1,0:T(8,128)(2,1)}), bf16[4,256,768]{2,1,0:T(8,128)(2,1)}, u32[]{:S(2)}, u32[]{:S(2)}) async-start(bf16[4,256,768]{2,1,0:T(8,128)(2,1)} %param.15), calls=%async_computation | async-start | bytes 3145728 | tf_op jit(solution)/shard_map/all_to_all | solution.py:338
  19.0 485.9 %reduce-scatter.10.cloned.1.call-start = ((), (), s32[]{:S(2)}) async-start(), calls=%async_computation.10 | async-start | bytes 3852288
  111.2 52.4 %copy-start = (bf16[768,1024]{1,0:T(8,128)(2,1)}, bf16[768,1024]{1,0:T(8,128)(2,1)S(1)}, u32[]{:S(2)}) copy-start(bf16[768,1024]{1,0:T(8,128)(2,1)S(1)} %get-tuple-element.123.kT_ref) | copy-start | bytes 4718596
  111.2 52.4 %copy-start.1 = (bf16[768,1024]{1,0:T(8,128)(2,1)}, bf16[768,1024]{1,0:T(8,128)(2,1)S(1)}, u32[]{:S(2)}) copy-start(bf16[768,1024]{1,0:T(8,128)(2,1)S(1)} %get-tuple-element.124.qT_ref) | copy-start | bytes 4718596
  123.1 1.2 copy-start.3
  181.9 3.5 copy-start.7
  185.3 108.2 %copy-start.2 = (bf16[768,1024]{1,0:T(8,128)(2,1)}, bf16[768,1024]{1,0:T(8,128)(2,1)S(1)}, u32[]{:S(2)}) copy-start(bf16[768,1024]{1,0:T(8,128)(2,1)S(1)} %get-tuple-element.126.kT_ref) | copy-start | bytes 4718596
  204.1 1.1 copy-start.4
  326.2 1.1 copy-start.5
  327.3 1.2 copy-start.6
  328.5 1.2 copy-start.8
  360.6 1.1 copy-start.9
  361.7 1.1 copy-start.10
  362.9 1.2 copy-start.11
  377.7 11.1 %copy-start.28 = (f32[1,768]{1,0:T(1,128)S(1)}, f32[1,768]{1,0:T(1,128)}, u32[]{:S(2)}) copy-start(f32[1,768]{1,0:T(1,128)} %get-tuple-element.63) | copy-start | bytes 9220
  377.7 11.1 %copy-start.27 = (f32[1,768]{1,0:T(1,128)S(1)}, f32[1,768]{1,0:T(1,128)}, u32[]{:S(2)}) copy-start(f32[1,768]{1,0:T(1,128)} %get-tuple-element.64) | copy-start | bytes 9220
  377.7 12.0 %copy-start.12 = (bf16[768,768]{1,0:T(8,128)(2,1)S(1)}, bf16[768,768]{1,0:T(8,128)(2,1)}, u32[]{:S(2)}) copy-start(bf16[768,768]{1,0:T(8,128)(2,1)} %shard_map.248) | copy-start | bytes 3538948
  377.7 12.0 %copy-start.13 = (bf16[768,768]{1,0:T(8,128)(2,1)S(1)}, bf16[768,768]{1,0:T(8,128)(2,1)}, u32[]{:S(2)}) copy-start(bf16[768,768]{1,0:T(8,128)(2,1)} %shard_map.249) | copy-start | bytes 3538948
  377.7 12.0 %copy-start.14 = (bf16[768,768]{1,0:T(8,128)(2,1)S(1)}, bf16[768,768]{1,0:T(8,128)(2,1)}, u32[]{:S(2)}) copy-start(bf16[768,768]{1,0:T(8,128)(2,1)} %shard_map.250) | copy-start | bytes 3538948
  392.6 229.5 %reduce-scatter.6.cloned.1.call-start = ((), (), s32[]{:S(2)}) async-start(), calls=%async_computation.8 | async-start | bytes 6082560 | tf_op jit(solution)/shard_map/reduce_scatter | solution.py:327
  406.3 4.8 copy-start.15
  406.3 5.9 copy-start.17
  411.1 2.4 copy-start.18
  411.1 3.5 copy-start.16
  412.3 3.5 copy-start.22
  417.0 2.0 copy-start.19
  417.0 345.5 %reduce-scatter.8.cloned.1.call-start = ((), (), s32[]{:S(2)}) async-start(), calls=%async_computation.9 | async-start | bytes 9732096 | tf_op jit(solution)/shard_map/reduce_scatter | solution.py:327
  427.1 0.7 copy-start.26
  427.1 0.9 copy-start.29
  427.1 0.9 copy-start.30
  434.6 331.7 %all-to-all-start.1 = ((bf16[4,256,768]{2,1,0:T(8,128)(2,1)}), bf16[4,256,768]{2,1,0:T(8,128)(2,1)S(1)}, u32[]{:S(2)}, u32[]{:S(2)}) async-start(bf16[4,256,768]{2,1,0:T(8,128)(2,1)} %bitcast.90), calls=%async_computation.1 | async-start | bytes 3145728 | tf_op jit(solution)/shard_map/all_to_all | solution.py:356
  505.8 0.7 copy-start.23
  763.6 47.5 %copy-start.20 = (f32[3,24,2048]{2,1,0:T(8,128)S(1)}, f32[3,24,2048]{2,1,0:T(8,128)}, u32[]{:S(2)}) copy-start(f32[3,24,2048]{2,1,0:T(8,128)} %param.22) | copy-start | bytes 1769476
  768.3 45.5 %copy-start.21 = (f32[8,24,768]{2,1,0:T(8,128)S(1)}, f32[8,24,768]{2,1,0:T(8,128)}, u32[]{:S(2)}) copy-start(f32[8,24,768]{2,1,0:T(8,128)} %param.19) | copy-start | bytes 1769476
  768.3 45.5 %copy-start.24 = (f32[8,24,768]{2,1,0:T(8,128)S(1)}, f32[8,24,768]{2,1,0:T(8,128)}, u32[]{:S(2)}) copy-start(f32[8,24,768]{2,1,0:T(8,128)} %param.20) | copy-start | bytes 1769476
Sparse Core Ops, SparseCore 0:
  11.4 79.0 all-gather.3
  93.9 66.4 all-gather.5
  163.8 81.0 all-gather.7
  392.7 112.0 reduce-scatter.9
  510.3 111.6 reduce-scatter.5
  627.8 134.6 reduce-scatter.7

commit v2 on v1

v2 whole, which is shorter than its diff:
```python
import functools, math
import jax, jax.numpy as jnp
from jax import lax
from jax.sharding import PartitionSpec as P
from jax.experimental import pallas as pl
from jax.experimental.pallas import tpu as pltpu
bf=jnp.bfloat16; f32=jnp.float32
HD=64; HEADS=12
NEG=-1e30
VA=24*2**20
LOG2E=math.log2(math.e)
TN=(((0,),(0,)),((),())); NN=(((1,),(0,)),((),())); NT=(((1,),(1,)),((),()))
def dg(a,b,dims): return lax.dot_general(a,b,dims,preferred_element_type=f32)
def rows16(cols, width, pad=16):
    idx=lax.broadcasted_iota(jnp.int32,(pad,width),0)
    out=jnp.zeros((pad,width),f32)
    for i,c in enumerate(cols): out=jnp.where(idx==i,c,out)
    return out.astype(bf)
def split3(x):
    hi=x.astype(bf).astype(f32); r=x-hi; mid=r.astype(bf).astype(f32); lo=r-mid
    return hi,mid,lo
def scaled_query(qT):
    s=qT.astype(f32)*(0.125*LOG2E)
    hi=s.astype(bf); lo=(s-hi.astype(f32)).astype(bf)
    return hi,lo


def causal_mask(x,q0,bq,fill):
    ki=lax.broadcasted_iota(jnp.int32,(bq,bq),0); qi=lax.broadcasted_iota(jnp.int32,(bq,bq),1)
    d=jnp.where(ki<=qi,x[q0:],fill)
    return jnp.concatenate([x[:q0],d],axis=0) if q0 else d

def fwd_kernel(len_ref,qT_ref,kT_ref,vT_ref,oT_ref,lse_ref,*,causal,bq,hs):
    L=qT_ref.shape[1]; K=kT_ref.shape[1]
    n=len_ref[0]
    kpos=lax.broadcasted_iota(jnp.int32,(1,K),1)
    kx=rows16([jnp.where(kpos<n,0.0,NEG)],K); qx=rows16([jnp.ones((1,L),f32)],L); vx=rows16([jnp.ones((1,K),f32)],K)
    ops=[]
    for h in range(hs):
        r=slice(h*HD,(h+1)*HD)
        kT=kT_ref[r,:]
        hi,lo=scaled_query(qT_ref[r,:])
        ops.append((jnp.concatenate([kT,kT,kx],axis=0),jnp.concatenate([hi,lo,qx],axis=0),jnp.concatenate([vT_ref[r,:],vx],axis=0)))
    jobs=[(h,q0) for h in range(hs) for q0 in range(0,L,bq)]
    def score(j):
        h,q0=j; ke=min(K,q0+bq) if causal else K
        return dg(ops[h][0][:,:ke],ops[h][1][:,q0:q0+bq],TN)
    nxt=score(jobs[0])
    for i,(h,q0) in enumerate(jobs):
        s=nxt
        if i+1<len(jobs): nxt=score(jobs[i+1])
        ke=s.shape[0]
        if causal: s=causal_mask(s,q0,bq,NEG)
        m=jnp.max(s,axis=0,keepdims=True)
        p=jnp.exp2(s-m).astype(bf)
        o=dg(ops[h][2][:,:ke],p,NN)
        l=o[HD:HD+1]
        oT_ref[h*HD:(h+1)*HD,q0:q0+bq]=(o[:HD]*(1.0/l)).astype(bf)
        lse_ref[h,:,q0:q0+bq]=m+jnp.log2(l)

def head_block(hs,w,offset=0):
    return pl.BlockSpec((hs*HD,w),lambda h:(h+offset//hs,0))
def attn_fwd(n,q,k,v,causal,bq=256,hs=2):
    L=q[0].shape[1]; K=k[0].shape[1]; D=HEADS*HD
    return pl.pallas_call(functools.partial(fwd_kernel,causal=causal,bq=bq,hs=hs),grid=(HEADS//hs,),
      in_specs=[pl.BlockSpec(memory_space=pltpu.SMEM),head_block(hs,L,q[1]),head_block(hs,K,k[1]),head_block(hs,K,v[1])],
      out_specs=[head_block(hs,L),pl.BlockSpec((hs,1,L),lambda h:(h,0,0))],
      out_shape=[jax.ShapeDtypeStruct((D,L),bf),jax.ShapeDtypeStruct((HEADS,1,L),f32)],
      compiler_params=pltpu.CompilerParams(vmem_limit_bytes=VA),
    )(n,q[0],k[0],v[0])

def bwd_kernel(len_ref,qT_ref,kT_ref,vT_ref,oT_ref,gT_ref,lse_ref,dq_ref,dk_ref,dv_ref,dka,dva,*,causal,bq,hs):
    L=qT_ref.shape[1]; K=kT_ref.shape[1]
    n=len_ref[0]
    kpos=lax.broadcasted_iota(jnp.int32,(1,K),1)
    bias=jnp.where(kpos<n,0.0,NEG)
    one_k=jnp.ones((1,K),f32)
    kx=rows16([bias,one_k,one_k,one_k],K); vx=rows16([one_k,one_k,one_k],K)
    ops=[]
    for h in range(hs):
        r=slice(h*HD,(h+1)*HD)
        kT=kT_ref[r,:]; qT=qT_ref[r,:]; gT=gT_ref[r,:]
        hi,lo=scaled_query(qT)
        delta=jnp.sum(oT_ref[r,:].astype(f32)*gT.astype(f32),axis=0,keepdims=True)
        ops.append(dict(k=kT,q=qT,g=gT,kaug=jnp.concatenate([kT,kT,kx],axis=0),
          qaug=jnp.concatenate([hi,lo,rows16([jnp.ones((1,L),f32),*split3(-lse_ref[h])],L)],axis=0),
          vaug=jnp.concatenate([vT_ref[r,:],vx],axis=0),
          gaug=jnp.concatenate([gT,rows16(list(split3(-delta)),L)],axis=0)))
    jobs=[(h,q0) for h in range(hs) for q0 in reversed(range(0,L,bq))]
    def score(j):
        h,q0=j; ke=min(K,q0+bq) if causal else K; sl=slice(q0,q0+bq); o=ops[h]
        return dg(o["kaug"][:,:ke],o["qaug"][:,sl],TN),dg(o["vaug"][:,:ke],o["gaug"][:,sl],TN)
    nxt=score(jobs[0])
    for i,(h,q0) in enumerate(jobs):
        s,dp=nxt
        if i+1<len(jobs): nxt=score(jobs[i+1])
        ke=s.shape[0]; sl=slice(q0,q0+bq); o=ops[h]; r=slice(h*HD,(h+1)*HD)
        p=jnp.exp2(s)
        if causal: p=causal_mask(p,q0,bq,0.0)
        ds=(p*dp).astype(bf)
        pb=p.astype(bf)
        dq_ref[r,sl]=(dg(o["k"][:,:ke],ds,NN)*0.125).astype(bf)
        dv=dg(o["g"][:,sl],pb,NT)
        dk=dg(o["q"][:,sl],ds,NT)
        if q0==L-bq:
            dka[r]=dk; dva[r]=dv
        else:
            dka[r,:ke]+=dk; dva[r,:ke]+=dv
    dk_ref[...]=(dka[...]*0.125).astype(bf)
    dv_ref[...]=dva[...].astype(bf)

def bwd_part_kernel(*refs,**kw):
    bwd_kernel(*refs[:7],*refs[10:],**kw)
def attn_bwd(n,q,k,v,oT,gT,lse,causal,bq=256,hs=2,part=None,into=None):
    L=q[0].shape[1]; K=k[0].shape[1]; D=HEADS*HD
    h0,hn=part or (0,HEADS)
    hb=lambda w,o=0: head_block(hs,w,o+h0)
    S=jax.ShapeDtypeStruct
    specs=[pl.BlockSpec(memory_space=pltpu.SMEM),hb(L,q[1]),hb(K,k[1]),hb(K,v[1]),hb(L),hb(L),pl.BlockSpec((hs,1,L),lambda h:(h+h0//hs,0,0))]
    args=(n,q[0],k[0],v[0],oT,gT,lse)
    if into is not None:
        specs+=[pl.BlockSpec(memory_space=pl.ANY)]*3
        args+=tuple(into)
    return pl.pallas_call(functools.partial(bwd_kernel if into is None else bwd_part_kernel,causal=causal,bq=bq,hs=hs),grid=(hn//hs,),
      in_specs=specs,out_specs=[hb(L),hb(K),hb(K)],
      out_shape=[S((D,L),bf),S((D,K),bf),S((D,K),bf)],
      input_output_aliases={} if into is None else {7:0,8:1,9:2},
      scratch_shapes=[pltpu.VMEM((hs*HD,K),f32),pltpu.VMEM((hs*HD,K),f32)],
      compiler_params=pltpu.CompilerParams(vmem_limit_bytes=VA),
    )(*args)

TT=(((0,),(1,)),((),()))
EPS=1e-6
VL=60*2**20
def cp(mb=24): return pltpu.CompilerParams(vmem_limit_bytes=mb*2**20)
def full(shape): return pl.BlockSpec(shape,lambda i:(0,)*len(shape))
GC=0.7978845608028654

def rms_r(v): return lax.rsqrt(jnp.mean(v*v,axis=-1,keepdims=True)+EPS)

def wcol(D,j): return pl.BlockSpec((D,D),lambda i:(0,j))
def gain_spec(D): return pl.BlockSpec((8,D),lambda i:(0,0))

def proj_kernel(x_ref,e_ref,w_ref,n_ref,yT_ref,g_ref):
    @pl.when(pl.program_id(0)==0)
    def _():
        g=e_ref[...].astype(f32).T[0:8,:]
        g_ref[...]=g
        x=x_ref[...].astype(f32)
        n_ref[...]=(x*rms_r(x)*g[0:1,:]).astype(bf)
    yT_ref[...]=dg(w_ref[...],n_ref[...],TT).astype(bf)
def norm_proj(x,w,fb=384):
    L,D=x.shape; F=3*D
    return pl.pallas_call(proj_kernel,grid=(F//fb,),
      in_specs=[full((L,D)),pl.BlockSpec((D,128),lambda i:(0,F//128)),pl.BlockSpec((D,fb),lambda i:(0,i))],
      out_specs=[full((L,D)),pl.BlockSpec((fb,L),lambda i:(i,0)),gain_spec(D)],
      out_shape=[jax.ShapeDtypeStruct((L,D),bf),jax.ShapeDtypeStruct((F,L),bf),jax.ShapeDtypeStruct((8,D),f32)],compiler_params=cp())(x,w,w)
def memproj_kernel(x_ref,w_ref,yT_ref):
    yT_ref[...]=dg(w_ref[...],x_ref[...],TT).astype(bf)
def mem_proj(x,w,first_col,fb=384):
    L,D=x.shape; F=2*D
    return pl.pallas_call(memproj_kernel,grid=(F//fb,),
      in_specs=[full((L,D)),pl.BlockSpec((D,fb),lambda i:(0,first_col//fb+i))],
      out_specs=pl.BlockSpec((fb,L),lambda i:(i,0)),
      out_shape=jax.ShapeDtypeStruct((F,L),bf),compiler_params=cp())(x,w)

def post_self_kernel(x_ref,oT_ref,w3_ref,w4_ref,g_ref,h_ref,n_ref,cT_ref):
    h=x_ref[...].astype(f32)+dg(oT_ref[...],w3_ref[...],TT)
    h_ref[...]=h
    n=(h*rms_r(h)*g_ref[1:2,:]).astype(bf)
    n_ref[...]=n
    cT_ref[...]=dg(n,w4_ref[...],NN).astype(bf).T
def post_self(x,oT,w,g,tb=256):
    L,D=x.shape
    tok=pl.BlockSpec((tb,D),lambda i:(i,0)); tokT=pl.BlockSpec((D,tb),lambda i:(0,i))
    return pl.pallas_call(post_self_kernel,grid=(L//tb,),
      in_specs=[tok,tokT,wcol(D,0),wcol(D,1),gain_spec(D)],
      out_specs=[tok,tok,tokT],
      out_shape=[jax.ShapeDtypeStruct((L,D),f32),jax.ShapeDtypeStruct((L,D),bf),jax.ShapeDtypeStruct((D,L),bf)],compiler_params=cp())(x,oT,w,w,g)

def mlp_chunk(n3,gb,wg,wu,wd,dw_ref,inner_s,dgate_s,dup_s,oacc,nacc,tb):
    L=n3.shape[0]; nt=L//tb
    def pre(t):
        sl=slice(t*tb,(t+1)*tb)
        a=n3[sl,:]
        return dg(a,wg[...],NN),dg(a,wu[...],NN),dg(gb[sl,:],wd[...],NN)
    nxt=pre(0)
    for t in range(nt):
        sl=slice(t*tb,(t+1)*tb)
        g,u,di=nxt
        if t+1<nt: nxt=pre(t+1)
        g2=g*g
        th=jnp.tanh(g*(GC+(GC*0.044715)*g2))
        hp=0.5+0.5*th
        ge=g*hp
        dge=hp+(0.5*g)*(1.0-th*th)*(GC+(3*GC*0.044715)*g2)
        inner=(ge*u).astype(bf)
        dgate=(di*u*dge).astype(bf)
        dup=(di*ge).astype(bf)
        inner_s[sl,:]=inner; dgate_s[sl,:]=dgate; dup_s[sl,:]=dup
        oacc[sl,:]+=dg(inner,wd[...],NT)
        nacc[sl,:]+=dg(dgate,wg[...],NT)+dg(dup,wu[...],NT)
    dw_ref[0]=dg(n3[...],dgate_s[...],TN).astype(bf)
    dw_ref[1]=dg(n3[...],dup_s[...],TN).astype(bf)
    dw_ref[2]=dg(gb[...],inner_s[...],TN).astype(bf)

def mlp_kernel(core_ref,len_ref,h1_ref,oT_ref,w7_ref,cot_ref,g_ref,wg_ref,wu_ref,wd_ref,
               out_ref,gh_ref,gmT_ref,gb2_ref,dg_ref,send_ref,keep_ref,
               h2,n3,gb,oacc,nacc,dw,inner_s,dgate_s,dup_s,sems,*,tb):
    L,D=h1_ref.shape
    fc=dw.shape[3]
    i=pl.program_id(0); count=pl.num_programs(0); half=count//2
    slot=lax.rem(i,2)
    def copy(step,to):
        col=pl.multiple_of(lax.rem(step,half)*fc,fc)
        return pltpu.make_async_copy(dw.at[lax.rem(step,2)],to.at[:,:,pl.ds(col,fc)],sems.at[lax.rem(step,2)])
    @pl.when(i==0)
    def _():
        n=len_ref[0]
        for t in range(L//tb):
            sl=slice(t*tb,(t+1)*tb)
            h=h1_ref[sl,:]+dg(oT_ref[:,sl],w7_ref[...],TT)
            h2[sl,:]=h
            oacc[sl,:]=h
            nacc[sl,:]=jnp.zeros((tb,D),f32)
            n3[sl,:]=(h*rms_r(h)*g_ref[2:3,:]).astype(bf)
            row=t*tb+lax.broadcasted_iota(jnp.int32,(tb,1),0)
            gb[sl,:]=jnp.where(row<n,cot_ref[sl,:].astype(f32),0.0).astype(bf)
    @pl.when(i>=2)
    def _():
        copy(i-2,send_ref).wait()
    mlp_chunk(n3,gb,wg_ref,wu_ref,wd_ref,dw.at[slot],inner_s,dgate_s,dup_s,oacc,nacc,tb)
    @pl.when(i<half)
    def _():
        copy(i,send_ref).start()
    @pl.when(i>=half)
    def _():
        copy(i,keep_ref).start()
    @pl.when(i==count-1)
    def _():
        acc=jnp.zeros((1,D),f32)
        for t in range(L//tb):
            sl=slice(t*tb,(t+1)*tb)
            h=h2[sl,:]; uu=nacc[sl,:]
            out_ref[sl,:]=oacc[sl,:].astype(bf)
            r=rms_r(h); ug=uu*g_ref[2:3,:]
            gh=gb[sl,:].astype(f32)+r*ug-h*((r*r*r)*jnp.mean(ug*h,axis=-1,keepdims=True))
            acc=acc+jnp.sum(uu*h*r,axis=0,keepdims=True)
            gh_ref[sl,:]=gh
            b=gh.astype(bf)
            gb2_ref[sl,:]=b
            gmT_ref[:,sl]=dg(b,w7_ref[...],NN).astype(bf).T
        dg_ref[...]=acc
        copy(i-1,keep_ref).wait()
        copy(i,keep_ref).wait()
def mlp(core,n,h1,oT,w_second,cot,g,wm,fc=512,tb=256):
    L,D=h1.shape; F=wm.shape[1]//3; nc=F//fc; hc=nc//2
    whole=lambda shape: pl.BlockSpec(shape,lambda i,c:(0,)*len(shape),pipeline_mode=pl.Buffered(1))
    wb=lambda j: pl.BlockSpec((D,fc),lambda i,c,j=j:(0,j*nc+lax.rem(i+(1-c[0])*hc,nc)))
    S=jax.ShapeDtypeStruct
    hbm=pl.BlockSpec(memory_space=pl.ANY)
    return pl.pallas_call(functools.partial(mlp_kernel,tb=tb),
      grid_spec=pltpu.PrefetchScalarGridSpec(num_scalar_prefetch=1,grid=(nc,),
      in_specs=[pl.BlockSpec(memory_space=pltpu.SMEM),whole((L,D)),whole((D,L)),pl.BlockSpec((D,D),lambda i,c:(0,4),pipeline_mode=pl.Buffered(1)),whole((L,D)),whole((8,D)),wb(0),wb(1),wb(2)],
      out_specs=[whole((L,D)),whole((L,D)),whole((D,L)),whole((L,D)),whole((1,D)),hbm,hbm],
      scratch_shapes=[pltpu.VMEM((L,D),f32),pltpu.VMEM((L,D),bf),pltpu.VMEM((L,D),bf),pltpu.VMEM((L,D),f32),pltpu.VMEM((L,D),f32),
        pltpu.VMEM((2,3,D,fc),bf),pltpu.VMEM((L,fc),bf),pltpu.VMEM((L,fc),bf),pltpu.VMEM((L,fc),bf),pltpu.SemaphoreType.DMA((2,))]),
      out_shape=[S((L,D),bf),S((L,D),f32),S((D,L),bf),S((L,D),bf),S((1,D),f32),S((3,D,F//2),bf),S((3,D,F//2),bf)],
      compiler_params=cp(48))(core,n,h1,oT,w_second,cot,g,wm,wm,wm)

def mid_kernel(h1_ref,gh2_ref,dcT_ref,w4_ref,w3_ref,g_ref,gh1_ref,gmT_ref,gb_ref,dg_ref):
    i=pl.program_id(0)
    u=dg(dcT_ref[...],w4_ref[...],TT)
    h=h1_ref[...]
    r=rms_r(h); ug=u*g_ref[1:2,:]
    gh=gh2_ref[...]+r*ug-h*((r*r*r)*jnp.mean(ug*h,axis=-1,keepdims=True))
    gh1_ref[...]=gh
    b=gh.astype(bf)
    gb_ref[...]=b
    gmT_ref[...]=dg(b,w3_ref[...],NN).astype(bf).T
    s=jnp.sum(u*h*r,axis=0,keepdims=True)
    @pl.when(i==0)
    def _(): dg_ref[...]=s
    @pl.when(i>0)
    def _(): dg_ref[...]+=s
def mid(h1,gh2,dcT,w,g,tb=256):
    L,D=h1.shape
    tok=pl.BlockSpec((tb,D),lambda i:(i,0)); tokT=pl.BlockSpec((D,tb),lambda i:(0,i))
    S=jax.ShapeDtypeStruct
    return pl.pallas_call(mid_kernel,grid=(L//tb,),
      in_specs=[tok,tok,tokT,wcol(D,1),wcol(D,0),gain_spec(D)],
      out_specs=[tok,tokT,tok,full((1,D))],
      out_shape=[S((L,D),f32),S((D,L),bf),S((L,D),bf),S((1,D),f32)],compiler_params=cp())(h1,gh2,dcT,w,w,g)

def wgrads_kernel(core_ref,*refs,pairs,na,ng):
    a_refs=refs[:na]; g_refs=refs[na:na+ng]; send_ref,keep_ref=refs[na+ng:]
    k=core_ref[0]
    W=send_ref.shape[2]
    for out,half in ((send_ref,1-k),(keep_ref,k)):
        start=pl.multiple_of(half*W,W)
        for m,(ia,ig) in enumerate(pairs):
            out[m]=dg(a_refs[ia][...],g_refs[ig][pl.ds(start,W),:],TT).astype(bf)
def wgrads(core,a,g,pairs):
    D=a[0].shape[1]; F=g[0].shape[0]
    v=pl.BlockSpec(memory_space=pltpu.VMEM)
    S=jax.ShapeDtypeStruct((len(pairs),D,F//2),bf)
    return pl.pallas_call(functools.partial(wgrads_kernel,pairs=tuple(pairs),na=len(a),ng=len(g)),
      in_specs=[pl.BlockSpec(memory_space=pltpu.SMEM)]+[v]*(len(a)+len(g)),out_specs=[v,v],
      out_shape=[S,S],compiler_params=cp(40))(core,*a,*g)

def gmem_kernel(kT_ref,vT_ref,w5_ref,w6_ref,o_ref):
    o_ref[...]=(dg(kT_ref[...],w5_ref[...],TT)+dg(vT_ref[...],w6_ref[...],TT)).astype(bf)
def gmem(kT,vT,w56,tb=256):
    D,L=kT.shape
    tokT=pl.BlockSpec((D,tb),lambda i:(0,i))
    return pl.pallas_call(gmem_kernel,grid=(L//tb,),
      in_specs=[tokT,tokT,wcol(D,2),wcol(D,3)],
      out_specs=pl.BlockSpec((tb,D),lambda i:(i,0)),
      out_shape=jax.ShapeDtypeStruct((L,D),bf),compiler_params=cp())(kT,vT,w56,w56)

def first_kernel(x_ref,gh1_ref,qT_ref,kT_ref,vT_ref,w0_ref,w1_ref,w2_ref,g_ref,gt_ref,dg_ref):
    i=pl.program_id(0)
    u=dg(qT_ref[...],w0_ref[...],TT)+dg(kT_ref[...],w1_ref[...],TT)+dg(vT_ref[...],w2_ref[...],TT)
    h=x_ref[...].astype(f32)
    r=rms_r(h); ug=u*g_ref[0:1,:]
    gt_ref[...]=gh1_ref[...]+r*ug-h*((r*r*r)*jnp.mean(ug*h,axis=-1,keepdims=True))
    s=jnp.sum(u*h*r,axis=0,keepdims=True)
    @pl.when(i==0)
    def _(): dg_ref[...]=s
    @pl.when(i>0)
    def _(): dg_ref[...]+=s
def first(x,gh1,qT,kT,vT,w,g,tb=256):
    L,D=x.shape
    tok=pl.BlockSpec((tb,D),lambda i:(i,0)); tokT=pl.BlockSpec((D,tb),lambda i:(0,i))
    S=jax.ShapeDtypeStruct
    wb=lambda j: pl.BlockSpec((D,D),lambda i,j=j:(0,j))
    return pl.pallas_call(first_kernel,grid=(L//tb,),
      in_specs=[tok,tok,tokT,tokT,tokT,wb(0),wb(1),wb(2),gain_spec(D)],
      out_specs=[tok,full((1,D))],
      out_shape=[S((L,D),f32),S((1,D),f32)],compiler_params=cp())(x,gh1,qT,kT,vT,w,w,w,g)

SEQ="seq"
MEM="mem"


def plane_bits(seq_size):
    return max(0,(seq_size//2).bit_length()-1)


def bit_order(core,bits):
    order=list(range(1,bits+1))
    return order if core==0 else order[::-1]


def subset_mask(core,subset,bits):
    order=bit_order(core,bits)
    mask=0
    for p in range(bits):
        if subset>>p&1:
            mask^=1<<(order[p]-1)
    return mask


def cross(x,position,seq_size):
    bits=plane_bits(seq_size)
    perm=[(s,s^(1<<bit_order(s&1,bits)[position])) for s in range(seq_size)]
    return lax.ppermute(x,SEQ,perm)


def swap_core(x,seq_size):
    return lax.ppermute(x,SEQ,[(s,s^1) for s in range(seq_size)])


def shift_mem(x,step,mem_size):
    return lax.ppermute(x,MEM,[(z,(z+step)%mem_size) for z in range(mem_size)])


def copy_kernel(index_ref,*refs,places):
    count=len(places)
    sources=refs[:count]; out=refs[count]; sems=refs[count+1]
    copies=[]
    for j,(source,place) in enumerate(zip(sources,places)):
        copies.append(pltpu.make_async_copy(source,out.at[index_ref[place]],sems.at[j]))
        copies[-1].start()
    for c in copies:
        c.wait()


def place_rows(index,pieces,places,slots):
    piece=pieces[0]
    return pl.pallas_call(functools.partial(copy_kernel,places=tuple(places)),
        in_specs=[pl.BlockSpec(memory_space=pltpu.SMEM)]+[pl.BlockSpec(memory_space=pl.ANY)]*len(pieces),
        out_specs=pl.BlockSpec(memory_space=pltpu.VMEM),
        out_shape=jax.ShapeDtypeStruct((slots,)+piece.shape,piece.dtype),
        scratch_shapes=[pltpu.SemaphoreType.DMA((len(pieces),))],
        compiler_params=cp(20),
    )(index,*pieces)


class Place:
    def __init__(self,seq_size,mem_size):
        self.S=seq_size; self.M=mem_size; self.bits=plane_bits(seq_size); self.NP=seq_size//2
        s=lax.axis_index(SEQ); self.z=lax.axis_index(MEM)
        self.core=s%2; self.plane=s//2

    def slab(self,subset,own=True):
        m0=subset_mask(0,subset,self.bits); m1=subset_mask(1,subset,self.bits)
        c=self.core if own else 1-self.core
        return self.plane^jnp.where(c==0,m0,m1)


def gather_mem_direct(shard,pl_):
    M=pl_.M
    pieces=[shard]+[shift_mem(shard,j,M) for j in range(1,M)]
    index=jnp.stack([(pl_.z-j)%M for j in range(M)]).astype(jnp.int32)
    return place_rows(index,pieces,range(M),M).reshape(M*shard.shape[0],shard.shape[1])


def tie(*values):
    return lax.optimization_barrier(values)


class Gather:
    def __init__(self,slab,here):
        self.here=here; self.pieces={0:slab}; self.other={}
        for p in range(here.bits):
            self.pieces[1<<p]=cross(slab,p,here.S)
        self.other[0]=swap_core(slab,here.S)

    def forward(self,dep):
        here=self.here
        self.pieces[1],dep=tie(self.pieces[1],dep)
        for subset in range(1,here.NP):
            top=subset.bit_length()-1
            if subset not in self.pieces:
                self.pieces[subset]=cross(self.pieces[subset^(1<<top)],top,here.S)
        for subset in range(1,here.NP-1):
            self.other[subset]=swap_core(self.pieces[subset],here.S)
        return dep

    def last(self,dep):
        end=self.here.NP-1
        if end and end not in self.other:
            self.pieces[end],dep=tie(self.pieces[end],dep)
            self.other[end]=swap_core(self.pieces[end],self.here.S)
        return dep

    def hold(self,dep):
        n=self.here.NP
        keys=list(range(n))
        out=tie(*[self.pieces[s] for s in keys],*[self.other[s] for s in keys],dep)
        self.pieces=dict(zip(keys,out[:n])); self.other=dict(zip(keys,out[n:2*n]))
        return out[-1]

    def place(self):
        here=self.here
        n=here.NP
        idx=[here.slab(s)*2+here.core for s in range(n)]+[here.slab(s,False)*2+1-here.core for s in range(n)]
        index=jnp.stack(idx).astype(jnp.int32)
        parts=[self.pieces[s] for s in range(n)]+[self.other[s] for s in range(n)]
        out=place_rows(index,parts,range(2*n),2*n)
        return out.reshape(-1,parts[0].shape[1])


def fold_kernel(index_ref,ka,kb,ra,rb,send,keep):
    send[...]=(kb[...].astype(f32)+rb[...].astype(f32)).astype(bf)
    keep[...]=(ka[...].astype(f32)+ra[...].astype(f32)).astype(bf)


def fold(index,keep,recv):
    G,n,R,W=keep.shape; h=n//2
    low=pl.BlockSpec((1,1,R,W),lambda i,m,ix:(m,ix[i],0,0))
    high=pl.BlockSpec((1,1,R,W),lambda i,m,ix:(m,ix[h+i],0,0))
    out=pl.BlockSpec((1,1,R,W),lambda i,m,ix:(m,i,0,0))
    S=jax.ShapeDtypeStruct((G,h,R,W),bf)
    return pl.pallas_call(fold_kernel,
        grid_spec=pltpu.PrefetchScalarGridSpec(num_scalar_prefetch=1,grid=(h,G),in_specs=[low,high,low,high],out_specs=[out,out]),
        out_shape=[S,S],compiler_params=cp(16))(index,keep,keep,recv,recv)


def split_kernel(index_ref,a,b,*outs):
    for j,o in enumerate(outs):
        z=index_ref[j]
        o[...]=(a[:,:,pl.ds(z,1)].astype(f32)+b[:,:,pl.ds(z,1)].astype(f32)).astype(bf)


def split_mem(index,a,b):
    G,two,M,r,W=a.shape
    full_=pl.BlockSpec(memory_space=pltpu.VMEM)
    S=jax.ShapeDtypeStruct((G,two,1,r,W),bf)
    return pl.pallas_call(split_kernel,in_specs=[pl.BlockSpec(memory_space=pltpu.SMEM),full_,full_],out_specs=[full_]*M,
        out_shape=[S]*M,compiler_params=cp(16))(index,a,b)


def order_kernel(a,b,o):
    for z in range(o.shape[0]):
        o[z]=(a[:,:,z].astype(f32)+b[:,:,z].astype(f32)).astype(bf)


def order_mem(a,b):
    G,two,M,r,W=a.shape
    v=pl.BlockSpec(memory_space=pltpu.VMEM)
    return pl.pallas_call(order_kernel,in_specs=[v,v],out_specs=v,
        out_shape=jax.ShapeDtypeStruct((M,G,two,r,W),bf),compiler_params=cp(16))(a,b)


class Reduce:
    def __init__(self,send,keep,here):
        G,D,W=send.shape
        NP=here.NP; R=D//NP
        self.here=here; self.r=R//2//here.M
        self.recv=swap_core(send,here.S).reshape(G,NP,R,W)
        self.keep=keep.reshape(G,NP,R,W)
        self.index=jnp.stack([here.slab(s) for s in range(NP)]).astype(jnp.int32)
        self.p=here.bits-1

    def fold(self,dep):
        self.recv,dep=tie(self.recv,dep)
        if self.p<0:
            return dep
        go,keep=fold(self.index,self.keep,self.recv)
        go,self.keep,dep=tie(go,keep,dep)
        self.recv=cross(go,self.p,self.here.S)
        self.index=jnp.arange(1<<self.p,dtype=jnp.int32)
        self.p-=1
        return dep

    def halves(self,dep):
        while self.p>=0:
            dep=self.fold(dep)
        self.recv,dep=tie(self.recv,dep)
        G,_,R,W=self.keep.shape
        shape=(G,2,self.here.M,self.r,W)
        return self.keep.reshape(shape),self.recv.reshape(shape),dep

    def over_mem(self,dep):
        a,b,dep=self.halves(dep)
        parts,dep=tie(order_mem(a,b),dep)
        return lax.psum_scatter(parts,MEM,scatter_dimension=0,tiled=True)[0],dep

    def over_mem_direct(self,dep):
        a,b,dep=self.halves(dep)
        M=self.here.M
        parts=split_mem(jnp.stack([(self.here.z+j)%M for j in range(M)]).astype(jnp.int32),a,b)
        total=parts[0].astype(f32)
        for j in range(1,M):
            total=total+shift_mem(parts[j],j,M).astype(f32)
        G,_,_,r,W=a.shape
        return total.reshape(G,2,r,W)


def own_rows(total,pl_):
    give=lax.dynamic_index_in_dim(total,1-pl_.core,1,keepdims=False)
    own=lax.dynamic_index_in_dim(total,pl_.core,1,keepdims=False)
    other=swap_core(give,pl_.S)
    low=jnp.where(pl_.core==0,own,other); high=jnp.where(pl_.core==0,other,own)
    return jnp.concatenate([low,high],axis=-1)


def sum_all(x,pl_):
    for b in range(pl_.S.bit_length()-1):
        x=x+lax.ppermute(x,SEQ,[(s,s^(1<<b)) for s in range(pl_.S)])
    for b in range(pl_.M.bit_length()-1):
        x=x+lax.ppermute(x,MEM,[(z,z^(1<<b)) for z in range(pl_.M)])
    return x

STEP=10
CLIP_NORM=1.0
BETA_FIRST=0.9
BETA_SECOND=0.999
ADAM_EPSILON=1e-08
RATE_MATRIX=0.06
RATE_GAIN=0.6
DECAY_MATRIX=0.01


def adam_step(master,grad,first_moment,second_moment,rate,decay):
    first_new=BETA_FIRST*first_moment+(1.0-BETA_FIRST)*grad
    second_new=BETA_SECOND*second_moment+(1.0-BETA_SECOND)*grad*grad
    first_hat=first_new/(1.0-BETA_FIRST**STEP)
    second_hat=second_new/(1.0-BETA_SECOND**STEP)
    master_new=master-rate*(first_hat/(jnp.sqrt(second_hat)+ADAM_EPSILON)+decay*master)
    return (master_new,first_new,second_new)


def columns(stack):
    return jnp.concatenate([stack[i] for i in range(stack.shape[0])],axis=1)


def on_device(seq_size,mem_size,tokens,memory,cotangent,table_len,patch_count,attn_master,attn_first,attn_second,mlp_master,mlp_first,mlp_second,gain_master,gain_first,gain_second):
    here=Place(seq_size,mem_size)
    core=here.core.reshape(1).astype(jnp.int32)
    rows,D=attn_master.shape[1:]
    aw=attn_master.astype(bf)
    gain_cols=jnp.pad(gain_master.T,((0,0),(0,125))).astype(bf)
    x=tokens[0]
    slab_first=gather_mem_direct(jnp.concatenate([columns(aw[:3]),gain_cols],axis=1),here)
    slab_second=lax.all_gather(columns(aw[3:]),MEM,axis=0,tiled=True)
    slab_mlp=lax.all_gather(columns(mlp_master.astype(bf)),MEM,axis=0,tiled=True)
    slab_first,memory=tie(slab_first,memory)
    mem=lax.all_to_all(memory,"mem",split_axis=0,concat_axis=0,tiled=True).reshape(-1,D)
    first_group=Gather(slab_first,here)
    x=first_group.last(first_group.forward(x))
    slab_second=first_group.hold(slab_second)
    second_group=Gather(slab_second,here)
    w_first=first_group.place()
    n1,qkv,gains=norm_proj(x,w_first)
    qkv=second_group.forward(qkv)
    q,k,v=(qkv,0),(qkv,HEADS),(qkv,2*HEADS)
    o1,lse1=attn_fwd(table_len,q,k,v,True,512,4)
    o1=second_group.last(o1)
    slab_mlp=second_group.hold(slab_mlp)
    mlp_group=Gather(slab_mlp,here)
    w_second=second_group.place()
    mkv=mem_proj(mem,w_second,2*D)
    mkv,o1=tie(mkv,o1)
    h1,n2,cq=post_self(x,o1,w_second,gains)
    cq=mlp_group.forward(cq)
    q2,k2,v2=(cq,0),(mkv,0),(mkv,HEADS)
    o2,lse2=attn_fwd(patch_count,q2,k2,v2,False,512,2)
    o2=mlp_group.last(o2)
    w_mlp=mlp_group.place()
    mixed_out,gh2,gm2,gb2,dg3,mlp_send,mlp_keep=mlp(core,table_len,h1,o2,w_second,cotangent[0],gains,w_mlp)
    red_mlp=Reduce(mlp_send,mlp_keep,here)
    half=HEADS//2
    part=attn_bwd(patch_count,q2,k2,v2,o2,gm2,lse2,False,256,2,(0,half))
    part=(red_mlp.fold(part[0]),)+tuple(part[1:])
    dcq,dmk,dmv=attn_bwd(patch_count,q2,k2,v2,o2,gm2,lse2,False,256,2,(half,half),part)
    gh1,gm1,gb1,dg2=mid(h1,gh2,dcq,w_second,gains)
    gb1=red_mlp.fold(gb1)
    second_send,second_keep=wgrads(core,[gb1,n2,mem,gb2],[o1,dcq,dmk,dmv,o2],[(0,0),(1,1),(2,2),(2,3),(3,4)])
    second_send,dmk=tie(second_send,dmk)
    red_second=Reduce(second_send,second_keep,here)
    gmem_local=gmem(dmk,dmv,w_second)
    gmem_local=red_second.fold(gmem_local)
    t_mlp,gmem_local=red_mlp.over_mem(gmem_local)
    grad_memory=lax.all_to_all(gmem_local.reshape(memory.shape),"mem",split_axis=0,concat_axis=0,tiled=True).astype(f32)
    gm1,gmem_local=tie(gm1,gmem_local)
    dq,dk,dv=attn_bwd(table_len,q,k,v,o1,gm1,lse1,True,256,2)
    first_send,first_keep=wgrads(core,[n1],[dq,dk,dv],[(0,0),(0,1),(0,2)])
    red_first=Reduce(first_send,first_keep,here)
    dq=red_second.fold(dq)
    dq=red_first.fold(dq)
    grad_tokens,dg1=first(x,gh1,dq,dk,dv,w_first,gains)
    dg1=red_first.fold(dg1)
    t_second,dg1=red_second.over_mem(dg1)
    gain_all=sum_all(jnp.concatenate([dg1,dg2,dg3],axis=0),here)
    t_first=red_first.over_mem_direct(dg1)
    totals=(t_first,t_second.astype(f32),t_mlp.astype(f32))
    squares=sum(jnp.sum(t*t) for t in totals)
    grad_norm=jnp.sqrt(sum_all(squares.reshape(1,1),here)[0,0]+jnp.sum(gain_all*gain_all))
    factor=CLIP_NORM/jnp.maximum(grad_norm,CLIP_NORM)
    red=[own_rows(t,here) for t in totals]
    attn_red=jnp.concatenate(red[:2],axis=0)
    mlp_red=red[2]
    device=lax.axis_index("seq")*mem_size+lax.axis_index("mem")
    gain_red=lax.dynamic_slice_in_dim(gain_all,device*rows,rows,1)
    a=adam_step(attn_master,attn_red*factor,attn_first,attn_second,RATE_MATRIX,DECAY_MATRIX)
    m=adam_step(mlp_master,mlp_red*factor,mlp_first,mlp_second,RATE_MATRIX,DECAY_MATRIX)
    gn=adam_step(gain_master,gain_red*factor,gain_first,gain_second,RATE_GAIN,0.0)
    return (mixed_out[None],grad_tokens[None],grad_memory,grad_norm)+a+m+gn


def solution(mesh):
    both=P(("seq","mem"),None,None)
    mid_split=P(None,("seq","mem"),None)
    gain_split=P(None,("seq","mem"))
    return jax.shard_map(functools.partial(on_device,mesh.shape["seq"],mesh.shape["mem"]),mesh=mesh,
        in_specs=(both,P("seq","mem",None),both,P(("seq","mem")),P(("seq","mem")))+(mid_split,)*6+(gain_split,)*3,
        out_specs=(both,both,P("seq","mem",None),P())+(mid_split,)*6+(gain_split,)*3,
        check_vma=False)
```

time: 835 us -> 479 us (0.57)
  waiting for transfers between devices: 467 us -> 101 us
  starting transfers between devices: 10.1 us -> 62.2 us
  blocking collectives: 39.4 us -> 19.9 us
  Pallas kernels: 215 us -> 200 us
  other arithmetic: 30 us -> 19.2 us
    reduce_scatter x2, waiting for transfers between devices: 254 us -> 0.02 us  [over_mem(): lax.psum_scatter(parts, MEM, scatter_dimension=0, tiled=True)[0]]
    all_gather x3 -> x1, waiting for transfers between devices: 146 us -> 0.53 us  [on_device(): lax.all_gather(columns(mlp_master.astype(bf)), MEM, axis=0, tiled=True)]
    ppermute x0 -> x49, waiting for transfers between devices: none -> 86.1 us  [the longest x15 51.4 us: cross(): return lax.ppermute(x, SEQ, perm)]
    unnamed x7 -> x3, waiting for transfers between devices: 66.8 us -> 0.05 us
    ppermute x0 -> x49, starting transfers between devices: none -> 53.8 us  [the longest x15 16.4 us: cross(): return lax.ppermute(x, SEQ, perm)]
    psum x1 -> x0, blocking collectives: 39.4 us -> none  [on_device(): grad_norm = jnp.sqrt(lax.psum(squares, AXES))]
    unnamed x81 -> x168, local copies, waits for them, and re-layouts: 19.3 us -> 47.5 us
    slice x9 -> x0, local copies, waits for them, and re-layouts: 21.2 us -> none  [the longest x1 4.04 us: on_device(): w_qkv = w_first[:, :3 * D]]
  transfers between devices with their start and end apart: 8 -> 54, of which waited for: 6 -> 23; matrix products, arithmetic and copies ran while one was open for 5% -> 3% of each run, Pallas kernels for 10% -> 23%
where the time goes in v2:
time: 479 us; the launch traced here: 475 us
  Pallas kernels  200 us (42%)
  waiting for transfers between devices  101 us (21%)
  starting transfers between devices  62.2 us (13%)
  local copies, waits for them, and re-layouts  49.1 us (10%)
  between operations  23.4 us (5%)
  blocking collectives  19.9 us (4%)
  other arithmetic  19.2 us (4%)
    ppermute x15, waiting for transfers between devices, cross(): return lax.ppermute(x, SEQ, perm)  51.4 us
    pallas_call x3, Pallas kernels, attn_bwd(): pl.pallas_call(functools.partial(bwd_kernel if into is None else bwd_part...  51.3 us
    unnamed x168, local copies, waits for them, and re-layouts  47.5 us
    pallas_call x1, Pallas kernels, mlp(): pl.pallas_call(functools.partial(mlp_kernel, tb=tb), grid_spec=pltpu.Pref...  42.6 us
    pallas_call x2, Pallas kernels, attn_fwd(): pl.pallas_call(functools.partial(fwd_kernel, causal=causal, bq=bq, hs=hs)...  28 us
    all_gather x1, blocking collectives, on_device(): slab_second = lax.all_gather(columns(aw[3:]), MEM, axis=0, tiled=True)  19.9 us
    pallas_call x6, Pallas kernels, fold(): pl.pallas_call(fold_kernel, grid_spec=pltpu.PrefetchScalarGridSpec(num_sc...  16.7 us
    pallas_call x2, Pallas kernels, wgrads(): pl.pallas_call(functools.partial(wgrads_kernel, pairs=tuple(pairs), na=le...  16.6 us
  transfers between devices with their start and end apart: 54, of which 23 were waited for; matrix products, arithmetic and copies ran while one was open for 3% of the time, Pallas kernels for 23%

profile of v2, /device:TPU:0, one launch (start us, length us, event | category | flops | bytes accessed | tf_op | source)
XLA Modules:
  0.0 474.6 jit_solution(88393265138108233)
XLA Ops:
  9.1 3.1 collective-permute-start
  12.2 2.6 collective-permute-start.1
  18.4 4.2 collective-permute-done.1.refs_2_
  26.9 10.1 %collective-permute-done.3.refs_1_ = bf16[96,2432]{1,0:T(8,128)(2,1)S(1)} collective-permute-done((bf16[96,2432]{1,0:T(8,128)(2,1)S(1)}, bf16[96,2432]{1,0:T(8,128)(2,1)S(1)}, u32[]{:S(2)}, u32[]{:S(2)}) %collective-permute-start.3) | collective-permute-done | bytes 466976 | tf_op jit(solution)/shard_map/ppermute | solution.py:367
  38.8 6.8 %collective-permute-done.4.refs_3_ = bf16[96,2432]{1,0:T(8,128)(2,1)S(1)} collective-permute-done((bf16[96,2432]{1,0:T(8,128)(2,1)S(1)}, bf16[96,2432]{1,0:T(8,128)(2,1)S(1)}, u32[]{:S(2)}, u32[]{:S(2)}) %collective-permute-start.4) | collective-permute-done | bytes 466976 | tf_op jit(solution)/shard_map/ppermute | solution.py:367
  45.6 19.9 %all_gather.6.refs_0_ = bf16[96,3840]{1,0:T(8,128)(2,1)S(1)} all-gather(bf16[24,3840]{1,0:T(8,128)(2,1)S(1)} %fusion.4), channel_id=1, replica_groups=mesh['seq'=8,'mem'=4] {'mem'}, dimensions={0}, use_global_device_ids=true | all-gather | bytes 921600 | tf_op jit(solution)/shard_map/all_gather | solution.py:598
  76.5 2.9 shard_map.238
  79.4 6.3 %shard_map.239 = (bf16[1024,768]{1,0:T(8,128)(2,1)S(1)}, bf16[2304,1024]{1,0:T(8,128)(2,1)S(1)}, f32[8,768]{1,0:T(8,128)S(1)}) custom-call(bf16[1024,768]{1,0:T(8,128)(2,1)S(1)} %bitcast.114, bf16[768,2432]{1,0:T(8,128)(2,1)S(1)} %bitcast.105, bf16[768,2432]{1,0:T(8,128)(2,1)S(1)} %bitcast.106), custom_call_target="tpu_custom_call" | custom-call | tf_op jit(solution)/shard_map/pallas_call | solution.py:154
  90.9 3.6 all-to-all-start
  96.1 2.3 copy-done.4
  98.4 10.5 %shard_map.240 = (bf16[768,1024]{1,0:T(8,128)(2,1)S(1)}, f32[12,1,1024]{2,1,0:T(1,128)S(1)}) custom-call(s32[1]{0:T(128)S(6)} %copy.38.len_ref, bf16[2304,1024]{1,0:T(8,128)(2,1)S(1)} %copy-done.4, bf16[2304,1024]{1,0:T(8,128)(2,1)S(1)} %copy-done.4, bf16[2304,1024]{1,0:T(8,128)(2,1)S(1)} %copy-done.4), custom_call_target="tpu_custom_call" | custom-call | tf_op jit(solution)/shard_map/pallas_call | solution.py:65
  114.6 3.5 shard_map.241
  118.1 2.5 copy-done
  120.6 13.3 %all-to-all-done = bf16[4,256,768]{2,1,0:T(8,128)(2,1)S(1)} async-done(((bf16[4,256,768]{2,1,0:T(8,128)(2,1)}), bf16[4,256,768]{2,1,0:T(8,128)(2,1)S(1)}, u32[]{:S(2)}, u32[]{:S(2)}) %all-to-all-start) | async-done | bytes 1572896 | tf_op jit(solution)/shard_map/all_to_all | solution.py:601
  135.0 2.7 copy-done.1
  139.1 3.6 shard_map.242.kT_ref.vT_ref.refs_2_.refs_3_
  142.7 5.6 %shard_map.243 = (f32[1024,768]{1,0:T(8,128)S(1)}, bf16[1024,768]{1,0:T(8,128)(2,1)S(1)}, bf16[768,1024]{1,0:T(8,128)(2,1)S(1)}) custom-call(bf16[1024,768]{1,0:T(8,128)(2,1)S(1)} %bitcast.115, bf16[768,1024]{1,0:T(8,128)(2,1)S(1)} %copy-done.15, bf16[768,3840]{1,0:T(8,128)(2,1)S(1)} %bitcast.94, bf16[768,3840]{1,0:T(8,128)(2,1)S(1)} %bitcast.95, ...), custom_call_target="tpu_custom_call" | custom-call | tf_op jit(solution)/shard_map/pallas_call | solution.py:176
  151.2 17.5 %shard_map.244 = (bf16[768,1024]{1,0:T(8,128)(2,1)S(1)}, f32[12,1,1024]{2,1,0:T(1,128)S(1)}) custom-call(s32[1]{0:T(128)S(6)} %copy.39.len_ref.refs_0_, bf16[768,1024]{1,0:T(8,128)(2,1)S(1)} %get-tuple-element.176.qT_ref.refs_1_, bf16[1536,1024]{1,0:T(8,128)(2,1)S(1)} %shard_map.242.kT_ref.vT_ref.refs_2_.refs_3_, ...), custom_call_target="tpu_custom_call" | custom-call | tf_op jit(solution)/shard_map/pallas_call | solution.py:65
  169.4 3.3 collective-permute-done.22.refs_6_
  173.4 2.5 shard_map.245
  175.9 3.7 copy-done.6
  179.6 42.6 %shard_map.246 = (bf16[1024,768]{1,0:T(8,128)(2,1)}, f32[1024,768]{1,0:T(8,128)}, bf16[768,1024]{1,0:T(8,128)(2,1)S(1)}, bf16[1024,768]{1,0:T(8,128)(2,1)S(1)}, ...) custom-call(s32[1]{0:T(128)} %bitcast.core_ref, s32[1]{0:T(128)S(6)} %copy.38.len_ref, ...), custom_call_target="tpu_custom_call" | custom-call | tf_op jit(solution)/shard_map/pallas_call | solution.py:262
  229.0 15.8 %shard_map.247 = (bf16[768,1024]{1,0:T(8,128)(2,1)S(1)}, bf16[768,1024]{1,0:T(8,128)(2,1)S(1)}, bf16[768,1024]{1,0:T(8,128)(2,1)S(1)}) custom-call(s32[1]{0:T(128)S(6)} %copy.39.len_ref.refs_0_, bf16[768,1024]{1,0:T(8,128)(2,1)S(1)} %copy-done.24, bf16[1536,1024]{1,0:T(8,128)(2,1)S(1)} %shard_map.242.kT_ref.vT_ref.refs_2_.refs_3_, ...), custom_call_target="tpu_custom_call" | custom-call | tf_op jit(solution)/shard_map/pallas_call | solution.py:124
  244.9 5.2 %shard_map.248 = (bf16[3,2,192,1024]{3,2,1,0:T(8,128)(2,1)S(1)}, bf16[3,2,192,1024]{3,2,1,0:T(8,128)(2,1)S(1)}) custom-call(s32[4]{0:T(128)S(1)} %get-tuple-element.294.index_ref, bf16[3,4,192,1024]{3,2,1,0:T(8,128)(2,1)S(1)} %bitcast.110, bf16[3,4,192,1024]{3,2,1,0:T(8,128)(2,1)S(1)} %bitcast.111, bf16[3,4,192,1024]{3,2,1,0:T(8,128)(2,1)} %bitcast.38.ra.rb, ...), custom_call_target="tpu_custom_call" | custom-call | tf_op jit(solution)/shard_map/pallas_call | solution.py:476
  251.1 15.7 %shard_map.249 = (bf16[768,1024]{1,0:T(8,128)(2,1)S(1)}, bf16[768,1024]{1,0:T(8,128)(2,1)S(1)}, bf16[768,1024]{1,0:T(8,128)(2,1)S(1)}) custom-call(s32[1]{0:T(128)S(6)} %copy.39.len_ref.refs_0_, bf16[768,1024]{1,0:T(8,128)(2,1)S(1)} %copy-done.25, ...), custom_call_target="tpu_custom_call", output_to_operand_aliasing={{0}: (7, {}), {1}: (8, {}), {2}: (9, {})} | custom-call | tf_op jit(solution)/shard_map/pallas_call | solution.py:124
  266.9 6.0 %shard_map.250 = (f32[1024,768]{1,0:T(8,128)S(1)}, bf16[768,1024]{1,0:T(8,128)(2,1)S(1)}, bf16[1024,768]{1,0:T(8,128)(2,1)S(1)}, f32[1,768]{1,0:T(1,128)S(1)}) custom-call(f32[1024,768]{1,0:T(8,128)S(1)} %copy-done.29, f32[1024,768]{1,0:T(8,128)S(1)} %copy-done.46, bf16[768,1024]{1,0:T(8,128)(2,1)S(1)} %get-tuple-element.195.dcT_ref.refs_5_, ...), custom_call_target="tpu_custom_call" | custom-call | tf_op jit(solution)/shard_map/pallas_call | solution.py:290
  272.9 6.1 %collective-permute-done.25.ra.rb = bf16[3,2,192,1024]{3,2,1,0:T(8,128)(2,1)S(1)} collective-permute-done((bf16[3,2,192,1024]{3,2,1,0:T(8,128)(2,1)S(1)}, bf16[3,2,192,1024]{3,2,1,0:T(8,128)(2,1)S(1)}, u32[]{:S(2)}, u32[]{:S(2)}) %collective-permute-start.25) | collective-permute-done | bytes 2359328 | tf_op jit(solution)/shard_map/ppermute | solution.py:367
  286.5 10.6 %shard_map.252 = (bf16[5,768,384]{2,1,0:T(8,128)(2,1)}, bf16[5,768,384]{2,1,0:T(8,128)(2,1)}) custom-call(s32[1]{0:T(128)} %bitcast.core_ref, bf16[1024,768]{1,0:T(8,128)(2,1)S(1)} %copy-done.54, bf16[1024,768]{1,0:T(8,128)(2,1)S(1)} %copy-done.50, bf16[1024,768]{1,0:T(8,128)(2,1)S(1)} %bitcast.113, bf16[1024,768]{1,0:T(8,128)(2,1)S(1)} %copy-done.52, ...), custom_call_target="tpu_custom_call" | custom-call | tf_op jit(solution)/shard_map/pallas_call | solution.py:307
  298.6 3.9 shard_map.253
  303.7 4.2 shard_map.254
  309.1 4.4 collective-permute-done.26
  317.2 19.8 %shard_map.256 = (bf16[768,1024]{1,0:T(8,128)(2,1)S(1)}, bf16[768,1024]{1,0:T(8,128)(2,1)S(1)}, bf16[768,1024]{1,0:T(8,128)(2,1)S(1)}) custom-call(s32[1]{0:T(128)S(6)} %copy.38.len_ref, bf16[2304,1024]{1,0:T(8,128)(2,1)S(1)} %copy-done.5, bf16[2304,1024]{1,0:T(8,128)(2,1)S(1)} %copy-done.5, bf16[2304,1024]{1,0:T(8,128)(2,1)S(1)} %copy-done.5, ...), custom_call_target="tpu_custom_call" | custom-call | tf_op jit(solution)/shard_map/pallas_call | solution.py:124
  337.1 6.0 %shard_map.257 = (bf16[3,768,384]{2,1,0:T(8,128)(2,1)}, bf16[3,768,384]{2,1,0:T(8,128)(2,1)S(1)}) custom-call(s32[1]{0:T(128)} %bitcast.core_ref, bf16[1024,768]{1,0:T(8,128)(2,1)S(1)} %copy-done.48, bf16[768,1024]{1,0:T(8,128)(2,1)S(1)} %get-tuple-element.243.refs_1_.qT_ref, bf16[768,1024]{1,0:T(8,128)(2,1)S(1)} %get-tuple-element.228.refs_2_.kT_ref, ...), custom_call_target="tpu_custom_call" | custom-call | tf_op jit(solution)/shard_map/pallas_call | solution.py:307
  344.2 4.4 all-to-all-start.1
  348.6 14.3 %collective-permute-done.29.ra.rb = bf16[5,2,192,384]{3,2,1,0:T(8,128)(2,1)} collective-permute-done((bf16[5,2,192,384]{3,2,1,0:T(8,128)(2,1)}, bf16[5,2,192,384]{3,2,1,0:T(8,128)(2,1)}, u32[]{:S(2)}, u32[]{:S(2)}) %collective-permute-start.29) | collective-permute-done | bytes 1474592 | tf_op jit(solution)/shard_map/ppermute | solution.py:367
  364.3 4.1 shard_map.258
  373.6 7.1 %shard_map.260 = (f32[1024,768]{1,0:T(8,128)}, f32[1,768]{1,0:T(1,128)S(1)}) custom-call(bf16[1024,768]{1,0:T(8,128)(2,1)S(1)} %bitcast.116, f32[1024,768]{1,0:T(8,128)S(1)} %copy-done.45, bf16[768,1024]{1,0:T(8,128)(2,1)S(1)} %copy-done.33, bf16[768,1024]{1,0:T(8,128)(2,1)S(1)} %copy-done.35, bf16[768,1024]{1,0:T(8,128)(2,1)S(1)} %copy-done.37, ...), custom_call_target="tpu_custom_call" | custom-call | tf_op jit(solution)/shard_map/pallas_call | solution.py:337
  380.7 9.6 %collective-permute-done.30.ra.rb = bf16[3,2,192,384]{3,2,1,0:T(8,128)(2,1)S(1)} collective-permute-done((bf16[3,2,192,384]{3,2,1,0:T(8,128)(2,1)S(1)}, bf16[3,2,192,384]{3,2,1,0:T(8,128)(2,1)S(1)}, u32[]{:S(2)}, u32[]{:S(2)}) %collective-permute-start.30) | collective-permute-done | bytes 884768 | tf_op jit(solution)/shard_map/ppermute | solution.py:367
  396.4 5.6 %collective-permute-done.42 = f32[3,768]{1,0:T(4,128)S(1)} collective-permute-done((f32[3,768]{1,0:T(4,128)S(1)}, f32[3,768]{1,0:T(4,128)S(1)}, u32[]{:S(2)}, u32[]{:S(2)}) %collective-permute-start.42) | collective-permute-done | bytes 9248 | tf_op jit(solution)/shard_map/ppermute | solution.py:562
  404.5 3.3 convert_element_type.34
  407.8 8.0 %collective-permute-start.44 = (f32[3,768]{1,0:T(4,128)S(1)}, f32[3,768]{1,0:T(4,128)S(1)}, u32[]{:S(2)}, u32[]{:S(2)}) collective-permute-start(f32[3,768]{1,0:T(4,128)S(1)} %add.229), channel_id=1, source_target_pairs={{0,1},{1,0},{2,3},{3,2},{4,5},{5,4},{6,7},{7,6},{8,9},{9,8},{10,11... | collective-permute-start | bytes 27656 | tf_op jit(solution)/shard_map/ppermute | solution.py:564
  416.5 3.4 collective-permute-start.35
  421.6 2.5 collective-permute-start.45
  425.5 7.3 %collective-permute-done.34 = bf16[3,2,1,24,384]{4,3,2,1,0:T(8,128)(2,1)S(1)} collective-permute-done((bf16[3,2,1,24,384]{4,3,2,1,0:T(8,128)(2,1)S(1)}, bf16[3,2,1,24,384]{4,3,2,1,0:T(8,128)(2,1)S(1)}, u32[]{:S(2)}, u32[]{:S(2)}) %collective-permute-start.34) | collective-permute-done | bytes 110624 | tf_op jit(solution)/shard_map/ppermute | solution.py:375
  442.8 2.8 collective-permute-start.37
  447.1 2.8 collective-permute-start.38
  452.8 2.3 collective-permute-done.39
  457.6 2.7 collective-permute-done.40
  (296 shorter events, 100.2 us)
Async XLA Ops:
  7.2 103.9 %all-gather.2.cloned.1.call-start = ((), (), s32[]{:S(2)}) async-start(), calls=%async_computation.4 | async-start | bytes 1474560 | tf_op jit(solution)/shard_map/all_gather | solution.py:599
  9.1 9.2 %collective-permute-start = (bf16[24,2432]{1,0:T(8,128)(2,1)S(1)}, bf16[24,2432]{1,0:T(8,128)(2,1)S(1)}, u32[]{:S(2)}, u32[]{:S(2)}) collective-permute-start(bf16[24,2432]{1,0:T(8,128)(2,1)S(1)} %fusion.3.refs_0_), channel_id=1, source_target_pairs={{0,1},{1,2},{2,3},{3,0},{4,5},{5,6},{6,7},{7,4},{8,9},{9,10},{10,1... | collective-permute-start | bytes 350216 | tf_op jit(solution)/shard_map/ppermute | solution.py:375
  12.2 10.3 %collective-permute-start.1 = (bf16[24,2432]{1,0:T(8,128)(2,1)S(1)}, bf16[24,2432]{1,0:T(8,128)(2,1)S(1)}, u32[]{:S(2)}, u32[]{:S(2)}) collective-permute-start(bf16[24,2432]{1,0:T(8,128)(2,1)S(1)} %fusion.3.refs_0_), channel_id=1, source_target_pairs={{0,2},{1,3},{2,0},{3,1},{4,6},{5,7},{6,4},{7,5},{8,10},{9,11},{10,... | collective-permute-start | bytes 350216 | tf_op jit(solution)/shard_map/ppermute | solution.py:375
  14.8 7.7 %collective-permute-start.2 = (bf16[24,2432]{1,0:T(8,128)(2,1)S(1)}, bf16[24,2432]{1,0:T(8,128)(2,1)S(1)}, u32[]{:S(2)}, u32[]{:S(2)}) collective-permute-start(bf16[24,2432]{1,0:T(8,128)(2,1)S(1)} %fusion.3.refs_0_), channel_id=1, source_target_pairs={{0,3},{1,0},{2,1},{3,2},{4,7},{5,4},{6,5},{7,6},{8,11},{9,8},{10,9... | collective-permute-start | bytes 350216 | tf_op jit(solution)/shard_map/ppermute | solution.py:375
  23.7 13.3 %collective-permute-start.3 = (bf16[96,2432]{1,0:T(8,128)(2,1)S(1)}, bf16[96,2432]{1,0:T(8,128)(2,1)S(1)}, u32[]{:S(2)}, u32[]{:S(2)}) collective-permute-start(bf16[96,2432]{1,0:T(8,128)(2,1)S(1)} %bitcast.126), channel_id=1, source_target_pairs={{0,8},{4,20},{8,0},{12,28},{16,24},{20,4},{24,16},{28,12},{1,9},{5... | collective-permute-start | bytes 1400840 | tf_op jit(solution)/shard_map/ppermute | solution.py:367
  25.3 13.4 %collective-permute-start.5 = (bf16[96,2432]{1,0:T(8,128)(2,1)S(1)}, bf16[96,2432]{1,0:T(8,128)(2,1)S(1)}, u32[]{:S(2)}, u32[]{:S(2)}) collective-permute-start(bf16[96,2432]{1,0:T(8,128)(2,1)S(1)} %bitcast.127), channel_id=1, source_target_pairs={{0,16},{4,12},{8,24},{12,4},{16,0},{20,28},{24,8},{28,20},{1,17},{... | collective-permute-start | bytes 1400840 | tf_op jit(solution)/shard_map/ppermute | solution.py:367
  37.1 8.6 %collective-permute-start.4 = (bf16[96,2432]{1,0:T(8,128)(2,1)S(1)}, bf16[96,2432]{1,0:T(8,128)(2,1)S(1)}, u32[]{:S(2)}, u32[]{:S(2)}) collective-permute-start(bf16[96,2432]{1,0:T(8,128)(2,1)S(1)} %collective-permute-done.3.refs_1_), channel_id=1, source_target_pairs={{0,16},{4,12},{8,24},{12,4},{16,0},{20,28},{24,8},{28,20},{1,17},{... | collective-permute-start | bytes 1400840 | tf_op jit(solution)/shard_map/ppermute | solution.py:367
  38.2 28.5 %collective-permute-start.6 = (bf16[96,2432]{1,0:T(8,128)(2,1)S(1)}, bf16[96,2432]{1,0:T(8,128)(2,1)S(1)}, u32[]{:S(2)}, u32[]{:S(2)}) collective-permute-start(bf16[96,2432]{1,0:T(8,128)(2,1)S(1)} %bitcast.128), channel_id=1, source_target_pairs={{0,4},{4,0},{8,12},{12,8},{16,20},{20,16},{24,28},{28,24},{1,5},{5... | collective-permute-start | bytes 1400840 | tf_op jit(solution)/shard_map/ppermute | solution.py:371
  38.3 29.2 %collective-permute-start.7 = (bf16[96,2432]{1,0:T(8,128)(2,1)S(1)}, bf16[96,2432]{1,0:T(8,128)(2,1)S(1)}, u32[]{:S(2)}, u32[]{:S(2)}) collective-permute-start(bf16[96,2432]{1,0:T(8,128)(2,1)S(1)} %collective-permute-done.3.refs_1_), channel_id=1, source_target_pairs={{0,4},{4,0},{8,12},{12,8},{16,20},{20,16},{24,28},{28,24},{1,5},{5... | collective-permute-start | bytes 1400840 | tf_op jit(solution)/shard_map/ppermute | solution.py:371
  38.8 29.5 %collective-permute-start.8 = (bf16[96,2432]{1,0:T(8,128)(2,1)S(1)}, bf16[96,2432]{1,0:T(8,128)(2,1)S(1)}, u32[]{:S(2)}, u32[]{:S(2)}) collective-permute-start(bf16[96,2432]{1,0:T(8,128)(2,1)S(1)} %collective-permute-done.5.refs_2_), channel_id=1, source_target_pairs={{0,4},{4,0},{8,12},{12,8},{16,20},{20,16},{24,28},{28,24},{1,5},{5... | collective-permute-start | bytes 1400840 | tf_op jit(solution)/shard_map/ppermute | solution.py:371
  45.6 23.4 %collective-permute-start.9 = (bf16[96,2432]{1,0:T(8,128)(2,1)S(1)}, bf16[96,2432]{1,0:T(8,128)(2,1)S(1)}, u32[]{:S(2)}, u32[]{:S(2)}) collective-permute-start(bf16[96,2432]{1,0:T(8,128)(2,1)S(1)} %collective-permute-done.4.refs_3_), channel_id=1, source_target_pairs={{0,4},{4,0},{8,12},{12,8},{16,20},{20,16},{24,28},{28,24},{1,5},{5... | collective-permute-start | bytes 1400840 | tf_op jit(solution)/shard_map/ppermute | solution.py:371
  69.8 19.3 %collective-permute-start.10 = (bf16[96,3840]{1,0:T(8,128)(2,1)S(1)}, bf16[96,3840]{1,0:T(8,128)(2,1)S(1)}, u32[]{:S(2)}, u32[]{:S(2)}) collective-permute-start(bf16[96,3840]{1,0:T(8,128)(2,1)S(1)} %all_gather.6.refs_0_), channel_id=1, source_target_pairs={{0,8},{4,20},{8,0},{12,28},{16,24},{20,4},{24,16},{28,12},{1,9},{5... | collective-permute-start | bytes 2211848 | tf_op jit(solution)/shard_map/ppermute | solution.py:367
  72.2 37.9 %collective-permute-start.11 = (bf16[96,3840]{1,0:T(8,128)(2,1)S(1)}, bf16[96,3840]{1,0:T(8,128)(2,1)}, u32[]{:S(2)}, u32[]{:S(2)}) collective-permute-start(bf16[96,3840]{1,0:T(8,128)(2,1)S(1)} %all_gather.6.refs_0_), channel_id=1, source_target_pairs={{0,16},{4,12},{8,24},{12,4},{16,0},{20,28},{24,8},{28,20},{1,17},{... | collective-permute-start | bytes 2211848 | tf_op jit(solution)/shard_map/ppermute | solution.py:367
  89.1 21.0 %collective-permute-start.12 = (bf16[96,3840]{1,0:T(8,128)(2,1)S(1)}, bf16[96,3840]{1,0:T(8,128)(2,1)}, u32[]{:S(2)}, u32[]{:S(2)}) collective-permute-start(bf16[96,3840]{1,0:T(8,128)(2,1)S(1)} %collective-permute-done.10.refs_1_), channel_id=1, source_target_pairs={{0,16},{4,12},{8,24},{12,4},{16,0},{20,28},{24,8},{28,20},{1,17},{... | collective-permute-start | bytes 2211848 | tf_op jit(solution)/shard_map/ppermute | solution.py:367
  90.9 43.0 %all-to-all-start = ((bf16[4,256,768]{2,1,0:T(8,128)(2,1)}), bf16[4,256,768]{2,1,0:T(8,128)(2,1)S(1)}, u32[]{:S(2)}, u32[]{:S(2)}) async-start(bf16[4,256,768]{2,1,0:T(8,128)(2,1)} %param.15), calls=%async_computation | async-start | bytes 3145728 | tf_op jit(solution)/shard_map/all_to_all | solution.py:601
  94.5 297.9 %reduce-scatter.5.cloned.1.call-start = ((), (), s32[]{:S(2)}) async-start(), calls=%async_computation.6 | async-start | bytes 1474560 | tf_op jit(solution)/shard_map/reduce_scatter | solution.py:539
  95.5 15.6 %collective-permute-start.13 = (bf16[96,3840]{1,0:T(8,128)(2,1)S(1)}, bf16[96,3840]{1,0:T(8,128)(2,1)}, u32[]{:S(2)}, u32[]{:S(2)}) collective-permute-start(bf16[96,3840]{1,0:T(8,128)(2,1)S(1)} %all_gather.6.refs_0_), channel_id=1, source_target_pairs={{0,4},{4,0},{8,12},{12,8},{16,20},{20,16},{24,28},{28,24},{1,5},{5... | collective-permute-start | bytes 2211848 | tf_op jit(solution)/shard_map/ppermute | solution.py:371
  95.6 15.5 %collective-permute-start.14 = (bf16[96,3840]{1,0:T(8,128)(2,1)S(1)}, bf16[96,3840]{1,0:T(8,128)(2,1)}, u32[]{:S(2)}, u32[]{:S(2)}) collective-permute-start(bf16[96,3840]{1,0:T(8,128)(2,1)S(1)} %collective-permute-done.10.refs_1_), channel_id=1, source_target_pairs={{0,4},{4,0},{8,12},{12,8},{16,20},{20,16},{24,28},{28,24},{1,5},{5... | collective-permute-start | bytes 2211848 | tf_op jit(solution)/shard_map/ppermute | solution.py:371
  113.6 34.7 %collective-permute-start.17 = (bf16[96,6144]{1,0:T(8,128)(2,1)}, bf16[96,6144]{1,0:T(8,128)(2,1)}, u32[]{:S(2)}, u32[]{:S(2)}) collective-permute-start(bf16[96,6144]{1,0:T(8,128)(2,1)} %all-gather.2.cloned.1.call-done.refs_0_), channel_id=1, source_target_pairs={{0,8},{4,20},{8,0},{12,28},{16,24},{20,4},{24,16},{28,12},{1,9},{5... | collective-permute-start | bytes 3538952 | tf_op jit(solution)/shard_map/ppermute | solution.py:367
  114.2 54.6 %collective-permute-start.19 = (bf16[96,6144]{1,0:T(8,128)(2,1)}, bf16[96,6144]{1,0:T(8,128)(2,1)}, u32[]{:S(2)}, u32[]{:S(2)}) collective-permute-start(bf16[96,6144]{1,0:T(8,128)(2,1)} %all-gather.2.cloned.1.call-done.refs_0_), channel_id=1, source_target_pairs={{0,16},{4,12},{8,24},{12,4},{16,0},{20,28},{24,8},{28,20},{1,17},{... | collective-permute-start | bytes 3538952 | tf_op jit(solution)/shard_map/ppermute | solution.py:367
  148.4 20.5 %collective-permute-start.18 = (bf16[96,6144]{1,0:T(8,128)(2,1)}, bf16[96,6144]{1,0:T(8,128)(2,1)S(1)}, u32[]{:S(2)}, u32[]{:S(2)}) collective-permute-start(bf16[96,6144]{1,0:T(8,128)(2,1)} %collective-permute-done.17.refs_1_), channel_id=1, source_target_pairs={{0,16},{4,12},{8,24},{12,4},{16,0},{20,28},{24,8},{28,20},{1,17},{... | collective-permute-start | bytes 3538952 | tf_op jit(solution)/shard_map/ppermute | solution.py:367
  150.6 18.8 %collective-permute-start.20 = (bf16[96,6144]{1,0:T(8,128)(2,1)S(1)}, bf16[96,6144]{1,0:T(8,128)(2,1)S(1)}, u32[]{:S(2)}, u32[]{:S(2)}) collective-permute-start(bf16[96,6144]{1,0:T(8,128)(2,1)S(1)} %copy-done.57), channel_id=1, source_target_pairs={{0,4},{4,0},{8,12},{12,8},{16,20},{20,16},{24,28},{28,24},{1,5},{5... | collective-permute-start | bytes 3538952 | tf_op jit(solution)/shard_map/ppermute | solution.py:371
  150.7 18.7 %collective-permute-start.21 = (bf16[96,6144]{1,0:T(8,128)(2,1)}, bf16[96,6144]{1,0:T(8,128)(2,1)S(1)}, u32[]{:S(2)}, u32[]{:S(2)}) collective-permute-start(bf16[96,6144]{1,0:T(8,128)(2,1)} %collective-permute-done.17.refs_1_), channel_id=1, source_target_pairs={{0,4},{4,0},{8,12},{12,8},{16,20},{20,16},{24,28},{28,24},{1,5},{5... | collective-permute-start | bytes 3538952 | tf_op jit(solution)/shard_map/ppermute | solution.py:371
  168.8 3.9 collective-permute-start.22
  168.9 4.5 collective-permute-start.23
  224.6 20.3 %collective-permute-start.24 = (bf16[3,768,1024]{2,1,0:T(8,128)(2,1)}, bf16[3,768,1024]{2,1,0:T(8,128)(2,1)}, u32[]{:S(2)}, u32[]{:S(2)}) collective-permute-start(bf16[3,768,1024]{2,1,0:T(8,128)(2,1)} %get-tuple-element.186), channel_id=1, source_target_pairs={{0,4},{4,0},{8,12},{12,8},{16,20},{20,16},{24,28},{28,24},{1,5},{5... | collective-permute-start | bytes 14155784 | tf_op jit(solution)/shard_map/ppermute | solution.py:371
  250.1 28.9 %collective-permute-start.25 = (bf16[3,2,192,1024]{3,2,1,0:T(8,128)(2,1)S(1)}, bf16[3,2,192,1024]{3,2,1,0:T(8,128)(2,1)S(1)}, u32[]{:S(2)}, u32[]{:S(2)}) collective-permute-start(bf16[3,2,192,1024]{3,2,1,0:T(8,128)(2,1)S(1)} %get-tuple-element.200), channel_id=1, source_target_pairs={{0,16},{4,12},{8,24},{12,4},{16,0},{20,28},{24,8},{28,20},{1,17},{... | collective-permute-start | bytes 7077896 | tf_op jit(solution)/shard_map/ppermute | solution.py:367
  297.1 6.6 %collective-permute-start.27 = (bf16[5,768,384]{2,1,0:T(8,128)(2,1)}, bf16[5,768,384]{2,1,0:T(8,128)(2,1)S(1)}, u32[]{:S(2)}, u32[]{:S(2)}) collective-permute-start(bf16[5,768,384]{2,1,0:T(8,128)(2,1)} %get-tuple-element.215), channel_id=1, source_target_pairs={{0,4},{4,0},{8,12},{12,8},{16,20},{20,16},{24,28},{28,24},{1,5},{5... | collective-permute-start | bytes 8847368 | tf_op jit(solution)/shard_map/ppermute | solution.py:371
  297.1 16.4 %collective-permute-start.26 = (bf16[3,1,192,1024]{3,2,1,0:T(8,128)(2,1)}, bf16[3,1,192,1024]{3,2,1,0:T(8,128)(2,1)S(1)}, u32[]{:S(2)}, u32[]{:S(2)}) collective-permute-start(bf16[3,1,192,1024]{3,2,1,0:T(8,128)(2,1)} %copy-done.68), channel_id=1, source_target_pairs={{0,8},{4,20},{8,0},{12,28},{16,24},{20,4},{24,16},{28,12},{1,9},{5... | collective-permute-start | bytes 3538952 | tf_op jit(solution)/shard_map/ppermute | solution.py:367
  343.1 25.3 %collective-permute-start.28 = (bf16[3,768,384]{2,1,0:T(8,128)(2,1)}, bf16[3,768,384]{2,1,0:T(8,128)(2,1)S(1)}, u32[]{:S(2)}, u32[]{:S(2)}) collective-permute-start(bf16[3,768,384]{2,1,0:T(8,128)(2,1)} %get-tuple-element.231), channel_id=1, source_target_pairs={{0,4},{4,0},{8,12},{12,8},{16,20},{20,16},{24,28},{28,24},{1,5},{5... | collective-permute-start | bytes 5308424 | tf_op jit(solution)/shard_map/ppermute | solution.py:371
  343.2 19.7 %collective-permute-start.29 = (bf16[5,2,192,384]{3,2,1,0:T(8,128)(2,1)}, bf16[5,2,192,384]{3,2,1,0:T(8,128)(2,1)}, u32[]{:S(2)}, u32[]{:S(2)}) collective-permute-start(bf16[5,2,192,384]{3,2,1,0:T(8,128)(2,1)} %get-tuple-element.233), channel_id=1, source_target_pairs={{0,16},{4,12},{8,24},{12,4},{16,0},{20,28},{24,8},{28,20},{1,17},{... | collective-permute-start | bytes 4423688 | tf_op jit(solution)/shard_map/ppermute | solution.py:367
  344.2 60.3 %all-to-all-start.1 = ((bf16[4,256,768]{2,1,0:T(8,128)(2,1)}), bf16[4,256,768]{2,1,0:T(8,128)(2,1)}, u32[]{:S(2)}, u32[]{:S(2)}) async-start(bf16[4,256,768]{2,1,0:T(8,128)(2,1)} %bitcast.125), calls=%async_computation.1 | async-start | bytes 3145728 | tf_op jit(solution)/shard_map/all_to_all | solution.py:637
  348.6 86.9 %reduce-scatter.3.cloned.1.call-start = ((), (), s32[]{:S(2)}) async-start(), calls=%async_computation.5 | async-start | bytes 921600 | tf_op jit(solution)/shard_map/reduce_scatter | solution.py:539
  369.5 20.8 %collective-permute-start.30 = (bf16[3,2,192,384]{3,2,1,0:T(8,128)(2,1)S(1)}, bf16[3,2,192,384]{3,2,1,0:T(8,128)(2,1)S(1)}, u32[]{:S(2)}, u32[]{:S(2)}) collective-permute-start(bf16[3,2,192,384]{3,2,1,0:T(8,128)(2,1)S(1)} %get-tuple-element.246), channel_id=1, source_target_pairs={{0,16},{4,12},{8,24},{12,4},{16,0},{20,28},{24,8},{28,20},{1,17},{... | collective-permute-start | bytes 2654216 | tf_op jit(solution)/shard_map/ppermute | solution.py:367
  370.5 20.7 %collective-permute-start.32 = (bf16[5,1,192,384]{3,2,1,0:T(8,128)(2,1)S(1)}, bf16[5,1,192,384]{3,2,1,0:T(8,128)(2,1)S(1)}, u32[]{:S(2)}, u32[]{:S(2)}) collective-permute-start(bf16[5,1,192,384]{3,2,1,0:T(8,128)(2,1)S(1)} %get-tuple-element.255), channel_id=1, source_target_pairs={{0,8},{4,20},{8,0},{12,28},{16,24},{20,4},{24,16},{28,12},{1,9},{5... | collective-permute-start | bytes 2211848 | tf_op jit(solution)/shard_map/ppermute | solution.py:367
  393.5 22.3 %collective-permute-start.31 = (bf16[3,1,192,384]{3,2,1,0:T(8,128)(2,1)S(1)}, bf16[3,1,192,384]{3,2,1,0:T(8,128)(2,1)S(1)}, u32[]{:S(2)}, u32[]{:S(2)}) collective-permute-start(bf16[3,1,192,384]{3,2,1,0:T(8,128)(2,1)S(1)} %get-tuple-element.253), channel_id=1, source_target_pairs={{0,8},{4,20},{8,0},{12,28},{16,24},{20,4},{24,16},{28,12},{1,9},{5... | collective-permute-start | bytes 1327112 | tf_op jit(solution)/shard_map/ppermute | solution.py:367
  394.2 7.8 %collective-permute-start.42 = (f32[3,768]{1,0:T(4,128)S(1)}, f32[3,768]{1,0:T(4,128)S(1)}, u32[]{:S(2)}, u32[]{:S(2)}) collective-permute-start(f32[3,768]{1,0:T(4,128)S(1)} %fusion.10), channel_id=1, source_target_pairs={{0,8},{4,12},{8,0},{12,4},{16,24},{20,28},{24,16},{28,20},{1,9},{5... | collective-permute-start | bytes 27656 | tf_op jit(solution)/shard_map/ppermute | solution.py:562
  396.4 24.1 %collective-permute-start.48 = (f32[3,24,1024]{2,1,0:T(8,128)}, f32[3,24,1024]{2,1,0:T(8,128)}, u32[]{:S(2)}, u32[]{:S(2)}) collective-permute-start(f32[3,24,1024]{2,1,0:T(8,128)} %dynamic-slice_bitcast_fusion), channel_id=1, source_target_pairs={{0,4},{4,0},{8,12},{12,8},{16,20},{20,16},{24,28},{28,24},{1,5},{5... | collective-permute-start | bytes 884744 | tf_op jit(solution)/shard_map/ppermute | solution.py:371
  402.0 5.7 %collective-permute-start.43 = (f32[3,768]{1,0:T(4,128)S(1)}, f32[3,768]{1,0:T(4,128)S(1)}, u32[]{:S(2)}, u32[]{:S(2)}) collective-permute-start(f32[3,768]{1,0:T(4,128)S(1)} %fusion.14), channel_id=1, source_target_pairs={{0,16},{4,20},{8,24},{12,28},{16,0},{20,4},{24,8},{28,12},{1,17},{... | collective-permute-start | bytes 27656 | tf_op jit(solution)/shard_map/ppermute | solution.py:562
  407.8 13.7 %collective-permute-start.44 = (f32[3,768]{1,0:T(4,128)S(1)}, f32[3,768]{1,0:T(4,128)S(1)}, u32[]{:S(2)}, u32[]{:S(2)}) collective-permute-start(f32[3,768]{1,0:T(4,128)S(1)} %add.229), channel_id=1, source_target_pairs={{0,1},{1,0},{2,3},{3,2},{4,5},{5,4},{6,7},{7,6},{8,9},{9,8},{10,11... | collective-permute-start | bytes 27656 | tf_op jit(solution)/shard_map/ppermute | solution.py:564
  416.5 9.0 %collective-permute-start.35 = (bf16[3,2,1,24,384]{4,3,2,1,0:T(8,128)(2,1)S(1)}, bf16[3,2,1,24,384]{4,3,2,1,0:T(8,128)(2,1)S(1)}, u32[]{:S(2)}, u32[]{:S(2)}) collective-permute-start(bf16[3,2,1,24,384]{4,3,2,1,0:T(8,128)(2,1)S(1)} %get-tuple-element.264), channel_id=1, source_target_pairs={{0,3},{1,0},{2,1},{3,2},{4,7},{5,4},{6,5},{7,6},{8,11},{9,8},{10,9... | collective-permute-start | bytes 331784 | tf_op jit(solution)/shard_map/ppermute | solution.py:375
  419.9 12.9 %collective-permute-start.34 = (bf16[3,2,1,24,384]{4,3,2,1,0:T(8,128)(2,1)S(1)}, bf16[3,2,1,24,384]{4,3,2,1,0:T(8,128)(2,1)S(1)}, u32[]{:S(2)}, u32[]{:S(2)}) collective-permute-start(bf16[3,2,1,24,384]{4,3,2,1,0:T(8,128)(2,1)S(1)} %get-tuple-element.263), channel_id=1, source_target_pairs={{0,2},{1,3},{2,0},{3,1},{4,6},{5,7},{6,4},{7,5},{8,10},{9,11},{10,... | collective-permute-start | bytes 331784 | tf_op jit(solution)/shard_map/ppermute | solution.py:375
  419.9 12.9 %collective-permute-start.33 = (bf16[3,2,1,24,384]{4,3,2,1,0:T(8,128)(2,1)S(1)}, bf16[3,2,1,24,384]{4,3,2,1,0:T(8,128)(2,1)S(1)}, u32[]{:S(2)}, u32[]{:S(2)}) collective-permute-start(bf16[3,2,1,24,384]{4,3,2,1,0:T(8,128)(2,1)S(1)} %get-tuple-element.262), channel_id=1, source_target_pairs={{0,1},{1,2},{2,3},{3,0},{4,5},{5,6},{6,7},{7,4},{8,9},{9,10},{10,1... | collective-permute-start | bytes 331784 | tf_op jit(solution)/shard_map/ppermute | solution.py:375
  421.6 12.0 %collective-permute-start.45 = (f32[3,768]{1,0:T(4,128)S(1)}, f32[3,768]{1,0:T(4,128)S(1)}, u32[]{:S(2)}, u32[]{:S(2)}) collective-permute-start(f32[3,768]{1,0:T(4,128)S(1)} %add.230), channel_id=1, source_target_pairs={{0,2},{1,3},{2,0},{3,1},{4,6},{5,7},{6,4},{7,5},{8,10},{9,11},{10,... | collective-permute-start | bytes 27656 | tf_op jit(solution)/shard_map/ppermute | solution.py:564
  441.9 22.1 %collective-permute-start.47 = (f32[5,24,384]{2,1,0:T(8,128)}, f32[5,24,384]{2,1,0:T(8,128)}, u32[]{:S(2)}, u32[]{:S(2)}) collective-permute-start(f32[5,24,384]{2,1,0:T(8,128)} %dynamic-slice_bitcast_fusion.1), channel_id=1, source_target_pairs={{0,4},{4,0},{8,12},{12,8},{16,20},{20,16},{24,28},{28,24},{1,5},{5... | collective-permute-start | bytes 552968 | tf_op jit(solution)/shard_map/ppermute | solution.py:371
  442.8 3.7 collective-permute-start.37
  447.1 3.7 collective-permute-start.38
  455.7 4.6 collective-permute-start.40
  (88 other events, 723.3 us)
Sparse Core Ops, SparseCore 0:
  72.2 38.8 all-gather.1
  344.3 44.9 reduce-scatter.4
  394.3 36.2 reduce-scatter.2

commit v3 on v2

--- a/solution.py
+++ b/solution.py
@@ -6,8 +6,10 @@
 from jax.experimental.pallas import tpu as pltpu
 bf=jnp.bfloat16; f32=jnp.float32
 HD=64; HEADS=12
+def cost(us):
+    return pl.CostEstimate(flops=int(us*1e+10),bytes_accessed=10**5,transcendentals=0)
 NEG=-1e30
-VA=24*2**20
+VA=16*2**20
 LOG2E=math.log2(math.e)
 TN=(((0,),(0,)),((),())); NN=(((1,),(0,)),((),())); NT=(((1,),(1,)),((),()))
 def dg(a,b,dims): return lax.dot_general(a,b,dims,preferred_element_type=f32)
@@ -60,14 +62,24 @@
 
 def head_block(hs,w,offset=0):
     return pl.BlockSpec((hs*HD,w),lambda h:(h+offset//hs,0))
-def attn_fwd(n,q,k,v,causal,bq=256,hs=2):
+def fwd_part_kernel(*refs,**kw):
+    fwd_kernel(*refs[:4],*refs[6:],**kw)
+def attn_fwd(n,q,k,v,causal,bq=256,hs=2,part=None,into=None):
     L=q[0].shape[1]; K=k[0].shape[1]; D=HEADS*HD
-    return pl.pallas_call(functools.partial(fwd_kernel,causal=causal,bq=bq,hs=hs),grid=(HEADS//hs,),
-      in_specs=[pl.BlockSpec(memory_space=pltpu.SMEM),head_block(hs,L,q[1]),head_block(hs,K,k[1]),head_block(hs,K,v[1])],
-      out_specs=[head_block(hs,L),pl.BlockSpec((hs,1,L),lambda h:(h,0,0))],
+    h0,hn=part or (0,HEADS)
+    hb=lambda w,o=0: head_block(hs,w,o+h0)
+    specs=[pl.BlockSpec(memory_space=pltpu.SMEM),hb(L,q[1]),hb(K,k[1]),hb(K,v[1])]
+    args=(n,q[0],k[0],v[0])
+    if into is not None:
+        specs+=[pl.BlockSpec(memory_space=pl.ANY)]*2
+        args+=tuple(into)
+    return pl.pallas_call(functools.partial(fwd_kernel if into is None else fwd_part_kernel,causal=causal,bq=bq,hs=hs),grid=(hn//hs,),
+      in_specs=specs,
+      out_specs=[hb(L),pl.BlockSpec((hs,1,L),lambda h:(h+h0//hs,0,0))],
       out_shape=[jax.ShapeDtypeStruct((D,L),bf),jax.ShapeDtypeStruct((HEADS,1,L),f32)],
-      compiler_params=pltpu.CompilerParams(vmem_limit_bytes=VA),
-    )(n,q[0],k[0],v[0])
+      input_output_aliases={} if into is None else {4:0,5:1},
+      cost_estimate=cost(0.3),compiler_params=pltpu.CompilerParams(vmem_limit_bytes=VA),
+    )(*args)
 
 def bwd_kernel(len_ref,qT_ref,kT_ref,vT_ref,oT_ref,gT_ref,lse_ref,dq_ref,dk_ref,dv_ref,dka,dva,*,causal,bq,hs):
     L=qT_ref.shape[1]; K=kT_ref.shape[1]
@@ -126,7 +138,7 @@
       out_shape=[S((D,L),bf),S((D,K),bf),S((D,K),bf)],
       input_output_aliases={} if into is None else {7:0,8:1,9:2},
       scratch_shapes=[pltpu.VMEM((hs*HD,K),f32),pltpu.VMEM((hs*HD,K),f32)],
-      compiler_params=pltpu.CompilerParams(vmem_limit_bytes=VA),
+      cost_estimate=cost(14),compiler_params=pltpu.CompilerParams(vmem_limit_bytes=VA),
     )(*args)
 
 TT=(((0,),(1,)),((),()))
@@ -154,7 +166,7 @@
     return pl.pallas_call(proj_kernel,grid=(F//fb,),
       in_specs=[full((L,D)),pl.BlockSpec((D,128),lambda i:(0,F//128)),pl.BlockSpec((D,fb),lambda i:(0,i))],
       out_specs=[full((L,D)),pl.BlockSpec((fb,L),lambda i:(i,0)),gain_spec(D)],
-      out_shape=[jax.ShapeDtypeStruct((L,D),bf),jax.ShapeDtypeStruct((F,L),bf),jax.ShapeDtypeStruct((8,D),f32)],compiler_params=cp())(x,w,w)
+      out_shape=[jax.ShapeDtypeStruct((L,D),bf),jax.ShapeDtypeStruct((F,L),bf),jax.ShapeDtypeStruct((8,D),f32)],cost_estimate=cost(6),compiler_params=cp())(x,w,w)
 def memproj_kernel(x_ref,w_ref,yT_ref):
     yT_ref[...]=dg(w_ref[...],x_ref[...],TT).astype(bf)
 def mem_proj(x,w,first_col,fb=384):
@@ -162,7 +174,7 @@
     return pl.pallas_call(memproj_kernel,grid=(F//fb,),
       in_specs=[full((L,D)),pl.BlockSpec((D,fb),lambda i:(0,first_col//fb+i))],
       out_specs=pl.BlockSpec((fb,L),lambda i:(i,0)),
-      out_shape=jax.ShapeDtypeStruct((F,L),bf),compiler_params=cp())(x,w)
+      out_shape=jax.ShapeDtypeStruct((F,L),bf),cost_estimate=cost(4),compiler_params=cp())(x,w)
 
 def post_self_kernel(x_ref,oT_ref,w3_ref,w4_ref,g_ref,h_ref,n_ref,cT_ref):
     h=x_ref[...].astype(f32)+dg(oT_ref[...],w3_ref[...],TT)
@@ -176,7 +188,7 @@
     return pl.pallas_call(post_self_kernel,grid=(L//tb,),
       in_specs=[tok,tokT,wcol(D,0),wcol(D,1),gain_spec(D)],
       out_specs=[tok,tok,tokT],
-      out_shape=[jax.ShapeDtypeStruct((L,D),f32),jax.ShapeDtypeStruct((L,D),bf),jax.ShapeDtypeStruct((D,L),bf)],compiler_params=cp())(x,oT,w,w,g)
+      out_shape=[jax.ShapeDtypeStruct((L,D),f32),jax.ShapeDtypeStruct((L,D),bf),jax.ShapeDtypeStruct((D,L),bf)],cost_estimate=cost(6),compiler_params=cp())(x,oT,w,w,g)
 
 def mlp_chunk(n3,gb,wg,wu,wd,dw_ref,inner_s,dgate_s,dup_s,oacc,nacc,tb):
     L=n3.shape[0]; nt=L//tb
@@ -266,7 +278,7 @@
       scratch_shapes=[pltpu.VMEM((L,D),f32),pltpu.VMEM((L,D),bf),pltpu.VMEM((L,D),bf),pltpu.VMEM((L,D),f32),pltpu.VMEM((L,D),f32),
         pltpu.VMEM((2,3,D,fc),bf),pltpu.VMEM((L,fc),bf),pltpu.VMEM((L,fc),bf),pltpu.VMEM((L,fc),bf),pltpu.SemaphoreType.DMA((2,))]),
       out_shape=[S((L,D),bf),S((L,D),f32),S((D,L),bf),S((L,D),bf),S((1,D),f32),S((3,D,F//2),bf),S((3,D,F//2),bf)],
-      compiler_params=cp(48))(core,n,h1,oT,w_second,cot,g,wm,wm,wm)
+      cost_estimate=cost(42),compiler_params=cp(48))(core,n,h1,oT,w_second,cot,g,wm,wm,wm)
 
 def mid_kernel(h1_ref,gh2_ref,dcT_ref,w4_ref,w3_ref,g_ref,gh1_ref,gmT_ref,gb_ref,dg_ref):
     i=pl.program_id(0)
@@ -290,7 +302,7 @@
     return pl.pallas_call(mid_kernel,grid=(L//tb,),
       in_specs=[tok,tok,tokT,wcol(D,1),wcol(D,0),gain_spec(D)],
       out_specs=[tok,tokT,tok,full((1,D))],
-      out_shape=[S((L,D),f32),S((D,L),bf),S((L,D),bf),S((1,D),f32)],compiler_params=cp())(h1,gh2,dcT,w,w,g)
+      out_shape=[S((L,D),f32),S((D,L),bf),S((L,D),bf),S((1,D),f32)],cost_estimate=cost(0.2),compiler_params=cp())(h1,gh2,dcT,w,w,g)
 
 def wgrads_kernel(core_ref,*refs,pairs,na,ng):
     a_refs=refs[:na]; g_refs=refs[na:na+ng]; send_ref,keep_ref=refs[na+ng:]
@@ -306,7 +318,7 @@
     S=jax.ShapeDtypeStruct((len(pairs),D,F//2),bf)
     return pl.pallas_call(functools.partial(wgrads_kernel,pairs=tuple(pairs),na=len(a),ng=len(g)),
       in_specs=[pl.BlockSpec(memory_space=pltpu.SMEM)]+[v]*(len(a)+len(g)),out_specs=[v,v],
-      out_shape=[S,S],compiler_params=cp(40))(core,*a,*g)
+      out_shape=[S,S],cost_estimate=cost(8),compiler_params=cp(40))(core,*a,*g)
 
 def gmem_kernel(kT_ref,vT_ref,w5_ref,w6_ref,o_ref):
     o_ref[...]=(dg(kT_ref[...],w5_ref[...],TT)+dg(vT_ref[...],w6_ref[...],TT)).astype(bf)
@@ -316,7 +328,7 @@
     return pl.pallas_call(gmem_kernel,grid=(L//tb,),
       in_specs=[tokT,tokT,wcol(D,2),wcol(D,3)],
       out_specs=pl.BlockSpec((tb,D),lambda i:(i,0)),
-      out_shape=jax.ShapeDtypeStruct((L,D),bf),compiler_params=cp())(kT,vT,w56,w56)
+      out_shape=jax.ShapeDtypeStruct((L,D),bf),cost_estimate=cost(0.2),compiler_params=cp())(kT,vT,w56,w56)
 
 def first_kernel(x_ref,gh1_ref,qT_ref,kT_ref,vT_ref,w0_ref,w1_ref,w2_ref,g_ref,gt_ref,dg_ref):
     i=pl.program_id(0)
@@ -337,7 +349,7 @@
     return pl.pallas_call(first_kernel,grid=(L//tb,),
       in_specs=[tok,tok,tokT,tokT,tokT,wb(0),wb(1),wb(2),gain_spec(D)],
       out_specs=[tok,full((1,D))],
-      out_shape=[S((L,D),f32),S((1,D),f32)],compiler_params=cp())(x,gh1,qT,kT,vT,w,w,w,g)
+      out_shape=[S((L,D),f32),S((1,D),f32)],cost_estimate=cost(7),compiler_params=cp())(x,gh1,qT,kT,vT,w,w,w,g)
 
 SEQ="seq"
 MEM="mem"
@@ -375,25 +387,28 @@
     return lax.ppermute(x,MEM,[(z,(z+step)%mem_size) for z in range(mem_size)])
 
 
-def copy_kernel(index_ref,*refs,places):
+def copy_kernel(index_ref,*refs,places,columns):
     count=len(places)
     sources=refs[:count]; out=refs[count]; sems=refs[count+1]
     copies=[]
     for j,(source,place) in enumerate(zip(sources,places)):
+        if columns is not None:
+            source=source.at[:,pl.ds(columns[0],columns[1]-columns[0])]
         copies.append(pltpu.make_async_copy(source,out.at[index_ref[place]],sems.at[j]))
         copies[-1].start()
     for c in copies:
         c.wait()
 
 
-def place_rows(index,pieces,places,slots):
+def place_rows(index,pieces,places,slots,us,columns=None):
     piece=pieces[0]
-    return pl.pallas_call(functools.partial(copy_kernel,places=tuple(places)),
-        in_specs=[pl.BlockSpec(memory_space=pltpu.SMEM)]+[pl.BlockSpec(memory_space=pl.ANY)]*len(pieces),
+    shape=piece.shape if columns is None else (piece.shape[0],columns[1]-columns[0])
+    return pl.pallas_call(functools.partial(copy_kernel,places=tuple(places),columns=columns),
+        in_specs=[pl.BlockSpec(memory_space=pltpu.SMEM)]+[pl.BlockSpec(memory_space=pltpu.HBM)]*len(pieces),
         out_specs=pl.BlockSpec(memory_space=pltpu.VMEM),
-        out_shape=jax.ShapeDtypeStruct((slots,)+piece.shape,piece.dtype),
+        out_shape=jax.ShapeDtypeStruct((slots,)+shape,piece.dtype),
         scratch_shapes=[pltpu.SemaphoreType.DMA((len(pieces),))],
-        compiler_params=cp(20),
+        cost_estimate=cost(us),compiler_params=cp(20),
     )(index,*pieces)
 
 
@@ -413,11 +428,44 @@
     M=pl_.M
     pieces=[shard]+[shift_mem(shard,j,M) for j in range(1,M)]
     index=jnp.stack([(pl_.z-j)%M for j in range(M)]).astype(jnp.int32)
-    return place_rows(index,pieces,range(M),M).reshape(M*shard.shape[0],shard.shape[1])
+    return place_rows(index,pieces,range(M),M,3).reshape(M*shard.shape[0],shard.shape[1])
+
+
+def gather_mem_exchange(shard,here):
+    M=here.M
+    copies=jnp.broadcast_to(shard[None],(M,)+shard.shape)
+    return lax.all_to_all(copies,MEM,split_axis=0,concat_axis=0,tiled=True).reshape(M*shard.shape[0],shard.shape[1])
 
 
 def tie(*values):
     return lax.optimization_barrier(values)
+
+
+class Ring:
+    def __init__(self,shard,here):
+        self.here=here; self.got=[shard]
+        self.next()
+
+    def next(self):
+        if len(self.got)<self.here.M:
+            self.got.append(shift_mem(self.got[-1],1,self.here.M))
+
+    def step(self,dep):
+        self.got[-1],dep=tie(self.got[-1],dep)
+        self.next()
+        return dep
+
+    def finish(self,dep):
+        while len(self.got)<self.here.M:
+            self.next()
+        self.got[-1],dep=tie(self.got[-1],dep)
+        return dep
+
+    def place(self,first,end):
+        M=self.here.M
+        index=jnp.stack([(self.here.z-j)%M for j in range(M)]).astype(jnp.int32)
+        rows=self.got[0].shape[0]
+        return place_rows(index,self.got,range(M),M,3,(first,end)).reshape(M*rows,end-first)
 
 
 class Gather:
@@ -425,32 +473,30 @@
         self.here=here; self.pieces={0:slab}; self.other={}
         for p in range(here.bits):
             self.pieces[1<<p]=cross(slab,p,here.S)
-        self.other[0]=swap_core(slab,here.S)
-
-    def forward(self,dep):
+
+    def arrived(self,dep,keys=None):
+        keys=sorted(self.pieces) if keys is None else keys
+        others=sorted(self.other)
+        out=tie(*[self.pieces[s] for s in keys],*[self.other[s] for s in others],dep)
+        self.pieces.update(zip(keys,out)); self.other.update(zip(others,out[len(keys):]))
+        return out[-1]
+
+    def forward(self):
         here=self.here
-        self.pieces[1],dep=tie(self.pieces[1],dep)
         for subset in range(1,here.NP):
             top=subset.bit_length()-1
             if subset not in self.pieces:
                 self.pieces[subset]=cross(self.pieces[subset^(1<<top)],top,here.S)
-        for subset in range(1,here.NP-1):
-            self.other[subset]=swap_core(self.pieces[subset],here.S)
-        return dep
-
-    def last(self,dep):
+
+    def swap(self):
+        for subset in sorted(self.pieces):
+            if subset not in self.other and subset!=self.here.NP-1:
+                self.other[subset]=swap_core(self.pieces[subset],self.here.S)
+
+    def swap_last(self):
         end=self.here.NP-1
-        if end and end not in self.other:
-            self.pieces[end],dep=tie(self.pieces[end],dep)
+        if end not in self.other:
             self.other[end]=swap_core(self.pieces[end],self.here.S)
-        return dep
-
-    def hold(self,dep):
-        n=self.here.NP
-        keys=list(range(n))
-        out=tie(*[self.pieces[s] for s in keys],*[self.other[s] for s in keys],dep)
-        self.pieces=dict(zip(keys,out[:n])); self.other=dict(zip(keys,out[n:2*n]))
-        return out[-1]
 
     def place(self):
         here=self.here
@@ -458,7 +504,7 @@
         idx=[here.slab(s)*2+here.core for s in range(n)]+[here.slab(s,False)*2+1-here.core for s in range(n)]
         index=jnp.stack(idx).astype(jnp.int32)
         parts=[self.pieces[s] for s in range(n)]+[self.other[s] for s in range(n)]
-        out=place_rows(index,parts,range(2*n),2*n)
+        out=place_rows(index,parts,range(2*n),2*n,0.05)
         return out.reshape(-1,parts[0].shape[1])
 
 
@@ -475,7 +521,7 @@
     S=jax.ShapeDtypeStruct((G,h,R,W),bf)
     return pl.pallas_call(fold_kernel,
         grid_spec=pltpu.PrefetchScalarGridSpec(num_scalar_prefetch=1,grid=(h,G),in_specs=[low,high,low,high],out_specs=[out,out]),
-        out_shape=[S,S],compiler_params=cp(16))(index,keep,keep,recv,recv)
+        out_shape=[S,S],cost_estimate=cost(3),compiler_params=cp(16))(index,keep,keep,recv,recv)
 
 
 def split_kernel(index_ref,a,b,*outs):
@@ -489,7 +535,7 @@
     full_=pl.BlockSpec(memory_space=pltpu.VMEM)
     S=jax.ShapeDtypeStruct((G,two,1,r,W),bf)
     return pl.pallas_call(split_kernel,in_specs=[pl.BlockSpec(memory_space=pltpu.SMEM),full_,full_],out_specs=[full_]*M,
-        out_shape=[S]*M,compiler_params=cp(16))(index,a,b)
+        out_shape=[S]*M,cost_estimate=cost(2),compiler_params=cp(16))(index,a,b)
 
 
 def order_kernel(a,b,o):
@@ -501,7 +547,7 @@
     G,two,M,r,W=a.shape
     v=pl.BlockSpec(memory_space=pltpu.VMEM)
     return pl.pallas_call(order_kernel,in_specs=[v,v],out_specs=v,
-        out_shape=jax.ShapeDtypeStruct((M,G,two,r,W),bf),compiler_params=cp(16))(a,b)
+        out_shape=jax.ShapeDtypeStruct((M,G,two,r,W),bf),cost_estimate=cost(2),compiler_params=cp(16))(a,b)
 
 
 class Reduce:
@@ -538,15 +584,22 @@
         parts,dep=tie(order_mem(a,b),dep)
         return lax.psum_scatter(parts,MEM,scatter_dimension=0,tiled=True)[0],dep
 
-    def over_mem_direct(self,dep):
+    def mem_start(self,dep):
         a,b,dep=self.halves(dep)
         M=self.here.M
         parts=split_mem(jnp.stack([(self.here.z+j)%M for j in range(M)]).astype(jnp.int32),a,b)
-        total=parts[0].astype(f32)
-        for j in range(1,M):
-            total=total+shift_mem(parts[j],j,M).astype(f32)
-        G,_,_,r,W=a.shape
-        return total.reshape(G,2,r,W)
+        out=tie(*parts,dep)
+        parts,dep=out[:-1],out[-1]
+        self.got=[parts[0]]+[shift_mem(parts[j],j,M) for j in range(1,M)]
+        return dep
+
+    def mem_sum(self,dep):
+        out=tie(*self.got,dep)
+        total=out[0].astype(f32)
+        for p in out[1:-1]:
+            total=total+p.astype(f32)
+        G,_,_,r,W=total.shape
+        return total.reshape(G,2,r,W),out[-1]
 
 
 def own_rows(total,pl_):
@@ -594,61 +647,80 @@
     aw=attn_master.astype(bf)
     gain_cols=jnp.pad(gain_master.T,((0,0),(0,125))).astype(bf)
     x=tokens[0]
-    slab_first=gather_mem_direct(jnp.concatenate([columns(aw[:3]),gain_cols],axis=1),here)
-    slab_second=lax.all_gather(columns(aw[3:]),MEM,axis=0,tiled=True)
-    slab_mlp=lax.all_gather(columns(mlp_master.astype(bf)),MEM,axis=0,tiled=True)
-    slab_first,memory=tie(slab_first,memory)
+    slab=gather_mem_direct(jnp.concatenate([columns(aw[:3]),gain_cols],axis=1),here)
+    later=jnp.concatenate([columns(aw[3:]),columns(mlp_master.astype(bf))],axis=1)
+    slab,later=tie(slab,later)
+    g1=Gather(slab,here)
+    ring=Ring(later,here)
+    g1.forward()
+    g1.pieces[2]=ring.step(g1.pieces[2])
+    x=g1.arrived(x)
+    g1.swap(); g1.swap_last()
+    g1.other[here.NP-1]=ring.step(g1.other[here.NP-1])
+    g1.other[here.NP-1],memory=tie(g1.other[here.NP-1],memory)
     mem=lax.all_to_all(memory,"mem",split_axis=0,concat_axis=0,tiled=True).reshape(-1,D)
-    first_group=Gather(slab_first,here)
-    x=first_group.last(first_group.forward(x))
-    slab_second=first_group.hold(slab_second)
-    second_group=Gather(slab_second,here)
-    w_first=first_group.place()
+    w_first=g1.place()
     n1,qkv,gains=norm_proj(x,w_first)
-    qkv=second_group.forward(qkv)
+    qkv=ring.finish(qkv)
+    g2=Gather(ring.place(0,5*D),here)
+    slab_mlp=ring.place(5*D,later.shape[1])
     q,k,v=(qkv,0),(qkv,HEADS),(qkv,2*HEADS)
-    o1,lse1=attn_fwd(table_len,q,k,v,True,512,4)
-    o1=second_group.last(o1)
-    slab_mlp=second_group.hold(slab_mlp)
-    mlp_group=Gather(slab_mlp,here)
-    w_second=second_group.place()
+    o1,lse1=attn_fwd(table_len,q,k,v,True,512,4,(0,8))
+    o1=g2.arrived(o1)
+    g2.forward(); g2.swap()
+    o1,lse1=attn_fwd(table_len,q,k,v,True,512,4,(8,4),(o1,lse1))
+    o1,slab_mlp=tie(o1,slab_mlp)
+    o1=g2.arrived(o1)
+    g2.swap_last()
+    g3=Gather(slab_mlp,here)
+    w_second=g2.place()
+    w_second,mem=tie(w_second,mem)
     mkv=mem_proj(mem,w_second,2*D)
     mkv,o1=tie(mkv,o1)
+    o1=g3.arrived(o1)
+    g3.forward(); g3.swap()
     h1,n2,cq=post_self(x,o1,w_second,gains)
-    cq=mlp_group.forward(cq)
     q2,k2,v2=(cq,0),(mkv,0),(mkv,HEADS)
-    o2,lse2=attn_fwd(patch_count,q2,k2,v2,False,512,2)
-    o2=mlp_group.last(o2)
-    w_mlp=mlp_group.place()
+    half=HEADS//2
+    o2,lse2=attn_fwd(patch_count,q2,k2,v2,False,512,2,(0,half))
+    o2=g3.arrived(o2)
+    g3.swap_last()
+    o2,lse2=attn_fwd(patch_count,q2,k2,v2,False,512,2,(half,half),(o2,lse2))
+    o2=g3.arrived(o2)
+    w_mlp=g3.place()
     mixed_out,gh2,gm2,gb2,dg3,mlp_send,mlp_keep=mlp(core,table_len,h1,o2,w_second,cotangent[0],gains,w_mlp)
-    red_mlp=Reduce(mlp_send,mlp_keep,here)
-    half=HEADS//2
+    r1=Reduce(mlp_send,mlp_keep,here)
     part=attn_bwd(patch_count,q2,k2,v2,o2,gm2,lse2,False,256,2,(0,half))
-    part=(red_mlp.fold(part[0]),)+tuple(part[1:])
+    part=(r1.fold(part[0]),)+tuple(part[1:])
     dcq,dmk,dmv=attn_bwd(patch_count,q2,k2,v2,o2,gm2,lse2,False,256,2,(half,half),part)
+    gmem_local,dcq=tie(gmem(dmk,dmv,w_second),dcq)
+    grad_memory=lax.all_to_all(gmem_local.reshape(memory.shape),"mem",split_axis=0,concat_axis=0,tiled=True).astype(f32)
     gh1,gm1,gb1,dg2=mid(h1,gh2,dcq,w_second,gains)
-    gb1=red_mlp.fold(gb1)
+    gb1=r1.fold(gb1)
     second_send,second_keep=wgrads(core,[gb1,n2,mem,gb2],[o1,dcq,dmk,dmv,o2],[(0,0),(1,1),(2,2),(2,3),(3,4)])
-    second_send,dmk=tie(second_send,dmk)
-    red_second=Reduce(second_send,second_keep,here)
-    gmem_local=gmem(dmk,dmv,w_second)
-    gmem_local=red_second.fold(gmem_local)
-    t_mlp,gmem_local=red_mlp.over_mem(gmem_local)
-    grad_memory=lax.all_to_all(gmem_local.reshape(memory.shape),"mem",split_axis=0,concat_axis=0,tiled=True).astype(f32)
-    gm1,gmem_local=tie(gm1,gmem_local)
-    dq,dk,dv=attn_bwd(table_len,q,k,v,o1,gm1,lse1,True,256,2)
+    second_send,gm1=tie(second_send,gm1)
+    r2=Reduce(second_send,second_keep,here)
+    gm1=r1.mem_start(gm1)
+    part=attn_bwd(table_len,q,k,v,o1,gm1,lse1,True,256,2,(0,half))
+    part=(r2.fold(part[0]),)+tuple(part[1:])
+    dq,dk,dv=attn_bwd(table_len,q,k,v,o1,gm1,lse1,True,256,2,(half,half),part)
     first_send,first_keep=wgrads(core,[n1],[dq,dk,dv],[(0,0),(0,1),(0,2)])
-    red_first=Reduce(first_send,first_keep,here)
-    dq=red_second.fold(dq)
-    dq=red_first.fold(dq)
+    r3=Reduce(first_send,first_keep,here)
+    dq,first_keep=tie(dq,first_keep)
+    dq=r2.fold(dq)
+    dq=r3.fold(dq)
+    t_mlp,dq=r1.mem_sum(dq)
     grad_tokens,dg1=first(x,gh1,dq,dk,dv,w_first,gains)
-    dg1=red_first.fold(dg1)
-    t_second,dg1=red_second.over_mem(dg1)
-    gain_all=sum_all(jnp.concatenate([dg1,dg2,dg3],axis=0),here)
-    t_first=red_first.over_mem_direct(dg1)
-    totals=(t_first,t_second.astype(f32),t_mlp.astype(f32))
-    squares=sum(jnp.sum(t*t) for t in totals)
-    grad_norm=jnp.sqrt(sum_all(squares.reshape(1,1),here)[0,0]+jnp.sum(gain_all*gain_all))
+    dg1=r3.fold(dg1)
+    dg1=r2.mem_start(dg1)
+    dg1=r3.mem_start(dg1)
+    t_second,dg1=r2.mem_sum(dg1)
+    t_first,dg1=r3.mem_sum(dg1)
+    totals=(t_first,t_second,t_mlp)
+    squares=jnp.sum(t_first*t_first)+(jnp.sum(t_second*t_second)+jnp.sum(t_mlp*t_mlp))
+    summed=sum_all(jnp.concatenate([dg1,dg2,dg3,jnp.broadcast_to(squares,(1,D))],axis=0),here)
+    gain_all=summed[:3]
+    grad_norm=jnp.sqrt(summed[3,0]+jnp.sum(gain_all*gain_all))
     factor=CLIP_NORM/jnp.maximum(grad_norm,CLIP_NORM)
     red=[own_rows(t,here) for t in totals]
     attn_red=jnp.concatenate(red[:2],axis=0)

time: 479 us -> 418 us (0.87)
  waiting for transfers between devices: 101 us -> 80.9 us
  blocking collectives: 19.9 us -> 0 us
  local copies, waits for them, and re-layouts: 49.1 us -> 32.1 us
  between operations: 23.4 us -> 7.82 us
  Pallas kernels: 200 us -> 211 us
    all_gather x1 -> x0, blocking collectives: 19.9 us -> none  [on_device(): slab_second = lax.all_gather(columns(aw[3:]), MEM, axis=0, tiled=True)]
    ppermute x6 -> x15, waiting for transfers between devices: 15 us -> 34.1 us  [shift_mem(): lax.ppermute(x, MEM, [(z, (z + step) % mem_size) for z in range(mem_size)])]
    ppermute x15, waiting for transfers between devices: 51.4 us -> 33.9 us  [cross(): return lax.ppermute(x, SEQ, perm)]
    unnamed x168 -> x177, local copies, waits for them, and re-layouts: 47.5 us -> 31.2 us
    ppermute x6 -> x15, starting transfers between devices: 11 us -> 25.4 us  [shift_mem(): lax.ppermute(x, MEM, [(z, (z + step) % mem_size) for z in range(mem_size)])]
    ppermute x4 -> x2, starting transfers between devices: 13.7 us -> 3.36 us  [sum_all(): x = x + lax.ppermute(x, MEM, [(z, z ^ 1 << b) for z in range(pl_.M)])]
    all_to_all x1, waiting for transfers between devices: 13.3 us -> 4.01 us  [on_device(): lax.all_to_all(memory, 'mem', split_axis=0, concat_axis=0, tiled=True)]
    ppermute x18, waiting for transfers between devices: 7.29 us -> 0.05 us  [swap_core(): return lax.ppermute(x, SEQ, [(s, s ^ 1) for s in range(seq_size)])]
  transfers between devices with their start and end apart: 54 -> 55, of which waited for: 23 -> 22; matrix products, arithmetic and copies ran while one was open for 3% -> 3% of each run, Pallas kernels for 23% -> 38%
where the time goes in v3:
time: 418 us; the launch traced here: 414 us
  Pallas kernels  211 us (50%)
  waiting for transfers between devices  80.9 us (19%)
  starting transfers between devices  66.7 us (16%)
  local copies, waits for them, and re-layouts  32.1 us (8%)
  other arithmetic  15.3 us (4%)
  between operations  7.82 us (2%)
    pallas_call x4, Pallas kernels, attn_bwd(): pl.pallas_call(functools.partial(bwd_kernel if into is None else bwd_part...  51.5 us
    pallas_call x1, Pallas kernels, mlp(): pl.pallas_call(functools.partial(mlp_kernel, tb=tb), grid_spec=pltpu.Pref...  42.3 us
    ppermute x15, waiting for transfers between devices, shift_mem(): lax.ppermute(x, MEM, [(z, (z + step) % mem_size) for z in range(mem_size)])  34.1 us
    ppermute x15, waiting for transfers between devices, cross(): return lax.ppermute(x, SEQ, perm)  33.9 us
    unnamed x177, local copies, waits for them, and re-layouts  31.2 us
    pallas_call x4, Pallas kernels, attn_fwd(): pl.pallas_call(functools.partial(fwd_kernel if into is None else fwd_part...  28.7 us
    ppermute x15, starting transfers between devices, shift_mem(): lax.ppermute(x, MEM, [(z, (z + step) % mem_size) for z in range(mem_size)])  25.4 us
    ppermute x15, starting transfers between devices, cross(): return lax.ppermute(x, SEQ, perm)  22.7 us
  transfers between devices with their start and end apart: 55, of which 22 were waited for; matrix products, arithmetic and copies ran while one was open for 3% of the time, Pallas kernels for 38%

profile of v3, /device:TPU:0, one launch (start us, length us, event | category | flops | bytes accessed | tf_op | source)
XLA Modules:
  0.0 414.2 jit_solution(1805350229096315033)
XLA Ops:
  2.6 3.1 collective-permute-start
  11.9 4.2 %collective-permute-done.1.refs_2_ = bf16[24,2432]{1,0:T(8,128)(2,1)S(1)} collective-permute-done((bf16[24,2432]{1,0:T(8,128)(2,1)S(1)}, bf16[24,2432]{1,0:T(8,128)(2,1)S(1)}, u32[]{:S(2)}, u32[]{:S(2)}) %collective-permute-start.1) | collective-permute-done | bytes 116768 | tf_op jit(solution)/shard_map/ppermute | solution.py:387
  18.8 3.0 collective-permute-start.4
  23.3 4.5 %collective-permute-done.3.refs_1_ = bf16[96,2432]{1,0:T(8,128)(2,1)S(1)} collective-permute-done((bf16[96,2432]{1,0:T(8,128)(2,1)S(1)}, bf16[96,2432]{1,0:T(8,128)(2,1)S(1)}, u32[]{:S(2)}, u32[]{:S(2)}) %collective-permute-start.3) | collective-permute-done | bytes 466976 | tf_op jit(solution)/shard_map/ppermute | solution.py:379
  30.4 2.8 collective-permute-done.4.refs_1_
  38.1 8.7 %collective-permute-done.7.refs_2_ = bf16[24,9984]{1,0:T(8,128)(2,1)} collective-permute-done((bf16[24,9984]{1,0:T(8,128)(2,1)}, bf16[24,9984]{1,0:T(8,128)(2,1)}, u32[]{:S(2)}, u32[]{:S(2)}) %collective-permute-start.7) | collective-permute-done | bytes 479264 | tf_op jit(solution)/shard_map/ppermute | solution.py:387
  47.3 3.4 shard_map.238
  50.6 6.3 %shard_map.239 = (bf16[1024,768]{1,0:T(8,128)(2,1)S(1)}, bf16[2304,1024]{1,0:T(8,128)(2,1)S(1)}, f32[8,768]{1,0:T(8,128)S(1)}) custom-call(bf16[1024,768]{1,0:T(8,128)(2,1)S(1)} %bitcast.132, bf16[768,2432]{1,0:T(8,128)(2,1)S(1)} %bitcast.117, bf16[768,2432]{1,0:T(8,128)(2,1)S(1)} %bitcast.118), custom_call_target="tpu_custom_call" | custom-call | flops 60000002048 | bytes 100000 | tf_op jit(solution)/shard_map/pallas_call | solution.py:166
  61.9 3.8 collective-permute-start.13
  66.4 3.8 all-to-all-start
  72.5 7.0 %shard_map.241 = (bf16[768,1024]{1,0:T(8,128)(2,1)S(1)}, f32[12,1,1024]{2,1,0:T(1,128)S(1)}) custom-call(s32[1]{0:T(128)S(6)} %copy.55.len_ref.refs_0_, bf16[2304,1024]{1,0:T(8,128)(2,1)S(1)} %copy-done.1, bf16[2304,1024]{1,0:T(8,128)(2,1)S(1)} %copy-done.1, bf16[2304,1024]{1,0:T(8,128)(2,1)S(1)} %copy-done.1), custom_call_target="tpu_custom_call" | custom-call | flops 3000000000 | bytes 100000 | tf_op jit(solution)/shard_map/pallas_call | solution.py:76
  82.8 2.7 shard_map.243
  85.5 3.5 shard_map.242
  101.2 4.0 all-to-all-done
  105.2 3.2 copy-done.3
  108.5 3.6 shard_map.245.kT_ref.vT_ref.refs_2_.refs_3_
  112.0 9.3 %collective-permute-done.15.refs_1_ = bf16[96,6144]{1,0:T(8,128)(2,1)} collective-permute-done((bf16[96,6144]{1,0:T(8,128)(2,1)}, bf16[96,6144]{1,0:T(8,128)(2,1)}, u32[]{:S(2)}, u32[]{:S(2)}) %collective-permute-start.15) | collective-permute-done | bytes 1179680 | tf_op jit(solution)/shard_map/ppermute | solution.py:379
  124.1 5.7 %shard_map.246 = (f32[1024,768]{1,0:T(8,128)S(1)}, bf16[1024,768]{1,0:T(8,128)(2,1)S(1)}, bf16[768,1024]{1,0:T(8,128)(2,1)S(1)}) custom-call(bf16[1024,768]{1,0:T(8,128)(2,1)S(1)} %bitcast.133, bf16[768,1024]{1,0:T(8,128)(2,1)S(1)} %get-tuple-element.241.oT_ref.refs_4_, bf16[768,3840]{1,0:T(8,128)(2,1)S(1)} %bitcast.106, bf16[768,3840]{1,0:T(8,128)(2,1)S(1)} %bitcast.107, ...), custom_call_target="tpu_custom_call" | custom-call | flops 60000002048 | bytes 100000 | tf_op jit(solution)/shard_map/pallas_call | solution.py:188
  129.8 9.4 %shard_map.247 = (bf16[768,1024]{1,0:T(8,128)(2,1)S(1)}, f32[12,1,1024]{2,1,0:T(1,128)S(1)}) custom-call(s32[1]{0:T(128)S(6)} %copy.56.len_ref.refs_0_, bf16[768,1024]{1,0:T(8,128)(2,1)S(1)} %get-tuple-element.247.qT_ref.refs_1_, bf16[1536,1024]{1,0:T(8,128)(2,1)S(1)} %shard_map.245.kT_ref.vT_ref.refs_2_.refs_3_, ...), custom_call_target="tpu_custom_call" | custom-call | flops 3000000000 | bytes 100000 | tf_op jit(solution)/shard_map/pallas_call | solution.py:76
  148.8 8.8 %shard_map.248 = (bf16[768,1024]{1,0:T(8,128)(2,1)S(1)}, f32[12,1,1024]{2,1,0:T(1,128)S(1)}) custom-call(s32[1]{0:T(128)S(6)} %copy.56.len_ref.refs_0_, bf16[768,1024]{1,0:T(8,128)(2,1)S(1)} %copy-done.52, bf16[1536,1024]{1,0:T(8,128)(2,1)S(1)} %copy-done.49, bf16[1536,1024]{1,0:T(8,128)(2,1)S(1)} %copy-done.49, ...), custom_call_target="tpu_custom_call", output_to_operand_aliasing={{0}: (4, {}), {1}: (5, {})} | custom-call | flops 3000000000 | bytes 100000 | tf_op jit(solution)/shard_map/pallas_call | solution.py:76
  161.4 3.6 copy-done.6
  165.0 42.3 %shard_map.250 = (bf16[1024,768]{1,0:T(8,128)(2,1)}, f32[1024,768]{1,0:T(8,128)}, bf16[768,1024]{1,0:T(8,128)(2,1)S(1)}, bf16[1024,768]{1,0:T(8,128)(2,1)S(1)}, ...) custom-call(s32[1]{0:T(128)} %bitcast.core_ref, s32[1]{0:T(128)S(6)} %copy.55.len_ref.refs_0_, ...), custom_call_target="tpu_custom_call" | custom-call | flops 420000006144 | bytes 100000 | tf_op jit(solution)/shard_map/pallas_call | solution.py:274
  207.4 15.9 %shard_map.251 = (bf16[768,1024]{1,0:T(8,128)(2,1)S(1)}, bf16[768,1024]{1,0:T(8,128)(2,1)S(1)}, bf16[768,1024]{1,0:T(8,128)(2,1)S(1)}) custom-call(s32[1]{0:T(128)S(6)} %copy.56.len_ref.refs_0_, bf16[768,1024]{1,0:T(8,128)(2,1)S(1)} %copy-done.53, bf16[1536,1024]{1,0:T(8,128)(2,1)S(1)} %copy-done.50, bf16[1536,1024]{1,0:T(8,128)(2,1)S(1)} %copy-done.50, ...), custom_call_target="tpu_custom_call" | custom-call | flops 140000002048 | bytes 100000 | tf_op jit(solution)/shard_map/pallas_call | solution.py:136
  223.4 3.4 shard_map.252
  227.9 15.7 %shard_map.253 = (bf16[768,1024]{1,0:T(8,128)(2,1)S(1)}, bf16[768,1024]{1,0:T(8,128)(2,1)S(1)}, bf16[768,1024]{1,0:T(8,128)(2,1)S(1)}) custom-call(s32[1]{0:T(128)S(6)} %copy.56.len_ref.refs_0_, bf16[768,1024]{1,0:T(8,128)(2,1)S(1)} %copy-done.53, bf16[1536,1024]{1,0:T(8,128)(2,1)S(1)} %copy-done.50, ...), custom_call_target="tpu_custom_call", output_to_operand_aliasing={{0}: (7, {}), {1}: (8, {}), {2}: (9, {})} | custom-call | flops 140000002048 | bytes 100000 | tf_op jit(solution)/shard_map/pallas_call | solution.py:136
  244.8 4.7 %shard_map.254 = bf16[1024,768]{1,0:T(8,128)(2,1)} custom-call(bf16[768,1024]{1,0:T(8,128)(2,1)S(1)} %get-tuple-element.283.kT_ref.refs_6_, bf16[768,1024]{1,0:T(8,128)(2,1)S(1)} %get-tuple-element.284.vT_ref.refs_7_, bf16[768,3840]{1,0:T(8,128)(2,1)S(1)} %bitcast.110, bf16[768,3840]{1,0:T(8,128)(2,1)S(1)} %bitcast.111), custom_call_target="tpu_custom_call" | custom-call | flops 2000000000 | bytes 100000 | tf_op jit(solution)/shard_map/pallas_call | solution.py:328
  249.5 4.8 %all-to-all-start.1 = ((bf16[4,256,768]{2,1,0:T(8,128)(2,1)}), bf16[4,256,768]{2,1,0:T(8,128)(2,1)}, u32[]{:S(2)}, u32[]{:S(2)}) async-start(bf16[4,256,768]{2,1,0:T(8,128)(2,1)} %bitcast.51), calls=%async_computation.1 | async-start | bytes 3145728 | tf_op jit(solution)/shard_map/all_to_all | solution.py:697
  260.4 6.1 %shard_map.255 = (f32[1024,768]{1,0:T(8,128)S(1)}, bf16[768,1024]{1,0:T(8,128)(2,1)S(1)}, bf16[1024,768]{1,0:T(8,128)(2,1)S(1)}, f32[1,768]{1,0:T(1,128)S(1)}) custom-call(f32[1024,768]{1,0:T(8,128)S(1)} %copy-done.10, f32[1024,768]{1,0:T(8,128)S(1)} %copy-done.11, bf16[768,1024]{1,0:T(8,128)(2,1)S(1)} %copy-done.17, bf16[768,3840]{1,0:T(8,128)(2,1)S(1)} %bitcast.112, ...), custom_call_target="tpu_custom_call" | custom-call | flops 2000000000 | bytes 100000 | tf_op jit(solution)/shard_map/pallas_call | solution.py:302
  266.6 5.4 %shard_map.256 = (bf16[3,1,192,1024]{3,2,1,0:T(8,128)(2,1)S(1)}, bf16[3,1,192,1024]{3,2,1,0:T(8,128)(2,1)S(1)}) custom-call(s32[2]{0:T(128)S(1)} %iota.9.index_ref, bf16[3,2,192,1024]{3,2,1,0:T(8,128)(2,1)S(1)} %copy-done.60, bf16[3,2,192,1024]{3,2,1,0:T(8,128)(2,1)S(1)} %copy-done.60, bf16[3,2,192,1024]{3,2,1,0:T(8,128)(2,1)} %collective-permute-done.28.ra.rb, ...), custom_call_target="tpu_custom_call" | custom-call | flops 30000001024 | bytes 100000 | tf_op jit(solution)/shard_map/pallas_call | solution.py:522
  273.0 10.6 %shard_map.257 = (bf16[5,768,384]{2,1,0:T(8,128)(2,1)}, bf16[5,768,384]{2,1,0:T(8,128)(2,1)}) custom-call(s32[1]{0:T(128)} %bitcast.core_ref, bf16[1024,768]{1,0:T(8,128)(2,1)S(1)} %get-tuple-element.297.refs_0_, bf16[1024,768]{1,0:T(8,128)(2,1)S(1)} %copy-done.62, bf16[1024,768]{1,0:T(8,128)(2,1)S(1)} %bitcast.123, bf16[1024,768]{1,0:T(8,128)(2,1)S(1)} %copy-done.68, ...), custom_call_target="tpu_custom_call" | custom-call | flops 80000000000 | bytes 100000 | tf_op jit(solution)/shard_map/pallas_call | solution.py:319
  284.3 4.0 collective-permute-done.29
  295.8 10.1 %shard_map.259 = (bf16[768,1024]{1,0:T(8,128)(2,1)S(1)}, bf16[768,1024]{1,0:T(8,128)(2,1)S(1)}, bf16[768,1024]{1,0:T(8,128)(2,1)S(1)}) custom-call(s32[1]{0:T(128)S(6)} %copy.55.len_ref.refs_0_, bf16[2304,1024]{1,0:T(8,128)(2,1)S(1)} %bitcast.103, bf16[2304,1024]{1,0:T(8,128)(2,1)S(1)} %bitcast.103, bf16[2304,1024]{1,0:T(8,128)(2,1)S(1)} %bitcast.103, ...), custom_call_target="tpu_custom_call" | custom-call | flops 140000002048 | bytes 100000 | tf_op jit(solution)/shard_map/pallas_call | solution.py:136
  305.9 7.4 %shard_map.260 = (bf16[5,2,192,384]{3,2,1,0:T(8,128)(2,1)}, bf16[5,2,192,384]{3,2,1,0:T(8,128)(2,1)S(1)}) custom-call(s32[4]{0:T(128)S(1)} %copy-done.37, bf16[5,4,192,384]{3,2,1,0:T(8,128)(2,1)S(1)} %bitcast.140, bf16[5,4,192,384]{3,2,1,0:T(8,128)(2,1)S(1)} %bitcast.141, bf16[5,4,192,384]{3,2,1,0:T(8,128)(2,1)} %bitcast.47.ra.rb, ...), custom_call_target="tpu_custom_call" | custom-call | flops 30000001024 | bytes 100000 | tf_op jit(solution)/shard_map/pallas_call | solution.py:522
  314.2 9.8 %shard_map.261 = (bf16[768,1024]{1,0:T(8,128)(2,1)S(1)}, bf16[768,1024]{1,0:T(8,128)(2,1)S(1)}, bf16[768,1024]{1,0:T(8,128)(2,1)S(1)}) custom-call(s32[1]{0:T(128)S(6)} %copy.55.len_ref.refs_0_, bf16[2304,1024]{1,0:T(8,128)(2,1)S(1)} %bitcast.103, bf16[2304,1024]{1,0:T(8,128)(2,1)S(1)} %bitcast.103, ...), custom_call_target="tpu_custom_call", output_to_operand_aliasing={{0}: (7, {}), {1}: (8, {}), {2}: (9, {})} | custom-call | flops 140000002048 | bytes 100000 | tf_op jit(solution)/shard_map/pallas_call | solution.py:136
  324.0 5.1 %shard_map.262 = (bf16[3,768,384]{2,1,0:T(8,128)(2,1)S(1)}, bf16[3,768,384]{2,1,0:T(8,128)(2,1)S(1)}) custom-call(s32[1]{0:T(128)} %bitcast.core_ref, bf16[1024,768]{1,0:T(8,128)(2,1)S(1)} %copy-done.64, bf16[768,1024]{1,0:T(8,128)(2,1)S(1)} %get-tuple-element.344.refs_1_.qT_ref, bf16[768,1024]{1,0:T(8,128)(2,1)S(1)} %get-tuple-element.327.refs_2_.kT_ref, ...), custom_call_target="tpu_custom_call" | custom-call | flops 80000000000 | bytes 100000 | tf_op jit(solution)/shard_map/pallas_call | solution.py:319
  329.2 3.7 collective-permute-done.35.ra.rb
  333.0 3.8 shard_map.263
  341.5 7.6 %shard_map.265 = (f32[1024,768]{1,0:T(8,128)}, f32[1,768]{1,0:T(1,128)S(1)}) custom-call(bf16[1024,768]{1,0:T(8,128)(2,1)S(1)} %bitcast.134, f32[1024,768]{1,0:T(8,128)S(1)} %copy-done.40, bf16[768,1024]{1,0:T(8,128)(2,1)S(1)} %copy-done.66, bf16[768,1024]{1,0:T(8,128)(2,1)S(1)} %get-tuple-element.327.refs_2_.kT_ref, ...), custom_call_target="tpu_custom_call" | custom-call | flops 70000001024 | bytes 100000 | tf_op jit(solution)/shard_map/pallas_call | solution.py:349
  349.1 2.8 multiply_reduce_fusion
  351.9 2.8 collective-permute-done.36.ra.rb
  358.0 2.7 collective-permute-start.44
  360.7 3.1 collective-permute-done.37
  365.7 2.7 collective-permute-start.41
  368.4 5.3 %collective-permute-done.43 = bf16[5,2,1,24,384]{4,3,2,1,0:T(8,128)(2,1)S(1)} collective-permute-done((bf16[5,2,1,24,384]{4,3,2,1,0:T(8,128)(2,1)S(1)}, bf16[5,2,1,24,384]{4,3,2,1,0:T(8,128)(2,1)S(1)}, u32[]{:S(2)}, u32[]{:S(2)}) %collective-permute-start.43) | collective-permute-done | bytes 184352 | tf_op jit(solution)/shard_map/ppermute | solution.py:387
  375.7 8.8 %collective-permute-done.40 = bf16[3,2,1,24,384]{4,3,2,1,0:T(8,128)(2,1)S(1)} collective-permute-done((bf16[3,2,1,24,384]{4,3,2,1,0:T(8,128)(2,1)S(1)}, bf16[3,2,1,24,384]{4,3,2,1,0:T(8,128)(2,1)S(1)}, u32[]{:S(2)}, u32[]{:S(2)}) %collective-permute-start.40) | collective-permute-done | bytes 110624 | tf_op jit(solution)/shard_map/ppermute | solution.py:387
  389.2 3.3 convert_element_type.50
  393.2 3.1 collective-permute-done.47
  401.5 3.5 collective-permute-done.49
  (309 shorter events, 103.8 us)
Async XLA Ops:
  2.6 9.2 %collective-permute-start = (bf16[24,2432]{1,0:T(8,128)(2,1)S(1)}, bf16[24,2432]{1,0:T(8,128)(2,1)S(1)}, u32[]{:S(2)}, u32[]{:S(2)}) collective-permute-start(bf16[24,2432]{1,0:T(8,128)(2,1)S(1)} %fusion.3.refs_0_), channel_id=1, source_target_pairs={{0,1},{1,2},{2,3},{3,0},{4,5},{5,6},{6,7},{7,4},{8,9},{9,10},{10,1... | collective-permute-start | bytes 350216 | tf_op jit(solution)/shard_map/ppermute | solution.py:387
  5.7 10.3 %collective-permute-start.1 = (bf16[24,2432]{1,0:T(8,128)(2,1)S(1)}, bf16[24,2432]{1,0:T(8,128)(2,1)S(1)}, u32[]{:S(2)}, u32[]{:S(2)}) collective-permute-start(bf16[24,2432]{1,0:T(8,128)(2,1)S(1)} %fusion.3.refs_0_), channel_id=1, source_target_pairs={{0,2},{1,3},{2,0},{3,1},{4,6},{5,7},{6,4},{7,5},{8,10},{9,11},{10,... | collective-permute-start | bytes 350216 | tf_op jit(solution)/shard_map/ppermute | solution.py:387
  8.3 7.7 %collective-permute-start.2 = (bf16[24,2432]{1,0:T(8,128)(2,1)S(1)}, bf16[24,2432]{1,0:T(8,128)(2,1)S(1)}, u32[]{:S(2)}, u32[]{:S(2)}) collective-permute-start(bf16[24,2432]{1,0:T(8,128)(2,1)S(1)} %fusion.3.refs_0_), channel_id=1, source_target_pairs={{0,3},{1,0},{2,1},{3,2},{4,7},{5,4},{6,5},{7,6},{8,11},{9,8},{10,9... | collective-permute-start | bytes 350216 | tf_op jit(solution)/shard_map/ppermute | solution.py:387
  17.2 10.5 %collective-permute-start.3 = (bf16[96,2432]{1,0:T(8,128)(2,1)S(1)}, bf16[96,2432]{1,0:T(8,128)(2,1)S(1)}, u32[]{:S(2)}, u32[]{:S(2)}) collective-permute-start(bf16[96,2432]{1,0:T(8,128)(2,1)S(1)} %bitcast.124), channel_id=1, source_target_pairs={{0,8},{4,20},{8,0},{12,28},{16,24},{20,4},{24,16},{28,12},{1,9},{5... | collective-permute-start | bytes 1400840 | tf_op jit(solution)/shard_map/ppermute | solution.py:379
  18.8 14.4 %collective-permute-start.4 = (bf16[24,9984]{1,0:T(8,128)(2,1)S(1)}, bf16[24,9984]{1,0:T(8,128)(2,1)}, u32[]{:S(2)}, u32[]{:S(2)}) collective-permute-start(bf16[24,9984]{1,0:T(8,128)(2,1)S(1)} %fusion.4.refs_0_), channel_id=1, source_target_pairs={{0,1},{1,2},{2,3},{3,0},{4,5},{5,6},{6,7},{7,4},{8,9},{9,10},{10,1... | collective-permute-start | bytes 1437704 | tf_op jit(solution)/shard_map/ppermute | solution.py:387
  21.8 8.6 %collective-permute-start.5 = (bf16[96,2432]{1,0:T(8,128)(2,1)S(1)}, bf16[96,2432]{1,0:T(8,128)(2,1)S(1)}, u32[]{:S(2)}, u32[]{:S(2)}) collective-permute-start(bf16[96,2432]{1,0:T(8,128)(2,1)S(1)} %bitcast.125), channel_id=1, source_target_pairs={{0,16},{4,12},{8,24},{12,4},{16,0},{20,28},{24,8},{28,20},{1,17},{... | collective-permute-start | bytes 1400840 | tf_op jit(solution)/shard_map/ppermute | solution.py:379
  27.8 9.2 %collective-permute-start.6 = (bf16[96,2432]{1,0:T(8,128)(2,1)S(1)}, bf16[96,2432]{1,0:T(8,128)(2,1)S(1)}, u32[]{:S(2)}, u32[]{:S(2)}) collective-permute-start(bf16[96,2432]{1,0:T(8,128)(2,1)S(1)} %collective-permute-done.3.refs_1_), channel_id=1, source_target_pairs={{0,16},{4,12},{8,24},{12,4},{16,0},{20,28},{24,8},{28,20},{1,17},{... | collective-permute-start | bytes 1400840 | tf_op jit(solution)/shard_map/ppermute | solution.py:379
  33.3 13.6 %collective-permute-start.7 = (bf16[24,9984]{1,0:T(8,128)(2,1)}, bf16[24,9984]{1,0:T(8,128)(2,1)}, u32[]{:S(2)}, u32[]{:S(2)}) collective-permute-start(bf16[24,9984]{1,0:T(8,128)(2,1)} %collective-permute-done.4.refs_1_), channel_id=1, source_target_pairs={{0,1},{1,2},{2,3},{3,0},{4,5},{5,6},{6,7},{7,4},{8,9},{9,10},{10,1... | collective-permute-start | bytes 1437704 | tf_op jit(solution)/shard_map/ppermute | solution.py:387
  37.0 9.8 %collective-permute-start.8 = (bf16[96,2432]{1,0:T(8,128)(2,1)S(1)}, bf16[96,2432]{1,0:T(8,128)(2,1)S(1)}, u32[]{:S(2)}, u32[]{:S(2)}) collective-permute-start(bf16[96,2432]{1,0:T(8,128)(2,1)S(1)} %collective-permute-done.6.refs_3_), channel_id=1, source_target_pairs={{0,4},{4,0},{8,12},{12,8},{16,20},{20,16},{24,28},{28,24},{1,5},{5... | collective-permute-start | bytes 1400840 | tf_op jit(solution)/shard_map/ppermute | solution.py:383
  37.0 10.3 %collective-permute-start.10 = (bf16[96,2432]{1,0:T(8,128)(2,1)S(1)}, bf16[96,2432]{1,0:T(8,128)(2,1)S(1)}, u32[]{:S(2)}, u32[]{:S(2)}) collective-permute-start(bf16[96,2432]{1,0:T(8,128)(2,1)S(1)} %bitcast.126), channel_id=1, source_target_pairs={{0,4},{4,0},{8,12},{12,8},{16,20},{20,16},{24,28},{28,24},{1,5},{5... | collective-permute-start | bytes 1400840 | tf_op jit(solution)/shard_map/ppermute | solution.py:383
  37.5 9.8 %collective-permute-start.11 = (bf16[96,2432]{1,0:T(8,128)(2,1)S(1)}, bf16[96,2432]{1,0:T(8,128)(2,1)S(1)}, u32[]{:S(2)}, u32[]{:S(2)}) collective-permute-start(bf16[96,2432]{1,0:T(8,128)(2,1)S(1)} %collective-permute-done.3.refs_1_), channel_id=1, source_target_pairs={{0,4},{4,0},{8,12},{12,8},{16,20},{20,16},{24,28},{28,24},{1,5},{5... | collective-permute-start | bytes 1400840 | tf_op jit(solution)/shard_map/ppermute | solution.py:383
  37.5 9.8 %collective-permute-start.12 = (bf16[96,2432]{1,0:T(8,128)(2,1)S(1)}, bf16[96,2432]{1,0:T(8,128)(2,1)}, u32[]{:S(2)}, u32[]{:S(2)}) collective-permute-start(bf16[96,2432]{1,0:T(8,128)(2,1)S(1)} %collective-permute-done.5.refs_2_), channel_id=1, source_target_pairs={{0,4},{4,0},{8,12},{12,8},{16,20},{20,16},{24,28},{28,24},{1,5},{5... | collective-permute-start | bytes 1400840 | tf_op jit(solution)/shard_map/ppermute | solution.py:383
  46.8 12.5 %collective-permute-start.9 = (bf16[24,9984]{1,0:T(8,128)(2,1)}, bf16[24,9984]{1,0:T(8,128)(2,1)S(1)}, u32[]{:S(2)}, u32[]{:S(2)}) collective-permute-start(bf16[24,9984]{1,0:T(8,128)(2,1)} %collective-permute-done.7.refs_2_), channel_id=1, source_target_pairs={{0,1},{1,2},{2,3},{3,0},{4,5},{5,6},{6,7},{7,4},{8,9},{9,10},{10,1... | collective-permute-start | bytes 1437704 | tf_op jit(solution)/shard_map/ppermute | solution.py:387
  61.9 18.7 %collective-permute-start.13 = (bf16[96,3840]{1,0:T(8,128)(2,1)}, bf16[96,3840]{1,0:T(8,128)(2,1)}, u32[]{:S(2)}, u32[]{:S(2)}) collective-permute-start(bf16[96,3840]{1,0:T(8,128)(2,1)} %bitcast.28.refs_0_), channel_id=1, source_target_pairs={{0,8},{4,20},{8,0},{12,28},{16,24},{20,4},{24,16},{28,12},{1,9},{5... | collective-permute-start | bytes 2211848 | tf_op jit(solution)/shard_map/ppermute | solution.py:379
  65.7 14.9 %collective-permute-start.14 = (bf16[96,3840]{1,0:T(8,128)(2,1)}, bf16[96,3840]{1,0:T(8,128)(2,1)}, u32[]{:S(2)}, u32[]{:S(2)}) collective-permute-start(bf16[96,3840]{1,0:T(8,128)(2,1)} %bitcast.28.refs_0_), channel_id=1, source_target_pairs={{0,16},{4,12},{8,24},{12,4},{16,0},{20,28},{24,8},{28,20},{1,17},{... | collective-permute-start | bytes 2211848 | tf_op jit(solution)/shard_map/ppermute | solution.py:379
  66.4 38.9 %all-to-all-start = ((bf16[4,256,768]{2,1,0:T(8,128)(2,1)}), bf16[4,256,768]{2,1,0:T(8,128)(2,1)S(1)}, u32[]{:S(2)}, u32[]{:S(2)}) async-start(bf16[4,256,768]{2,1,0:T(8,128)(2,1)} %param.15), calls=%async_computation | async-start | bytes 3145728 | tf_op jit(solution)/shard_map/all_to_all | solution.py:661
  80.6 11.7 %collective-permute-start.17 = (bf16[96,3840]{1,0:T(8,128)(2,1)}, bf16[96,3840]{1,0:T(8,128)(2,1)S(1)}, u32[]{:S(2)}, u32[]{:S(2)}) collective-permute-start(bf16[96,3840]{1,0:T(8,128)(2,1)} %collective-permute-done.13.refs_1_), channel_id=1, source_target_pairs={{0,16},{4,12},{8,24},{12,4},{16,0},{20,28},{24,8},{28,20},{1,17},{... | collective-permute-start | bytes 2211848 | tf_op jit(solution)/shard_map/ppermute | solution.py:379
  82.3 10.0 %collective-permute-start.19 = (bf16[96,3840]{1,0:T(8,128)(2,1)}, bf16[96,3840]{1,0:T(8,128)(2,1)S(1)}, u32[]{:S(2)}, u32[]{:S(2)}) collective-permute-start(bf16[96,3840]{1,0:T(8,128)(2,1)} %collective-permute-done.13.refs_1_), channel_id=1, source_target_pairs={{0,4},{4,0},{8,12},{12,8},{16,20},{20,16},{24,28},{28,24},{1,5},{5... | collective-permute-start | bytes 2211848 | tf_op jit(solution)/shard_map/ppermute | solution.py:383
  82.3 10.0 %collective-permute-start.18 = (bf16[96,3840]{1,0:T(8,128)(2,1)}, bf16[96,3840]{1,0:T(8,128)(2,1)S(1)}, u32[]{:S(2)}, u32[]{:S(2)}) collective-permute-start(bf16[96,3840]{1,0:T(8,128)(2,1)} %bitcast.28.refs_0_), channel_id=1, source_target_pairs={{0,4},{4,0},{8,12},{12,8},{16,20},{20,16},{24,28},{28,24},{1,5},{5... | collective-permute-start | bytes 2211848 | tf_op jit(solution)/shard_map/ppermute | solution.py:383
  82.8 9.5 %collective-permute-start.20 = (bf16[96,3840]{1,0:T(8,128)(2,1)}, bf16[96,3840]{1,0:T(8,128)(2,1)S(1)}, u32[]{:S(2)}, u32[]{:S(2)}) collective-permute-start(bf16[96,3840]{1,0:T(8,128)(2,1)} %collective-permute-done.14.refs_2_), channel_id=1, source_target_pairs={{0,4},{4,0},{8,12},{12,8},{16,20},{20,16},{24,28},{28,24},{1,5},{5... | collective-permute-start | bytes 2211848 | tf_op jit(solution)/shard_map/ppermute | solution.py:383
  93.0 28.3 %collective-permute-start.15 = (bf16[96,6144]{1,0:T(8,128)(2,1)}, bf16[96,6144]{1,0:T(8,128)(2,1)}, u32[]{:S(2)}, u32[]{:S(2)}) collective-permute-start(bf16[96,6144]{1,0:T(8,128)(2,1)} %bitcast.29.refs_0_), channel_id=1, source_target_pairs={{0,8},{4,20},{8,0},{12,28},{16,24},{20,4},{24,16},{28,12},{1,9},{5... | collective-permute-start | bytes 3538952 | tf_op jit(solution)/shard_map/ppermute | solution.py:379
  94.8 26.9 %collective-permute-start.16 = (bf16[96,6144]{1,0:T(8,128)(2,1)}, bf16[96,6144]{1,0:T(8,128)(2,1)}, u32[]{:S(2)}, u32[]{:S(2)}) collective-permute-start(bf16[96,6144]{1,0:T(8,128)(2,1)} %bitcast.29.refs_0_), channel_id=1, source_target_pairs={{0,16},{4,12},{8,24},{12,4},{16,0},{20,28},{24,8},{28,20},{1,17},{... | collective-permute-start | bytes 3538952 | tf_op jit(solution)/shard_map/ppermute | solution.py:379
  121.8 18.6 %collective-permute-start.22 = (bf16[96,6144]{1,0:T(8,128)(2,1)}, bf16[96,6144]{1,0:T(8,128)(2,1)S(1)}, u32[]{:S(2)}, u32[]{:S(2)}) collective-permute-start(bf16[96,6144]{1,0:T(8,128)(2,1)} %collective-permute-done.15.refs_1_), channel_id=1, source_target_pairs={{0,16},{4,12},{8,24},{12,4},{16,0},{20,28},{24,8},{28,20},{1,17},{... | collective-permute-start | bytes 3538952 | tf_op jit(solution)/shard_map/ppermute | solution.py:379
  123.6 17.8 %collective-permute-start.24 = (bf16[96,6144]{1,0:T(8,128)(2,1)}, bf16[96,6144]{1,0:T(8,128)(2,1)S(1)}, u32[]{:S(2)}, u32[]{:S(2)}) collective-permute-start(bf16[96,6144]{1,0:T(8,128)(2,1)} %collective-permute-done.15.refs_1_), channel_id=1, source_target_pairs={{0,4},{4,0},{8,12},{12,8},{16,20},{20,16},{24,28},{28,24},{1,5},{5... | collective-permute-start | bytes 3538952 | tf_op jit(solution)/shard_map/ppermute | solution.py:383
  123.6 16.8 %collective-permute-start.23 = (bf16[96,6144]{1,0:T(8,128)(2,1)}, bf16[96,6144]{1,0:T(8,128)(2,1)S(1)}, u32[]{:S(2)}, u32[]{:S(2)}) collective-permute-start(bf16[96,6144]{1,0:T(8,128)(2,1)} %bitcast.29.refs_0_), channel_id=1, source_target_pairs={{0,4},{4,0},{8,12},{12,8},{16,20},{20,16},{24,28},{28,24},{1,5},{5... | collective-permute-start | bytes 3538952 | tf_op jit(solution)/shard_map/ppermute | solution.py:383
  124.1 18.4 %collective-permute-start.25 = (bf16[96,6144]{1,0:T(8,128)(2,1)}, bf16[96,6144]{1,0:T(8,128)(2,1)S(1)}, u32[]{:S(2)}, u32[]{:S(2)}) collective-permute-start(bf16[96,6144]{1,0:T(8,128)(2,1)} %collective-permute-done.16.refs_2_), channel_id=1, source_target_pairs={{0,4},{4,0},{8,12},{12,8},{16,20},{20,16},{24,28},{28,24},{1,5},{5... | collective-permute-start | bytes 3538952 | tf_op jit(solution)/shard_map/ppermute | solution.py:383
  143.5 15.3 %collective-permute-start.26 = (bf16[96,6144]{1,0:T(8,128)(2,1)S(1)}, bf16[96,6144]{1,0:T(8,128)(2,1)S(1)}, u32[]{:S(2)}, u32[]{:S(2)}) collective-permute-start(bf16[96,6144]{1,0:T(8,128)(2,1)S(1)} %collective-permute-done.22.refs_3_), channel_id=1, source_target_pairs={{0,4},{4,0},{8,12},{12,8},{16,20},{20,16},{24,28},{28,24},{1,5},{5... | collective-permute-start | bytes 3538952 | tf_op jit(solution)/shard_map/ppermute | solution.py:383
  207.3 16.0 %collective-permute-start.27 = (bf16[3,768,1024]{2,1,0:T(8,128)(2,1)}, bf16[3,768,1024]{2,1,0:T(8,128)(2,1)S(1)}, u32[]{:S(2)}, u32[]{:S(2)}) collective-permute-start(bf16[3,768,1024]{2,1,0:T(8,128)(2,1)} %get-tuple-element.274), channel_id=1, source_target_pairs={{0,4},{4,0},{8,12},{12,8},{16,20},{20,16},{24,28},{28,24},{1,5},{5... | collective-permute-start | bytes 14155784 | tf_op jit(solution)/shard_map/ppermute | solution.py:383
  226.8 39.7 %collective-permute-start.28 = (bf16[3,2,192,1024]{3,2,1,0:T(8,128)(2,1)}, bf16[3,2,192,1024]{3,2,1,0:T(8,128)(2,1)}, u32[]{:S(2)}, u32[]{:S(2)}) collective-permute-start(bf16[3,2,192,1024]{3,2,1,0:T(8,128)(2,1)} %get-tuple-element.289), channel_id=1, source_target_pairs={{0,16},{4,12},{8,24},{12,4},{16,0},{20,28},{24,8},{28,20},{1,17},{... | collective-permute-start | bytes 7077896 | tf_op jit(solution)/shard_map/ppermute | solution.py:379
  249.5 139.7 %all-to-all-start.1 = ((bf16[4,256,768]{2,1,0:T(8,128)(2,1)}), bf16[4,256,768]{2,1,0:T(8,128)(2,1)}, u32[]{:S(2)}, u32[]{:S(2)}) async-start(bf16[4,256,768]{2,1,0:T(8,128)(2,1)} %bitcast.51), calls=%async_computation.1 | async-start | bytes 3145728 | tf_op jit(solution)/shard_map/all_to_all | solution.py:697
  272.1 16.3 %collective-permute-start.29 = (bf16[3,1,192,1024]{3,2,1,0:T(8,128)(2,1)S(1)}, bf16[3,1,192,1024]{3,2,1,0:T(8,128)(2,1)S(1)}, u32[]{:S(2)}, u32[]{:S(2)}) collective-permute-start(bf16[3,1,192,1024]{3,2,1,0:T(8,128)(2,1)S(1)} %get-tuple-element.296), channel_id=1, source_target_pairs={{0,8},{4,20},{8,0},{12,28},{16,24},{20,4},{24,16},{28,12},{1,9},{5... | collective-permute-start | bytes 3538952 | tf_op jit(solution)/shard_map/ppermute | solution.py:379
  283.6 22.3 %collective-permute-start.33 = (bf16[5,768,384]{2,1,0:T(8,128)(2,1)}, bf16[5,768,384]{2,1,0:T(8,128)(2,1)}, u32[]{:S(2)}, u32[]{:S(2)}) collective-permute-start(bf16[5,768,384]{2,1,0:T(8,128)(2,1)} %get-tuple-element.317), channel_id=1, source_target_pairs={{0,4},{4,0},{8,12},{12,8},{16,20},{20,16},{24,28},{28,24},{1,5},{5... | collective-permute-start | bytes 8847368 | tf_op jit(solution)/shard_map/ppermute | solution.py:383
  289.9 48.9 %collective-permute-start.30 = (bf16[3,2,1,24,1024]{4,3,2,1,0:T(8,128)(2,1)}, bf16[3,2,1,24,1024]{4,3,2,1,0:T(8,128)(2,1)}, u32[]{:S(2)}, u32[]{:S(2)}) collective-permute-start(bf16[3,2,1,24,1024]{4,3,2,1,0:T(8,128)(2,1)} %get-tuple-element.310), channel_id=1, source_target_pairs={{0,1},{1,2},{2,3},{3,0},{4,5},{5,6},{6,7},{7,4},{8,9},{9,10},{10,1... | collective-permute-start | bytes 884744 | tf_op jit(solution)/shard_map/ppermute | solution.py:387
  291.9 46.9 %collective-permute-start.31 = (bf16[3,2,1,24,1024]{4,3,2,1,0:T(8,128)(2,1)}, bf16[3,2,1,24,1024]{4,3,2,1,0:T(8,128)(2,1)}, u32[]{:S(2)}, u32[]{:S(2)}) collective-permute-start(bf16[3,2,1,24,1024]{4,3,2,1,0:T(8,128)(2,1)} %get-tuple-element.311), channel_id=1, source_target_pairs={{0,2},{1,3},{2,0},{3,1},{4,6},{5,7},{6,4},{7,5},{8,10},{9,11},{10,... | collective-permute-start | bytes 884744 | tf_op jit(solution)/shard_map/ppermute | solution.py:387
  294.3 44.6 %collective-permute-start.32 = (bf16[3,2,1,24,1024]{4,3,2,1,0:T(8,128)(2,1)}, bf16[3,2,1,24,1024]{4,3,2,1,0:T(8,128)(2,1)}, u32[]{:S(2)}, u32[]{:S(2)}) collective-permute-start(bf16[3,2,1,24,1024]{4,3,2,1,0:T(8,128)(2,1)} %get-tuple-element.312), channel_id=1, source_target_pairs={{0,3},{1,0},{2,1},{3,2},{4,7},{5,4},{6,5},{7,6},{8,11},{9,8},{10,9... | collective-permute-start | bytes 884744 | tf_op jit(solution)/shard_map/ppermute | solution.py:387
  313.3 19.7 %collective-permute-start.35 = (bf16[5,2,192,384]{3,2,1,0:T(8,128)(2,1)}, bf16[5,2,192,384]{3,2,1,0:T(8,128)(2,1)}, u32[]{:S(2)}, u32[]{:S(2)}) collective-permute-start(bf16[5,2,192,384]{3,2,1,0:T(8,128)(2,1)} %get-tuple-element.332), channel_id=1, source_target_pairs={{0,16},{4,12},{8,24},{12,4},{16,0},{20,28},{24,8},{28,20},{1,17},{... | collective-permute-start | bytes 4423688 | tf_op jit(solution)/shard_map/ppermute | solution.py:379
  329.1 8.5 %collective-permute-start.34 = (bf16[3,768,384]{2,1,0:T(8,128)(2,1)S(1)}, bf16[3,768,384]{2,1,0:T(8,128)(2,1)S(1)}, u32[]{:S(2)}, u32[]{:S(2)}) collective-permute-start(bf16[3,768,384]{2,1,0:T(8,128)(2,1)S(1)} %get-tuple-element.330), channel_id=1, source_target_pairs={{0,4},{4,0},{8,12},{12,8},{16,20},{20,16},{24,28},{28,24},{1,5},{5... | collective-permute-start | bytes 5308424 | tf_op jit(solution)/shard_map/ppermute | solution.py:383
  336.8 19.3 %collective-permute-start.38 = (bf16[5,1,192,384]{3,2,1,0:T(8,128)(2,1)S(1)}, bf16[5,1,192,384]{3,2,1,0:T(8,128)(2,1)S(1)}, u32[]{:S(2)}, u32[]{:S(2)}) collective-permute-start(bf16[5,1,192,384]{3,2,1,0:T(8,128)(2,1)S(1)} %get-tuple-element.357), channel_id=1, source_target_pairs={{0,8},{4,20},{8,0},{12,28},{16,24},{20,4},{24,16},{28,12},{1,9},{5... | collective-permute-start | bytes 2211848 | tf_op jit(solution)/shard_map/ppermute | solution.py:379
  338.8 15.8 %collective-permute-start.36 = (bf16[3,2,192,384]{3,2,1,0:T(8,128)(2,1)S(1)}, bf16[3,2,192,384]{3,2,1,0:T(8,128)(2,1)S(1)}, u32[]{:S(2)}, u32[]{:S(2)}) collective-permute-start(bf16[3,2,192,384]{3,2,1,0:T(8,128)(2,1)S(1)} %get-tuple-element.348), channel_id=1, source_target_pairs={{0,16},{4,12},{8,24},{12,4},{16,0},{20,28},{24,8},{28,20},{1,17},{... | collective-permute-start | bytes 2654216 | tf_op jit(solution)/shard_map/ppermute | solution.py:379
  355.5 8.4 %collective-permute-start.37 = (bf16[3,1,192,384]{3,2,1,0:T(8,128)(2,1)S(1)}, bf16[3,1,192,384]{3,2,1,0:T(8,128)(2,1)S(1)}, u32[]{:S(2)}, u32[]{:S(2)}) collective-permute-start(bf16[3,1,192,384]{3,2,1,0:T(8,128)(2,1)S(1)} %get-tuple-element.355), channel_id=1, source_target_pairs={{0,8},{4,20},{8,0},{12,28},{16,24},{20,4},{24,16},{28,12},{1,9},{5... | collective-permute-start | bytes 1327112 | tf_op jit(solution)/shard_map/ppermute | solution.py:379
  356.9 8.9 %collective-permute-start.42 = (bf16[5,2,1,24,384]{4,3,2,1,0:T(8,128)(2,1)S(1)}, bf16[5,2,1,24,384]{4,3,2,1,0:T(8,128)(2,1)S(1)}, u32[]{:S(2)}, u32[]{:S(2)}) collective-permute-start(bf16[5,2,1,24,384]{4,3,2,1,0:T(8,128)(2,1)S(1)} %get-tuple-element.377), channel_id=1, source_target_pairs={{0,1},{1,2},{2,3},{3,0},{4,5},{5,6},{6,7},{7,4},{8,9},{9,10},{10,1... | collective-permute-start | bytes 552968 | tf_op jit(solution)/shard_map/ppermute | solution.py:387
  357.5 16.2 %collective-permute-start.43 = (bf16[5,2,1,24,384]{4,3,2,1,0:T(8,128)(2,1)S(1)}, bf16[5,2,1,24,384]{4,3,2,1,0:T(8,128)(2,1)S(1)}, u32[]{:S(2)}, u32[]{:S(2)}) collective-permute-start(bf16[5,2,1,24,384]{4,3,2,1,0:T(8,128)(2,1)S(1)} %get-tuple-element.378), channel_id=1, source_target_pairs={{0,2},{1,3},{2,0},{3,1},{4,6},{5,7},{6,4},{7,5},{8,10},{9,11},{10,... | collective-permute-start | bytes 552968 | tf_op jit(solution)/shard_map/ppermute | solution.py:387
  358.0 15.7 %collective-permute-start.44 = (bf16[5,2,1,24,384]{4,3,2,1,0:T(8,128)(2,1)S(1)}, bf16[5,2,1,24,384]{4,3,2,1,0:T(8,128)(2,1)S(1)}, u32[]{:S(2)}, u32[]{:S(2)}) collective-permute-start(bf16[5,2,1,24,384]{4,3,2,1,0:T(8,128)(2,1)S(1)} %get-tuple-element.379), channel_id=1, source_target_pairs={{0,3},{1,0},{2,1},{3,2},{4,7},{5,4},{6,5},{7,6},{8,11},{9,8},{10,9... | collective-permute-start | bytes 552968 | tf_op jit(solution)/shard_map/ppermute | solution.py:387
  364.5 11.2 %collective-permute-start.39 = (bf16[3,2,1,24,384]{4,3,2,1,0:T(8,128)(2,1)S(1)}, bf16[3,2,1,24,384]{4,3,2,1,0:T(8,128)(2,1)S(1)}, u32[]{:S(2)}, u32[]{:S(2)}) collective-permute-start(bf16[3,2,1,24,384]{4,3,2,1,0:T(8,128)(2,1)S(1)} %get-tuple-element.373), channel_id=1, source_target_pairs={{0,1},{1,2},{2,3},{3,0},{4,5},{5,6},{6,7},{7,4},{8,9},{9,10},{10,1... | collective-permute-start | bytes 331784 | tf_op jit(solution)/shard_map/ppermute | solution.py:387
  365.3 19.2 %collective-permute-start.40 = (bf16[3,2,1,24,384]{4,3,2,1,0:T(8,128)(2,1)S(1)}, bf16[3,2,1,24,384]{4,3,2,1,0:T(8,128)(2,1)S(1)}, u32[]{:S(2)}, u32[]{:S(2)}) collective-permute-start(bf16[3,2,1,24,384]{4,3,2,1,0:T(8,128)(2,1)S(1)} %get-tuple-element.374), channel_id=1, source_target_pairs={{0,2},{1,3},{2,0},{3,1},{4,6},{5,7},{6,4},{7,5},{8,10},{9,11},{10,... | collective-permute-start | bytes 331784 | tf_op jit(solution)/shard_map/ppermute | solution.py:387
  365.7 18.7 %collective-permute-start.41 = (bf16[3,2,1,24,384]{4,3,2,1,0:T(8,128)(2,1)S(1)}, bf16[3,2,1,24,384]{4,3,2,1,0:T(8,128)(2,1)S(1)}, u32[]{:S(2)}, u32[]{:S(2)}) collective-permute-start(bf16[3,2,1,24,384]{4,3,2,1,0:T(8,128)(2,1)S(1)} %get-tuple-element.375), channel_id=1, source_target_pairs={{0,3},{1,0},{2,1},{3,2},{4,7},{5,4},{6,5},{7,6},{8,11},{9,8},{10,9... | collective-permute-start | bytes 331784 | tf_op jit(solution)/shard_map/ppermute | solution.py:387
  398.7 12.2 %collective-permute-start.51 = (f32[5,24,384]{2,1,0:T(8,128)S(1)}, f32[5,24,384]{2,1,0:T(8,128)S(1)}, u32[]{:S(2)}, u32[]{:S(2)}) collective-permute-start(f32[5,24,384]{2,1,0:T(8,128)S(1)} %dynamic-slice_bitcast_fusion.1), channel_id=1, source_target_pairs={{0,4},{4,0},{8,12},{12,8},{16,20},{20,16},{24,28},{28,24},{1,5},{5... | collective-permute-start | bytes 552968 | tf_op jit(solution)/shard_map/ppermute | solution.py:383
  401.4 9.5 %collective-permute-start.50 = (f32[3,24,384]{2,1,0:T(8,128)S(1)}, f32[3,24,384]{2,1,0:T(8,128)S(1)}, u32[]{:S(2)}, u32[]{:S(2)}) collective-permute-start(f32[3,24,384]{2,1,0:T(8,128)S(1)} %dynamic-slice_bitcast_fusion.2), channel_id=1, source_target_pairs={{0,4},{4,0},{8,12},{12,8},{16,20},{20,16},{24,28},{28,24},{1,5},{5... | collective-permute-start | bytes 331784 | tf_op jit(solution)/shard_map/ppermute | solution.py:383
  (92 other events, 929.9 us)

commit v4 on v3

--- a/solution.py
+++ b/solution.py
@@ -10,6 +10,7 @@
     return pl.CostEstimate(flops=int(us*1e+10),bytes_accessed=10**5,transcendentals=0)
 NEG=-1e30
 VA=16*2**20
+VB=60*2**20
 LOG2E=math.log2(math.e)
 TN=(((0,),(0,)),((),())); NN=(((1,),(0,)),((),())); NT=(((1,),(1,)),((),()))
 def dg(a,b,dims): return lax.dot_general(a,b,dims,preferred_element_type=f32)
@@ -64,7 +65,7 @@
     return pl.BlockSpec((hs*HD,w),lambda h:(h+offset//hs,0))
 def fwd_part_kernel(*refs,**kw):
     fwd_kernel(*refs[:4],*refs[6:],**kw)
-def attn_fwd(n,q,k,v,causal,bq=256,hs=2,part=None,into=None):
+def attn_fwd(n,q,k,v,causal,bq=256,hs=2,part=None,into=None,vmem=VA):
     L=q[0].shape[1]; K=k[0].shape[1]; D=HEADS*HD
     h0,hn=part or (0,HEADS)
     hb=lambda w,o=0: head_block(hs,w,o+h0)
@@ -78,7 +79,7 @@
       out_specs=[hb(L),pl.BlockSpec((hs,1,L),lambda h:(h+h0//hs,0,0))],
       out_shape=[jax.ShapeDtypeStruct((D,L),bf),jax.ShapeDtypeStruct((HEADS,1,L),f32)],
       input_output_aliases={} if into is None else {4:0,5:1},
-      cost_estimate=cost(0.3),compiler_params=pltpu.CompilerParams(vmem_limit_bytes=VA),
+      cost_estimate=cost(0.3),compiler_params=pltpu.CompilerParams(vmem_limit_bytes=vmem),
     )(*args)
 
 def bwd_kernel(len_ref,qT_ref,kT_ref,vT_ref,oT_ref,gT_ref,lse_ref,dq_ref,dk_ref,dv_ref,dka,dva,*,causal,bq,hs):
@@ -174,7 +175,7 @@
     return pl.pallas_call(memproj_kernel,grid=(F//fb,),
       in_specs=[full((L,D)),pl.BlockSpec((D,fb),lambda i:(0,first_col//fb+i))],
       out_specs=pl.BlockSpec((fb,L),lambda i:(i,0)),
-      out_shape=jax.ShapeDtypeStruct((F,L),bf),cost_estimate=cost(4),compiler_params=cp())(x,w)
+      out_shape=jax.ShapeDtypeStruct((F,L),bf),cost_estimate=cost(0.1),compiler_params=cp())(x,w)
 
 def post_self_kernel(x_ref,oT_ref,w3_ref,w4_ref,g_ref,h_ref,n_ref,cT_ref):
     h=x_ref[...].astype(f32)+dg(oT_ref[...],w3_ref[...],TT)
@@ -188,7 +189,7 @@
     return pl.pallas_call(post_self_kernel,grid=(L//tb,),
       in_specs=[tok,tokT,wcol(D,0),wcol(D,1),gain_spec(D)],
       out_specs=[tok,tok,tokT],
-      out_shape=[jax.ShapeDtypeStruct((L,D),f32),jax.ShapeDtypeStruct((L,D),bf),jax.ShapeDtypeStruct((D,L),bf)],cost_estimate=cost(6),compiler_params=cp())(x,oT,w,w,g)
+      out_shape=[jax.ShapeDtypeStruct((L,D),f32),jax.ShapeDtypeStruct((L,D),bf),jax.ShapeDtypeStruct((D,L),bf)],cost_estimate=cost(0.3),compiler_params=cp())(x,oT,w,w,g)
 
 def mlp_chunk(n3,gb,wg,wu,wd,dw_ref,inner_s,dgate_s,dup_s,oacc,nacc,tb):
     L=n3.shape[0]; nt=L//tb
@@ -404,7 +405,7 @@
     piece=pieces[0]
     shape=piece.shape if columns is None else (piece.shape[0],columns[1]-columns[0])
     return pl.pallas_call(functools.partial(copy_kernel,places=tuple(places),columns=columns),
-        in_specs=[pl.BlockSpec(memory_space=pltpu.SMEM)]+[pl.BlockSpec(memory_space=pltpu.HBM)]*len(pieces),
+        in_specs=[pl.BlockSpec(memory_space=pltpu.SMEM)]+[pl.BlockSpec(memory_space=pl.ANY)]*len(pieces),
         out_specs=pl.BlockSpec(memory_space=pltpu.VMEM),
         out_shape=jax.ShapeDtypeStruct((slots,)+shape,piece.dtype),
         scratch_shapes=[pltpu.SemaphoreType.DMA((len(pieces),))],
@@ -465,7 +466,7 @@
         M=self.here.M
         index=jnp.stack([(self.here.z-j)%M for j in range(M)]).astype(jnp.int32)
         rows=self.got[0].shape[0]
-        return place_rows(index,self.got,range(M),M,3,(first,end)).reshape(M*rows,end-first)
+        return place_rows(index,self.got,range(M),M,0.05,(first,end)).reshape(M*rows,end-first)
 
 
 class Gather:
@@ -668,11 +669,11 @@
     o1,lse1=attn_fwd(table_len,q,k,v,True,512,4,(0,8))
     o1=g2.arrived(o1)
     g2.forward(); g2.swap()
+    o1,slab_mlp=tie(o1,slab_mlp)
+    g3=Gather(slab_mlp,here)
     o1,lse1=attn_fwd(table_len,q,k,v,True,512,4,(8,4),(o1,lse1))
-    o1,slab_mlp=tie(o1,slab_mlp)
     o1=g2.arrived(o1)
     g2.swap_last()
-    g3=Gather(slab_mlp,here)
     w_second=g2.place()
     w_second,mem=tie(w_second,mem)
     mkv=mem_proj(mem,w_second,2*D)
@@ -682,10 +683,10 @@
     h1,n2,cq=post_self(x,o1,w_second,gains)
     q2,k2,v2=(cq,0),(mkv,0),(mkv,HEADS)
     half=HEADS//2
-    o2,lse2=attn_fwd(patch_count,q2,k2,v2,False,512,2,(0,half))
+    o2,lse2=attn_fwd(patch_count,q2,k2,v2,False,512,2,(0,half),None,VB)
     o2=g3.arrived(o2)
     g3.swap_last()
-    o2,lse2=attn_fwd(patch_count,q2,k2,v2,False,512,2,(half,half),(o2,lse2))
+    o2,lse2=attn_fwd(patch_count,q2,k2,v2,False,512,2,(half,half),(o2,lse2),VB)
     o2=g3.arrived(o2)
     w_mlp=g3.place()
     mixed_out,gh2,gm2,gb2,dg3,mlp_send,mlp_keep=mlp(core,table_len,h1,o2,w_second,cotangent[0],gains,w_mlp)
@@ -701,16 +702,15 @@
     second_send,gm1=tie(second_send,gm1)
     r2=Reduce(second_send,second_keep,here)
     gm1=r1.mem_start(gm1)
-    part=attn_bwd(table_len,q,k,v,o1,gm1,lse1,True,256,2,(0,half))
-    part=(r2.fold(part[0]),)+tuple(part[1:])
-    dq,dk,dv=attn_bwd(table_len,q,k,v,o1,gm1,lse1,True,256,2,(half,half),part)
+    gm1=r2.fold(gm1)
+    dq,dk,dv=attn_bwd(table_len,q,k,v,o1,gm1,lse1,True,256,2)
     first_send,first_keep=wgrads(core,[n1],[dq,dk,dv],[(0,0),(0,1),(0,2)])
     r3=Reduce(first_send,first_keep,here)
     dq,first_keep=tie(dq,first_keep)
     dq=r2.fold(dq)
     dq=r3.fold(dq)
-    t_mlp,dq=r1.mem_sum(dq)
     grad_tokens,dg1=first(x,gh1,dq,dk,dv,w_first,gains)
+    t_mlp,dg1=r1.mem_sum(dg1)
     dg1=r3.fold(dg1)
     dg1=r2.mem_start(dg1)
     dg1=r3.mem_start(dg1)

time: 418 us -> 407 us (0.974)
  waiting for transfers between devices: 80.9 us -> 74.3 us
    ppermute x15, waiting for transfers between devices: 33.9 us -> 29.6 us  [cross(): return lax.ppermute(x, SEQ, perm)]
    unnamed x177 -> x149, local copies, waits for them, and re-layouts: 31.2 us -> 28.4 us
    pallas_call x4 -> x3, Pallas kernels: 51.5 us -> 51 us  [attn_bwd(): pl.pallas_call(functools.partial(bwd_kernel if into is None else bwd_part...]
  transfers between devices with their start and end apart: 55 -> 55, of which waited for: 22 -> 20; matrix products, arithmetic and copies ran while one was open for 3% -> 3% of each run, Pallas kernels for 38% -> 38%
where the time goes in v4:
time: 407 us; the launch traced here: 403 us
  Pallas kernels  209 us (51%)
  waiting for transfers between devices  74.3 us (18%)
  starting transfers between devices  66.3 us (16%)
  local copies, waits for them, and re-layouts  29.2 us (7%)
  other arithmetic  15.9 us (4%)
  between operations  8.04 us (2%)
    pallas_call x3, Pallas kernels, attn_bwd(): pl.pallas_call(functools.partial(bwd_kernel if into is None else bwd_part...  51 us
    pallas_call x1, Pallas kernels, mlp(): pl.pallas_call(functools.partial(mlp_kernel, tb=tb), grid_spec=pltpu.Pref...  42.3 us
    ppermute x15, waiting for transfers between devices, shift_mem(): lax.ppermute(x, MEM, [(z, (z + step) % mem_size) for z in range(mem_size)])  33.9 us
    pallas_call x4, Pallas kernels, attn_fwd(): pl.pallas_call(functools.partial(fwd_kernel if into is None else fwd_part...  32.2 us
    ppermute x15, waiting for transfers between devices, cross(): return lax.ppermute(x, SEQ, perm)  29.6 us
    unnamed x149, local copies, waits for them, and re-layouts  28.4 us
    ppermute x15, starting transfers between devices, shift_mem(): lax.ppermute(x, MEM, [(z, (z + step) % mem_size) for z in range(mem_size)])  26.4 us
    ppermute x15, starting transfers between devices, cross(): return lax.ppermute(x, SEQ, perm)  21.6 us
  transfers between devices with their start and end apart: 55, of which 20 were waited for; matrix products, arithmetic and copies ran while one was open for 3% of the time, Pallas kernels for 38%

profile of v4, /device:TPU:0, one launch (start us, length us, event | category | flops | bytes accessed | tf_op | source)
XLA Modules:
  0.0 403.3 jit_solution(16272888679534845053)
XLA Ops:
  2.6 3.1 collective-permute-start
  5.7 2.6 collective-permute-start.1
  11.9 4.2 %collective-permute-done.1.refs_2_ = bf16[24,2432]{1,0:T(8,128)(2,1)S(1)} collective-permute-done((bf16[24,2432]{1,0:T(8,128)(2,1)S(1)}, bf16[24,2432]{1,0:T(8,128)(2,1)S(1)}, u32[]{:S(2)}, u32[]{:S(2)}) %collective-permute-start.1) | collective-permute-done | bytes 116768 | tf_op jit(solution)/shard_map/ppermute | solution.py:388
  18.8 3.0 collective-permute-start.4
  23.3 4.5 %collective-permute-done.3.refs_1_ = bf16[96,2432]{1,0:T(8,128)(2,1)S(1)} collective-permute-done((bf16[96,2432]{1,0:T(8,128)(2,1)S(1)}, bf16[96,2432]{1,0:T(8,128)(2,1)S(1)}, u32[]{:S(2)}, u32[]{:S(2)}) %collective-permute-start.3) | collective-permute-done | bytes 466976 | tf_op jit(solution)/shard_map/ppermute | solution.py:380
  27.8 2.7 collective-permute-start.6
  30.4 2.7 collective-permute-done.4.refs_1_
  38.1 8.3 %collective-permute-done.7.refs_2_ = bf16[24,9984]{1,0:T(8,128)(2,1)S(1)} collective-permute-done((bf16[24,9984]{1,0:T(8,128)(2,1)S(1)}, bf16[24,9984]{1,0:T(8,128)(2,1)S(1)}, u32[]{:S(2)}, u32[]{:S(2)}) %collective-permute-start.7) | collective-permute-done | bytes 479264 | tf_op jit(solution)/shard_map/ppermute | solution.py:388
  46.8 3.2 shard_map.238
  50.1 6.3 %shard_map.239 = (bf16[1024,768]{1,0:T(8,128)(2,1)S(1)}, bf16[2304,1024]{1,0:T(8,128)(2,1)S(1)}, f32[8,768]{1,0:T(8,128)S(1)}) custom-call(bf16[1024,768]{1,0:T(8,128)(2,1)S(1)} %bitcast.129, bf16[768,2432]{1,0:T(8,128)(2,1)S(1)} %bitcast.124, bf16[768,2432]{1,0:T(8,128)(2,1)S(1)} %bitcast.125), custom_call_target="tpu_custom_call" | custom-call | flops 60000002048 | bytes 100000 | tf_op jit(solution)/shard_map/pallas_call | solution.py:167
  60.5 3.8 collective-permute-start.13
  64.3 3.9 all-to-all-start
  71.3 7.0 %shard_map.241 = (bf16[768,1024]{1,0:T(8,128)(2,1)S(1)}, f32[12,1,1024]{2,1,0:T(1,128)S(1)}) custom-call(s32[1]{0:T(128)S(6)} %copy.49.len_ref.refs_0_, bf16[2304,1024]{1,0:T(8,128)(2,1)S(1)} %copy-done.4, bf16[2304,1024]{1,0:T(8,128)(2,1)S(1)} %copy-done.4, bf16[2304,1024]{1,0:T(8,128)(2,1)S(1)} %copy-done.4), custom_call_target="tpu_custom_call" | custom-call | flops 3000000000 | bytes 100000 | tf_op jit(solution)/shard_map/pallas_call | solution.py:77
  83.9 12.7 %collective-permute-done.17.refs_3_ = bf16[96,3840]{1,0:T(8,128)(2,1)S(1)} collective-permute-done((bf16[96,3840]{1,0:T(8,128)(2,1)}, bf16[96,3840]{1,0:T(8,128)(2,1)S(1)}, u32[]{:S(2)}, u32[]{:S(2)}) %collective-permute-start.17) | collective-permute-done | bytes 737312 | tf_op jit(solution)/shard_map/ppermute | solution.py:380
  96.6 2.4 collective-permute-start.16
  99.0 3.5 shard_map.243
  108.8 2.5 copy-done
  111.3 2.7 copy-done.1
  114.0 3.6 shard_map.245.kT_ref.vT_ref.refs_2_.refs_3_
  122.5 5.7 %shard_map.246 = (f32[1024,768]{1,0:T(8,128)S(1)}, bf16[1024,768]{1,0:T(8,128)(2,1)S(1)}, bf16[768,1024]{1,0:T(8,128)(2,1)S(1)}) custom-call(bf16[1024,768]{1,0:T(8,128)(2,1)S(1)} %bitcast.130, bf16[768,1024]{1,0:T(8,128)(2,1)S(1)} %copy-done.8, bf16[768,3840]{1,0:T(8,128)(2,1)S(1)} %bitcast.102, bf16[768,3840]{1,0:T(8,128)(2,1)S(1)} %bitcast.103, ...), custom_call_target="tpu_custom_call" | custom-call | flops 3000000000 | bytes 100000 | tf_op jit(solution)/shard_map/pallas_call | solution.py:189
  132.1 11.0 %shard_map.247 = (bf16[768,1024]{1,0:T(8,128)(2,1)}, f32[12,1,1024]{2,1,0:T(1,128)}) custom-call(s32[1]{0:T(128)S(6)} %copy.50.len_ref.refs_0_, bf16[768,1024]{1,0:T(8,128)(2,1)} %copy-done.38, bf16[1536,1024]{1,0:T(8,128)(2,1)} %copy-done.13, bf16[1536,1024]{1,0:T(8,128)(2,1)} %copy-done.13), custom_call_target="tpu_custom_call" | custom-call | flops 3000000000 | bytes 100000 | tf_op jit(solution)/shard_map/pallas_call | solution.py:77
  143.4 10.6 %shard_map.248 = (bf16[768,1024]{1,0:T(8,128)(2,1)}, f32[12,1,1024]{2,1,0:T(1,128)}) custom-call(s32[1]{0:T(128)S(6)} %copy.50.len_ref.refs_0_, bf16[768,1024]{1,0:T(8,128)(2,1)} %copy-done.38, bf16[1536,1024]{1,0:T(8,128)(2,1)} %copy-done.13, bf16[1536,1024]{1,0:T(8,128)(2,1)} %copy-done.13, ...), custom_call_target="tpu_custom_call", output_to_operand_aliasing={{0}: (4, {}), {1}: (5, {})} | custom-call | flops 3000000000 | bytes 100000 | tf_op jit(solution)/shard_map/pallas_call | solution.py:77
  154.0 4.2 %shard_map.249 = bf16[8,96,6144]{2,1,0:T(8,128)(2,1)S(1)} custom-call(s32[8]{0:T(128)S(1)} %stack.59.index_ref, bf16[96,6144]{1,0:T(8,128)(2,1)S(1)} %bitcast.123, bf16[96,6144]{1,0:T(8,128)(2,1)} %collective-permute-done.15.refs_1_, bf16[96,6144]{1,0:T(8,128)(2,1)} %collective-permute-done.16.refs_2_, bf16[96,6144]{1,0:T(8,128)(2,1)} %collective-permute-done.22.refs_3_, ...), custom_call_target="tpu_custom_call" | custom-call | flops 500000000 | bytes 100000 | tf_op jit(solution)/shard_map/pallas_call | solution.py:407
  158.3 3.7 copy-done.5
  161.9 42.3 %shard_map.250 = (bf16[1024,768]{1,0:T(8,128)(2,1)}, f32[1024,768]{1,0:T(8,128)}, bf16[768,1024]{1,0:T(8,128)(2,1)S(1)}, bf16[1024,768]{1,0:T(8,128)(2,1)S(1)}, ...) custom-call(s32[1]{0:T(128)} %bitcast.core_ref, s32[1]{0:T(128)S(6)} %copy.49.len_ref.refs_0_, ...), custom_call_target="tpu_custom_call" | custom-call | flops 420000006144 | bytes 100000 | tf_op jit(solution)/shard_map/pallas_call | solution.py:275
  208.7 15.8 %shard_map.251 = (bf16[768,1024]{1,0:T(8,128)(2,1)S(1)}, bf16[768,1024]{1,0:T(8,128)(2,1)S(1)}, bf16[768,1024]{1,0:T(8,128)(2,1)S(1)}) custom-call(s32[1]{0:T(128)S(6)} %copy.50.len_ref.refs_0_, bf16[768,1024]{1,0:T(8,128)(2,1)S(1)} %copy-done.39, bf16[1536,1024]{1,0:T(8,128)(2,1)S(1)} %copy-done.14, bf16[1536,1024]{1,0:T(8,128)(2,1)S(1)} %copy-done.14, ...), custom_call_target="tpu_custom_call" | custom-call | flops 140000002048 | bytes 100000 | tf_op jit(solution)/shard_map/pallas_call | solution.py:137
  224.6 3.4 shard_map.252
  228.5 15.6 %shard_map.253 = (bf16[768,1024]{1,0:T(8,128)(2,1)S(1)}, bf16[768,1024]{1,0:T(8,128)(2,1)S(1)}, bf16[768,1024]{1,0:T(8,128)(2,1)S(1)}) custom-call(s32[1]{0:T(128)S(6)} %copy.50.len_ref.refs_0_, bf16[768,1024]{1,0:T(8,128)(2,1)S(1)} %copy-done.39, bf16[1536,1024]{1,0:T(8,128)(2,1)S(1)} %copy-done.14, ...), custom_call_target="tpu_custom_call", output_to_operand_aliasing={{0}: (7, {}), {1}: (8, {}), {2}: (9, {})} | custom-call | flops 140000002048 | bytes 100000 | tf_op jit(solution)/shard_map/pallas_call | solution.py:137
  244.2 3.9 shard_map.254
  249.3 6.0 %shard_map.255 = (f32[1024,768]{1,0:T(8,128)S(1)}, bf16[768,1024]{1,0:T(8,128)(2,1)S(1)}, bf16[1024,768]{1,0:T(8,128)(2,1)S(1)}, f32[1,768]{1,0:T(1,128)S(1)}) custom-call(f32[1024,768]{1,0:T(8,128)S(1)} %copy-done.16, f32[1024,768]{1,0:T(8,128)S(1)} %copy-done.17, bf16[768,1024]{1,0:T(8,128)(2,1)S(1)} %get-tuple-element.283.dcT_ref.refs_5_, ...), custom_call_target="tpu_custom_call" | custom-call | flops 2000000000 | bytes 100000 | tf_op jit(solution)/shard_map/pallas_call | solution.py:303
  257.2 4.8 %shard_map.256 = (bf16[3,1,192,1024]{3,2,1,0:T(8,128)(2,1)}, bf16[3,1,192,1024]{3,2,1,0:T(8,128)(2,1)S(1)}) custom-call(s32[2]{0:T(128)S(1)} %iota.9.index_ref, bf16[3,2,192,1024]{3,2,1,0:T(8,128)(2,1)S(1)} %get-tuple-element.286.ka.kb, bf16[3,2,192,1024]{3,2,1,0:T(8,128)(2,1)S(1)} %get-tuple-element.286.ka.kb, ...), custom_call_target="tpu_custom_call" | custom-call | flops 30000001024 | bytes 100000 | tf_op jit(solution)/shard_map/pallas_call | solution.py:523
  264.1 10.7 %shard_map.257 = (bf16[5,768,384]{2,1,0:T(8,128)(2,1)}, bf16[5,768,384]{2,1,0:T(8,128)(2,1)}) custom-call(s32[1]{0:T(128)} %bitcast.core_ref, bf16[1024,768]{1,0:T(8,128)(2,1)S(1)} %get-tuple-element.293.refs_0_, bf16[1024,768]{1,0:T(8,128)(2,1)S(1)} %copy-done.37, bf16[1024,768]{1,0:T(8,128)(2,1)S(1)} %bitcast.118, bf16[1024,768]{1,0:T(8,128)(2,1)S(1)} %copy-done.53, ...), custom_call_target="tpu_custom_call" | custom-call | flops 80000000000 | bytes 100000 | tf_op jit(solution)/shard_map/pallas_call | solution.py:320
  274.8 4.3 %all-to-all-start.1 = ((bf16[4,256,768]{2,1,0:T(8,128)(2,1)}), bf16[4,256,768]{2,1,0:T(8,128)(2,1)}, u32[]{:S(2)}, u32[]{:S(2)}) async-start(bf16[4,256,768]{2,1,0:T(8,128)(2,1)} %bitcast.119), calls=%async_computation.1 | async-start | bytes 3145728 | tf_op jit(solution)/shard_map/all_to_all | solution.py:698
  280.4 2.5 shard_map.258
  288.7 4.4 %shard_map.259 = (bf16[5,2,192,384]{3,2,1,0:T(8,128)(2,1)}, bf16[5,2,192,384]{3,2,1,0:T(8,128)(2,1)S(1)}) custom-call(s32[4]{0:T(128)S(1)} %copy-done.32, bf16[5,4,192,384]{3,2,1,0:T(8,128)(2,1)S(1)} %bitcast.146, bf16[5,4,192,384]{3,2,1,0:T(8,128)(2,1)S(1)} %bitcast.147, bf16[5,4,192,384]{3,2,1,0:T(8,128)(2,1)S(1)} %bitcast.138, ...), custom_call_target="tpu_custom_call" | custom-call | flops 30000001024 | bytes 100000 | tf_op jit(solution)/shard_map/pallas_call | solution.py:523
  293.8 19.6 %shard_map.260 = (bf16[768,1024]{1,0:T(8,128)(2,1)S(1)}, bf16[768,1024]{1,0:T(8,128)(2,1)S(1)}, bf16[768,1024]{1,0:T(8,128)(2,1)S(1)}) custom-call(s32[1]{0:T(128)S(6)} %copy.49.len_ref.refs_0_, bf16[2304,1024]{1,0:T(8,128)(2,1)S(1)} %bitcast.113, bf16[2304,1024]{1,0:T(8,128)(2,1)S(1)} %bitcast.113, bf16[2304,1024]{1,0:T(8,128)(2,1)S(1)} %bitcast.113, ...), custom_call_target="tpu_custom_call" | custom-call | flops 140000002048 | bytes 100000 | tf_op jit(solution)/shard_map/pallas_call | solution.py:137
  313.4 5.1 %shard_map.261 = (bf16[3,768,384]{2,1,0:T(8,128)(2,1)S(1)}, bf16[3,768,384]{2,1,0:T(8,128)(2,1)S(1)}) custom-call(s32[1]{0:T(128)} %bitcast.core_ref, bf16[1024,768]{1,0:T(8,128)(2,1)S(1)} %copy-done.51, bf16[768,1024]{1,0:T(8,128)(2,1)S(1)} %get-tuple-element.333.refs_1_.qT_ref, bf16[768,1024]{1,0:T(8,128)(2,1)S(1)} %get-tuple-element.317.refs_2_.kT_ref, ...), custom_call_target="tpu_custom_call" | custom-call | flops 80000000000 | bytes 100000 | tf_op jit(solution)/shard_map/pallas_call | solution.py:320
  318.6 3.8 shard_map.262
  326.8 7.2 %shard_map.264 = (f32[1024,768]{1,0:T(8,128)}, f32[1,768]{1,0:T(1,128)S(1)}) custom-call(bf16[1024,768]{1,0:T(8,128)(2,1)S(1)} %bitcast.131, f32[1024,768]{1,0:T(8,128)S(1)} %copy-done.35, bf16[768,1024]{1,0:T(8,128)(2,1)S(1)} %get-tuple-element.333.refs_1_.qT_ref, bf16[768,1024]{1,0:T(8,128)(2,1)S(1)} %get-tuple-element.317.refs_2_.kT_ref, ...), custom_call_target="tpu_custom_call" | custom-call | flops 70000001024 | bytes 100000 | tf_op jit(solution)/shard_map/pallas_call | solution.py:350
  334.0 2.4 collective-permute-done.35
  338.4 4.6 %collective-permute-done.33.ra.rb = bf16[3,2,192,384]{3,2,1,0:T(8,128)(2,1)S(1)} collective-permute-done((bf16[3,2,192,384]{3,2,1,0:T(8,128)(2,1)S(1)}, bf16[3,2,192,384]{3,2,1,0:T(8,128)(2,1)S(1)}, u32[]{:S(2)}, u32[]{:S(2)}) %collective-permute-start.33) | collective-permute-done | bytes 884768 | tf_op jit(solution)/shard_map/ppermute | solution.py:380
  349.4 2.8 collective-permute-done.37
  357.6 9.7 %collective-permute-done.43 = bf16[5,2,1,24,384]{4,3,2,1,0:T(8,128)(2,1)S(1)} collective-permute-done((bf16[5,2,1,24,384]{4,3,2,1,0:T(8,128)(2,1)S(1)}, bf16[5,2,1,24,384]{4,3,2,1,0:T(8,128)(2,1)S(1)}, u32[]{:S(2)}, u32[]{:S(2)}) %collective-permute-start.43) | collective-permute-done | bytes 184352 | tf_op jit(solution)/shard_map/ppermute | solution.py:388
  369.3 4.4 %collective-permute-done.40 = bf16[3,2,1,24,384]{4,3,2,1,0:T(8,128)(2,1)S(1)} collective-permute-done((bf16[3,2,1,24,384]{4,3,2,1,0:T(8,128)(2,1)S(1)}, bf16[3,2,1,24,384]{4,3,2,1,0:T(8,128)(2,1)S(1)}, u32[]{:S(2)}, u32[]{:S(2)}) %collective-permute-start.40) | collective-permute-done | bytes 110624 | tf_op jit(solution)/shard_map/ppermute | solution.py:388
  377.0 3.3 convert_element_type.50
  381.3 2.9 collective-permute-done.47
  389.2 3.5 collective-permute-done.49
  395.9 2.6 multiply_subtract_fusion
  (280 shorter events, 91.8 us)
Async XLA Ops:
  2.6 9.2 %collective-permute-start = (bf16[24,2432]{1,0:T(8,128)(2,1)S(1)}, bf16[24,2432]{1,0:T(8,128)(2,1)S(1)}, u32[]{:S(2)}, u32[]{:S(2)}) collective-permute-start(bf16[24,2432]{1,0:T(8,128)(2,1)S(1)} %fusion.3.refs_0_), channel_id=1, source_target_pairs={{0,1},{1,2},{2,3},{3,0},{4,5},{5,6},{6,7},{7,4},{8,9},{9,10},{10,1... | collective-permute-start | bytes 350216 | tf_op jit(solution)/shard_map/ppermute | solution.py:388
  5.7 10.3 %collective-permute-start.1 = (bf16[24,2432]{1,0:T(8,128)(2,1)S(1)}, bf16[24,2432]{1,0:T(8,128)(2,1)S(1)}, u32[]{:S(2)}, u32[]{:S(2)}) collective-permute-start(bf16[24,2432]{1,0:T(8,128)(2,1)S(1)} %fusion.3.refs_0_), channel_id=1, source_target_pairs={{0,2},{1,3},{2,0},{3,1},{4,6},{5,7},{6,4},{7,5},{8,10},{9,11},{10,... | collective-permute-start | bytes 350216 | tf_op jit(solution)/shard_map/ppermute | solution.py:388
  8.3 7.7 %collective-permute-start.2 = (bf16[24,2432]{1,0:T(8,128)(2,1)S(1)}, bf16[24,2432]{1,0:T(8,128)(2,1)S(1)}, u32[]{:S(2)}, u32[]{:S(2)}) collective-permute-start(bf16[24,2432]{1,0:T(8,128)(2,1)S(1)} %fusion.3.refs_0_), channel_id=1, source_target_pairs={{0,3},{1,0},{2,1},{3,2},{4,7},{5,4},{6,5},{7,6},{8,11},{9,8},{10,9... | collective-permute-start | bytes 350216 | tf_op jit(solution)/shard_map/ppermute | solution.py:388
  17.2 10.5 %collective-permute-start.3 = (bf16[96,2432]{1,0:T(8,128)(2,1)S(1)}, bf16[96,2432]{1,0:T(8,128)(2,1)S(1)}, u32[]{:S(2)}, u32[]{:S(2)}) collective-permute-start(bf16[96,2432]{1,0:T(8,128)(2,1)S(1)} %bitcast.132), channel_id=1, source_target_pairs={{0,8},{4,20},{8,0},{12,28},{16,24},{20,4},{24,16},{28,12},{1,9},{5... | collective-permute-start | bytes 1400840 | tf_op jit(solution)/shard_map/ppermute | solution.py:380
  18.8 14.3 %collective-permute-start.4 = (bf16[24,9984]{1,0:T(8,128)(2,1)S(1)}, bf16[24,9984]{1,0:T(8,128)(2,1)S(1)}, u32[]{:S(2)}, u32[]{:S(2)}) collective-permute-start(bf16[24,9984]{1,0:T(8,128)(2,1)S(1)} %fusion.4.refs_0_), channel_id=1, source_target_pairs={{0,1},{1,2},{2,3},{3,0},{4,5},{5,6},{6,7},{7,4},{8,9},{9,10},{10,1... | collective-permute-start | bytes 1437704 | tf_op jit(solution)/shard_map/ppermute | solution.py:388
  21.8 8.6 %collective-permute-start.5 = (bf16[96,2432]{1,0:T(8,128)(2,1)S(1)}, bf16[96,2432]{1,0:T(8,128)(2,1)S(1)}, u32[]{:S(2)}, u32[]{:S(2)}) collective-permute-start(bf16[96,2432]{1,0:T(8,128)(2,1)S(1)} %bitcast.133), channel_id=1, source_target_pairs={{0,16},{4,12},{8,24},{12,4},{16,0},{20,28},{24,8},{28,20},{1,17},{... | collective-permute-start | bytes 1400840 | tf_op jit(solution)/shard_map/ppermute | solution.py:380
  27.8 9.2 %collective-permute-start.6 = (bf16[96,2432]{1,0:T(8,128)(2,1)S(1)}, bf16[96,2432]{1,0:T(8,128)(2,1)S(1)}, u32[]{:S(2)}, u32[]{:S(2)}) collective-permute-start(bf16[96,2432]{1,0:T(8,128)(2,1)S(1)} %collective-permute-done.3.refs_1_), channel_id=1, source_target_pairs={{0,16},{4,12},{8,24},{12,4},{16,0},{20,28},{24,8},{28,20},{1,17},{... | collective-permute-start | bytes 1400840 | tf_op jit(solution)/shard_map/ppermute | solution.py:380
  33.2 13.2 %collective-permute-start.7 = (bf16[24,9984]{1,0:T(8,128)(2,1)S(1)}, bf16[24,9984]{1,0:T(8,128)(2,1)S(1)}, u32[]{:S(2)}, u32[]{:S(2)}) collective-permute-start(bf16[24,9984]{1,0:T(8,128)(2,1)S(1)} %collective-permute-done.4.refs_1_), channel_id=1, source_target_pairs={{0,1},{1,2},{2,3},{3,0},{4,5},{5,6},{6,7},{7,4},{8,9},{9,10},{10,1... | collective-permute-start | bytes 1437704 | tf_op jit(solution)/shard_map/ppermute | solution.py:388
  37.0 9.4 %collective-permute-start.8 = (bf16[96,2432]{1,0:T(8,128)(2,1)S(1)}, bf16[96,2432]{1,0:T(8,128)(2,1)}, u32[]{:S(2)}, u32[]{:S(2)}) collective-permute-start(bf16[96,2432]{1,0:T(8,128)(2,1)S(1)} %collective-permute-done.6.refs_3_), channel_id=1, source_target_pairs={{0,4},{4,0},{8,12},{12,8},{16,20},{20,16},{24,28},{28,24},{1,5},{5... | collective-permute-start | bytes 1400840 | tf_op jit(solution)/shard_map/ppermute | solution.py:384
  37.0 9.8 %collective-permute-start.10 = (bf16[96,2432]{1,0:T(8,128)(2,1)S(1)}, bf16[96,2432]{1,0:T(8,128)(2,1)}, u32[]{:S(2)}, u32[]{:S(2)}) collective-permute-start(bf16[96,2432]{1,0:T(8,128)(2,1)S(1)} %bitcast.134), channel_id=1, source_target_pairs={{0,4},{4,0},{8,12},{12,8},{16,20},{20,16},{24,28},{28,24},{1,5},{5... | collective-permute-start | bytes 1400840 | tf_op jit(solution)/shard_map/ppermute | solution.py:384
  37.5 9.3 %collective-permute-start.11 = (bf16[96,2432]{1,0:T(8,128)(2,1)S(1)}, bf16[96,2432]{1,0:T(8,128)(2,1)}, u32[]{:S(2)}, u32[]{:S(2)}) collective-permute-start(bf16[96,2432]{1,0:T(8,128)(2,1)S(1)} %collective-permute-done.3.refs_1_), channel_id=1, source_target_pairs={{0,4},{4,0},{8,12},{12,8},{16,20},{20,16},{24,28},{28,24},{1,5},{5... | collective-permute-start | bytes 1400840 | tf_op jit(solution)/shard_map/ppermute | solution.py:384
  37.5 9.3 %collective-permute-start.12 = (bf16[96,2432]{1,0:T(8,128)(2,1)S(1)}, bf16[96,2432]{1,0:T(8,128)(2,1)}, u32[]{:S(2)}, u32[]{:S(2)}) collective-permute-start(bf16[96,2432]{1,0:T(8,128)(2,1)S(1)} %collective-permute-done.5.refs_2_), channel_id=1, source_target_pairs={{0,4},{4,0},{8,12},{12,8},{16,20},{20,16},{24,28},{28,24},{1,5},{5... | collective-permute-start | bytes 1400840 | tf_op jit(solution)/shard_map/ppermute | solution.py:384
  46.4 12.3 %collective-permute-start.9 = (bf16[24,9984]{1,0:T(8,128)(2,1)S(1)}, bf16[24,9984]{1,0:T(8,128)(2,1)S(1)}, u32[]{:S(2)}, u32[]{:S(2)}) collective-permute-start(bf16[24,9984]{1,0:T(8,128)(2,1)S(1)} %collective-permute-done.7.refs_2_), channel_id=1, source_target_pairs={{0,1},{1,2},{2,3},{3,0},{4,5},{5,6},{6,7},{7,4},{8,9},{9,10},{10,1... | collective-permute-start | bytes 1437704 | tf_op jit(solution)/shard_map/ppermute | solution.py:388
  60.5 18.7 %collective-permute-start.13 = (bf16[96,3840]{1,0:T(8,128)(2,1)}, bf16[96,3840]{1,0:T(8,128)(2,1)}, u32[]{:S(2)}, u32[]{:S(2)}) collective-permute-start(bf16[96,3840]{1,0:T(8,128)(2,1)} %bitcast.28.refs_0_), channel_id=1, source_target_pairs={{0,8},{4,20},{8,0},{12,28},{16,24},{20,4},{24,16},{28,12},{1,9},{5... | collective-permute-start | bytes 2211848 | tf_op jit(solution)/shard_map/ppermute | solution.py:380
  64.3 14.9 %collective-permute-start.14 = (bf16[96,3840]{1,0:T(8,128)(2,1)}, bf16[96,3840]{1,0:T(8,128)(2,1)}, u32[]{:S(2)}, u32[]{:S(2)}) collective-permute-start(bf16[96,3840]{1,0:T(8,128)(2,1)} %bitcast.28.refs_0_), channel_id=1, source_target_pairs={{0,16},{4,12},{8,24},{12,4},{16,0},{20,28},{24,8},{28,20},{1,17},{... | collective-permute-start | bytes 2211848 | tf_op jit(solution)/shard_map/ppermute | solution.py:380
  64.3 47.0 %all-to-all-start = ((bf16[4,256,768]{2,1,0:T(8,128)(2,1)}), bf16[4,256,768]{2,1,0:T(8,128)(2,1)S(1)}, u32[]{:S(2)}, u32[]{:S(2)}) async-start(bf16[4,256,768]{2,1,0:T(8,128)(2,1)} %param.15), calls=%async_computation | async-start | bytes 3145728 | tf_op jit(solution)/shard_map/all_to_all | solution.py:662
  79.2 17.4 %collective-permute-start.17 = (bf16[96,3840]{1,0:T(8,128)(2,1)}, bf16[96,3840]{1,0:T(8,128)(2,1)S(1)}, u32[]{:S(2)}, u32[]{:S(2)}) collective-permute-start(bf16[96,3840]{1,0:T(8,128)(2,1)} %collective-permute-done.13.refs_1_), channel_id=1, source_target_pairs={{0,16},{4,12},{8,24},{12,4},{16,0},{20,28},{24,8},{28,20},{1,17},{... | collective-permute-start | bytes 2211848 | tf_op jit(solution)/shard_map/ppermute | solution.py:380
  80.9 23.4 %collective-permute-start.19 = (bf16[96,3840]{1,0:T(8,128)(2,1)}, bf16[96,3840]{1,0:T(8,128)(2,1)S(1)}, u32[]{:S(2)}, u32[]{:S(2)}) collective-permute-start(bf16[96,3840]{1,0:T(8,128)(2,1)} %collective-permute-done.13.refs_1_), channel_id=1, source_target_pairs={{0,4},{4,0},{8,12},{12,8},{16,20},{20,16},{24,28},{28,24},{1,5},{5... | collective-permute-start | bytes 2211848 | tf_op jit(solution)/shard_map/ppermute | solution.py:384
  80.9 23.4 %collective-permute-start.18 = (bf16[96,3840]{1,0:T(8,128)(2,1)}, bf16[96,3840]{1,0:T(8,128)(2,1)S(1)}, u32[]{:S(2)}, u32[]{:S(2)}) collective-permute-start(bf16[96,3840]{1,0:T(8,128)(2,1)} %bitcast.28.refs_0_), channel_id=1, source_target_pairs={{0,4},{4,0},{8,12},{12,8},{16,20},{20,16},{24,28},{28,24},{1,5},{5... | collective-permute-start | bytes 2211848 | tf_op jit(solution)/shard_map/ppermute | solution.py:384
  81.4 22.9 %collective-permute-start.20 = (bf16[96,3840]{1,0:T(8,128)(2,1)}, bf16[96,3840]{1,0:T(8,128)(2,1)S(1)}, u32[]{:S(2)}, u32[]{:S(2)}) collective-permute-start(bf16[96,3840]{1,0:T(8,128)(2,1)} %collective-permute-done.14.refs_2_), channel_id=1, source_target_pairs={{0,4},{4,0},{8,12},{12,8},{16,20},{20,16},{24,28},{28,24},{1,5},{5... | collective-permute-start | bytes 2211848 | tf_op jit(solution)/shard_map/ppermute | solution.py:384
  82.1 37.1 %collective-permute-start.15 = (bf16[96,6144]{1,0:T(8,128)(2,1)S(1)}, bf16[96,6144]{1,0:T(8,128)(2,1)}, u32[]{:S(2)}, u32[]{:S(2)}) collective-permute-start(bf16[96,6144]{1,0:T(8,128)(2,1)S(1)} %bitcast.120), channel_id=1, source_target_pairs={{0,8},{4,20},{8,0},{12,28},{16,24},{20,4},{24,16},{28,12},{1,9},{5... | collective-permute-start | bytes 3538952 | tf_op jit(solution)/shard_map/ppermute | solution.py:380
  96.6 22.6 %collective-permute-start.16 = (bf16[96,6144]{1,0:T(8,128)(2,1)S(1)}, bf16[96,6144]{1,0:T(8,128)(2,1)}, u32[]{:S(2)}, u32[]{:S(2)}) collective-permute-start(bf16[96,6144]{1,0:T(8,128)(2,1)S(1)} %bitcast.121), channel_id=1, source_target_pairs={{0,16},{4,12},{8,24},{12,4},{16,0},{20,28},{24,8},{28,20},{1,17},{... | collective-permute-start | bytes 3538952 | tf_op jit(solution)/shard_map/ppermute | solution.py:380
  119.2 23.9 %collective-permute-start.22 = (bf16[96,6144]{1,0:T(8,128)(2,1)}, bf16[96,6144]{1,0:T(8,128)(2,1)}, u32[]{:S(2)}, u32[]{:S(2)}) collective-permute-start(bf16[96,6144]{1,0:T(8,128)(2,1)} %collective-permute-done.15.refs_1_), channel_id=1, source_target_pairs={{0,16},{4,12},{8,24},{12,4},{16,0},{20,28},{24,8},{28,20},{1,17},{... | collective-permute-start | bytes 3538952 | tf_op jit(solution)/shard_map/ppermute | solution.py:380
  119.2 23.9 %collective-permute-start.24 = (bf16[96,6144]{1,0:T(8,128)(2,1)}, bf16[96,6144]{1,0:T(8,128)(2,1)}, u32[]{:S(2)}, u32[]{:S(2)}) collective-permute-start(bf16[96,6144]{1,0:T(8,128)(2,1)} %collective-permute-done.15.refs_1_), channel_id=1, source_target_pairs={{0,4},{4,0},{8,12},{12,8},{16,20},{20,16},{24,28},{28,24},{1,5},{5... | collective-permute-start | bytes 3538952 | tf_op jit(solution)/shard_map/ppermute | solution.py:384
  121.3 21.9 %collective-permute-start.23 = (bf16[96,6144]{1,0:T(8,128)(2,1)S(1)}, bf16[96,6144]{1,0:T(8,128)(2,1)}, u32[]{:S(2)}, u32[]{:S(2)}) collective-permute-start(bf16[96,6144]{1,0:T(8,128)(2,1)S(1)} %bitcast.122), channel_id=1, source_target_pairs={{0,4},{4,0},{8,12},{12,8},{16,20},{20,16},{24,28},{28,24},{1,5},{5... | collective-permute-start | bytes 3538952 | tf_op jit(solution)/shard_map/ppermute | solution.py:384
  121.3 21.9 %collective-permute-start.25 = (bf16[96,6144]{1,0:T(8,128)(2,1)}, bf16[96,6144]{1,0:T(8,128)(2,1)}, u32[]{:S(2)}, u32[]{:S(2)}) collective-permute-start(bf16[96,6144]{1,0:T(8,128)(2,1)} %collective-permute-done.16.refs_2_), channel_id=1, source_target_pairs={{0,4},{4,0},{8,12},{12,8},{16,20},{20,16},{24,28},{28,24},{1,5},{5... | collective-permute-start | bytes 3538952 | tf_op jit(solution)/shard_map/ppermute | solution.py:384
  143.2 10.8 %collective-permute-start.26 = (bf16[96,6144]{1,0:T(8,128)(2,1)}, bf16[96,6144]{1,0:T(8,128)(2,1)}, u32[]{:S(2)}, u32[]{:S(2)}) collective-permute-start(bf16[96,6144]{1,0:T(8,128)(2,1)} %collective-permute-done.22.refs_3_), channel_id=1, source_target_pairs={{0,4},{4,0},{8,12},{12,8},{16,20},{20,16},{24,28},{28,24},{1,5},{5... | collective-permute-start | bytes 3538952 | tf_op jit(solution)/shard_map/ppermute | solution.py:384
  205.4 19.2 %collective-permute-start.27 = (bf16[3,768,1024]{2,1,0:T(8,128)(2,1)}, bf16[3,768,1024]{2,1,0:T(8,128)(2,1)S(1)}, u32[]{:S(2)}, u32[]{:S(2)}) collective-permute-start(bf16[3,768,1024]{2,1,0:T(8,128)(2,1)} %get-tuple-element.271), channel_id=1, source_target_pairs={{0,4},{4,0},{8,12},{12,8},{16,20},{20,16},{24,28},{28,24},{1,5},{5... | collective-permute-start | bytes 14155784 | tf_op jit(solution)/shard_map/ppermute | solution.py:384
  228.0 29.2 %collective-permute-start.28 = (bf16[3,2,192,1024]{3,2,1,0:T(8,128)(2,1)}, bf16[3,2,192,1024]{3,2,1,0:T(8,128)(2,1)}, u32[]{:S(2)}, u32[]{:S(2)}) collective-permute-start(bf16[3,2,192,1024]{3,2,1,0:T(8,128)(2,1)} %get-tuple-element.287), channel_id=1, source_target_pairs={{0,16},{4,12},{8,24},{12,4},{16,0},{20,28},{24,8},{28,20},{1,17},{... | collective-permute-start | bytes 7077896 | tf_op jit(solution)/shard_map/ppermute | solution.py:380
  262.0 17.2 %collective-permute-start.30 = (bf16[3,1,192,1024]{3,2,1,0:T(8,128)(2,1)}, bf16[3,1,192,1024]{3,2,1,0:T(8,128)(2,1)}, u32[]{:S(2)}, u32[]{:S(2)}) collective-permute-start(bf16[3,1,192,1024]{3,2,1,0:T(8,128)(2,1)} %get-tuple-element.301), channel_id=1, source_target_pairs={{0,8},{4,20},{8,0},{12,28},{16,24},{20,4},{24,16},{28,12},{1,9},{5... | collective-permute-start | bytes 3538952 | tf_op jit(solution)/shard_map/ppermute | solution.py:380
  274.8 13.9 %collective-permute-start.29 = (bf16[5,768,384]{2,1,0:T(8,128)(2,1)}, bf16[5,768,384]{2,1,0:T(8,128)(2,1)S(1)}, u32[]{:S(2)}, u32[]{:S(2)}) collective-permute-start(bf16[5,768,384]{2,1,0:T(8,128)(2,1)} %get-tuple-element.299), channel_id=1, source_target_pairs={{0,4},{4,0},{8,12},{12,8},{16,20},{20,16},{24,28},{28,24},{1,5},{5... | collective-permute-start | bytes 8847368 | tf_op jit(solution)/shard_map/ppermute | solution.py:384
  274.8 102.3 %all-to-all-start.1 = ((bf16[4,256,768]{2,1,0:T(8,128)(2,1)}), bf16[4,256,768]{2,1,0:T(8,128)(2,1)}, u32[]{:S(2)}, u32[]{:S(2)}) async-start(bf16[4,256,768]{2,1,0:T(8,128)(2,1)} %bitcast.119), calls=%async_computation.1 | async-start | bytes 3145728 | tf_op jit(solution)/shard_map/all_to_all | solution.py:698
  282.9 51.1 %collective-permute-start.34 = (bf16[3,2,1,24,1024]{4,3,2,1,0:T(8,128)(2,1)}, bf16[3,2,1,24,1024]{4,3,2,1,0:T(8,128)(2,1)}, u32[]{:S(2)}, u32[]{:S(2)}) collective-permute-start(bf16[3,2,1,24,1024]{4,3,2,1,0:T(8,128)(2,1)} %get-tuple-element.339), channel_id=1, source_target_pairs={{0,1},{1,2},{2,3},{3,0},{4,5},{5,6},{6,7},{7,4},{8,9},{9,10},{10,1... | collective-permute-start | bytes 884744 | tf_op jit(solution)/shard_map/ppermute | solution.py:388
  284.9 51.6 %collective-permute-start.35 = (bf16[3,2,1,24,1024]{4,3,2,1,0:T(8,128)(2,1)}, bf16[3,2,1,24,1024]{4,3,2,1,0:T(8,128)(2,1)}, u32[]{:S(2)}, u32[]{:S(2)}) collective-permute-start(bf16[3,2,1,24,1024]{4,3,2,1,0:T(8,128)(2,1)} %get-tuple-element.340), channel_id=1, source_target_pairs={{0,2},{1,3},{2,0},{3,1},{4,6},{5,7},{6,4},{7,5},{8,10},{9,11},{10,... | collective-permute-start | bytes 884744 | tf_op jit(solution)/shard_map/ppermute | solution.py:388
  287.2 49.2 %collective-permute-start.36 = (bf16[3,2,1,24,1024]{4,3,2,1,0:T(8,128)(2,1)}, bf16[3,2,1,24,1024]{4,3,2,1,0:T(8,128)(2,1)}, u32[]{:S(2)}, u32[]{:S(2)}) collective-permute-start(bf16[3,2,1,24,1024]{4,3,2,1,0:T(8,128)(2,1)} %get-tuple-element.341), channel_id=1, source_target_pairs={{0,3},{1,0},{2,1},{3,2},{4,7},{5,4},{6,5},{7,6},{8,11},{9,8},{10,9... | collective-permute-start | bytes 884744 | tf_op jit(solution)/shard_map/ppermute | solution.py:388
  293.2 25.4 %collective-permute-start.32 = (bf16[5,2,192,384]{3,2,1,0:T(8,128)(2,1)}, bf16[5,2,192,384]{3,2,1,0:T(8,128)(2,1)}, u32[]{:S(2)}, u32[]{:S(2)}) collective-permute-start(bf16[5,2,192,384]{3,2,1,0:T(8,128)(2,1)} %get-tuple-element.322), channel_id=1, source_target_pairs={{0,16},{4,12},{8,24},{12,4},{16,0},{20,28},{24,8},{28,20},{1,17},{... | collective-permute-start | bytes 4423688 | tf_op jit(solution)/shard_map/ppermute | solution.py:380
  322.5 22.1 %collective-permute-start.38 = (bf16[5,1,192,384]{3,2,1,0:T(8,128)(2,1)S(1)}, bf16[5,1,192,384]{3,2,1,0:T(8,128)(2,1)S(1)}, u32[]{:S(2)}, u32[]{:S(2)}) collective-permute-start(bf16[5,1,192,384]{3,2,1,0:T(8,128)(2,1)S(1)} %get-tuple-element.351), channel_id=1, source_target_pairs={{0,8},{4,20},{8,0},{12,28},{16,24},{20,4},{24,16},{28,12},{1,9},{5... | collective-permute-start | bytes 2211848 | tf_op jit(solution)/shard_map/ppermute | solution.py:380
  324.4 18.6 %collective-permute-start.33 = (bf16[3,2,192,384]{3,2,1,0:T(8,128)(2,1)S(1)}, bf16[3,2,192,384]{3,2,1,0:T(8,128)(2,1)S(1)}, u32[]{:S(2)}, u32[]{:S(2)}) collective-permute-start(bf16[3,2,192,384]{3,2,1,0:T(8,128)(2,1)S(1)} %get-tuple-element.337), channel_id=1, source_target_pairs={{0,16},{4,12},{8,24},{12,4},{16,0},{20,28},{24,8},{28,20},{1,17},{... | collective-permute-start | bytes 2654216 | tf_op jit(solution)/shard_map/ppermute | solution.py:380
  343.8 8.4 %collective-permute-start.37 = (bf16[3,1,192,384]{3,2,1,0:T(8,128)(2,1)S(1)}, bf16[3,1,192,384]{3,2,1,0:T(8,128)(2,1)S(1)}, u32[]{:S(2)}, u32[]{:S(2)}) collective-permute-start(bf16[3,1,192,384]{3,2,1,0:T(8,128)(2,1)S(1)} %get-tuple-element.349), channel_id=1, source_target_pairs={{0,8},{4,20},{8,0},{12,28},{16,24},{20,4},{24,16},{28,12},{1,9},{5... | collective-permute-start | bytes 1327112 | tf_op jit(solution)/shard_map/ppermute | solution.py:380
  345.3 11.0 %collective-permute-start.42 = (bf16[5,2,1,24,384]{4,3,2,1,0:T(8,128)(2,1)S(1)}, bf16[5,2,1,24,384]{4,3,2,1,0:T(8,128)(2,1)S(1)}, u32[]{:S(2)}, u32[]{:S(2)}) collective-permute-start(bf16[5,2,1,24,384]{4,3,2,1,0:T(8,128)(2,1)S(1)} %get-tuple-element.371), channel_id=1, source_target_pairs={{0,1},{1,2},{2,3},{3,0},{4,5},{5,6},{6,7},{7,4},{8,9},{9,10},{10,1... | collective-permute-start | bytes 552968 | tf_op jit(solution)/shard_map/ppermute | solution.py:388
  346.9 20.3 %collective-permute-start.43 = (bf16[5,2,1,24,384]{4,3,2,1,0:T(8,128)(2,1)S(1)}, bf16[5,2,1,24,384]{4,3,2,1,0:T(8,128)(2,1)S(1)}, u32[]{:S(2)}, u32[]{:S(2)}) collective-permute-start(bf16[5,2,1,24,384]{4,3,2,1,0:T(8,128)(2,1)S(1)} %get-tuple-element.372), channel_id=1, source_target_pairs={{0,2},{1,3},{2,0},{3,1},{4,6},{5,7},{6,4},{7,5},{8,10},{9,11},{10,... | collective-permute-start | bytes 552968 | tf_op jit(solution)/shard_map/ppermute | solution.py:388
  348.4 18.8 %collective-permute-start.44 = (bf16[5,2,1,24,384]{4,3,2,1,0:T(8,128)(2,1)S(1)}, bf16[5,2,1,24,384]{4,3,2,1,0:T(8,128)(2,1)S(1)}, u32[]{:S(2)}, u32[]{:S(2)}) collective-permute-start(bf16[5,2,1,24,384]{4,3,2,1,0:T(8,128)(2,1)S(1)} %get-tuple-element.373), channel_id=1, source_target_pairs={{0,3},{1,0},{2,1},{3,2},{4,7},{5,4},{6,5},{7,6},{8,11},{9,8},{10,9... | collective-permute-start | bytes 552968 | tf_op jit(solution)/shard_map/ppermute | solution.py:388
  352.8 16.4 %collective-permute-start.39 = (bf16[3,2,1,24,384]{4,3,2,1,0:T(8,128)(2,1)S(1)}, bf16[3,2,1,24,384]{4,3,2,1,0:T(8,128)(2,1)S(1)}, u32[]{:S(2)}, u32[]{:S(2)}) collective-permute-start(bf16[3,2,1,24,384]{4,3,2,1,0:T(8,128)(2,1)S(1)} %get-tuple-element.367), channel_id=1, source_target_pairs={{0,1},{1,2},{2,3},{3,0},{4,5},{5,6},{6,7},{7,4},{8,9},{9,10},{10,1... | collective-permute-start | bytes 331784 | tf_op jit(solution)/shard_map/ppermute | solution.py:388
  354.8 18.9 %collective-permute-start.40 = (bf16[3,2,1,24,384]{4,3,2,1,0:T(8,128)(2,1)S(1)}, bf16[3,2,1,24,384]{4,3,2,1,0:T(8,128)(2,1)S(1)}, u32[]{:S(2)}, u32[]{:S(2)}) collective-permute-start(bf16[3,2,1,24,384]{4,3,2,1,0:T(8,128)(2,1)S(1)} %get-tuple-element.368), channel_id=1, source_target_pairs={{0,2},{1,3},{2,0},{3,1},{4,6},{5,7},{6,4},{7,5},{8,10},{9,11},{10,... | collective-permute-start | bytes 331784 | tf_op jit(solution)/shard_map/ppermute | solution.py:388
  356.3 17.4 %collective-permute-start.41 = (bf16[3,2,1,24,384]{4,3,2,1,0:T(8,128)(2,1)S(1)}, bf16[3,2,1,24,384]{4,3,2,1,0:T(8,128)(2,1)S(1)}, u32[]{:S(2)}, u32[]{:S(2)}) collective-permute-start(bf16[3,2,1,24,384]{4,3,2,1,0:T(8,128)(2,1)S(1)} %get-tuple-element.369), channel_id=1, source_target_pairs={{0,3},{1,0},{2,1},{3,2},{4,7},{5,4},{6,5},{7,6},{8,11},{9,8},{10,9... | collective-permute-start | bytes 331784 | tf_op jit(solution)/shard_map/ppermute | solution.py:388
  375.2 6.0 %collective-permute-start.52 = (f32[3,24,1024]{2,1,0:T(8,128)S(1)}, f32[3,24,1024]{2,1,0:T(8,128)S(1)}, u32[]{:S(2)}, u32[]{:S(2)}) collective-permute-start(f32[3,24,1024]{2,1,0:T(8,128)S(1)} %dynamic-slice_bitcast_fusion), channel_id=1, source_target_pairs={{0,4},{4,0},{8,12},{12,8},{16,20},{20,16},{24,28},{28,24},{1,5},{5... | collective-permute-start | bytes 884744 | tf_op jit(solution)/shard_map/ppermute | solution.py:384
  386.4 13.6 %collective-permute-start.51 = (f32[5,24,384]{2,1,0:T(8,128)S(1)}, f32[5,24,384]{2,1,0:T(8,128)S(1)}, u32[]{:S(2)}, u32[]{:S(2)}) collective-permute-start(f32[5,24,384]{2,1,0:T(8,128)S(1)} %dynamic-slice_bitcast_fusion.1), channel_id=1, source_target_pairs={{0,4},{4,0},{8,12},{12,8},{16,20},{20,16},{24,28},{28,24},{1,5},{5... | collective-permute-start | bytes 552968 | tf_op jit(solution)/shard_map/ppermute | solution.py:384
  389.1 10.9 %collective-permute-start.50 = (f32[3,24,384]{2,1,0:T(8,128)S(1)}, f32[3,24,384]{2,1,0:T(8,128)S(1)}, u32[]{:S(2)}, u32[]{:S(2)}) collective-permute-start(f32[3,24,384]{2,1,0:T(8,128)S(1)} %dynamic-slice_bitcast_fusion.2), channel_id=1, source_target_pairs={{0,4},{4,0},{8,12},{12,8},{16,20},{20,16},{24,28},{28,24},{1,5},{5... | collective-permute-start | bytes 331784 | tf_op jit(solution)/shard_map/ppermute | solution.py:384
  (78 other events, 786.5 us)

commit v5 on v4

--- a/solution.py
+++ b/solution.py
@@ -196,7 +196,7 @@
     def pre(t):
         sl=slice(t*tb,(t+1)*tb)
         a=n3[sl,:]
-        return dg(a,wg[...],NN),dg(a,wu[...],NN),dg(gb[sl,:],wd[...],NN)
+        return dg(a,wg(),NN),dg(a,wu(),NN),dg(gb[sl,:],wd(),NN)
     nxt=pre(0)
     for t in range(nt):
         sl=slice(t*tb,(t+1)*tb)
@@ -211,22 +211,35 @@
         dgate=(di*u*dge).astype(bf)
         dup=(di*ge).astype(bf)
         inner_s[sl,:]=inner; dgate_s[sl,:]=dgate; dup_s[sl,:]=dup
-        oacc[sl,:]+=dg(inner,wd[...],NT)
-        nacc[sl,:]+=dg(dgate,wg[...],NT)+dg(dup,wu[...],NT)
+        oacc[sl,:]+=dg(inner,wd(),NT)
+        nacc[sl,:]+=dg(dgate,wg(),NT)+dg(dup,wu(),NT)
     dw_ref[0]=dg(n3[...],dgate_s[...],TN).astype(bf)
     dw_ref[1]=dg(n3[...],dup_s[...],TN).astype(bf)
     dw_ref[2]=dg(gb[...],inner_s[...],TN).astype(bf)
 
-def mlp_kernel(core_ref,len_ref,h1_ref,oT_ref,w7_ref,cot_ref,g_ref,wg_ref,wu_ref,wd_ref,
-               out_ref,gh_ref,gmT_ref,gb2_ref,dg_ref,send_ref,keep_ref,
-               h2,n3,gb,oacc,nacc,dw,inner_s,dgate_s,dup_s,sems,*,tb):
+def mlp_kernel(core_ref,index_ref,len_ref,h1_ref,oT_ref,w7_ref,cot_ref,g_ref,*refs,tb,pieces):
+    w_refs=refs[:pieces]
+    (out_ref,gh_ref,gmT_ref,gb2_ref,dg_ref,send_ref,keep_ref,
+     h2,n3,gb,oacc,nacc,dw,inner_s,dgate_s,dup_s,sems,w,wsems)=refs[pieces:]
     L,D=h1_ref.shape
+    F=w_refs[0].shape[1]//3
     fc=dw.shape[3]
     i=pl.program_id(0); count=pl.num_programs(0); half=count//2
     slot=lax.rem(i,2)
     def copy(step,to):
         col=pl.multiple_of(lax.rem(step,half)*fc,fc)
         return pltpu.make_async_copy(dw.at[lax.rem(step,2)],to.at[:,:,pl.ds(col,fc)],sems.at[lax.rem(step,2)])
+    def weights(step):
+        chunk=lax.rem(step+(1-core_ref[0])*half,count)
+        to=lax.rem(step,2)
+        return [pltpu.make_async_copy(w_refs[p].at[:,pl.ds(pl.multiple_of(j*F+chunk*fc,fc),fc)],w.at[to,j,index_ref[p]],wsems.at[to,j*pieces+p])
+                for j in range(3) for p in range(pieces)]
+    @pl.when(i==0)
+    def _():
+        for c in weights(0): c.start()
+    @pl.when(i+1<count)
+    def _():
+        for c in weights(i+1): c.start()
     @pl.when(i==0)
     def _():
         n=len_ref[0]
@@ -242,7 +255,9 @@
     @pl.when(i>=2)
     def _():
         copy(i-2,send_ref).wait()
-    mlp_chunk(n3,gb,wg_ref,wu_ref,wd_ref,dw.at[slot],inner_s,dgate_s,dup_s,oacc,nacc,tb)
+    for c in weights(i): c.wait()
+    wv=[lambda j=j: w[slot,j].reshape(D,fc) for j in range(3)]
+    mlp_chunk(n3,gb,wv[0],wv[1],wv[2],dw.at[slot],inner_s,dgate_s,dup_s,oacc,nacc,tb)
     @pl.when(i<half)
     def _():
         copy(i,send_ref).start()
@@ -266,20 +281,20 @@
         dg_ref[...]=acc
         copy(i-1,keep_ref).wait()
         copy(i,keep_ref).wait()
-def mlp(core,n,h1,oT,w_second,cot,g,wm,fc=512,tb=256):
-    L,D=h1.shape; F=wm.shape[1]//3; nc=F//fc; hc=nc//2
-    whole=lambda shape: pl.BlockSpec(shape,lambda i,c:(0,)*len(shape),pipeline_mode=pl.Buffered(1))
-    wb=lambda j: pl.BlockSpec((D,fc),lambda i,c,j=j:(0,j*nc+lax.rem(i+(1-c[0])*hc,nc)))
+def mlp(core,index,n,h1,oT,w_second,cot,g,parts,fc=512,tb=256):
+    L,D=h1.shape; F=parts[0].shape[1]//3; nc=F//fc; count=len(parts)
+    whole=lambda shape: pl.BlockSpec(shape,lambda i,c,x:(0,)*len(shape),pipeline_mode=pl.Buffered(1))
     S=jax.ShapeDtypeStruct
     hbm=pl.BlockSpec(memory_space=pl.ANY)
-    return pl.pallas_call(functools.partial(mlp_kernel,tb=tb),
-      grid_spec=pltpu.PrefetchScalarGridSpec(num_scalar_prefetch=1,grid=(nc,),
-      in_specs=[pl.BlockSpec(memory_space=pltpu.SMEM),whole((L,D)),whole((D,L)),pl.BlockSpec((D,D),lambda i,c:(0,4),pipeline_mode=pl.Buffered(1)),whole((L,D)),whole((8,D)),wb(0),wb(1),wb(2)],
+    return pl.pallas_call(functools.partial(mlp_kernel,tb=tb,pieces=count),
+      grid_spec=pltpu.PrefetchScalarGridSpec(num_scalar_prefetch=2,grid=(nc,),
+      in_specs=[pl.BlockSpec(memory_space=pltpu.SMEM),whole((L,D)),whole((D,L)),pl.BlockSpec((D,D),lambda i,c,x:(0,4),pipeline_mode=pl.Buffered(1)),whole((L,D)),whole((8,D))]+[hbm]*count,
       out_specs=[whole((L,D)),whole((L,D)),whole((D,L)),whole((L,D)),whole((1,D)),hbm,hbm],
       scratch_shapes=[pltpu.VMEM((L,D),f32),pltpu.VMEM((L,D),bf),pltpu.VMEM((L,D),bf),pltpu.VMEM((L,D),f32),pltpu.VMEM((L,D),f32),
-        pltpu.VMEM((2,3,D,fc),bf),pltpu.VMEM((L,fc),bf),pltpu.VMEM((L,fc),bf),pltpu.VMEM((L,fc),bf),pltpu.SemaphoreType.DMA((2,))]),
+        pltpu.VMEM((2,3,D,fc),bf),pltpu.VMEM((L,fc),bf),pltpu.VMEM((L,fc),bf),pltpu.VMEM((L,fc),bf),pltpu.SemaphoreType.DMA((2,)),
+        pltpu.VMEM((2,3,count,D//count,fc),bf),pltpu.SemaphoreType.DMA((2,3*count))]),
       out_shape=[S((L,D),bf),S((L,D),f32),S((D,L),bf),S((L,D),bf),S((1,D),f32),S((3,D,F//2),bf),S((3,D,F//2),bf)],
-      cost_estimate=cost(42),compiler_params=cp(48))(core,n,h1,oT,w_second,cot,g,wm,wm,wm)
+      cost_estimate=cost(42),compiler_params=cp(48))(core,index,n,h1,oT,w_second,cot,g,*parts)
 
 def mid_kernel(h1_ref,gh2_ref,dcT_ref,w4_ref,w3_ref,g_ref,gh1_ref,gmT_ref,gb_ref,dg_ref):
     i=pl.program_id(0)
@@ -499,13 +514,17 @@
         if end not in self.other:
             self.other[end]=swap_core(self.pieces[end],self.here.S)
 
-    def place(self):
+    def parts(self):
         here=self.here
         n=here.NP
         idx=[here.slab(s)*2+here.core for s in range(n)]+[here.slab(s,False)*2+1-here.core for s in range(n)]
         index=jnp.stack(idx).astype(jnp.int32)
         parts=[self.pieces[s] for s in range(n)]+[self.other[s] for s in range(n)]
-        out=place_rows(index,parts,range(2*n),2*n,0.05)
+        return index,parts
+
+    def place(self):
+        index,parts=self.parts()
+        out=place_rows(index,parts,range(len(parts)),len(parts),0.05)
         return out.reshape(-1,parts[0].shape[1])
 
 
@@ -688,8 +707,8 @@
     g3.swap_last()
     o2,lse2=attn_fwd(patch_count,q2,k2,v2,False,512,2,(half,half),(o2,lse2),VB)
     o2=g3.arrived(o2)
-    w_mlp=g3.place()
-    mixed_out,gh2,gm2,gb2,dg3,mlp_send,mlp_keep=mlp(core,table_len,h1,o2,w_second,cotangent[0],gains,w_mlp)
+    w_index,w_parts=g3.parts()
+    mixed_out,gh2,gm2,gb2,dg3,mlp_send,mlp_keep=mlp(core,w_index,table_len,h1,o2,w_second,cotangent[0],gains,w_parts)
     r1=Reduce(mlp_send,mlp_keep,here)
     part=attn_bwd(patch_count,q2,k2,v2,o2,gm2,lse2,False,256,2,(0,half))
     part=(r1.fold(part[0]),)+tuple(part[1:])

time: 407 us -> 400 us (0.983)
  waiting for transfers between devices: 74.3 us -> 68.2 us
    pallas_call x6 -> x5, Pallas kernels: 13.3 us -> 9.25 us  [place_rows(): pl.pallas_call(functools.partial(copy_kernel, places=tuple(places), colum...]
    unnamed x149 -> x143, local copies, waits for them, and re-layouts: 28.4 us -> 26.8 us
  transfers between devices with their start and end apart: 55 -> 55, of which waited for: 20 -> 20; matrix products, arithmetic and copies ran while one was open for 3% -> 4% of each run, Pallas kernels for 38% -> 39%
where the time goes in v5:
time: 400 us; the launch traced here: 396 us
  Pallas kernels  207 us (52%)
  starting transfers between devices  68.2 us (17%)
  waiting for transfers between devices  68.2 us (17%)
  local copies, waits for them, and re-layouts  27.7 us (7%)
  other arithmetic  16.8 us (4%)
  between operations  7.95 us (2%)
    pallas_call x3, Pallas kernels, attn_bwd(): pl.pallas_call(functools.partial(bwd_kernel if into is None else bwd_part...  51 us
    pallas_call x1, Pallas kernels, mlp(): pl.pallas_call(functools.partial(mlp_kernel, tb=tb, pieces=count), grid_s...  44.6 us
    pallas_call x4, Pallas kernels, attn_fwd(): pl.pallas_call(functools.partial(fwd_kernel if into is None else fwd_part...  32.2 us
    ppermute x15, waiting for transfers between devices, shift_mem(): lax.ppermute(x, MEM, [(z, (z + step) % mem_size) for z in range(mem_size)])  31.9 us
    ppermute x15, starting transfers between devices, shift_mem(): lax.ppermute(x, MEM, [(z, (z + step) % mem_size) for z in range(mem_size)])  27.5 us
    unnamed x143, local copies, waits for them, and re-layouts  26.8 us
    ppermute x15, waiting for transfers between devices, cross(): return lax.ppermute(x, SEQ, perm)  25.6 us
    ppermute x15, starting transfers between devices, cross(): return lax.ppermute(x, SEQ, perm)  20.9 us
  transfers between devices with their start and end apart: 55, of which 20 were waited for; matrix products, arithmetic and copies ran while one was open for 4% of the time, Pallas kernels for 39%

profile of v5, /device:TPU:0, one launch (start us, length us, event | category | flops | bytes accessed | tf_op | source)
XLA Modules:
  0.0 396.2 jit_solution(8967826926253836730)
XLA Ops:
  2.6 3.1 collective-permute-start
  5.7 2.6 collective-permute-start.1
  11.9 4.2 %collective-permute-done.1.refs_2_ = bf16[24,2432]{1,0:T(8,128)(2,1)S(1)} collective-permute-done((bf16[24,2432]{1,0:T(8,128)(2,1)S(1)}, bf16[24,2432]{1,0:T(8,128)(2,1)S(1)}, u32[]{:S(2)}, u32[]{:S(2)}) %collective-permute-start.1) | collective-permute-done | bytes 116768 | tf_op jit(solution)/shard_map/ppermute | solution.py:403
  18.8 3.0 collective-permute-start.4
  23.3 4.5 %collective-permute-done.3.refs_1_ = bf16[96,2432]{1,0:T(8,128)(2,1)S(1)} collective-permute-done((bf16[96,2432]{1,0:T(8,128)(2,1)S(1)}, bf16[96,2432]{1,0:T(8,128)(2,1)S(1)}, u32[]{:S(2)}, u32[]{:S(2)}) %collective-permute-start.3) | collective-permute-done | bytes 466976 | tf_op jit(solution)/shard_map/ppermute | solution.py:395
  27.8 2.7 collective-permute-start.6
  30.5 2.7 collective-permute-done.4.refs_1_
  38.9 7.5 %collective-permute-done.7.refs_2_ = bf16[24,9984]{1,0:T(8,128)(2,1)S(1)} collective-permute-done((bf16[24,9984]{1,0:T(8,128)(2,1)S(1)}, bf16[24,9984]{1,0:T(8,128)(2,1)S(1)}, u32[]{:S(2)}, u32[]{:S(2)}) %collective-permute-start.7) | collective-permute-done | bytes 479264 | tf_op jit(solution)/shard_map/ppermute | solution.py:403
  47.9 2.9 shard_map.238
  50.8 6.3 %shard_map.239 = (bf16[1024,768]{1,0:T(8,128)(2,1)S(1)}, bf16[2304,1024]{1,0:T(8,128)(2,1)S(1)}, f32[8,768]{1,0:T(8,128)S(1)}) custom-call(bf16[1024,768]{1,0:T(8,128)(2,1)S(1)} %bitcast.125, bf16[768,2432]{1,0:T(8,128)(2,1)S(1)} %bitcast.116, bf16[768,2432]{1,0:T(8,128)(2,1)S(1)} %bitcast.117), custom_call_target="tpu_custom_call" | custom-call | flops 60000002048 | bytes 100000 | tf_op jit(solution)/shard_map/pallas_call | solution.py:167
  60.2 3.2 collective-permute-start.13
  63.4 4.5 %all-to-all-start = ((bf16[4,256,768]{2,1,0:T(8,128)(2,1)}), bf16[4,256,768]{2,1,0:T(8,128)(2,1)S(1)}, u32[]{:S(2)}, u32[]{:S(2)}) async-start(bf16[4,256,768]{2,1,0:T(8,128)(2,1)} %param.15), calls=%async_computation | async-start | bytes 3145728 | tf_op jit(solution)/shard_map/all_to_all | solution.py:681
  70.9 7.0 %shard_map.241 = (bf16[768,1024]{1,0:T(8,128)(2,1)S(1)}, f32[12,1,1024]{2,1,0:T(1,128)S(1)}) custom-call(s32[1]{0:T(128)S(6)} %copy.49.len_ref.refs_0_, bf16[2304,1024]{1,0:T(8,128)(2,1)S(1)} %copy-done.4, bf16[2304,1024]{1,0:T(8,128)(2,1)S(1)} %copy-done.4, bf16[2304,1024]{1,0:T(8,128)(2,1)S(1)} %copy-done.4), custom_call_target="tpu_custom_call" | custom-call | flops 3000000000 | bytes 100000 | tf_op jit(solution)/shard_map/pallas_call | solution.py:77
  84.0 10.7 %collective-permute-done.17.refs_3_ = bf16[96,3840]{1,0:T(8,128)(2,1)S(1)} collective-permute-done((bf16[96,3840]{1,0:T(8,128)(2,1)}, bf16[96,3840]{1,0:T(8,128)(2,1)S(1)}, u32[]{:S(2)}, u32[]{:S(2)}) %collective-permute-start.17) | collective-permute-done | bytes 737312 | tf_op jit(solution)/shard_map/ppermute | solution.py:395
  94.6 2.4 collective-permute-start.16
  97.0 3.5 shard_map.243
  104.6 2.5 shard_map.244
  107.1 2.5 copy-done
  109.6 2.7 copy-done.1
  112.3 3.6 shard_map.245.kT_ref.vT_ref.refs_2_.refs_3_
  120.4 5.7 %shard_map.246 = (f32[1024,768]{1,0:T(8,128)S(1)}, bf16[1024,768]{1,0:T(8,128)(2,1)S(1)}, bf16[768,1024]{1,0:T(8,128)(2,1)S(1)}) custom-call(bf16[1024,768]{1,0:T(8,128)(2,1)S(1)} %bitcast.126, bf16[768,1024]{1,0:T(8,128)(2,1)S(1)} %copy-done.7, bf16[768,3840]{1,0:T(8,128)(2,1)S(1)} %bitcast.101, bf16[768,3840]{1,0:T(8,128)(2,1)S(1)} %bitcast.102, ...), custom_call_target="tpu_custom_call" | custom-call | flops 3000000000 | bytes 100000 | tf_op jit(solution)/shard_map/pallas_call | solution.py:189
  130.1 11.0 %shard_map.247 = (bf16[768,1024]{1,0:T(8,128)(2,1)}, f32[12,1,1024]{2,1,0:T(1,128)}) custom-call(s32[1]{0:T(128)S(6)} %copy.50.len_ref.refs_0_, bf16[768,1024]{1,0:T(8,128)(2,1)} %copy-done.37, bf16[1536,1024]{1,0:T(8,128)(2,1)} %copy-done.12, bf16[1536,1024]{1,0:T(8,128)(2,1)} %copy-done.12), custom_call_target="tpu_custom_call" | custom-call | flops 3000000000 | bytes 100000 | tf_op jit(solution)/shard_map/pallas_call | solution.py:77
  141.4 10.6 %shard_map.248 = (bf16[768,1024]{1,0:T(8,128)(2,1)}, f32[12,1,1024]{2,1,0:T(1,128)}) custom-call(s32[1]{0:T(128)S(6)} %copy.50.len_ref.refs_0_, bf16[768,1024]{1,0:T(8,128)(2,1)} %copy-done.37, bf16[1536,1024]{1,0:T(8,128)(2,1)} %copy-done.12, bf16[1536,1024]{1,0:T(8,128)(2,1)} %copy-done.12, ...), custom_call_target="tpu_custom_call", output_to_operand_aliasing={{0}: (4, {}), {1}: (5, {})} | custom-call | flops 3000000000 | bytes 100000 | tf_op jit(solution)/shard_map/pallas_call | solution.py:77
  152.0 44.6 %shard_map.249 = (bf16[1024,768]{1,0:T(8,128)(2,1)}, f32[1024,768]{1,0:T(8,128)}, bf16[768,1024]{1,0:T(8,128)(2,1)}, bf16[1024,768]{1,0:T(8,128)(2,1)}, f32[1,76...) custom-call(s32[1]{0:T(128)} %bitcast.core_ref, s32[8]{0:T(128)S(1)} %stack.54.index_ref, ...), custom_call_target="tpu_custom_call" | custom-call | flops 420000006144 | bytes 100000 | tf_op jit(solution)/shard_map/pallas_call | solution.py:289
  201.4 15.7 %shard_map.250 = (bf16[768,1024]{1,0:T(8,128)(2,1)S(1)}, bf16[768,1024]{1,0:T(8,128)(2,1)S(1)}, bf16[768,1024]{1,0:T(8,128)(2,1)S(1)}) custom-call(s32[1]{0:T(128)S(6)} %copy.50.len_ref.refs_0_, bf16[768,1024]{1,0:T(8,128)(2,1)S(1)} %copy-done.38, bf16[1536,1024]{1,0:T(8,128)(2,1)S(1)} %copy-done.13, bf16[1536,1024]{1,0:T(8,128)(2,1)S(1)} %copy-done.13, ...), custom_call_target="tpu_custom_call" | custom-call | flops 140000002048 | bytes 100000 | tf_op jit(solution)/shard_map/pallas_call | solution.py:137
  217.1 3.4 shard_map.251
  220.9 15.7 %shard_map.252 = (bf16[768,1024]{1,0:T(8,128)(2,1)S(1)}, bf16[768,1024]{1,0:T(8,128)(2,1)S(1)}, bf16[768,1024]{1,0:T(8,128)(2,1)S(1)}) custom-call(s32[1]{0:T(128)S(6)} %copy.50.len_ref.refs_0_, bf16[768,1024]{1,0:T(8,128)(2,1)S(1)} %copy-done.38, bf16[1536,1024]{1,0:T(8,128)(2,1)S(1)} %copy-done.13, ...), custom_call_target="tpu_custom_call", output_to_operand_aliasing={{0}: (7, {}), {1}: (8, {}), {2}: (9, {})} | custom-call | flops 140000002048 | bytes 100000 | tf_op jit(solution)/shard_map/pallas_call | solution.py:137
  236.6 3.9 shard_map.253
  241.7 6.0 %shard_map.254 = (f32[1024,768]{1,0:T(8,128)S(1)}, bf16[768,1024]{1,0:T(8,128)(2,1)S(1)}, bf16[1024,768]{1,0:T(8,128)(2,1)S(1)}, f32[1,768]{1,0:T(1,128)S(1)}) custom-call(f32[1024,768]{1,0:T(8,128)S(1)} %copy-done.15, f32[1024,768]{1,0:T(8,128)S(1)} %copy-done.16, bf16[768,1024]{1,0:T(8,128)(2,1)S(1)} %get-tuple-element.283.dcT_ref.refs_5_, ...), custom_call_target="tpu_custom_call" | custom-call | flops 2000000000 | bytes 100000 | tf_op jit(solution)/shard_map/pallas_call | solution.py:318
  249.7 4.6 %shard_map.255 = (bf16[3,1,192,1024]{3,2,1,0:T(8,128)(2,1)}, bf16[3,1,192,1024]{3,2,1,0:T(8,128)(2,1)S(1)}) custom-call(s32[2]{0:T(128)S(1)} %iota.9.index_ref, bf16[3,2,192,1024]{3,2,1,0:T(8,128)(2,1)S(1)} %get-tuple-element.286.ka.kb, bf16[3,2,192,1024]{3,2,1,0:T(8,128)(2,1)S(1)} %get-tuple-element.286.ka.kb, ...), custom_call_target="tpu_custom_call" | custom-call | flops 30000001024 | bytes 100000 | tf_op jit(solution)/shard_map/pallas_call | solution.py:542
  256.0 10.7 %shard_map.256 = (bf16[5,768,384]{2,1,0:T(8,128)(2,1)}, bf16[5,768,384]{2,1,0:T(8,128)(2,1)}) custom-call(s32[1]{0:T(128)} %bitcast.core_ref, bf16[1024,768]{1,0:T(8,128)(2,1)S(1)} %get-tuple-element.293.refs_0_, bf16[1024,768]{1,0:T(8,128)(2,1)S(1)} %copy-done.36, bf16[1024,768]{1,0:T(8,128)(2,1)S(1)} %bitcast.114, bf16[1024,768]{1,0:T(8,128)(2,1)S(1)} %copy-done.50, ...), custom_call_target="tpu_custom_call" | custom-call | flops 80000000000 | bytes 100000 | tf_op jit(solution)/shard_map/pallas_call | solution.py:335
  266.7 4.6 %all-to-all-start.1 = ((bf16[4,256,768]{2,1,0:T(8,128)(2,1)}), bf16[4,256,768]{2,1,0:T(8,128)(2,1)}, u32[]{:S(2)}, u32[]{:S(2)}) async-start(bf16[4,256,768]{2,1,0:T(8,128)(2,1)} %bitcast.115), calls=%async_computation.1 | async-start | bytes 3145728 | tf_op jit(solution)/shard_map/all_to_all | solution.py:717
  272.5 2.5 shard_map.257
  277.0 2.4 collective-permute-start.35
  280.9 4.4 %shard_map.258 = (bf16[5,2,192,384]{3,2,1,0:T(8,128)(2,1)}, bf16[5,2,192,384]{3,2,1,0:T(8,128)(2,1)S(1)}) custom-call(s32[4]{0:T(128)S(1)} %copy-done.31, bf16[5,4,192,384]{3,2,1,0:T(8,128)(2,1)S(1)} %bitcast.142, bf16[5,4,192,384]{3,2,1,0:T(8,128)(2,1)S(1)} %bitcast.143, bf16[5,4,192,384]{3,2,1,0:T(8,128)(2,1)S(1)} %bitcast.134, ...), custom_call_target="tpu_custom_call" | custom-call | flops 30000001024 | bytes 100000 | tf_op jit(solution)/shard_map/pallas_call | solution.py:542
  286.2 19.6 %shard_map.259 = (bf16[768,1024]{1,0:T(8,128)(2,1)S(1)}, bf16[768,1024]{1,0:T(8,128)(2,1)S(1)}, bf16[768,1024]{1,0:T(8,128)(2,1)S(1)}) custom-call(s32[1]{0:T(128)S(6)} %copy.49.len_ref.refs_0_, bf16[2304,1024]{1,0:T(8,128)(2,1)S(1)} %bitcast.112, bf16[2304,1024]{1,0:T(8,128)(2,1)S(1)} %bitcast.112, bf16[2304,1024]{1,0:T(8,128)(2,1)S(1)} %bitcast.112, ...), custom_call_target="tpu_custom_call" | custom-call | flops 140000002048 | bytes 100000 | tf_op jit(solution)/shard_map/pallas_call | solution.py:137
  305.8 5.1 %shard_map.260 = (bf16[3,768,384]{2,1,0:T(8,128)(2,1)S(1)}, bf16[3,768,384]{2,1,0:T(8,128)(2,1)S(1)}) custom-call(s32[1]{0:T(128)} %bitcast.core_ref, bf16[1024,768]{1,0:T(8,128)(2,1)S(1)} %copy-done.49, bf16[768,1024]{1,0:T(8,128)(2,1)S(1)} %get-tuple-element.333.refs_1_.qT_ref, bf16[768,1024]{1,0:T(8,128)(2,1)S(1)} %get-tuple-element.317.refs_2_.kT_ref, ...), custom_call_target="tpu_custom_call" | custom-call | flops 80000000000 | bytes 100000 | tf_op jit(solution)/shard_map/pallas_call | solution.py:335
  311.1 3.8 shard_map.261
  319.4 7.1 %shard_map.263 = (f32[1024,768]{1,0:T(8,128)}, f32[1,768]{1,0:T(1,128)S(1)}) custom-call(bf16[1024,768]{1,0:T(8,128)(2,1)S(1)} %bitcast.127, f32[1024,768]{1,0:T(8,128)S(1)} %copy-done.34, bf16[768,1024]{1,0:T(8,128)(2,1)S(1)} %get-tuple-element.333.refs_1_.qT_ref, bf16[768,1024]{1,0:T(8,128)(2,1)S(1)} %get-tuple-element.317.refs_2_.kT_ref, ...), custom_call_target="tpu_custom_call" | custom-call | flops 70000001024 | bytes 100000 | tf_op jit(solution)/shard_map/pallas_call | solution.py:365
  328.6 2.8 multiply_reduce_fusion
  331.4 4.0 %collective-permute-done.33.ra.rb = bf16[3,2,192,384]{3,2,1,0:T(8,128)(2,1)S(1)} collective-permute-done((bf16[3,2,192,384]{3,2,1,0:T(8,128)(2,1)S(1)}, bf16[3,2,192,384]{3,2,1,0:T(8,128)(2,1)S(1)}, u32[]{:S(2)}, u32[]{:S(2)}) %collective-permute-start.33) | collective-permute-done | bytes 884768 | tf_op jit(solution)/shard_map/ppermute | solution.py:395
  350.3 5.2 %collective-permute-done.43 = bf16[5,2,1,24,384]{4,3,2,1,0:T(8,128)(2,1)S(1)} collective-permute-done((bf16[5,2,1,24,384]{4,3,2,1,0:T(8,128)(2,1)S(1)}, bf16[5,2,1,24,384]{4,3,2,1,0:T(8,128)(2,1)S(1)}, u32[]{:S(2)}, u32[]{:S(2)}) %collective-permute-start.43) | collective-permute-done | bytes 184352 | tf_op jit(solution)/shard_map/ppermute | solution.py:403
  357.8 8.0 %collective-permute-done.40 = bf16[3,2,1,24,384]{4,3,2,1,0:T(8,128)(2,1)S(1)} collective-permute-done((bf16[3,2,1,24,384]{4,3,2,1,0:T(8,128)(2,1)S(1)}, bf16[3,2,1,24,384]{4,3,2,1,0:T(8,128)(2,1)S(1)}, u32[]{:S(2)}, u32[]{:S(2)}) %collective-permute-start.40) | collective-permute-done | bytes 110624 | tf_op jit(solution)/shard_map/ppermute | solution.py:403
  369.6 3.3 convert_element_type.50
  373.9 2.8 collective-permute-done.47
  376.7 2.6 collective-permute-start.48
  382.1 3.5 collective-permute-done.49
  388.7 2.7 multiply_subtract_fusion
  (273 shorter events, 90.2 us)
Async XLA Ops:
  2.6 9.2 %collective-permute-start = (bf16[24,2432]{1,0:T(8,128)(2,1)S(1)}, bf16[24,2432]{1,0:T(8,128)(2,1)S(1)}, u32[]{:S(2)}, u32[]{:S(2)}) collective-permute-start(bf16[24,2432]{1,0:T(8,128)(2,1)S(1)} %fusion.3.refs_0_), channel_id=1, source_target_pairs={{0,1},{1,2},{2,3},{3,0},{4,5},{5,6},{6,7},{7,4},{8,9},{9,10},{10,1... | collective-permute-start | bytes 350216 | tf_op jit(solution)/shard_map/ppermute | solution.py:403
  5.7 10.3 %collective-permute-start.1 = (bf16[24,2432]{1,0:T(8,128)(2,1)S(1)}, bf16[24,2432]{1,0:T(8,128)(2,1)S(1)}, u32[]{:S(2)}, u32[]{:S(2)}) collective-permute-start(bf16[24,2432]{1,0:T(8,128)(2,1)S(1)} %fusion.3.refs_0_), channel_id=1, source_target_pairs={{0,2},{1,3},{2,0},{3,1},{4,6},{5,7},{6,4},{7,5},{8,10},{9,11},{10,... | collective-permute-start | bytes 350216 | tf_op jit(solution)/shard_map/ppermute | solution.py:403
  8.3 7.7 %collective-permute-start.2 = (bf16[24,2432]{1,0:T(8,128)(2,1)S(1)}, bf16[24,2432]{1,0:T(8,128)(2,1)S(1)}, u32[]{:S(2)}, u32[]{:S(2)}) collective-permute-start(bf16[24,2432]{1,0:T(8,128)(2,1)S(1)} %fusion.3.refs_0_), channel_id=1, source_target_pairs={{0,3},{1,0},{2,1},{3,2},{4,7},{5,4},{6,5},{7,6},{8,11},{9,8},{10,9... | collective-permute-start | bytes 350216 | tf_op jit(solution)/shard_map/ppermute | solution.py:403
  17.2 10.5 %collective-permute-start.3 = (bf16[96,2432]{1,0:T(8,128)(2,1)S(1)}, bf16[96,2432]{1,0:T(8,128)(2,1)S(1)}, u32[]{:S(2)}, u32[]{:S(2)}) collective-permute-start(bf16[96,2432]{1,0:T(8,128)(2,1)S(1)} %bitcast.128), channel_id=1, source_target_pairs={{0,8},{4,20},{8,0},{12,28},{16,24},{20,4},{24,16},{28,12},{1,9},{5... | collective-permute-start | bytes 1400840 | tf_op jit(solution)/shard_map/ppermute | solution.py:395
  18.8 14.3 %collective-permute-start.4 = (bf16[24,9984]{1,0:T(8,128)(2,1)S(1)}, bf16[24,9984]{1,0:T(8,128)(2,1)S(1)}, u32[]{:S(2)}, u32[]{:S(2)}) collective-permute-start(bf16[24,9984]{1,0:T(8,128)(2,1)S(1)} %fusion.4.refs_0_), channel_id=1, source_target_pairs={{0,1},{1,2},{2,3},{3,0},{4,5},{5,6},{6,7},{7,4},{8,9},{9,10},{10,1... | collective-permute-start | bytes 1437704 | tf_op jit(solution)/shard_map/ppermute | solution.py:403
  21.8 8.7 %collective-permute-start.5 = (bf16[96,2432]{1,0:T(8,128)(2,1)S(1)}, bf16[96,2432]{1,0:T(8,128)(2,1)}, u32[]{:S(2)}, u32[]{:S(2)}) collective-permute-start(bf16[96,2432]{1,0:T(8,128)(2,1)S(1)} %bitcast.129), channel_id=1, source_target_pairs={{0,16},{4,12},{8,24},{12,4},{16,0},{20,28},{24,8},{28,20},{1,17},{... | collective-permute-start | bytes 1400840 | tf_op jit(solution)/shard_map/ppermute | solution.py:395
  27.8 9.2 %collective-permute-start.6 = (bf16[96,2432]{1,0:T(8,128)(2,1)S(1)}, bf16[96,2432]{1,0:T(8,128)(2,1)S(1)}, u32[]{:S(2)}, u32[]{:S(2)}) collective-permute-start(bf16[96,2432]{1,0:T(8,128)(2,1)S(1)} %collective-permute-done.3.refs_1_), channel_id=1, source_target_pairs={{0,16},{4,12},{8,24},{12,4},{16,0},{20,28},{24,8},{28,20},{1,17},{... | collective-permute-start | bytes 1400840 | tf_op jit(solution)/shard_map/ppermute | solution.py:395
  33.2 13.2 %collective-permute-start.7 = (bf16[24,9984]{1,0:T(8,128)(2,1)S(1)}, bf16[24,9984]{1,0:T(8,128)(2,1)S(1)}, u32[]{:S(2)}, u32[]{:S(2)}) collective-permute-start(bf16[24,9984]{1,0:T(8,128)(2,1)S(1)} %collective-permute-done.4.refs_1_), channel_id=1, source_target_pairs={{0,1},{1,2},{2,3},{3,0},{4,5},{5,6},{6,7},{7,4},{8,9},{9,10},{10,1... | collective-permute-start | bytes 1437704 | tf_op jit(solution)/shard_map/ppermute | solution.py:403
  37.0 9.4 %collective-permute-start.8 = (bf16[96,2432]{1,0:T(8,128)(2,1)S(1)}, bf16[96,2432]{1,0:T(8,128)(2,1)}, u32[]{:S(2)}, u32[]{:S(2)}) collective-permute-start(bf16[96,2432]{1,0:T(8,128)(2,1)S(1)} %collective-permute-done.6.refs_3_), channel_id=1, source_target_pairs={{0,4},{4,0},{8,12},{12,8},{16,20},{20,16},{24,28},{28,24},{1,5},{5... | collective-permute-start | bytes 1400840 | tf_op jit(solution)/shard_map/ppermute | solution.py:399
  37.8 9.1 %collective-permute-start.10 = (bf16[96,2432]{1,0:T(8,128)(2,1)S(1)}, bf16[96,2432]{1,0:T(8,128)(2,1)}, u32[]{:S(2)}, u32[]{:S(2)}) collective-permute-start(bf16[96,2432]{1,0:T(8,128)(2,1)S(1)} %bitcast.130), channel_id=1, source_target_pairs={{0,4},{4,0},{8,12},{12,8},{16,20},{20,16},{24,28},{28,24},{1,5},{5... | collective-permute-start | bytes 1400840 | tf_op jit(solution)/shard_map/ppermute | solution.py:399
  38.3 8.6 %collective-permute-start.11 = (bf16[96,2432]{1,0:T(8,128)(2,1)S(1)}, bf16[96,2432]{1,0:T(8,128)(2,1)}, u32[]{:S(2)}, u32[]{:S(2)}) collective-permute-start(bf16[96,2432]{1,0:T(8,128)(2,1)S(1)} %collective-permute-done.3.refs_1_), channel_id=1, source_target_pairs={{0,4},{4,0},{8,12},{12,8},{16,20},{20,16},{24,28},{28,24},{1,5},{5... | collective-permute-start | bytes 1400840 | tf_op jit(solution)/shard_map/ppermute | solution.py:399
  38.3 8.6 %collective-permute-start.12 = (bf16[96,2432]{1,0:T(8,128)(2,1)}, bf16[96,2432]{1,0:T(8,128)(2,1)}, u32[]{:S(2)}, u32[]{:S(2)}) collective-permute-start(bf16[96,2432]{1,0:T(8,128)(2,1)} %collective-permute-done.5.refs_2_), channel_id=1, source_target_pairs={{0,4},{4,0},{8,12},{12,8},{16,20},{20,16},{24,28},{28,24},{1,5},{5... | collective-permute-start | bytes 1400840 | tf_op jit(solution)/shard_map/ppermute | solution.py:399
  46.4 12.9 %collective-permute-start.9 = (bf16[24,9984]{1,0:T(8,128)(2,1)S(1)}, bf16[24,9984]{1,0:T(8,128)(2,1)S(1)}, u32[]{:S(2)}, u32[]{:S(2)}) collective-permute-start(bf16[24,9984]{1,0:T(8,128)(2,1)S(1)} %collective-permute-done.7.refs_2_), channel_id=1, source_target_pairs={{0,1},{1,2},{2,3},{3,0},{4,5},{5,6},{6,7},{7,4},{8,9},{9,10},{10,1... | collective-permute-start | bytes 1437704 | tf_op jit(solution)/shard_map/ppermute | solution.py:403
  60.2 18.1 %collective-permute-start.13 = (bf16[96,3840]{1,0:T(8,128)(2,1)S(1)}, bf16[96,3840]{1,0:T(8,128)(2,1)}, u32[]{:S(2)}, u32[]{:S(2)}) collective-permute-start(bf16[96,3840]{1,0:T(8,128)(2,1)S(1)} %bitcast.121), channel_id=1, source_target_pairs={{0,8},{4,20},{8,0},{12,28},{16,24},{20,4},{24,16},{28,12},{1,9},{5... | collective-permute-start | bytes 2211848 | tf_op jit(solution)/shard_map/ppermute | solution.py:395
  63.4 14.9 %collective-permute-start.14 = (bf16[96,3840]{1,0:T(8,128)(2,1)S(1)}, bf16[96,3840]{1,0:T(8,128)(2,1)}, u32[]{:S(2)}, u32[]{:S(2)}) collective-permute-start(bf16[96,3840]{1,0:T(8,128)(2,1)S(1)} %bitcast.122), channel_id=1, source_target_pairs={{0,16},{4,12},{8,24},{12,4},{16,0},{20,28},{24,8},{28,20},{1,17},{... | collective-permute-start | bytes 2211848 | tf_op jit(solution)/shard_map/ppermute | solution.py:395
  63.4 46.2 %all-to-all-start = ((bf16[4,256,768]{2,1,0:T(8,128)(2,1)}), bf16[4,256,768]{2,1,0:T(8,128)(2,1)S(1)}, u32[]{:S(2)}, u32[]{:S(2)}) async-start(bf16[4,256,768]{2,1,0:T(8,128)(2,1)} %param.15), calls=%async_computation | async-start | bytes 3145728 | tf_op jit(solution)/shard_map/all_to_all | solution.py:681
  78.3 16.3 %collective-permute-start.17 = (bf16[96,3840]{1,0:T(8,128)(2,1)}, bf16[96,3840]{1,0:T(8,128)(2,1)S(1)}, u32[]{:S(2)}, u32[]{:S(2)}) collective-permute-start(bf16[96,3840]{1,0:T(8,128)(2,1)} %collective-permute-done.13.refs_1_), channel_id=1, source_target_pairs={{0,16},{4,12},{8,24},{12,4},{16,0},{20,28},{24,8},{28,20},{1,17},{... | collective-permute-start | bytes 2211848 | tf_op jit(solution)/shard_map/ppermute | solution.py:395
  80.1 22.2 %collective-permute-start.19 = (bf16[96,3840]{1,0:T(8,128)(2,1)}, bf16[96,3840]{1,0:T(8,128)(2,1)S(1)}, u32[]{:S(2)}, u32[]{:S(2)}) collective-permute-start(bf16[96,3840]{1,0:T(8,128)(2,1)} %collective-permute-done.13.refs_1_), channel_id=1, source_target_pairs={{0,4},{4,0},{8,12},{12,8},{16,20},{20,16},{24,28},{28,24},{1,5},{5... | collective-permute-start | bytes 2211848 | tf_op jit(solution)/shard_map/ppermute | solution.py:399
  80.1 22.2 %collective-permute-start.18 = (bf16[96,3840]{1,0:T(8,128)(2,1)S(1)}, bf16[96,3840]{1,0:T(8,128)(2,1)S(1)}, u32[]{:S(2)}, u32[]{:S(2)}) collective-permute-start(bf16[96,3840]{1,0:T(8,128)(2,1)S(1)} %bitcast.123), channel_id=1, source_target_pairs={{0,4},{4,0},{8,12},{12,8},{16,20},{20,16},{24,28},{28,24},{1,5},{5... | collective-permute-start | bytes 2211848 | tf_op jit(solution)/shard_map/ppermute | solution.py:399
  80.6 21.7 %collective-permute-start.20 = (bf16[96,3840]{1,0:T(8,128)(2,1)}, bf16[96,3840]{1,0:T(8,128)(2,1)S(1)}, u32[]{:S(2)}, u32[]{:S(2)}) collective-permute-start(bf16[96,3840]{1,0:T(8,128)(2,1)} %collective-permute-done.14.refs_2_), channel_id=1, source_target_pairs={{0,4},{4,0},{8,12},{12,8},{16,20},{20,16},{24,28},{28,24},{1,5},{5... | collective-permute-start | bytes 2211848 | tf_op jit(solution)/shard_map/ppermute | solution.py:399
  82.3 35.2 %collective-permute-start.15 = (bf16[96,6144]{1,0:T(8,128)(2,1)}, bf16[96,6144]{1,0:T(8,128)(2,1)}, u32[]{:S(2)}, u32[]{:S(2)}) collective-permute-start(bf16[96,6144]{1,0:T(8,128)(2,1)} %bitcast.29.refs_0_), channel_id=1, source_target_pairs={{0,8},{4,20},{8,0},{12,28},{16,24},{20,4},{24,16},{28,12},{1,9},{5... | collective-permute-start | bytes 3538952 | tf_op jit(solution)/shard_map/ppermute | solution.py:395
  94.6 22.9 %collective-permute-start.16 = (bf16[96,6144]{1,0:T(8,128)(2,1)}, bf16[96,6144]{1,0:T(8,128)(2,1)}, u32[]{:S(2)}, u32[]{:S(2)}) collective-permute-start(bf16[96,6144]{1,0:T(8,128)(2,1)} %bitcast.29.refs_0_), channel_id=1, source_target_pairs={{0,16},{4,12},{8,24},{12,4},{16,0},{20,28},{24,8},{28,20},{1,17},{... | collective-permute-start | bytes 3538952 | tf_op jit(solution)/shard_map/ppermute | solution.py:395
  117.5 23.6 %collective-permute-start.22 = (bf16[96,6144]{1,0:T(8,128)(2,1)}, bf16[96,6144]{1,0:T(8,128)(2,1)S(1)}, u32[]{:S(2)}, u32[]{:S(2)}) collective-permute-start(bf16[96,6144]{1,0:T(8,128)(2,1)} %collective-permute-done.15.refs_1_), channel_id=1, source_target_pairs={{0,16},{4,12},{8,24},{12,4},{16,0},{20,28},{24,8},{28,20},{1,17},{... | collective-permute-start | bytes 3538952 | tf_op jit(solution)/shard_map/ppermute | solution.py:395
  117.5 23.6 %collective-permute-start.24 = (bf16[96,6144]{1,0:T(8,128)(2,1)}, bf16[96,6144]{1,0:T(8,128)(2,1)}, u32[]{:S(2)}, u32[]{:S(2)}) collective-permute-start(bf16[96,6144]{1,0:T(8,128)(2,1)} %collective-permute-done.15.refs_1_), channel_id=1, source_target_pairs={{0,4},{4,0},{8,12},{12,8},{16,20},{20,16},{24,28},{28,24},{1,5},{5... | collective-permute-start | bytes 3538952 | tf_op jit(solution)/shard_map/ppermute | solution.py:399
  119.2 21.9 %collective-permute-start.23 = (bf16[96,6144]{1,0:T(8,128)(2,1)}, bf16[96,6144]{1,0:T(8,128)(2,1)}, u32[]{:S(2)}, u32[]{:S(2)}) collective-permute-start(bf16[96,6144]{1,0:T(8,128)(2,1)} %bitcast.29.refs_0_), channel_id=1, source_target_pairs={{0,4},{4,0},{8,12},{12,8},{16,20},{20,16},{24,28},{28,24},{1,5},{5... | collective-permute-start | bytes 3538952 | tf_op jit(solution)/shard_map/ppermute | solution.py:399
  119.3 21.9 %collective-permute-start.25 = (bf16[96,6144]{1,0:T(8,128)(2,1)}, bf16[96,6144]{1,0:T(8,128)(2,1)}, u32[]{:S(2)}, u32[]{:S(2)}) collective-permute-start(bf16[96,6144]{1,0:T(8,128)(2,1)} %collective-permute-done.16.refs_2_), channel_id=1, source_target_pairs={{0,4},{4,0},{8,12},{12,8},{16,20},{20,16},{24,28},{28,24},{1,5},{5... | collective-permute-start | bytes 3538952 | tf_op jit(solution)/shard_map/ppermute | solution.py:399
  141.2 10.8 %collective-permute-start.26 = (bf16[96,6144]{1,0:T(8,128)(2,1)S(1)}, bf16[96,6144]{1,0:T(8,128)(2,1)}, u32[]{:S(2)}, u32[]{:S(2)}) collective-permute-start(bf16[96,6144]{1,0:T(8,128)(2,1)S(1)} %collective-permute-done.22.refs_3_), channel_id=1, source_target_pairs={{0,4},{4,0},{8,12},{12,8},{16,20},{20,16},{24,28},{28,24},{1,5},{5... | collective-permute-start | bytes 3538952 | tf_op jit(solution)/shard_map/ppermute | solution.py:399
  196.6 20.5 %collective-permute-start.27 = (bf16[3,768,1024]{2,1,0:T(8,128)(2,1)}, bf16[3,768,1024]{2,1,0:T(8,128)(2,1)S(1)}, u32[]{:S(2)}, u32[]{:S(2)}) collective-permute-start(bf16[3,768,1024]{2,1,0:T(8,128)(2,1)} %get-tuple-element.271), channel_id=1, source_target_pairs={{0,4},{4,0},{8,12},{12,8},{16,20},{20,16},{24,28},{28,24},{1,5},{5... | collective-permute-start | bytes 14155784 | tf_op jit(solution)/shard_map/ppermute | solution.py:399
  220.5 29.2 %collective-permute-start.28 = (bf16[3,2,192,1024]{3,2,1,0:T(8,128)(2,1)}, bf16[3,2,192,1024]{3,2,1,0:T(8,128)(2,1)}, u32[]{:S(2)}, u32[]{:S(2)}) collective-permute-start(bf16[3,2,192,1024]{3,2,1,0:T(8,128)(2,1)} %get-tuple-element.287), channel_id=1, source_target_pairs={{0,16},{4,12},{8,24},{12,4},{16,0},{20,28},{24,8},{28,20},{1,17},{... | collective-permute-start | bytes 7077896 | tf_op jit(solution)/shard_map/ppermute | solution.py:395
  254.4 16.9 %collective-permute-start.30 = (bf16[3,1,192,1024]{3,2,1,0:T(8,128)(2,1)}, bf16[3,1,192,1024]{3,2,1,0:T(8,128)(2,1)}, u32[]{:S(2)}, u32[]{:S(2)}) collective-permute-start(bf16[3,1,192,1024]{3,2,1,0:T(8,128)(2,1)} %get-tuple-element.301), channel_id=1, source_target_pairs={{0,8},{4,20},{8,0},{12,28},{16,24},{20,4},{24,16},{28,12},{1,9},{5... | collective-permute-start | bytes 3538952 | tf_op jit(solution)/shard_map/ppermute | solution.py:395
  266.7 14.2 %collective-permute-start.29 = (bf16[5,768,384]{2,1,0:T(8,128)(2,1)}, bf16[5,768,384]{2,1,0:T(8,128)(2,1)S(1)}, u32[]{:S(2)}, u32[]{:S(2)}) collective-permute-start(bf16[5,768,384]{2,1,0:T(8,128)(2,1)} %get-tuple-element.299), channel_id=1, source_target_pairs={{0,4},{4,0},{8,12},{12,8},{16,20},{20,16},{24,28},{28,24},{1,5},{5... | collective-permute-start | bytes 8847368 | tf_op jit(solution)/shard_map/ppermute | solution.py:399
  266.7 102.9 %all-to-all-start.1 = ((bf16[4,256,768]{2,1,0:T(8,128)(2,1)}), bf16[4,256,768]{2,1,0:T(8,128)(2,1)}, u32[]{:S(2)}, u32[]{:S(2)}) async-start(bf16[4,256,768]{2,1,0:T(8,128)(2,1)} %bitcast.115), calls=%async_computation.1 | async-start | bytes 3145728 | tf_op jit(solution)/shard_map/all_to_all | solution.py:717
  275.0 51.6 %collective-permute-start.34 = (bf16[3,2,1,24,1024]{4,3,2,1,0:T(8,128)(2,1)}, bf16[3,2,1,24,1024]{4,3,2,1,0:T(8,128)(2,1)}, u32[]{:S(2)}, u32[]{:S(2)}) collective-permute-start(bf16[3,2,1,24,1024]{4,3,2,1,0:T(8,128)(2,1)} %get-tuple-element.339), channel_id=1, source_target_pairs={{0,1},{1,2},{2,3},{3,0},{4,5},{5,6},{6,7},{7,4},{8,9},{9,10},{10,1... | collective-permute-start | bytes 884744 | tf_op jit(solution)/shard_map/ppermute | solution.py:403
  277.0 51.6 %collective-permute-start.35 = (bf16[3,2,1,24,1024]{4,3,2,1,0:T(8,128)(2,1)}, bf16[3,2,1,24,1024]{4,3,2,1,0:T(8,128)(2,1)}, u32[]{:S(2)}, u32[]{:S(2)}) collective-permute-start(bf16[3,2,1,24,1024]{4,3,2,1,0:T(8,128)(2,1)} %get-tuple-element.340), channel_id=1, source_target_pairs={{0,2},{1,3},{2,0},{3,1},{4,6},{5,7},{6,4},{7,5},{8,10},{9,11},{10,... | collective-permute-start | bytes 884744 | tf_op jit(solution)/shard_map/ppermute | solution.py:403
  279.4 49.3 %collective-permute-start.36 = (bf16[3,2,1,24,1024]{4,3,2,1,0:T(8,128)(2,1)}, bf16[3,2,1,24,1024]{4,3,2,1,0:T(8,128)(2,1)}, u32[]{:S(2)}, u32[]{:S(2)}) collective-permute-start(bf16[3,2,1,24,1024]{4,3,2,1,0:T(8,128)(2,1)} %get-tuple-element.341), channel_id=1, source_target_pairs={{0,3},{1,0},{2,1},{3,2},{4,7},{5,4},{6,5},{7,6},{8,11},{9,8},{10,9... | collective-permute-start | bytes 884744 | tf_op jit(solution)/shard_map/ppermute | solution.py:403
  285.3 25.7 %collective-permute-start.32 = (bf16[5,2,192,384]{3,2,1,0:T(8,128)(2,1)}, bf16[5,2,192,384]{3,2,1,0:T(8,128)(2,1)}, u32[]{:S(2)}, u32[]{:S(2)}) collective-permute-start(bf16[5,2,192,384]{3,2,1,0:T(8,128)(2,1)} %get-tuple-element.322), channel_id=1, source_target_pairs={{0,16},{4,12},{8,24},{12,4},{16,0},{20,28},{24,8},{28,20},{1,17},{... | collective-permute-start | bytes 4423688 | tf_op jit(solution)/shard_map/ppermute | solution.py:395
  314.9 22.4 %collective-permute-start.38 = (bf16[5,1,192,384]{3,2,1,0:T(8,128)(2,1)S(1)}, bf16[5,1,192,384]{3,2,1,0:T(8,128)(2,1)S(1)}, u32[]{:S(2)}, u32[]{:S(2)}) collective-permute-start(bf16[5,1,192,384]{3,2,1,0:T(8,128)(2,1)S(1)} %get-tuple-element.351), channel_id=1, source_target_pairs={{0,8},{4,20},{8,0},{12,28},{16,24},{20,4},{24,16},{28,12},{1,9},{5... | collective-permute-start | bytes 2211848 | tf_op jit(solution)/shard_map/ppermute | solution.py:395
  317.1 18.3 %collective-permute-start.33 = (bf16[3,2,192,384]{3,2,1,0:T(8,128)(2,1)S(1)}, bf16[3,2,192,384]{3,2,1,0:T(8,128)(2,1)S(1)}, u32[]{:S(2)}, u32[]{:S(2)}) collective-permute-start(bf16[3,2,192,384]{3,2,1,0:T(8,128)(2,1)S(1)} %get-tuple-element.337), channel_id=1, source_target_pairs={{0,16},{4,12},{8,24},{12,4},{16,0},{20,28},{24,8},{28,20},{1,17},{... | collective-permute-start | bytes 2654216 | tf_op jit(solution)/shard_map/ppermute | solution.py:395
  336.2 8.4 %collective-permute-start.37 = (bf16[3,1,192,384]{3,2,1,0:T(8,128)(2,1)S(1)}, bf16[3,1,192,384]{3,2,1,0:T(8,128)(2,1)S(1)}, u32[]{:S(2)}, u32[]{:S(2)}) collective-permute-start(bf16[3,1,192,384]{3,2,1,0:T(8,128)(2,1)S(1)} %get-tuple-element.349), channel_id=1, source_target_pairs={{0,8},{4,20},{8,0},{12,28},{16,24},{20,4},{24,16},{28,12},{1,9},{5... | collective-permute-start | bytes 1327112 | tf_op jit(solution)/shard_map/ppermute | solution.py:395
  338.0 11.0 %collective-permute-start.42 = (bf16[5,2,1,24,384]{4,3,2,1,0:T(8,128)(2,1)S(1)}, bf16[5,2,1,24,384]{4,3,2,1,0:T(8,128)(2,1)S(1)}, u32[]{:S(2)}, u32[]{:S(2)}) collective-permute-start(bf16[5,2,1,24,384]{4,3,2,1,0:T(8,128)(2,1)S(1)} %get-tuple-element.371), channel_id=1, source_target_pairs={{0,1},{1,2},{2,3},{3,0},{4,5},{5,6},{6,7},{7,4},{8,9},{9,10},{10,1... | collective-permute-start | bytes 552968 | tf_op jit(solution)/shard_map/ppermute | solution.py:403
  340.3 15.1 %collective-permute-start.43 = (bf16[5,2,1,24,384]{4,3,2,1,0:T(8,128)(2,1)S(1)}, bf16[5,2,1,24,384]{4,3,2,1,0:T(8,128)(2,1)S(1)}, u32[]{:S(2)}, u32[]{:S(2)}) collective-permute-start(bf16[5,2,1,24,384]{4,3,2,1,0:T(8,128)(2,1)S(1)} %get-tuple-element.372), channel_id=1, source_target_pairs={{0,2},{1,3},{2,0},{3,1},{4,6},{5,7},{6,4},{7,5},{8,10},{9,11},{10,... | collective-permute-start | bytes 552968 | tf_op jit(solution)/shard_map/ppermute | solution.py:403
  341.8 13.6 %collective-permute-start.44 = (bf16[5,2,1,24,384]{4,3,2,1,0:T(8,128)(2,1)S(1)}, bf16[5,2,1,24,384]{4,3,2,1,0:T(8,128)(2,1)S(1)}, u32[]{:S(2)}, u32[]{:S(2)}) collective-permute-start(bf16[5,2,1,24,384]{4,3,2,1,0:T(8,128)(2,1)S(1)} %get-tuple-element.373), channel_id=1, source_target_pairs={{0,3},{1,0},{2,1},{3,2},{4,7},{5,4},{6,5},{7,6},{8,11},{9,8},{10,9... | collective-permute-start | bytes 552968 | tf_op jit(solution)/shard_map/ppermute | solution.py:403
  345.3 12.5 %collective-permute-start.39 = (bf16[3,2,1,24,384]{4,3,2,1,0:T(8,128)(2,1)S(1)}, bf16[3,2,1,24,384]{4,3,2,1,0:T(8,128)(2,1)S(1)}, u32[]{:S(2)}, u32[]{:S(2)}) collective-permute-start(bf16[3,2,1,24,384]{4,3,2,1,0:T(8,128)(2,1)S(1)} %get-tuple-element.367), channel_id=1, source_target_pairs={{0,1},{1,2},{2,3},{3,0},{4,5},{5,6},{6,7},{7,4},{8,9},{9,10},{10,1... | collective-permute-start | bytes 331784 | tf_op jit(solution)/shard_map/ppermute | solution.py:403
  347.6 18.2 %collective-permute-start.40 = (bf16[3,2,1,24,384]{4,3,2,1,0:T(8,128)(2,1)S(1)}, bf16[3,2,1,24,384]{4,3,2,1,0:T(8,128)(2,1)S(1)}, u32[]{:S(2)}, u32[]{:S(2)}) collective-permute-start(bf16[3,2,1,24,384]{4,3,2,1,0:T(8,128)(2,1)S(1)} %get-tuple-element.368), channel_id=1, source_target_pairs={{0,2},{1,3},{2,0},{3,1},{4,6},{5,7},{6,4},{7,5},{8,10},{9,11},{10,... | collective-permute-start | bytes 331784 | tf_op jit(solution)/shard_map/ppermute | solution.py:403
  349.0 16.7 %collective-permute-start.41 = (bf16[3,2,1,24,384]{4,3,2,1,0:T(8,128)(2,1)S(1)}, bf16[3,2,1,24,384]{4,3,2,1,0:T(8,128)(2,1)S(1)}, u32[]{:S(2)}, u32[]{:S(2)}) collective-permute-start(bf16[3,2,1,24,384]{4,3,2,1,0:T(8,128)(2,1)S(1)} %get-tuple-element.369), channel_id=1, source_target_pairs={{0,3},{1,0},{2,1},{3,2},{4,7},{5,4},{6,5},{7,6},{8,11},{9,8},{10,9... | collective-permute-start | bytes 331784 | tf_op jit(solution)/shard_map/ppermute | solution.py:403
  367.3 6.5 %collective-permute-start.52 = (f32[3,24,1024]{2,1,0:T(8,128)S(1)}, f32[3,24,1024]{2,1,0:T(8,128)S(1)}, u32[]{:S(2)}, u32[]{:S(2)}) collective-permute-start(f32[3,24,1024]{2,1,0:T(8,128)S(1)} %dynamic-slice_bitcast_fusion), channel_id=1, source_target_pairs={{0,4},{4,0},{8,12},{12,8},{16,20},{20,16},{24,28},{28,24},{1,5},{5... | collective-permute-start | bytes 884744 | tf_op jit(solution)/shard_map/ppermute | solution.py:399
  379.3 13.6 %collective-permute-start.51 = (f32[5,24,384]{2,1,0:T(8,128)S(1)}, f32[5,24,384]{2,1,0:T(8,128)S(1)}, u32[]{:S(2)}, u32[]{:S(2)}) collective-permute-start(f32[5,24,384]{2,1,0:T(8,128)S(1)} %dynamic-slice_bitcast_fusion.1), channel_id=1, source_target_pairs={{0,4},{4,0},{8,12},{12,8},{16,20},{20,16},{24,28},{28,24},{1,5},{5... | collective-permute-start | bytes 552968 | tf_op jit(solution)/shard_map/ppermute | solution.py:399
  382.0 10.9 %collective-permute-start.50 = (f32[3,24,384]{2,1,0:T(8,128)S(1)}, f32[3,24,384]{2,1,0:T(8,128)S(1)}, u32[]{:S(2)}, u32[]{:S(2)}) collective-permute-start(f32[3,24,384]{2,1,0:T(8,128)S(1)} %dynamic-slice_bitcast_fusion.2), channel_id=1, source_target_pairs={{0,4},{4,0},{8,12},{12,8},{16,20},{20,16},{24,28},{28,24},{1,5},{5... | collective-permute-start | bytes 331784 | tf_op jit(solution)/shard_map/ppermute | solution.py:399
  (75 other events, 666.5 us)

commit v6 on v5

--- a/solution.py
+++ b/solution.py
@@ -124,7 +124,7 @@
 
 def bwd_part_kernel(*refs,**kw):
     bwd_kernel(*refs[:7],*refs[10:],**kw)
-def attn_bwd(n,q,k,v,oT,gT,lse,causal,bq=256,hs=2,part=None,into=None):
+def attn_bwd(n,q,k,v,oT,gT,lse,causal,bq=256,hs=2,part=None,into=None,vmem=VA):
     L=q[0].shape[1]; K=k[0].shape[1]; D=HEADS*HD
     h0,hn=part or (0,HEADS)
     hb=lambda w,o=0: head_block(hs,w,o+h0)
@@ -139,7 +139,7 @@
       out_shape=[S((D,L),bf),S((D,K),bf),S((D,K),bf)],
       input_output_aliases={} if into is None else {7:0,8:1,9:2},
       scratch_shapes=[pltpu.VMEM((hs*HD,K),f32),pltpu.VMEM((hs*HD,K),f32)],
-      cost_estimate=cost(14),compiler_params=pltpu.CompilerParams(vmem_limit_bytes=VA),
+      cost_estimate=cost(14),compiler_params=pltpu.CompilerParams(vmem_limit_bytes=vmem),
     )(*args)
 
 TT=(((0,),(1,)),((),()))
@@ -710,7 +710,7 @@
     w_index,w_parts=g3.parts()
     mixed_out,gh2,gm2,gb2,dg3,mlp_send,mlp_keep=mlp(core,w_index,table_len,h1,o2,w_second,cotangent[0],gains,w_parts)
     r1=Reduce(mlp_send,mlp_keep,here)
-    part=attn_bwd(patch_count,q2,k2,v2,o2,gm2,lse2,False,256,2,(0,half))
+    part=attn_bwd(patch_count,q2,k2,v2,o2,gm2,lse2,False,256,2,(0,half),None,VB)
     part=(r1.fold(part[0]),)+tuple(part[1:])
     dcq,dmk,dmv=attn_bwd(patch_count,q2,k2,v2,o2,gm2,lse2,False,256,2,(half,half),part)
     gmem_local,dcq=tie(gmem(dmk,dmv,w_second),dcq)

time: 400 us -> 404 us (1.010)
  Pallas kernels: 207 us -> 213 us
    pallas_call x6, Pallas kernels: 18.2 us -> 22.3 us  [fold(): pl.pallas_call(fold_kernel, grid_spec=pltpu.PrefetchScalarGridSpec(num_sc...]
    unnamed x143 -> x149, local copies, waits for them, and re-layouts: 26.8 us -> 24.8 us
where the time goes in v6:
time: 404 us; the launch traced here: 400 us
  Pallas kernels  213 us (53%)
  starting transfers between devices  68.5 us (17%)
  waiting for transfers between devices  68.1 us (17%)
  local copies, waits for them, and re-layouts  25.7 us (6%)
  other arithmetic  16.8 us (4%)
  between operations  8.03 us (2%)
    pallas_call x3, Pallas kernels, attn_bwd(): pl.pallas_call(functools.partial(bwd_kernel if into is None else bwd_part...  53.2 us
    pallas_call x1, Pallas kernels, mlp(): pl.pallas_call(functools.partial(mlp_kernel, tb=tb, pieces=count), grid_s...  44.1 us
    pallas_call x4, Pallas kernels, attn_fwd(): pl.pallas_call(functools.partial(fwd_kernel if into is None else fwd_part...  32.2 us
    ppermute x15, waiting for transfers between devices, shift_mem(): lax.ppermute(x, MEM, [(z, (z + step) % mem_size) for z in range(mem_size)])  32 us
    ppermute x15, starting transfers between devices, shift_mem(): lax.ppermute(x, MEM, [(z, (z + step) % mem_size) for z in range(mem_size)])  27.6 us
    ppermute x15, waiting for transfers between devices, cross(): return lax.ppermute(x, SEQ, perm)  25.3 us
    unnamed x149, local copies, waits for them, and re-layouts  24.8 us
    pallas_call x6, Pallas kernels, fold(): pl.pallas_call(fold_kernel, grid_spec=pltpu.PrefetchScalarGridSpec(num_sc...  22.3 us
  transfers between devices with their start and end apart: 55, of which 20 were waited for; matrix products, arithmetic and copies ran while one was open for 4% of the time, Pallas kernels for 39%

profile of v6, /device:TPU:0, one launch (start us, length us, event | category | flops | bytes accessed | tf_op | source)
XLA Modules:
  0.0 400.3 jit_solution(8444496482376318863)
XLA Ops:
  2.6 3.1 collective-permute-start
  5.7 2.6 collective-permute-start.1
  11.9 4.2 %collective-permute-done.1.refs_2_ = bf16[24,2432]{1,0:T(8,128)(2,1)S(1)} collective-permute-done((bf16[24,2432]{1,0:T(8,128)(2,1)S(1)}, bf16[24,2432]{1,0:T(8,128)(2,1)S(1)}, u32[]{:S(2)}, u32[]{:S(2)}) %collective-permute-start.1) | collective-permute-done | bytes 116768 | tf_op jit(solution)/shard_map/ppermute | solution.py:403
  18.8 3.0 collective-permute-start.4
  23.3 4.5 %collective-permute-done.3.refs_1_ = bf16[96,2432]{1,0:T(8,128)(2,1)S(1)} collective-permute-done((bf16[96,2432]{1,0:T(8,128)(2,1)S(1)}, bf16[96,2432]{1,0:T(8,128)(2,1)S(1)}, u32[]{:S(2)}, u32[]{:S(2)}) %collective-permute-start.3) | collective-permute-done | bytes 466976 | tf_op jit(solution)/shard_map/ppermute | solution.py:395
  27.8 2.7 collective-permute-start.6
  30.5 2.7 collective-permute-done.4.refs_1_
  38.9 7.5 %collective-permute-done.7.refs_2_ = bf16[24,9984]{1,0:T(8,128)(2,1)S(1)} collective-permute-done((bf16[24,9984]{1,0:T(8,128)(2,1)S(1)}, bf16[24,9984]{1,0:T(8,128)(2,1)S(1)}, u32[]{:S(2)}, u32[]{:S(2)}) %collective-permute-start.7) | collective-permute-done | bytes 479264 | tf_op jit(solution)/shard_map/ppermute | solution.py:403
  47.9 2.9 shard_map.238
  50.8 6.3 %shard_map.239 = (bf16[1024,768]{1,0:T(8,128)(2,1)S(1)}, bf16[2304,1024]{1,0:T(8,128)(2,1)S(1)}, f32[8,768]{1,0:T(8,128)S(1)}) custom-call(bf16[1024,768]{1,0:T(8,128)(2,1)S(1)} %bitcast.125, bf16[768,2432]{1,0:T(8,128)(2,1)S(1)} %bitcast.116, bf16[768,2432]{1,0:T(8,128)(2,1)S(1)} %bitcast.117), custom_call_target="tpu_custom_call" | custom-call | flops 60000002048 | bytes 100000 | tf_op jit(solution)/shard_map/pallas_call | solution.py:167
  60.2 3.2 collective-permute-start.13
  63.4 4.5 %all-to-all-start = ((bf16[4,256,768]{2,1,0:T(8,128)(2,1)}), bf16[4,256,768]{2,1,0:T(8,128)(2,1)S(1)}, u32[]{:S(2)}, u32[]{:S(2)}) async-start(bf16[4,256,768]{2,1,0:T(8,128)(2,1)} %param.15), calls=%async_computation | async-start | bytes 3145728 | tf_op jit(solution)/shard_map/all_to_all | solution.py:681
  71.0 7.0 %shard_map.241 = (bf16[768,1024]{1,0:T(8,128)(2,1)S(1)}, f32[12,1,1024]{2,1,0:T(1,128)S(1)}) custom-call(s32[1]{0:T(128)S(6)} %copy.49.len_ref.refs_0_, bf16[2304,1024]{1,0:T(8,128)(2,1)S(1)} %copy-done.4, bf16[2304,1024]{1,0:T(8,128)(2,1)S(1)} %copy-done.4, bf16[2304,1024]{1,0:T(8,128)(2,1)S(1)} %copy-done.4), custom_call_target="tpu_custom_call" | custom-call | flops 3000000000 | bytes 100000 | tf_op jit(solution)/shard_map/pallas_call | solution.py:77
  84.0 10.6 %collective-permute-done.17.refs_3_ = bf16[96,3840]{1,0:T(8,128)(2,1)S(1)} collective-permute-done((bf16[96,3840]{1,0:T(8,128)(2,1)}, bf16[96,3840]{1,0:T(8,128)(2,1)S(1)}, u32[]{:S(2)}, u32[]{:S(2)}) %collective-permute-start.17) | collective-permute-done | bytes 737312 | tf_op jit(solution)/shard_map/ppermute | solution.py:395
  94.6 2.4 collective-permute-start.16
  97.0 3.5 shard_map.243
  104.6 2.5 shard_map.244
  107.1 2.5 copy-done
  109.6 2.7 copy-done.1
  112.2 3.6 shard_map.245.kT_ref.vT_ref.refs_2_.refs_3_
  120.4 5.7 %shard_map.246 = (f32[1024,768]{1,0:T(8,128)S(1)}, bf16[1024,768]{1,0:T(8,128)(2,1)S(1)}, bf16[768,1024]{1,0:T(8,128)(2,1)S(1)}) custom-call(bf16[1024,768]{1,0:T(8,128)(2,1)S(1)} %bitcast.126, bf16[768,1024]{1,0:T(8,128)(2,1)S(1)} %copy-done.7, bf16[768,3840]{1,0:T(8,128)(2,1)S(1)} %bitcast.101, bf16[768,3840]{1,0:T(8,128)(2,1)S(1)} %bitcast.102, ...), custom_call_target="tpu_custom_call" | custom-call | flops 3000000000 | bytes 100000 | tf_op jit(solution)/shard_map/pallas_call | solution.py:189
  130.1 11.1 %shard_map.247 = (bf16[768,1024]{1,0:T(8,128)(2,1)}, f32[12,1,1024]{2,1,0:T(1,128)}) custom-call(s32[1]{0:T(128)S(6)} %copy.50.len_ref.refs_0_, bf16[768,1024]{1,0:T(8,128)(2,1)} %copy-done.40, bf16[1536,1024]{1,0:T(8,128)(2,1)} %copy-done.12, bf16[1536,1024]{1,0:T(8,128)(2,1)} %copy-done.12), custom_call_target="tpu_custom_call" | custom-call | flops 3000000000 | bytes 100000 | tf_op jit(solution)/shard_map/pallas_call | solution.py:77
  141.4 10.7 %shard_map.248 = (bf16[768,1024]{1,0:T(8,128)(2,1)}, f32[12,1,1024]{2,1,0:T(1,128)}) custom-call(s32[1]{0:T(128)S(6)} %copy.50.len_ref.refs_0_, bf16[768,1024]{1,0:T(8,128)(2,1)} %copy-done.40, bf16[1536,1024]{1,0:T(8,128)(2,1)} %copy-done.12, bf16[1536,1024]{1,0:T(8,128)(2,1)} %copy-done.12, ...), custom_call_target="tpu_custom_call", output_to_operand_aliasing={{0}: (4, {}), {1}: (5, {})} | custom-call | flops 3000000000 | bytes 100000 | tf_op jit(solution)/shard_map/pallas_call | solution.py:77
  152.1 44.1 %shard_map.249 = (bf16[1024,768]{1,0:T(8,128)(2,1)}, f32[1024,768]{1,0:T(8,128)}, bf16[768,1024]{1,0:T(8,128)(2,1)}, bf16[1024,768]{1,0:T(8,128)(2,1)}, f32[1,76...) custom-call(s32[1]{0:T(128)} %bitcast.core_ref, s32[8]{0:T(128)S(1)} %stack.54.index_ref, ...), custom_call_target="tpu_custom_call" | custom-call | flops 420000006144 | bytes 100000 | tf_op jit(solution)/shard_map/pallas_call | solution.py:289
  196.7 18.0 %shard_map.250 = (bf16[768,1024]{1,0:T(8,128)(2,1)}, bf16[768,1024]{1,0:T(8,128)(2,1)}, bf16[768,1024]{1,0:T(8,128)(2,1)}) custom-call(s32[1]{0:T(128)S(6)} %copy.50.len_ref.refs_0_, bf16[768,1024]{1,0:T(8,128)(2,1)} %copy-done.40, bf16[1536,1024]{1,0:T(8,128)(2,1)} %copy-done.12, bf16[1536,1024]{1,0:T(8,128)(2,1)} %copy-done.12, ...), custom_call_target="tpu_custom_call" | custom-call | flops 140000002048 | bytes 100000 | tf_op jit(solution)/shard_map/pallas_call | solution.py:137
  217.1 7.4 %shard_map.251 = (bf16[3,2,192,1024]{3,2,1,0:T(8,128)(2,1)}, bf16[3,2,192,1024]{3,2,1,0:T(8,128)(2,1)S(1)}) custom-call(s32[4]{0:T(128)S(1)} %get-tuple-element.417.index_ref, bf16[3,4,192,1024]{3,2,1,0:T(8,128)(2,1)S(1)} %bitcast.138, bf16[3,4,192,1024]{3,2,1,0:T(8,128)(2,1)S(1)} %bitcast.139, bf16[3,4,192,1024]{3,2,1,0:T(8,128)(2,1)} %bitcast.39.ra.rb, ...), custom_call_target="tpu_custom_call" | custom-call | flops 30000001024 | bytes 100000 | tf_op jit(solution)/shard_map/pallas_call | solution.py:542
  224.8 15.7 %shard_map.252 = (bf16[768,1024]{1,0:T(8,128)(2,1)S(1)}, bf16[768,1024]{1,0:T(8,128)(2,1)S(1)}, bf16[768,1024]{1,0:T(8,128)(2,1)S(1)}) custom-call(s32[1]{0:T(128)S(6)} %copy.50.len_ref.refs_0_, bf16[768,1024]{1,0:T(8,128)(2,1)S(1)} %copy-done.41, bf16[1536,1024]{1,0:T(8,128)(2,1)S(1)} %copy-done.13, ...), custom_call_target="tpu_custom_call", output_to_operand_aliasing={{0}: (7, {}), {1}: (8, {}), {2}: (9, {})} | custom-call | flops 140000002048 | bytes 100000 | tf_op jit(solution)/shard_map/pallas_call | solution.py:137
  240.6 3.9 shard_map.253
  245.7 6.0 %shard_map.254 = (f32[1024,768]{1,0:T(8,128)S(1)}, bf16[768,1024]{1,0:T(8,128)(2,1)S(1)}, bf16[1024,768]{1,0:T(8,128)(2,1)S(1)}, f32[1,768]{1,0:T(1,128)S(1)}) custom-call(f32[1024,768]{1,0:T(8,128)S(1)} %copy-done.15, f32[1024,768]{1,0:T(8,128)S(1)} %copy-done.16, bf16[768,1024]{1,0:T(8,128)(2,1)S(1)} %get-tuple-element.283.dcT_ref.refs_5_, ...), custom_call_target="tpu_custom_call" | custom-call | flops 2000000000 | bytes 100000 | tf_op jit(solution)/shard_map/pallas_call | solution.py:318
  253.6 4.8 %shard_map.255 = (bf16[3,1,192,1024]{3,2,1,0:T(8,128)(2,1)}, bf16[3,1,192,1024]{3,2,1,0:T(8,128)(2,1)S(1)}) custom-call(s32[2]{0:T(128)S(1)} %iota.9.index_ref, bf16[3,2,192,1024]{3,2,1,0:T(8,128)(2,1)S(1)} %get-tuple-element.286.ka.kb, bf16[3,2,192,1024]{3,2,1,0:T(8,128)(2,1)S(1)} %get-tuple-element.286.ka.kb, ...), custom_call_target="tpu_custom_call" | custom-call | flops 30000001024 | bytes 100000 | tf_op jit(solution)/shard_map/pallas_call | solution.py:542
  260.2 10.6 %shard_map.256 = (bf16[5,768,384]{2,1,0:T(8,128)(2,1)}, bf16[5,768,384]{2,1,0:T(8,128)(2,1)}) custom-call(s32[1]{0:T(128)} %bitcast.core_ref, bf16[1024,768]{1,0:T(8,128)(2,1)S(1)} %get-tuple-element.293.refs_0_, bf16[1024,768]{1,0:T(8,128)(2,1)S(1)} %copy-done.39, bf16[1024,768]{1,0:T(8,128)(2,1)S(1)} %bitcast.114, bf16[1024,768]{1,0:T(8,128)(2,1)S(1)} %copy-done.53, ...), custom_call_target="tpu_custom_call" | custom-call | flops 80000000000 | bytes 100000 | tf_op jit(solution)/shard_map/pallas_call | solution.py:335
  270.8 4.6 %all-to-all-start.1 = ((bf16[4,256,768]{2,1,0:T(8,128)(2,1)}), bf16[4,256,768]{2,1,0:T(8,128)(2,1)}, u32[]{:S(2)}, u32[]{:S(2)}) async-start(bf16[4,256,768]{2,1,0:T(8,128)(2,1)} %bitcast.115), calls=%async_computation.1 | async-start | bytes 3145728 | tf_op jit(solution)/shard_map/all_to_all | solution.py:717
  276.7 2.5 shard_map.257
  285.0 4.4 %shard_map.258 = (bf16[5,2,192,384]{3,2,1,0:T(8,128)(2,1)}, bf16[5,2,192,384]{3,2,1,0:T(8,128)(2,1)S(1)}) custom-call(s32[4]{0:T(128)S(1)} %copy-done.34, bf16[5,4,192,384]{3,2,1,0:T(8,128)(2,1)S(1)} %bitcast.140, bf16[5,4,192,384]{3,2,1,0:T(8,128)(2,1)S(1)} %bitcast.141, bf16[5,4,192,384]{3,2,1,0:T(8,128)(2,1)S(1)} %bitcast.132, ...), custom_call_target="tpu_custom_call" | custom-call | flops 30000001024 | bytes 100000 | tf_op jit(solution)/shard_map/pallas_call | solution.py:542
  290.3 19.6 %shard_map.259 = (bf16[768,1024]{1,0:T(8,128)(2,1)S(1)}, bf16[768,1024]{1,0:T(8,128)(2,1)S(1)}, bf16[768,1024]{1,0:T(8,128)(2,1)S(1)}) custom-call(s32[1]{0:T(128)S(6)} %copy.49.len_ref.refs_0_, bf16[2304,1024]{1,0:T(8,128)(2,1)S(1)} %bitcast.112, bf16[2304,1024]{1,0:T(8,128)(2,1)S(1)} %bitcast.112, bf16[2304,1024]{1,0:T(8,128)(2,1)S(1)} %bitcast.112, ...), custom_call_target="tpu_custom_call" | custom-call | flops 140000002048 | bytes 100000 | tf_op jit(solution)/shard_map/pallas_call | solution.py:137
  309.9 5.1 %shard_map.260 = (bf16[3,768,384]{2,1,0:T(8,128)(2,1)S(1)}, bf16[3,768,384]{2,1,0:T(8,128)(2,1)S(1)}) custom-call(s32[1]{0:T(128)} %bitcast.core_ref, bf16[1024,768]{1,0:T(8,128)(2,1)S(1)} %copy-done.52, bf16[768,1024]{1,0:T(8,128)(2,1)S(1)} %get-tuple-element.333.refs_1_.qT_ref, bf16[768,1024]{1,0:T(8,128)(2,1)S(1)} %get-tuple-element.317.refs_2_.kT_ref, ...), custom_call_target="tpu_custom_call" | custom-call | flops 80000000000 | bytes 100000 | tf_op jit(solution)/shard_map/pallas_call | solution.py:335
  315.2 3.8 shard_map.261
  323.5 7.1 %shard_map.263 = (f32[1024,768]{1,0:T(8,128)}, f32[1,768]{1,0:T(1,128)S(1)}) custom-call(bf16[1024,768]{1,0:T(8,128)(2,1)S(1)} %bitcast.127, f32[1024,768]{1,0:T(8,128)S(1)} %copy-done.37, bf16[768,1024]{1,0:T(8,128)(2,1)S(1)} %get-tuple-element.333.refs_1_.qT_ref, bf16[768,1024]{1,0:T(8,128)(2,1)S(1)} %get-tuple-element.317.refs_2_.kT_ref, ...), custom_call_target="tpu_custom_call" | custom-call | flops 70000001024 | bytes 100000 | tf_op jit(solution)/shard_map/pallas_call | solution.py:365
  332.8 2.8 multiply_reduce_fusion
  335.6 3.9 collective-permute-done.33.ra.rb
  342.1 2.4 collective-permute-start.42
  354.4 5.1 %collective-permute-done.43 = bf16[5,2,1,24,384]{4,3,2,1,0:T(8,128)(2,1)S(1)} collective-permute-done((bf16[5,2,1,24,384]{4,3,2,1,0:T(8,128)(2,1)S(1)}, bf16[5,2,1,24,384]{4,3,2,1,0:T(8,128)(2,1)S(1)}, u32[]{:S(2)}, u32[]{:S(2)}) %collective-permute-start.43) | collective-permute-done | bytes 184352 | tf_op jit(solution)/shard_map/ppermute | solution.py:403
  361.9 8.0 %collective-permute-done.40 = bf16[3,2,1,24,384]{4,3,2,1,0:T(8,128)(2,1)S(1)} collective-permute-done((bf16[3,2,1,24,384]{4,3,2,1,0:T(8,128)(2,1)S(1)}, bf16[3,2,1,24,384]{4,3,2,1,0:T(8,128)(2,1)S(1)}, u32[]{:S(2)}, u32[]{:S(2)}) %collective-permute-start.40) | collective-permute-done | bytes 110624 | tf_op jit(solution)/shard_map/ppermute | solution.py:403
  373.7 3.3 convert_element_type.50
  378.0 2.9 collective-permute-done.47
  380.9 2.6 collective-permute-start.48
  386.2 3.5 collective-permute-done.49
  392.9 2.7 multiply_subtract_fusion
  (279 shorter events, 88.4 us)
Async XLA Ops:
  2.6 9.2 %collective-permute-start = (bf16[24,2432]{1,0:T(8,128)(2,1)S(1)}, bf16[24,2432]{1,0:T(8,128)(2,1)S(1)}, u32[]{:S(2)}, u32[]{:S(2)}) collective-permute-start(bf16[24,2432]{1,0:T(8,128)(2,1)S(1)} %fusion.3.refs_0_), channel_id=1, source_target_pairs={{0,1},{1,2},{2,3},{3,0},{4,5},{5,6},{6,7},{7,4},{8,9},{9,10},{10,1... | collective-permute-start | bytes 350216 | tf_op jit(solution)/shard_map/ppermute | solution.py:403
  5.7 10.3 %collective-permute-start.1 = (bf16[24,2432]{1,0:T(8,128)(2,1)S(1)}, bf16[24,2432]{1,0:T(8,128)(2,1)S(1)}, u32[]{:S(2)}, u32[]{:S(2)}) collective-permute-start(bf16[24,2432]{1,0:T(8,128)(2,1)S(1)} %fusion.3.refs_0_), channel_id=1, source_target_pairs={{0,2},{1,3},{2,0},{3,1},{4,6},{5,7},{6,4},{7,5},{8,10},{9,11},{10,... | collective-permute-start | bytes 350216 | tf_op jit(solution)/shard_map/ppermute | solution.py:403
  8.3 7.7 %collective-permute-start.2 = (bf16[24,2432]{1,0:T(8,128)(2,1)S(1)}, bf16[24,2432]{1,0:T(8,128)(2,1)S(1)}, u32[]{:S(2)}, u32[]{:S(2)}) collective-permute-start(bf16[24,2432]{1,0:T(8,128)(2,1)S(1)} %fusion.3.refs_0_), channel_id=1, source_target_pairs={{0,3},{1,0},{2,1},{3,2},{4,7},{5,4},{6,5},{7,6},{8,11},{9,8},{10,9... | collective-permute-start | bytes 350216 | tf_op jit(solution)/shard_map/ppermute | solution.py:403
  17.2 10.5 %collective-permute-start.3 = (bf16[96,2432]{1,0:T(8,128)(2,1)S(1)}, bf16[96,2432]{1,0:T(8,128)(2,1)S(1)}, u32[]{:S(2)}, u32[]{:S(2)}) collective-permute-start(bf16[96,2432]{1,0:T(8,128)(2,1)S(1)} %bitcast.128), channel_id=1, source_target_pairs={{0,8},{4,20},{8,0},{12,28},{16,24},{20,4},{24,16},{28,12},{1,9},{5... | collective-permute-start | bytes 1400840 | tf_op jit(solution)/shard_map/ppermute | solution.py:395
  18.8 14.3 %collective-permute-start.4 = (bf16[24,9984]{1,0:T(8,128)(2,1)S(1)}, bf16[24,9984]{1,0:T(8,128)(2,1)S(1)}, u32[]{:S(2)}, u32[]{:S(2)}) collective-permute-start(bf16[24,9984]{1,0:T(8,128)(2,1)S(1)} %fusion.4.refs_0_), channel_id=1, source_target_pairs={{0,1},{1,2},{2,3},{3,0},{4,5},{5,6},{6,7},{7,4},{8,9},{9,10},{10,1... | collective-permute-start | bytes 1437704 | tf_op jit(solution)/shard_map/ppermute | solution.py:403
  21.8 8.7 %collective-permute-start.5 = (bf16[96,2432]{1,0:T(8,128)(2,1)S(1)}, bf16[96,2432]{1,0:T(8,128)(2,1)}, u32[]{:S(2)}, u32[]{:S(2)}) collective-permute-start(bf16[96,2432]{1,0:T(8,128)(2,1)S(1)} %bitcast.129), channel_id=1, source_target_pairs={{0,16},{4,12},{8,24},{12,4},{16,0},{20,28},{24,8},{28,20},{1,17},{... | collective-permute-start | bytes 1400840 | tf_op jit(solution)/shard_map/ppermute | solution.py:395
  27.8 9.2 %collective-permute-start.6 = (bf16[96,2432]{1,0:T(8,128)(2,1)S(1)}, bf16[96,2432]{1,0:T(8,128)(2,1)S(1)}, u32[]{:S(2)}, u32[]{:S(2)}) collective-permute-start(bf16[96,2432]{1,0:T(8,128)(2,1)S(1)} %collective-permute-done.3.refs_1_), channel_id=1, source_target_pairs={{0,16},{4,12},{8,24},{12,4},{16,0},{20,28},{24,8},{28,20},{1,17},{... | collective-permute-start | bytes 1400840 | tf_op jit(solution)/shard_map/ppermute | solution.py:395
  33.2 13.2 %collective-permute-start.7 = (bf16[24,9984]{1,0:T(8,128)(2,1)S(1)}, bf16[24,9984]{1,0:T(8,128)(2,1)S(1)}, u32[]{:S(2)}, u32[]{:S(2)}) collective-permute-start(bf16[24,9984]{1,0:T(8,128)(2,1)S(1)} %collective-permute-done.4.refs_1_), channel_id=1, source_target_pairs={{0,1},{1,2},{2,3},{3,0},{4,5},{5,6},{6,7},{7,4},{8,9},{9,10},{10,1... | collective-permute-start | bytes 1437704 | tf_op jit(solution)/shard_map/ppermute | solution.py:403
  37.0 9.4 %collective-permute-start.8 = (bf16[96,2432]{1,0:T(8,128)(2,1)S(1)}, bf16[96,2432]{1,0:T(8,128)(2,1)}, u32[]{:S(2)}, u32[]{:S(2)}) collective-permute-start(bf16[96,2432]{1,0:T(8,128)(2,1)S(1)} %collective-permute-done.6.refs_3_), channel_id=1, source_target_pairs={{0,4},{4,0},{8,12},{12,8},{16,20},{20,16},{24,28},{28,24},{1,5},{5... | collective-permute-start | bytes 1400840 | tf_op jit(solution)/shard_map/ppermute | solution.py:399
  37.8 9.1 %collective-permute-start.10 = (bf16[96,2432]{1,0:T(8,128)(2,1)S(1)}, bf16[96,2432]{1,0:T(8,128)(2,1)}, u32[]{:S(2)}, u32[]{:S(2)}) collective-permute-start(bf16[96,2432]{1,0:T(8,128)(2,1)S(1)} %bitcast.130), channel_id=1, source_target_pairs={{0,4},{4,0},{8,12},{12,8},{16,20},{20,16},{24,28},{28,24},{1,5},{5... | collective-permute-start | bytes 1400840 | tf_op jit(solution)/shard_map/ppermute | solution.py:399
  38.3 8.6 %collective-permute-start.11 = (bf16[96,2432]{1,0:T(8,128)(2,1)S(1)}, bf16[96,2432]{1,0:T(8,128)(2,1)}, u32[]{:S(2)}, u32[]{:S(2)}) collective-permute-start(bf16[96,2432]{1,0:T(8,128)(2,1)S(1)} %collective-permute-done.3.refs_1_), channel_id=1, source_target_pairs={{0,4},{4,0},{8,12},{12,8},{16,20},{20,16},{24,28},{28,24},{1,5},{5... | collective-permute-start | bytes 1400840 | tf_op jit(solution)/shard_map/ppermute | solution.py:399
  38.3 8.6 %collective-permute-start.12 = (bf16[96,2432]{1,0:T(8,128)(2,1)}, bf16[96,2432]{1,0:T(8,128)(2,1)}, u32[]{:S(2)}, u32[]{:S(2)}) collective-permute-start(bf16[96,2432]{1,0:T(8,128)(2,1)} %collective-permute-done.5.refs_2_), channel_id=1, source_target_pairs={{0,4},{4,0},{8,12},{12,8},{16,20},{20,16},{24,28},{28,24},{1,5},{5... | collective-permute-start | bytes 1400840 | tf_op jit(solution)/shard_map/ppermute | solution.py:399
  46.4 12.9 %collective-permute-start.9 = (bf16[24,9984]{1,0:T(8,128)(2,1)S(1)}, bf16[24,9984]{1,0:T(8,128)(2,1)S(1)}, u32[]{:S(2)}, u32[]{:S(2)}) collective-permute-start(bf16[24,9984]{1,0:T(8,128)(2,1)S(1)} %collective-permute-done.7.refs_2_), channel_id=1, source_target_pairs={{0,1},{1,2},{2,3},{3,0},{4,5},{5,6},{6,7},{7,4},{8,9},{9,10},{10,1... | collective-permute-start | bytes 1437704 | tf_op jit(solution)/shard_map/ppermute | solution.py:403
  60.2 18.1 %collective-permute-start.13 = (bf16[96,3840]{1,0:T(8,128)(2,1)S(1)}, bf16[96,3840]{1,0:T(8,128)(2,1)}, u32[]{:S(2)}, u32[]{:S(2)}) collective-permute-start(bf16[96,3840]{1,0:T(8,128)(2,1)S(1)} %bitcast.121), channel_id=1, source_target_pairs={{0,8},{4,20},{8,0},{12,28},{16,24},{20,4},{24,16},{28,12},{1,9},{5... | collective-permute-start | bytes 2211848 | tf_op jit(solution)/shard_map/ppermute | solution.py:395
  63.4 14.9 %collective-permute-start.14 = (bf16[96,3840]{1,0:T(8,128)(2,1)S(1)}, bf16[96,3840]{1,0:T(8,128)(2,1)}, u32[]{:S(2)}, u32[]{:S(2)}) collective-permute-start(bf16[96,3840]{1,0:T(8,128)(2,1)S(1)} %bitcast.122), channel_id=1, source_target_pairs={{0,16},{4,12},{8,24},{12,4},{16,0},{20,28},{24,8},{28,20},{1,17},{... | collective-permute-start | bytes 2211848 | tf_op jit(solution)/shard_map/ppermute | solution.py:395
  63.4 46.1 %all-to-all-start = ((bf16[4,256,768]{2,1,0:T(8,128)(2,1)}), bf16[4,256,768]{2,1,0:T(8,128)(2,1)S(1)}, u32[]{:S(2)}, u32[]{:S(2)}) async-start(bf16[4,256,768]{2,1,0:T(8,128)(2,1)} %param.15), calls=%async_computation | async-start | bytes 3145728 | tf_op jit(solution)/shard_map/all_to_all | solution.py:681
  78.3 16.3 %collective-permute-start.17 = (bf16[96,3840]{1,0:T(8,128)(2,1)}, bf16[96,3840]{1,0:T(8,128)(2,1)S(1)}, u32[]{:S(2)}, u32[]{:S(2)}) collective-permute-start(bf16[96,3840]{1,0:T(8,128)(2,1)} %collective-permute-done.13.refs_1_), channel_id=1, source_target_pairs={{0,16},{4,12},{8,24},{12,4},{16,0},{20,28},{24,8},{28,20},{1,17},{... | collective-permute-start | bytes 2211848 | tf_op jit(solution)/shard_map/ppermute | solution.py:395
  80.1 22.2 %collective-permute-start.19 = (bf16[96,3840]{1,0:T(8,128)(2,1)}, bf16[96,3840]{1,0:T(8,128)(2,1)S(1)}, u32[]{:S(2)}, u32[]{:S(2)}) collective-permute-start(bf16[96,3840]{1,0:T(8,128)(2,1)} %collective-permute-done.13.refs_1_), channel_id=1, source_target_pairs={{0,4},{4,0},{8,12},{12,8},{16,20},{20,16},{24,28},{28,24},{1,5},{5... | collective-permute-start | bytes 2211848 | tf_op jit(solution)/shard_map/ppermute | solution.py:399
  80.1 22.2 %collective-permute-start.18 = (bf16[96,3840]{1,0:T(8,128)(2,1)S(1)}, bf16[96,3840]{1,0:T(8,128)(2,1)S(1)}, u32[]{:S(2)}, u32[]{:S(2)}) collective-permute-start(bf16[96,3840]{1,0:T(8,128)(2,1)S(1)} %bitcast.123), channel_id=1, source_target_pairs={{0,4},{4,0},{8,12},{12,8},{16,20},{20,16},{24,28},{28,24},{1,5},{5... | collective-permute-start | bytes 2211848 | tf_op jit(solution)/shard_map/ppermute | solution.py:399
  80.6 21.7 %collective-permute-start.20 = (bf16[96,3840]{1,0:T(8,128)(2,1)}, bf16[96,3840]{1,0:T(8,128)(2,1)S(1)}, u32[]{:S(2)}, u32[]{:S(2)}) collective-permute-start(bf16[96,3840]{1,0:T(8,128)(2,1)} %collective-permute-done.14.refs_2_), channel_id=1, source_target_pairs={{0,4},{4,0},{8,12},{12,8},{16,20},{20,16},{24,28},{28,24},{1,5},{5... | collective-permute-start | bytes 2211848 | tf_op jit(solution)/shard_map/ppermute | solution.py:399
  82.3 35.2 %collective-permute-start.15 = (bf16[96,6144]{1,0:T(8,128)(2,1)}, bf16[96,6144]{1,0:T(8,128)(2,1)}, u32[]{:S(2)}, u32[]{:S(2)}) collective-permute-start(bf16[96,6144]{1,0:T(8,128)(2,1)} %bitcast.29.refs_0_), channel_id=1, source_target_pairs={{0,8},{4,20},{8,0},{12,28},{16,24},{20,4},{24,16},{28,12},{1,9},{5... | collective-permute-start | bytes 3538952 | tf_op jit(solution)/shard_map/ppermute | solution.py:395
  94.6 22.9 %collective-permute-start.16 = (bf16[96,6144]{1,0:T(8,128)(2,1)}, bf16[96,6144]{1,0:T(8,128)(2,1)}, u32[]{:S(2)}, u32[]{:S(2)}) collective-permute-start(bf16[96,6144]{1,0:T(8,128)(2,1)} %bitcast.29.refs_0_), channel_id=1, source_target_pairs={{0,16},{4,12},{8,24},{12,4},{16,0},{20,28},{24,8},{28,20},{1,17},{... | collective-permute-start | bytes 3538952 | tf_op jit(solution)/shard_map/ppermute | solution.py:395
  117.5 23.7 %collective-permute-start.22 = (bf16[96,6144]{1,0:T(8,128)(2,1)}, bf16[96,6144]{1,0:T(8,128)(2,1)S(1)}, u32[]{:S(2)}, u32[]{:S(2)}) collective-permute-start(bf16[96,6144]{1,0:T(8,128)(2,1)} %collective-permute-done.15.refs_1_), channel_id=1, source_target_pairs={{0,16},{4,12},{8,24},{12,4},{16,0},{20,28},{24,8},{28,20},{1,17},{... | collective-permute-start | bytes 3538952 | tf_op jit(solution)/shard_map/ppermute | solution.py:395
  117.5 23.7 %collective-permute-start.24 = (bf16[96,6144]{1,0:T(8,128)(2,1)}, bf16[96,6144]{1,0:T(8,128)(2,1)}, u32[]{:S(2)}, u32[]{:S(2)}) collective-permute-start(bf16[96,6144]{1,0:T(8,128)(2,1)} %collective-permute-done.15.refs_1_), channel_id=1, source_target_pairs={{0,4},{4,0},{8,12},{12,8},{16,20},{20,16},{24,28},{28,24},{1,5},{5... | collective-permute-start | bytes 3538952 | tf_op jit(solution)/shard_map/ppermute | solution.py:399
  119.2 21.9 %collective-permute-start.23 = (bf16[96,6144]{1,0:T(8,128)(2,1)}, bf16[96,6144]{1,0:T(8,128)(2,1)}, u32[]{:S(2)}, u32[]{:S(2)}) collective-permute-start(bf16[96,6144]{1,0:T(8,128)(2,1)} %bitcast.29.refs_0_), channel_id=1, source_target_pairs={{0,4},{4,0},{8,12},{12,8},{16,20},{20,16},{24,28},{28,24},{1,5},{5... | collective-permute-start | bytes 3538952 | tf_op jit(solution)/shard_map/ppermute | solution.py:399
  119.2 21.9 %collective-permute-start.25 = (bf16[96,6144]{1,0:T(8,128)(2,1)}, bf16[96,6144]{1,0:T(8,128)(2,1)}, u32[]{:S(2)}, u32[]{:S(2)}) collective-permute-start(bf16[96,6144]{1,0:T(8,128)(2,1)} %collective-permute-done.16.refs_2_), channel_id=1, source_target_pairs={{0,4},{4,0},{8,12},{12,8},{16,20},{20,16},{24,28},{28,24},{1,5},{5... | collective-permute-start | bytes 3538952 | tf_op jit(solution)/shard_map/ppermute | solution.py:399
  141.2 10.9 %collective-permute-start.26 = (bf16[96,6144]{1,0:T(8,128)(2,1)S(1)}, bf16[96,6144]{1,0:T(8,128)(2,1)}, u32[]{:S(2)}, u32[]{:S(2)}) collective-permute-start(bf16[96,6144]{1,0:T(8,128)(2,1)S(1)} %collective-permute-done.22.refs_3_), channel_id=1, source_target_pairs={{0,4},{4,0},{8,12},{12,8},{16,20},{20,16},{24,28},{28,24},{1,5},{5... | collective-permute-start | bytes 3538952 | tf_op jit(solution)/shard_map/ppermute | solution.py:399
  196.2 18.5 %collective-permute-start.27 = (bf16[3,768,1024]{2,1,0:T(8,128)(2,1)}, bf16[3,768,1024]{2,1,0:T(8,128)(2,1)}, u32[]{:S(2)}, u32[]{:S(2)}) collective-permute-start(bf16[3,768,1024]{2,1,0:T(8,128)(2,1)} %get-tuple-element.271), channel_id=1, source_target_pairs={{0,4},{4,0},{8,12},{12,8},{16,20},{20,16},{24,28},{28,24},{1,5},{5... | collective-permute-start | bytes 14155784 | tf_op jit(solution)/shard_map/ppermute | solution.py:399
  224.4 29.2 %collective-permute-start.28 = (bf16[3,2,192,1024]{3,2,1,0:T(8,128)(2,1)}, bf16[3,2,192,1024]{3,2,1,0:T(8,128)(2,1)}, u32[]{:S(2)}, u32[]{:S(2)}) collective-permute-start(bf16[3,2,192,1024]{3,2,1,0:T(8,128)(2,1)} %get-tuple-element.287), channel_id=1, source_target_pairs={{0,16},{4,12},{8,24},{12,4},{16,0},{20,28},{24,8},{28,20},{1,17},{... | collective-permute-start | bytes 7077896 | tf_op jit(solution)/shard_map/ppermute | solution.py:395
  258.4 17.0 %collective-permute-start.30 = (bf16[3,1,192,1024]{3,2,1,0:T(8,128)(2,1)}, bf16[3,1,192,1024]{3,2,1,0:T(8,128)(2,1)}, u32[]{:S(2)}, u32[]{:S(2)}) collective-permute-start(bf16[3,1,192,1024]{3,2,1,0:T(8,128)(2,1)} %get-tuple-element.301), channel_id=1, source_target_pairs={{0,8},{4,20},{8,0},{12,28},{16,24},{20,4},{24,16},{28,12},{1,9},{5... | collective-permute-start | bytes 3538952 | tf_op jit(solution)/shard_map/ppermute | solution.py:395
  270.8 14.2 %collective-permute-start.29 = (bf16[5,768,384]{2,1,0:T(8,128)(2,1)}, bf16[5,768,384]{2,1,0:T(8,128)(2,1)S(1)}, u32[]{:S(2)}, u32[]{:S(2)}) collective-permute-start(bf16[5,768,384]{2,1,0:T(8,128)(2,1)} %get-tuple-element.299), channel_id=1, source_target_pairs={{0,4},{4,0},{8,12},{12,8},{16,20},{20,16},{24,28},{28,24},{1,5},{5... | collective-permute-start | bytes 8847368 | tf_op jit(solution)/shard_map/ppermute | solution.py:399
  270.8 102.9 %all-to-all-start.1 = ((bf16[4,256,768]{2,1,0:T(8,128)(2,1)}), bf16[4,256,768]{2,1,0:T(8,128)(2,1)}, u32[]{:S(2)}, u32[]{:S(2)}) async-start(bf16[4,256,768]{2,1,0:T(8,128)(2,1)} %bitcast.115), calls=%async_computation.1 | async-start | bytes 3145728 | tf_op jit(solution)/shard_map/all_to_all | solution.py:717
  279.1 51.5 %collective-permute-start.34 = (bf16[3,2,1,24,1024]{4,3,2,1,0:T(8,128)(2,1)}, bf16[3,2,1,24,1024]{4,3,2,1,0:T(8,128)(2,1)}, u32[]{:S(2)}, u32[]{:S(2)}) collective-permute-start(bf16[3,2,1,24,1024]{4,3,2,1,0:T(8,128)(2,1)} %get-tuple-element.339), channel_id=1, source_target_pairs={{0,1},{1,2},{2,3},{3,0},{4,5},{5,6},{6,7},{7,4},{8,9},{9,10},{10,1... | collective-permute-start | bytes 884744 | tf_op jit(solution)/shard_map/ppermute | solution.py:403
  281.2 51.6 %collective-permute-start.35 = (bf16[3,2,1,24,1024]{4,3,2,1,0:T(8,128)(2,1)}, bf16[3,2,1,24,1024]{4,3,2,1,0:T(8,128)(2,1)}, u32[]{:S(2)}, u32[]{:S(2)}) collective-permute-start(bf16[3,2,1,24,1024]{4,3,2,1,0:T(8,128)(2,1)} %get-tuple-element.340), channel_id=1, source_target_pairs={{0,2},{1,3},{2,0},{3,1},{4,6},{5,7},{6,4},{7,5},{8,10},{9,11},{10,... | collective-permute-start | bytes 884744 | tf_op jit(solution)/shard_map/ppermute | solution.py:403
  283.5 49.3 %collective-permute-start.36 = (bf16[3,2,1,24,1024]{4,3,2,1,0:T(8,128)(2,1)}, bf16[3,2,1,24,1024]{4,3,2,1,0:T(8,128)(2,1)}, u32[]{:S(2)}, u32[]{:S(2)}) collective-permute-start(bf16[3,2,1,24,1024]{4,3,2,1,0:T(8,128)(2,1)} %get-tuple-element.341), channel_id=1, source_target_pairs={{0,3},{1,0},{2,1},{3,2},{4,7},{5,4},{6,5},{7,6},{8,11},{9,8},{10,9... | collective-permute-start | bytes 884744 | tf_op jit(solution)/shard_map/ppermute | solution.py:403
  289.5 25.7 %collective-permute-start.32 = (bf16[5,2,192,384]{3,2,1,0:T(8,128)(2,1)}, bf16[5,2,192,384]{3,2,1,0:T(8,128)(2,1)}, u32[]{:S(2)}, u32[]{:S(2)}) collective-permute-start(bf16[5,2,192,384]{3,2,1,0:T(8,128)(2,1)} %get-tuple-element.322), channel_id=1, source_target_pairs={{0,16},{4,12},{8,24},{12,4},{16,0},{20,28},{24,8},{28,20},{1,17},{... | collective-permute-start | bytes 4423688 | tf_op jit(solution)/shard_map/ppermute | solution.py:395
  319.0 22.4 %collective-permute-start.38 = (bf16[5,1,192,384]{3,2,1,0:T(8,128)(2,1)S(1)}, bf16[5,1,192,384]{3,2,1,0:T(8,128)(2,1)S(1)}, u32[]{:S(2)}, u32[]{:S(2)}) collective-permute-start(bf16[5,1,192,384]{3,2,1,0:T(8,128)(2,1)S(1)} %get-tuple-element.351), channel_id=1, source_target_pairs={{0,8},{4,20},{8,0},{12,28},{16,24},{20,4},{24,16},{28,12},{1,9},{5... | collective-permute-start | bytes 2211848 | tf_op jit(solution)/shard_map/ppermute | solution.py:395
  321.2 18.3 %collective-permute-start.33 = (bf16[3,2,192,384]{3,2,1,0:T(8,128)(2,1)S(1)}, bf16[3,2,192,384]{3,2,1,0:T(8,128)(2,1)S(1)}, u32[]{:S(2)}, u32[]{:S(2)}) collective-permute-start(bf16[3,2,192,384]{3,2,1,0:T(8,128)(2,1)S(1)} %get-tuple-element.337), channel_id=1, source_target_pairs={{0,16},{4,12},{8,24},{12,4},{16,0},{20,28},{24,8},{28,20},{1,17},{... | collective-permute-start | bytes 2654216 | tf_op jit(solution)/shard_map/ppermute | solution.py:395
  340.3 8.4 %collective-permute-start.37 = (bf16[3,1,192,384]{3,2,1,0:T(8,128)(2,1)S(1)}, bf16[3,1,192,384]{3,2,1,0:T(8,128)(2,1)S(1)}, u32[]{:S(2)}, u32[]{:S(2)}) collective-permute-start(bf16[3,1,192,384]{3,2,1,0:T(8,128)(2,1)S(1)} %get-tuple-element.349), channel_id=1, source_target_pairs={{0,8},{4,20},{8,0},{12,28},{16,24},{20,4},{24,16},{28,12},{1,9},{5... | collective-permute-start | bytes 1327112 | tf_op jit(solution)/shard_map/ppermute | solution.py:395
  342.1 11.1 %collective-permute-start.42 = (bf16[5,2,1,24,384]{4,3,2,1,0:T(8,128)(2,1)S(1)}, bf16[5,2,1,24,384]{4,3,2,1,0:T(8,128)(2,1)S(1)}, u32[]{:S(2)}, u32[]{:S(2)}) collective-permute-start(bf16[5,2,1,24,384]{4,3,2,1,0:T(8,128)(2,1)S(1)} %get-tuple-element.371), channel_id=1, source_target_pairs={{0,1},{1,2},{2,3},{3,0},{4,5},{5,6},{6,7},{7,4},{8,9},{9,10},{10,1... | collective-permute-start | bytes 552968 | tf_op jit(solution)/shard_map/ppermute | solution.py:403
  344.5 15.0 %collective-permute-start.43 = (bf16[5,2,1,24,384]{4,3,2,1,0:T(8,128)(2,1)S(1)}, bf16[5,2,1,24,384]{4,3,2,1,0:T(8,128)(2,1)S(1)}, u32[]{:S(2)}, u32[]{:S(2)}) collective-permute-start(bf16[5,2,1,24,384]{4,3,2,1,0:T(8,128)(2,1)S(1)} %get-tuple-element.372), channel_id=1, source_target_pairs={{0,2},{1,3},{2,0},{3,1},{4,6},{5,7},{6,4},{7,5},{8,10},{9,11},{10,... | collective-permute-start | bytes 552968 | tf_op jit(solution)/shard_map/ppermute | solution.py:403
  346.0 13.5 %collective-permute-start.44 = (bf16[5,2,1,24,384]{4,3,2,1,0:T(8,128)(2,1)S(1)}, bf16[5,2,1,24,384]{4,3,2,1,0:T(8,128)(2,1)S(1)}, u32[]{:S(2)}, u32[]{:S(2)}) collective-permute-start(bf16[5,2,1,24,384]{4,3,2,1,0:T(8,128)(2,1)S(1)} %get-tuple-element.373), channel_id=1, source_target_pairs={{0,3},{1,0},{2,1},{3,2},{4,7},{5,4},{6,5},{7,6},{8,11},{9,8},{10,9... | collective-permute-start | bytes 552968 | tf_op jit(solution)/shard_map/ppermute | solution.py:403
  349.4 12.5 %collective-permute-start.39 = (bf16[3,2,1,24,384]{4,3,2,1,0:T(8,128)(2,1)S(1)}, bf16[3,2,1,24,384]{4,3,2,1,0:T(8,128)(2,1)S(1)}, u32[]{:S(2)}, u32[]{:S(2)}) collective-permute-start(bf16[3,2,1,24,384]{4,3,2,1,0:T(8,128)(2,1)S(1)} %get-tuple-element.367), channel_id=1, source_target_pairs={{0,1},{1,2},{2,3},{3,0},{4,5},{5,6},{6,7},{7,4},{8,9},{9,10},{10,1... | collective-permute-start | bytes 331784 | tf_op jit(solution)/shard_map/ppermute | solution.py:403
  351.7 18.2 %collective-permute-start.40 = (bf16[3,2,1,24,384]{4,3,2,1,0:T(8,128)(2,1)S(1)}, bf16[3,2,1,24,384]{4,3,2,1,0:T(8,128)(2,1)S(1)}, u32[]{:S(2)}, u32[]{:S(2)}) collective-permute-start(bf16[3,2,1,24,384]{4,3,2,1,0:T(8,128)(2,1)S(1)} %get-tuple-element.368), channel_id=1, source_target_pairs={{0,2},{1,3},{2,0},{3,1},{4,6},{5,7},{6,4},{7,5},{8,10},{9,11},{10,... | collective-permute-start | bytes 331784 | tf_op jit(solution)/shard_map/ppermute | solution.py:403
  353.2 16.8 %collective-permute-start.41 = (bf16[3,2,1,24,384]{4,3,2,1,0:T(8,128)(2,1)S(1)}, bf16[3,2,1,24,384]{4,3,2,1,0:T(8,128)(2,1)S(1)}, u32[]{:S(2)}, u32[]{:S(2)}) collective-permute-start(bf16[3,2,1,24,384]{4,3,2,1,0:T(8,128)(2,1)S(1)} %get-tuple-element.369), channel_id=1, source_target_pairs={{0,3},{1,0},{2,1},{3,2},{4,7},{5,4},{6,5},{7,6},{8,11},{9,8},{10,9... | collective-permute-start | bytes 331784 | tf_op jit(solution)/shard_map/ppermute | solution.py:403
  371.5 6.4 %collective-permute-start.52 = (f32[3,24,1024]{2,1,0:T(8,128)S(1)}, f32[3,24,1024]{2,1,0:T(8,128)S(1)}, u32[]{:S(2)}, u32[]{:S(2)}) collective-permute-start(f32[3,24,1024]{2,1,0:T(8,128)S(1)} %dynamic-slice_bitcast_fusion), channel_id=1, source_target_pairs={{0,4},{4,0},{8,12},{12,8},{16,20},{20,16},{24,28},{28,24},{1,5},{5... | collective-permute-start | bytes 884744 | tf_op jit(solution)/shard_map/ppermute | solution.py:399
  383.5 13.6 %collective-permute-start.51 = (f32[5,24,384]{2,1,0:T(8,128)S(1)}, f32[5,24,384]{2,1,0:T(8,128)S(1)}, u32[]{:S(2)}, u32[]{:S(2)}) collective-permute-start(f32[5,24,384]{2,1,0:T(8,128)S(1)} %dynamic-slice_bitcast_fusion.1), channel_id=1, source_target_pairs={{0,4},{4,0},{8,12},{12,8},{16,20},{20,16},{24,28},{28,24},{1,5},{5... | collective-permute-start | bytes 552968 | tf_op jit(solution)/shard_map/ppermute | solution.py:399
  386.2 10.9 %collective-permute-start.50 = (f32[3,24,384]{2,1,0:T(8,128)S(1)}, f32[3,24,384]{2,1,0:T(8,128)S(1)}, u32[]{:S(2)}, u32[]{:S(2)}) collective-permute-start(f32[3,24,384]{2,1,0:T(8,128)S(1)} %dynamic-slice_bitcast_fusion.2), channel_id=1, source_target_pairs={{0,4},{4,0},{8,12},{12,8},{16,20},{20,16},{24,28},{28,24},{1,5},{5... | collective-permute-start | bytes 331784 | tf_op jit(solution)/shard_map/ppermute | solution.py:399
  (78 other events, 619.7 us)
